TPU v7x, 32 devices: a whole 2x2x4 slice. The times are simulated.
32 devices in a mesh: seq: 8 (over y, x, core), chan: 4 (over z).
Axes of the slice: x: 2, y: 2, z: 4, core: 2. Of those that a mesh axis runs over, the one named last changes fastest.
Arguments:
- tokens: bfloat16 [4096, 2048], P(('seq', 'chan')), may hold values from -6 to 6
- norm_gains: bfloat16 [2, 2048], replicated, may hold values from 0.5 to 1.5
- conv_weight: bfloat16 [3, 2048], P(None, 'chan'), may hold values from -3 to 3
- in_weight: bfloat16 [3, 2048, 2048], P(None, None, 'chan'), may hold values from -0.125 to 0.125
- out_weight: bfloat16 [2048, 2048], P('chan'), may hold values from -0.125 to 0.125
- gate_up_weight: bfloat16 [2, 2048, 8192], P(None, None, 'chan'), may hold values from -0.125 to 0.125
- down_weight: bfloat16 [8192, 2048], P('chan'), may hold values from -0.0625 to 0.0625
- starts: int32 [10], replicated, may hold values from 0 to 4095, as said below
- cotangent: bfloat16 [4096, 2048], P(('seq', 'chan')), may hold values from -6 to 6
Outputs:
- block_output: bfloat16 [4096, 2048], P(('seq', 'chan'))
- input_grad: float32 [4096, 2048], P(('seq', 'chan'))
- gains_grad: float32 [2, 2048], replicated
- conv_grad: float32 [3, 2048], P(None, 'chan')
- in_weight_grad: float32 [3, 2048, 2048], P(None, 'seq', 'chan')
- out_weight_grad: float32 [2048, 2048], P('chan', 'seq')
- gate_up_grad: float32 [2, 2048, 8192], P(None, 'seq', 'chan')
- down_grad: float32 [8192, 2048], P('chan', 'seq')
Inputs may be any that keep to these rules, and one draw needn't show every extreme that they name: Positions where documents start, in no order and possibly repeated; position 0 starts the stream in any case. No document is longer than 2048 tokens and one is exactly 2048 long. No entry p has p % 512 < 2.
All inputs are finite; a program needn't handle non-finite values.
Results may differ from a plain program's by a relative error of at most 0.0099.
Values may be sent and summed in bfloat16 or wider, within the bound.
No kernel may reach another device: no remote copies, remote signals or barrier semaphores. Data moves between devices by JAX's collectives and lax.ppermute only.
A program may use at most 320 MiB of HBM per device.

v0:
```python
import jax
import jax.numpy as jnp
from jax import lax
from jax.sharding import PartitionSpec as P

EPS = 1e-05


def passed_along(block, axis, distance):
    devices = range(lax.axis_size(axis))
    route = [(i - distance, i) for i in devices if i - distance in devices]
    return lax.ppermute(block, axis, route)


def keep_masks(positions, starts):
    at_start = jnp.any(positions[:, None] == starts[None, :], axis=1)
    prev_start = jnp.any((positions - 1)[:, None] == starts[None, :], axis=1)
    keep_one = ((positions >= 1) & jnp.logical_not(at_start)).astype(jnp.float32)[:, None]
    keep_two = ((positions >= 2) & jnp.logical_not(at_start) & jnp.logical_not(prev_start)).astype(
        jnp.float32
    )[:, None]
    return (keep_one, keep_two)


def unit_rows(values):
    inv_scale = lax.rsqrt(jnp.mean(values * values, axis=-1, keepdims=True) + EPS)
    return (values * inv_scale, inv_scale)


def norm_back(grad_normed, unit_vals, inv_scale, gain_row):
    weighted = grad_normed * gain_row
    return inv_scale * (
        weighted - unit_vals * jnp.mean(weighted * unit_vals, axis=-1, keepdims=True)
    )


def on_device(
    tokens,
    norm_gains,
    conv_weight,
    in_weight,
    out_weight,
    gate_up_weight,
    down_weight,
    starts,
    cotangent,
):
    shard_rows = tokens.shape[0]
    chan_count = lax.axis_size("chan")
    seq_rows = shard_rows * chan_count
    chan_cols = conv_weight.shape[1]
    chan_index = lax.axis_index("chan")
    own_start = chan_index * shard_rows
    base_pos = lax.axis_index("seq") * seq_rows
    positions = base_pos + jnp.arange(seq_rows, dtype=jnp.int32)
    keep_one, keep_two = keep_masks(positions, starts)
    next_one, unused_one = keep_masks(positions + 1, starts)
    unused_two, next_two = keep_masks(positions + 2, starts)
    gain_one = norm_gains[0].astype(jnp.float32)
    gain_two = norm_gains[1].astype(jnp.float32)
    conv_taps = conv_weight.astype(jnp.float32)
    input_rows = tokens.astype(jnp.float32)
    unit_one, scale_one = unit_rows(input_rows)
    normed_own = (unit_one * gain_one).astype(jnp.bfloat16)
    normed_one, inputs_all, grad_out = (
        lax.all_gather(normed_own, "chan", axis=0, tiled=True),
        lax.all_gather(tokens, "chan", axis=0, tiled=True),
        lax.all_gather(cotangent, "chan", axis=0, tiled=True),
    )
    projected = jnp.einsum("td,kde->kte", normed_one, in_weight, preferred_element_type=jnp.float32)
    mixed_in = (projected[0] * projected[2]).astype(jnp.bfloat16)
    rim_rows = passed_along(mixed_in[seq_rows - 2 :], "seq", 1)
    extended = jnp.concatenate([rim_rows, mixed_in], axis=0).astype(jnp.float32)
    lag_one = keep_one * extended[1 : seq_rows + 1]
    lag_two = keep_two * extended[0:seq_rows]
    conv_out = conv_taps[0] * extended[2:] + conv_taps[1] * lag_one + conv_taps[2] * lag_two
    gated_mix = (projected[1] * conv_out).astype(jnp.bfloat16)
    mixer_out = lax.psum(jnp.dot(gated_mix, out_weight, preferred_element_type=jnp.float32), "chan")
    hidden_state = inputs_all.astype(jnp.float32) + mixer_out
    unit_two, scale_two = unit_rows(hidden_state)
    normed_two = (unit_two * gain_two).astype(jnp.bfloat16)
    state_own = lax.dynamic_slice_in_dim(hidden_state, own_start, shard_rows, 0)
    gate_up = jnp.einsum(
        "td,kdf->ktf", normed_two, gate_up_weight, preferred_element_type=jnp.float32
    )
    sigmoid_gate = jax.nn.sigmoid(gate_up[0])
    activated = gate_up[0] * sigmoid_gate
    hidden = (activated * gate_up[1]).astype(jnp.bfloat16)
    piece_rows = hidden
    ffn_own = lax.psum_scatter(
        jnp.dot(piece_rows, down_weight, preferred_element_type=jnp.float32),
        "chan",
        scatter_dimension=0,
        tiled=True,
    )
    block_output = (state_own + ffn_own).astype(jnp.bfloat16)
    grad_down = jnp.einsum("tf,td->fd", hidden, grad_out, preferred_element_type=jnp.float32)
    grad_hidden = jnp.einsum("td,fd->tf", grad_out, down_weight, preferred_element_type=jnp.float32)
    grad_gate = grad_hidden * gate_up[1] * sigmoid_gate * (1.0 + gate_up[0] * (1.0 - sigmoid_gate))
    grad_up = grad_hidden * activated
    grad_pair = jnp.stack([grad_gate, grad_up]).astype(jnp.bfloat16)
    grad_gate_up = jnp.einsum(
        "td,ktf->kdf", normed_two, grad_pair, preferred_element_type=jnp.float32
    )
    piece_rows = grad_pair
    grad_normed_two = lax.psum(
        jnp.einsum("ktf,kdf->td", piece_rows, gate_up_weight, preferred_element_type=jnp.float32),
        "chan",
    )
    grad_state = grad_out.astype(jnp.float32) + norm_back(
        grad_normed_two, unit_two, scale_two, gain_two
    )
    gain_two_part = jnp.sum(
        lax.dynamic_slice_in_dim(grad_normed_two * unit_two, own_start, shard_rows, 0), axis=0
    )
    grad_mix = grad_state.astype(jnp.bfloat16)
    grad_state_own = lax.dynamic_slice_in_dim(grad_state, own_start, shard_rows, 0)
    grad_out_weight = jnp.einsum(
        "te,td->ed", gated_mix, grad_mix, preferred_element_type=jnp.float32
    )
    grad_gated = jnp.einsum("td,ed->te", grad_mix, out_weight, preferred_element_type=jnp.float32)
    grad_conv = (grad_gated * projected[1]).astype(jnp.bfloat16)
    grad_c = grad_gated * conv_out
    rim_back = passed_along(grad_conv[:2], "seq", -1)
    ext_back = jnp.concatenate([grad_conv, rim_back], axis=0).astype(jnp.float32)
    grad_here = ext_back[:seq_rows]
    grad_mixed = (
        conv_taps[0] * grad_here
        + conv_taps[1] * next_one * ext_back[1 : seq_rows + 1]
        + conv_taps[2] * next_two * ext_back[2:]
    )
    tap_part = jnp.stack(
        [
            jnp.sum(grad_here * extended[2:], axis=0),
            jnp.sum(grad_here * lag_one, axis=0),
            jnp.sum(grad_here * lag_two, axis=0),
        ]
    )
    grad_projected = jnp.stack(
        [grad_mixed * projected[2], grad_c, grad_mixed * projected[0]]
    ).astype(jnp.bfloat16)
    grad_in_weight = jnp.einsum(
        "td,kte->kde", normed_one, grad_projected, preferred_element_type=jnp.float32
    )
    piece_rows = grad_projected
    grad_normed_one = lax.psum_scatter(
        jnp.einsum("kte,kde->td", piece_rows, in_weight, preferred_element_type=jnp.float32),
        "chan",
        scatter_dimension=0,
        tiled=True,
    )
    input_grad = grad_state_own + norm_back(grad_normed_one, unit_one, scale_one, gain_one)
    gain_one_part = jnp.sum(grad_normed_one * unit_one, axis=0)
    summed_grads = (
        lax.psum_scatter(grad_in_weight, "seq", scatter_dimension=1, tiled=True),
        lax.psum_scatter(grad_out_weight, "seq", scatter_dimension=1, tiled=True),
        lax.psum_scatter(grad_gate_up, "seq", scatter_dimension=1, tiled=True),
        lax.psum_scatter(grad_down, "seq", scatter_dimension=1, tiled=True),
    )
    padded_taps = jnp.zeros((3, chan_count, chan_cols), jnp.float32)
    padded_taps = lax.dynamic_update_slice_in_dim(padded_taps, tap_part[:, None, :], chan_index, 1)
    gains_grad, taps_total = lax.psum(
        (jnp.stack([gain_one_part, gain_two_part]), padded_taps.reshape(3, chan_count * chan_cols)),
        ("seq", "chan"),
    )
    conv_grad = lax.dynamic_slice_in_dim(
        taps_total.reshape(3, chan_count, chan_cols), chan_index, 1, 1
    ).reshape(3, chan_cols)
    return (
        block_output,
        input_grad,
        gains_grad,
        conv_grad,
        summed_grads[0],
        summed_grads[1],
        summed_grads[2],
        summed_grads[3],
    )


def solution(mesh):
    placed = (
        P(("seq", "chan"), None),
        P(),
        P(None, "chan"),
        P(None, None, "chan"),
        P("chan", None),
        P(None, None, "chan"),
        P("chan", None),
        P(),
        P(("seq", "chan"), None),
    )
    return jax.shard_map(
        on_device,
        mesh=mesh,
        in_specs=placed,
        out_specs=(
            P(("seq", "chan"), None),
            P(("seq", "chan"), None),
            P(),
            P(None, "chan"),
            P(None, "seq", "chan"),
            P("chan", "seq"),
            P(None, "seq", "chan"),
            P("chan", "seq"),
        ),
        check_vma=False,
    )
```

profile of v0, /device:TPU:0, one launch (start us, length us, event | category | flops | bytes accessed | tf_op | source)
XLA Modules:
  0.0 1140.2 jit_solution(6901339305219648687)
XLA Ops:
  7.2 1.4 fusion.20
  10.0 2.0 fusion.14
  14.5 46.4 %all-gather.6.cloned.1.call-done = bf16[512,2048]{1,0:T(8,128)(2,1)} async-done(((bf16[128,2048]{1,0:T(8,128)(2,1)}), bf16[512,2048]{1,0:T(8,128)(2,1)}) %all-gather.6.cloned.1.call-update) | async-done | bytes 2097168 | tf_op jit(solution)/shard_map/all_gather | solution.py:66
  60.8 6.2 fusion.7
  67.3 1.7 collective-permute-start
  70.0 1.5 multiply_convert_fusion.8
  72.2 3.3 fusion.50
  76.2 30.9 %all-gather.4.cloned.1.call-done = bf16[512,2048]{1,0:T(8,128)(2,1)} async-done(((bf16[128,2048]{1,0:T(8,128)(2,1)}), bf16[512,2048]{1,0:T(8,128)(2,1)}) %all-gather.4.cloned.1.call-update) | async-done | bytes 2097168 | tf_op jit(solution)/shard_map/all_gather | solution.py:67
  107.1 156.7 %all-reduce.4.cloned.1.call-done = f32[512,2048]{1,0:T(8,128)} async-done(((f32[512,2048]{1,0:T(8,128)}), f32[512,2048]{1,0:T(8,128)}) %all-reduce.4.cloned.1.call-update) | async-done | bytes 4194320 | tf_op jit(solution)/shard_map/psum | solution.py:78
  263.8 3.5 multiply_reduce_fusion.1
  267.6 1.6 copy-done.2
  269.2 2.0 copy-done.9
  271.2 15.0 %convolution_bitcast_fusion.2 = f32[2,512,2048]{2,1,0:T(8,128)} fusion(bf16[2,2048,2048]{2,1,0:T(8,128)(2,1)} %param.14, f32[512,2048]{1,0:T(8,128)S(1)} %broadcast_multiply_fusion, f32[2048]{0:T(1024)S(1)} %bitcast.108), kind=kOutput, calls=%fused_computation.2 | convolution fusion | flops 8592031744 | bytes 29368320 | tf_op jit(solution)/shard_map/td,kdf->ktf/dot_general | solution.py:83
  286.2 24.1 %all-gather.8.cloned.1.call-done = bf16[512,2048]{1,0:T(8,128)(2,1)} async-done(((bf16[128,2048]{1,0:T(8,128)(2,1)}), bf16[512,2048]{1,0:T(8,128)(2,1)}) %all-gather.8.cloned.1.call-update) | async-done | bytes 2097168 | tf_op jit(solution)/shard_map/all_gather | solution.py:68
  310.3 13.6 %fusion.6 = (bf16[1,512,2048]{2,1,0:T(8,128)(2,1)S(1)}, bf16[1,512,2048]{2,1,0:T(8,128)(2,1)S(1)}, bf16[512,2048]{1,0:T(8,128)(2,1)}) fusion(f32[2,512,2048]{2,1,0:T(8,128)} %convolution_bitcast_fusion.2, bf16[512,2048]{1,0:T(8,128)(2,1)} %all-gather.8.cloned.1.call-done, bf16[2048,2048]{1,0:T(8,128)(2,1)} %param.15), kind=kOutput, calls=%fused_computation.24 | convolution fusion | flops 4310695936 | bytes 25165824 | tf_op jit(solution)/shard_map/td,fd->tf/dot_general | solution.py:98
  323.8 1.3 copy-done.20
  325.8 13.9 %convolution_bitcast_fusion.4 = f32[512,2048]{1,0:T(8,128)} fusion(bf16[2,2048,2048]{2,1,0:T(8,128)(2,1)} %param.14, bf16[1,512,2048]{2,1,0:T(8,128)(2,1)S(1)} %get-tuple-element.42, bf16[1,512,2048]{2,1,0:T(8,128)(2,1)S(1)} %get-tuple-element.41), kind=kOutput, calls=%fused_computation.17 | convolution fusion | flops 8592031744 | bytes 25165824 | tf_op jit(solution)/shard_map/ktf,kdf->td/dot_general | solution.py:107
  339.9 10.6 fusion.51
  350.6 142.9 %all-reduce.6.cloned.1.call-done = f32[512,2048]{1,0:T(8,128)} async-done(((f32[512,2048]{1,0:T(8,128)}), f32[512,2048]{1,0:T(8,128)}) %all-reduce.6.cloned.1.call-update) | async-done | bytes 4194320 | tf_op jit(solution)/shard_map/psum | solution.py:106
  493.5 4.3 multiply_reduce_fusion
  498.1 1.3 copy-done.4
  499.4 2.7 multiply_add_fusion
  502.1 1.3 fusion.26
  504.2 1.3 copy-done.8
  506.2 1.6 collective-permute-start.1
  507.8 1.7 collective-permute-done.1
  509.7 1.1 multiply_reduce_fusion.4
  511.3 5.1 convolution_bitcast_fusion.3
  517.5 8.0 convolution_bitcast_fusion.1
  525.7 1.3 copy-done.21
  527.0 17.9 %convolution_bitcast_fusion = f32[2,2048,2048]{1,2,0:T(8,128)} fusion(bf16[1,512,2048]{2,1,0:T(8,128)(2,1)} %copy-done.22, bf16[1,512,2048]{2,1,0:T(8,128)(2,1)S(1)} %copy-done.21, f32[512,2048]{1,0:T(8,128)} %copy-done.9, f32[2048]{0:T(1024)S(1)} %bitcast.111), kind=kOutput, calls=%fused_computation | convolution fusion | flops 8594128896 | bytes 41951232 | tf_op jit(solution)/shard_map/td,ktf->kdf/dot_general | solution.py:102
  545.0 1.0 copy-done.11
  546.0 5.5 fusion.24
  551.5 1.5 copy-done.13
  553.1 9.9 fusion.52
  563.0 1.7 fusion.21
  564.8 7.3 reduce-scatter.7.cloned.1.call-done
  572.0 2.5 add_convert_fusion
  574.5 77.2 %reduce-scatter.9.cloned.1.call-done = f32[128,2048]{1,0:T(8,128)} async-done(((f32[512,2048]{1,0:T(8,128)}), f32[128,2048]{1,0:T(8,128)}) %reduce-scatter.9.cloned.1.call-update) | async-done | bytes 1048592 | tf_op jit(solution)/shard_map/reduce_scatter | solution.py:146
  651.7 1.6 fusion.19
  653.4 41.5 %all-reduce = (f32[2,2048]{1,0:T(2,128)}, f32[3,4,512]{2,0,1:T(4,128)S(1)}) all-reduce(f32[2,2048]{1,0:T(2,128)S(1)} %pad_maximum_fusion.6, f32[3,4,512]{2,0,1:T(4,128)S(1)} %fusion.33), channel_id=1, replica_groups=mesh['seq'=8,'chan'=4] {'seq','chan'}, use_global_device_ids=true, to_apply=%region_14.0 | all-reduce | flops 10240 | bytes 81920 | tf_op jit(solution)/shard_map/psum | solution.py:162
  695.4 2.9 fusion.18
  698.3 50.4 %reduce-scatter.11.cloned.1.call-done = f32[3,256,512]{1,2,0:T(8,128)} async-done(((f32[3,2048,512]{1,2,0:T(8,128)}), f32[3,256,512]{1,2,0:T(8,128)}) %reduce-scatter.11.cloned.1.call-update) | async-done | bytes 1572880 | tf_op jit(solution)/shard_map/reduce_scatter | solution.py:155
  748.8 3.2 copy.23
  751.9 205.7 %reduce-scatter.15.cloned.1.call-done = f32[2,256,2048]{1,2,0:T(8,128)} async-done(((f32[2,2048,2048]{1,2,0:T(8,128)}), f32[2,256,2048]{1,2,0:T(8,128)}) %reduce-scatter.15.cloned.1.call-update) | async-done | bytes 4194320 | tf_op jit(solution)/shard_map/reduce_scatter | solution.py:157
  957.6 5.3 copy.24
  962.9 50.1 %reduce-scatter.13.cloned.1.call-done = f32[512,256]{1,0:T(8,128)} async-done(((f32[512,2048]{1,0:T(8,128)}), f32[512,256]{1,0:T(8,128)}) %reduce-scatter.13.cloned.1.call-update) | async-done | bytes 524304 | tf_op jit(solution)/shard_map/reduce_scatter | solution.py:156
  1013.1 120.2 %reduce-scatter.17.cloned.1.call-done = f32[2048,256]{1,0:T(8,128)} async-done(((f32[2048,2048]{1,0:T(8,128)}), f32[2048,256]{1,0:T(8,128)}) %reduce-scatter.17.cloned.1.call-update) | async-done | bytes 2097168 | tf_op jit(solution)/shard_map/reduce_scatter | solution.py:158
  (89 shorter events, 12.3 us)
Async XLA Ops:
  7.2 65.1 %copy-start = (bf16[512,2048]{1,0:T(8,128)(2,1)S(1)}, bf16[512,2048]{1,0:T(8,128)(2,1)}, u32[]{:S(2)}) copy-start(bf16[512,2048]{1,0:T(8,128)(2,1)} %param.13) | copy-start | bytes 6291460
  7.2 53.7 %all-gather.6.cloned.1.call-start = ((), (), s32[]{:S(2)}) async-start(), calls=%async_computation.7 | async-start | bytes 2621440 | tf_op jit(solution)/shard_map/all_gather | solution.py:66
  8.6 0.8 copy-start.18
  9.4 0.6 copy-start.16
  12.1 95.0 %all-gather.4.cloned.1.call-start = ((), (), s32[]{:S(2)}) async-start(), calls=%async_computation.6 | async-start | bytes 2621440 | tf_op jit(solution)/shard_map/all_gather | solution.py:67
  12.8 251.0 %all-reduce.4.cloned.1.call-start = ((), (), s32[]{:S(2)}) async-start(), calls=%async_computation.8 | async-start | bytes 8388608 | tf_op jit(solution)/shard_map/psum | solution.py:78
  67.1 4.4 copy-start.7
  67.3 2.6 collective-permute-start
  71.4 0.8 copy-start.10
  75.5 234.7 %all-gather.8.cloned.1.call-start = ((), (), s32[]{:S(2)}) async-start(), calls=%async_computation.10 | async-start | bytes 2621440 | tf_op jit(solution)/shard_map/all_gather | solution.py:68
  76.1 417.4 %all-reduce.6.cloned.1.call-start = ((), (), s32[]{:S(2)}) async-start(), calls=%async_computation.11 | async-start | bytes 8388608 | tf_op jit(solution)/shard_map/psum | solution.py:106
  267.3 1.9 copy-start.2
  269.2 2.0 copy-start.9
  323.8 1.3 copy-start.20
  323.8 2.0 copy-start.22
  339.7 232.4 %reduce-scatter.7.cloned.1.call-start = ((), (), s32[]{:S(2)}) async-start(), calls=%async_computation.9 | async-start | bytes 5242880 | tf_op jit(solution)/shard_map/reduce_scatter | solution.py:90
  350.6 301.2 %reduce-scatter.9.cloned.1.call-start = ((), (), s32[]{:S(2)}) async-start(), calls=%async_computation.12 | async-start | bytes 5242880 | tf_op jit(solution)/shard_map/reduce_scatter | solution.py:146
  493.5 4.6 copy-start.3
  493.5 5.9 copy-start.4
  502.1 2.1 copy-start.5
  502.1 3.4 copy-start.8
  502.1 3.7 copy-start.12
  505.8 5.3 slice-start
  506.2 4.9 copy-start.14
  506.2 3.3 collective-permute-start.1
  509.7 1.7 slice-start.1
  516.4 1.0 copy-start.15
  516.4 232.3 %reduce-scatter.11.cloned.1.call-start = ((), (), s32[]{:S(2)}) async-start(), calls=%async_computation.13 | async-start | bytes 14155776 | tf_op jit(solution)/shard_map/reduce_scatter | solution.py:155
  525.4 1.6 copy-start.21
  525.4 432.2 %reduce-scatter.15.cloned.1.call-start = ((), (), s32[]{:S(2)}) async-start(), calls=%async_computation.15 | async-start | bytes 37748736 | tf_op jit(solution)/shard_map/reduce_scatter | solution.py:157
  544.9 1.0 copy-start.11
  544.9 468.1 %reduce-scatter.13.cloned.1.call-start = ((), (), s32[]{:S(2)}) async-start(), calls=%async_computation.14 | async-start | bytes 4718592 | tf_op jit(solution)/shard_map/reduce_scatter | solution.py:156
  551.5 1.6 copy-start.13
  551.5 581.7 %reduce-scatter.17.cloned.1.call-start = ((), (), s32[]{:S(2)}) async-start(), calls=%async_computation.16 | async-start | bytes 18874368 | tf_op jit(solution)/shard_map/reduce_scatter | solution.py:158
  563.0 88.7 %copy-start.6 = (bf16[128,2048]{1,0:T(8,128)(2,1)S(1)}, bf16[128,2048]{1,0:T(8,128)(2,1)}, u32[]{:S(2)}) copy-start(bf16[128,2048]{1,0:T(8,128)(2,1)} %param.9) | copy-start | bytes 1572868
  563.0 88.7 %copy-start.17 = (f32[1,2048]{1,0:T(1,128)S(1)}, f32[1,2048]{1,0:T(1,128)}, u32[]{:S(2)}) copy-start(f32[1,2048]{1,0:T(1,128)} %copy-done.16) | copy-start | bytes 24580
  563.0 88.7 %copy-start.19 = (f32[128]{0:T(128)S(1)}, f32[128]{0:T(128)}, u32[]{:S(2)}) copy-start(f32[128]{0:T(128)} %copy-done.18) | copy-start | bytes 1540
  748.8 384.5 %copy-start.1 = (bf16[512,2048]{1,0:T(8,128)(2,1)S(1)}, bf16[512,2048]{1,0:T(8,128)(2,1)}, u32[]{:S(2)}) copy-start(bf16[512,2048]{1,0:T(8,128)(2,1)} %param.13) | copy-start | bytes 6291460
Sparse Core Ops, SparseCore 0:
  12.2 48.6 all-gather.5
  62.4 44.6 all-gather.3
  110.0 153.6 all-reduce.3
  265.3 44.9 all-gather.7
  339.8 153.6 all-reduce.5
  496.2 75.7 reduce-scatter.6
  574.4 77.2 reduce-scatter.8
  655.2 93.5 reduce-scatter.10
  752.3 205.2 reduce-scatter.14
  961.7 51.2 reduce-scatter.12
  1017.2 115.9 reduce-scatter.16
where the time goes:
time: 1150 us; the launch traced here: 1140 us
  waiting for transfers between devices  916 us (80%)
  matrix products  110 us (10%)
  blocking collectives  41.5 us (4%)
  other arithmetic  28.2 us (2%)
  local copies, waits for them, and re-layouts  25.9 us (2%)
  between operations  14.6 us (1%)
    reduce_scatter x1, waiting for transfers between devices, on_device(): lax.psum_scatter(grad_gate_up, 'seq', scatter_dimension=1, tiled=True)  206 us
    psum x1, waiting for transfers between devices, on_device(): lax.psum(jnp.dot(gated_mix, out_weight, preferred_element_type=jnp.float3...  157 us
    psum x1, waiting for transfers between devices, on_device(): lax.psum(jnp.einsum('ktf,kdf->td', piece_rows, gate_up_weight, preferred_...  143 us
    reduce_scatter x1, waiting for transfers between devices, on_device(): lax.psum_scatter(grad_down, 'seq', scatter_dimension=1, tiled=True)  120 us
    reduce_scatter x1, waiting for transfers between devices, on_device(): lax.psum_scatter(jnp.einsum('kte,kde->td', piece_rows, in_weight, preferr...  77.2 us
    reduce_scatter x1, waiting for transfers between devices, on_device(): lax.psum_scatter(grad_in_weight, 'seq', scatter_dimension=1, tiled=True)  50.4 us
    reduce_scatter x1, waiting for transfers between devices, on_device(): lax.psum_scatter(grad_out_weight, 'seq', scatter_dimension=1, tiled=True)  50.1 us
    all_gather x1, waiting for transfers between devices, on_device(): lax.all_gather(normed_own, 'chan', axis=0, tiled=True)  46.4 us
  transfers between devices with their start and end apart: 13, of which 13 were waited for; matrix products, arithmetic and copies ran while one was open for 10% of the time, Pallas kernels for 0%

commit v1 on v0

v1 whole, which is shorter than its diff:
```python
import jax
import jax.numpy as jnp
from jax import lax
from jax.sharding import PartitionSpec as P

EPS = 1e-05
BF = jnp.bfloat16
F32 = jnp.float32


def passed_along(block, axis, distance):
    devices = range(lax.axis_size(axis))
    route = [(i - distance, i) for i in devices if i - distance in devices]
    return lax.ppermute(block, axis, route)


def swapped(block, axis, bit):
    return lax.ppermute(block, axis, [(i, i ^ bit) for i in range(lax.axis_size(axis))])


def summed(block, axis):
    bit = 1
    while bit < lax.axis_size(axis):
        block = block + swapped(block, axis, bit)
        bit *= 2
    return block


def keep_masks(positions, starts):
    at_start = jnp.any(positions[:, None] == starts[None, :], axis=1)
    prev_start = jnp.any((positions - 1)[:, None] == starts[None, :], axis=1)
    keep_one = ((positions >= 1) & jnp.logical_not(at_start)).astype(F32)[:, None]
    keep_two = ((positions >= 2) & jnp.logical_not(at_start) & jnp.logical_not(prev_start)).astype(
        F32
    )[:, None]
    return (keep_one, keep_two)


def unit_rows(values):
    inv_scale = lax.rsqrt(jnp.mean(values * values, axis=-1, keepdims=True) + EPS)
    return (values * inv_scale, inv_scale)


def norm_back(grad_normed, unit_vals, inv_scale, gain_row):
    weighted = grad_normed * gain_row
    return inv_scale * (
        weighted - unit_vals * jnp.mean(weighted * unit_vals, axis=-1, keepdims=True)
    )


def both_cores(block):
    return jnp.concatenate([block, swapped(block, "seq", 1)], axis=0)


def own_slices(block):
    count = lax.axis_size("seq")
    rows, width = block.shape
    split = block.reshape(rows, count // 2, 2, width // count)
    core = lax.axis_index("seq") % 2
    mine = lax.dynamic_index_in_dim(split, core, 2, keepdims=False)
    other = lax.dynamic_index_in_dim(split, 1 - core, 2, keepdims=False)
    return jnp.concatenate([mine, swapped(other, "seq", 1)], axis=0)


def scattered(product, slices, order):
    group = lax.axis_index("seq") // 2
    received = []
    for step, bit in enumerate(order):
        own = (group // bit) % 2
        keep = lax.dynamic_index_in_dim(slices, own, 1, keepdims=False)
        send = lax.dynamic_index_in_dim(slices, 1 - own, 1, keepdims=False)
        total = product(send)
        for earlier, owns in received:
            part = earlier
            for place, index in enumerate(owns):
                part = lax.dynamic_index_in_dim(part, index, 0, keepdims=False)
            part = lax.dynamic_index_in_dim(part, 1 - own, 0, keepdims=False)
            total = total + part.astype(F32)
        arrived = swapped(total.astype(BF), "seq", 2 * bit)
        received = [(earlier, owns + [own]) for earlier, owns in received] + [(arrived, [])]
        slices = keep
    total = product(slices)
    for earlier, owns in received:
        part = earlier
        for index in owns:
            part = lax.dynamic_index_in_dim(part, index, 0, keepdims=False)
        total = total + part.astype(F32)
    return total


def ordered(slices, order, bits):
    rows, groups, width = slices.shape
    split = slices.reshape((rows,) + (2,) * len(bits) + (width,))
    return jnp.transpose(split, (0, *[1 + bits.index(bit) for bit in order], len(bits) + 1))


def group_bits():
    groups = lax.axis_size("seq") // 2
    bits = []
    while groups > 1:
        groups //= 2
        bits.append(groups)
    return bits


def on_device(
    tokens,
    norm_gains,
    conv_weight,
    in_weight,
    out_weight,
    gate_up_weight,
    down_weight,
    starts,
    cotangent,
):
    shard_rows = tokens.shape[0]
    chan_count = lax.axis_size("chan")
    seq_rows = shard_rows * chan_count
    chan_cols = conv_weight.shape[1]
    chan_index = lax.axis_index("chan")
    base_pos = lax.axis_index("seq") * seq_rows
    positions = base_pos + jnp.arange(seq_rows, dtype=jnp.int32)
    keep_one, keep_two = keep_masks(positions, starts)
    next_one, unused_one = keep_masks(positions + 1, starts)
    unused_two, next_two = keep_masks(positions + 2, starts)
    gain_one = norm_gains[0].astype(F32)
    gain_two = norm_gains[1].astype(F32)
    conv_taps = conv_weight.astype(F32)
    bits = group_bits()
    orders = (bits[::-1], bits)

    inputs_all = lax.all_gather(tokens, "chan", axis=0, tiled=True)
    grad_out = lax.all_gather(cotangent, "chan", axis=0, tiled=True)
    input_rows = tokens.astype(F32)
    unit_all, scale_all = unit_rows(inputs_all.astype(F32))
    normed_one = (unit_all * gain_one).astype(BF)

    projected = jnp.einsum("td,kde->kte", normed_one, in_weight, preferred_element_type=F32)
    mixed_in = (projected[0] * projected[2]).astype(BF)
    rim_rows = passed_along(mixed_in[seq_rows - 2 :], "seq", 1)
    extended = jnp.concatenate([rim_rows, mixed_in], axis=0).astype(F32)
    lag_one = keep_one * extended[1 : seq_rows + 1]
    lag_two = keep_two * extended[0:seq_rows]
    conv_out = conv_taps[0] * extended[2:] + conv_taps[1] * lag_one + conv_taps[2] * lag_two
    gated_mix = (projected[1] * conv_out).astype(BF)
    mixer_own = lax.psum_scatter(
        jnp.dot(gated_mix, out_weight, preferred_element_type=F32).astype(BF),
        "chan",
        scatter_dimension=0,
        tiled=True,
    ).astype(F32)
    state_own = input_rows + mixer_own
    unit_two, scale_two = unit_rows(state_own)
    normed_two = lax.all_gather((unit_two * gain_two).astype(BF), "chan", axis=0, tiled=True)
    gate_up = jnp.einsum("td,kdf->ktf", normed_two, gate_up_weight, preferred_element_type=F32)
    sigmoid_gate = jax.nn.sigmoid(gate_up[0])
    activated = gate_up[0] * sigmoid_gate
    hidden = (activated * gate_up[1]).astype(BF)
    ffn_own = lax.psum_scatter(
        jnp.dot(hidden, down_weight, preferred_element_type=F32).astype(BF),
        "chan",
        scatter_dimension=0,
        tiled=True,
    ).astype(F32)
    block_output = (state_own + ffn_own).astype(BF)

    grad_hidden = jnp.einsum("td,fd->tf", grad_out, down_weight, preferred_element_type=F32)
    grad_gate = grad_hidden * gate_up[1] * sigmoid_gate * (1.0 + gate_up[0] * (1.0 - sigmoid_gate))
    grad_up = grad_hidden * activated
    grad_pair = jnp.stack([grad_gate, grad_up]).astype(BF)
    grad_two_own = lax.psum_scatter(
        jnp.einsum("ktf,kdf->td", grad_pair, gate_up_weight, preferred_element_type=F32).astype(BF),
        "chan",
        scatter_dimension=0,
        tiled=True,
    ).astype(F32)

    cot_slices = own_slices(grad_out)
    hidden_both = both_cores(hidden)
    half = hidden.shape[1] // 2
    down_parts = []
    for place, order in enumerate(orders):
        units = hidden_both[:, place * half : (place + 1) * half]
        down_parts.append(
            scattered(
                lambda s, u=units: jnp.moveaxis(
                    jnp.einsum("tf,t...d->f...d", u, s, preferred_element_type=F32), 0, -2
                ),
                ordered(cot_slices, order, bits),
                order,
            )
        )
    down_grad = jnp.concatenate(down_parts, axis=0)

    normed_two_slices = own_slices(normed_two)
    gate_up_parts = []
    for place, order in enumerate(orders):
        units = both_cores(grad_pair[place])
        gate_up_parts.append(
            scattered(
                lambda s, u=units: jnp.einsum("t...d,tf->...df", s, u, preferred_element_type=F32),
                ordered(normed_two_slices, order, bits),
                order,
            )
        )
    gate_up_grad = jnp.stack(gate_up_parts)

    grad_state_own = cotangent.astype(F32) + norm_back(grad_two_own, unit_two, scale_two, gain_two)
    gain_two_part = jnp.sum(grad_two_own * unit_two, axis=0)
    grad_mix = lax.all_gather(grad_state_own.astype(BF), "chan", axis=0, tiled=True)

    grad_gated = jnp.einsum("td,ed->te", grad_mix, out_weight, preferred_element_type=F32)
    grad_conv = (grad_gated * projected[1]).astype(BF)
    grad_c = grad_gated * conv_out
    rim_back = passed_along(grad_conv[:2], "seq", -1)
    ext_back = jnp.concatenate([grad_conv, rim_back], axis=0).astype(F32)
    grad_here = ext_back[:seq_rows]
    grad_mixed = (
        conv_taps[0] * grad_here
        + conv_taps[1] * next_one * ext_back[1 : seq_rows + 1]
        + conv_taps[2] * next_two * ext_back[2:]
    )
    tap_part = jnp.stack(
        [
            jnp.sum(grad_here * extended[2:], axis=0),
            jnp.sum(grad_here * lag_one, axis=0),
            jnp.sum(grad_here * lag_two, axis=0),
        ]
    )
    grad_projected = jnp.stack(
        [grad_mixed * projected[2], grad_c, grad_mixed * projected[0]]
    ).astype(BF)
    grad_one_part = jnp.einsum("kte,kde->td", grad_projected, in_weight, preferred_element_type=F32)
    grad_one_own = lax.psum_scatter(
        grad_one_part.astype(BF), "chan", scatter_dimension=0, tiled=True
    ).astype(F32)
    gain_one_part = jnp.sum(grad_one_part * unit_all, axis=0)

    mix_slices = own_slices(grad_mix)
    gated_both = both_cores(gated_mix)
    half = gated_mix.shape[1] // 2
    out_parts = []
    for place, order in enumerate(orders):
        chans = gated_both[:, place * half : (place + 1) * half]
        out_parts.append(
            scattered(
                lambda s, u=chans: jnp.moveaxis(
                    jnp.einsum("te,t...d->e...d", u, s, preferred_element_type=F32), 0, -2
                ),
                ordered(mix_slices, order, bits),
                order,
            )
        )
    out_grad = jnp.concatenate(out_parts, axis=0)

    normed_one_slices = own_slices(normed_one)
    grad_both = jnp.concatenate([grad_projected, swapped(grad_projected, "seq", 1)], axis=1)
    half = chan_cols // 2
    in_parts = []
    for place, order in enumerate(orders):
        chans = grad_both[:, :, place * half : (place + 1) * half]
        in_parts.append(
            scattered(
                lambda s, u=chans: jnp.einsum("t...d,kte->...kde", s, u, preferred_element_type=F32),
                ordered(normed_one_slices, order, bits),
                order,
            )
        )
    in_grad = jnp.concatenate(in_parts, axis=2)

    own_start = chan_index * shard_rows
    unit_one = lax.dynamic_slice_in_dim(unit_all, own_start, shard_rows, 0)
    scale_one = lax.dynamic_slice_in_dim(scale_all, own_start, shard_rows, 0)
    input_grad = grad_state_own + norm_back(grad_one_own, unit_one, scale_one, gain_one)

    small = summed(
        jnp.concatenate([jnp.concatenate([gain_one_part, gain_two_part]), tap_part.reshape(-1)]),
        "seq",
    )
    width = gain_one.shape[0]
    gains_grad = summed(small[: 2 * width], "chan").reshape(2, width)
    conv_grad = small[2 * width :].reshape(3, chan_cols)
    return (
        block_output,
        input_grad,
        gains_grad,
        conv_grad,
        in_grad,
        out_grad,
        gate_up_grad,
        down_grad,
    )


def solution(mesh):
    placed = (
        P(("seq", "chan"), None),
        P(),
        P(None, "chan"),
        P(None, None, "chan"),
        P("chan", None),
        P(None, None, "chan"),
        P("chan", None),
        P(),
        P(("seq", "chan"), None),
    )
    return jax.shard_map(
        on_device,
        mesh=mesh,
        in_specs=placed,
        out_specs=(
            P(("seq", "chan"), None),
            P(("seq", "chan"), None),
            P(),
            P(None, "chan"),
            P(None, "seq", "chan"),
            P("chan", "seq"),
            P(None, "seq", "chan"),
            P("chan", "seq"),
        ),
        check_vma=False,
    )
```

time: 1150 us -> 595 us (0.52)
  waiting for transfers between devices: 916 us -> 324 us
  blocking collectives: 41.5 us -> 0 us
  starting transfers between devices: 4.21 us -> 28.8 us
  local copies, waits for them, and re-layouts: 25.9 us -> 48.4 us
  matrix products: 110 us -> 128 us
    reduce_scatter x6 -> x4, waiting for transfers between devices: 511 us -> 87.3 us  [the longest x1 45 us: on_device(): lax.psum_scatter(jnp.dot(gated_mix, out_weight, preferred_element_type=F3...]
    psum x2 -> x0, waiting for transfers between devices: 300 us -> none  [the longest x1 157 us: on_device(): lax.psum(jnp.dot(gated_mix, out_weight, preferred_element_type=jnp.float3...]
    ppermute x0 -> x30, waiting for transfers between devices: none -> 67.2 us  [swapped(): lax.ppermute(block, axis, [(i, i ^ bit) for i in range(lax.axis_size(axis...]
    all_gather x3 -> x4, waiting for transfers between devices: 101 us -> 168 us  [the longest x1 47.9 us: on_device(): inputs_all = lax.all_gather(tokens, 'chan', axis=0, tiled=True)]
    psum x1 -> x0, blocking collectives: 41.5 us -> none  [on_device(): lax.psum((jnp.stack([gain_one_part, gain_two_part]), padded_taps.reshape(...]
    ppermute x0 -> x30, starting transfers between devices: none -> 24.9 us  [swapped(): lax.ppermute(block, axis, [(i, i ^ bit) for i in range(lax.axis_size(axis...]
    dynamic_slice x0 -> x6, local copies, waits for them, and re-layouts: none -> 21.6 us  [the longest x5 19.1 us: own_slices(): other = lax.dynamic_index_in_dim(split, 1 - core, 2, keepdims=False)]
    dot_general x11 -> x31, matrix products: 95.2 us -> 113 us  [the longest x6 28.9 us: on_device(): jnp.einsum('t...d,tf->...df', s, u, preferred_element_type=F32)]
  transfers between devices with their start and end apart: 13 -> 40, of which waited for: 13 -> 13; matrix products, arithmetic and copies ran while one was open for 10% -> 26% of each run, Pallas kernels for 0% -> 0%
where the time goes in v1:
time: 595 us; the launch traced here: 584 us
  waiting for transfers between devices  324 us (54%)
  matrix products  128 us (22%)
  local copies, waits for them, and re-layouts  48.4 us (8%)
  other arithmetic  38.7 us (7%)
  starting transfers between devices  28.8 us (5%)
  between operations  15.4 us (3%)
    ppermute x30, waiting for transfers between devices, swapped(): lax.ppermute(block, axis, [(i, i ^ bit) for i in range(lax.axis_size(axis...  67.2 us
    all_gather x1, waiting for transfers between devices, on_device(): inputs_all = lax.all_gather(tokens, 'chan', axis=0, tiled=True)  47.9 us
    all_gather x1, waiting for transfers between devices, on_device(): lax.all_gather(grad_state_own.astype(BF), 'chan', axis=0, tiled=True)  45.3 us
    reduce_scatter x1, waiting for transfers between devices, on_device(): lax.psum_scatter(jnp.dot(gated_mix, out_weight, preferred_element_type=F3...  45 us
    all_gather x1, waiting for transfers between devices, on_device(): lax.all_gather((unit_two * gain_two).astype(BF), 'chan', axis=0, tiled=True)  42.7 us
    reduce_scatter x1, waiting for transfers between devices, on_device(): lax.psum_scatter(jnp.einsum('ktf,kdf->td', grad_pair, gate_up_weight, pre...  42.2 us
    all_gather x1, waiting for transfers between devices, on_device(): grad_out = lax.all_gather(cotangent, 'chan', axis=0, tiled=True)  32.1 us
    dot_general x6, matrix products, on_device(): jnp.einsum('t...d,tf->...df', s, u, preferred_element_type=F32)  28.9 us
  transfers between devices with their start and end apart: 40, of which 13 were waited for; matrix products, arithmetic and copies ran while one was open for 26% of the time, Pallas kernels for 0%

profile of v1, /device:TPU:0, one launch (start us, length us, event | category | flops | bytes accessed | tf_op | source)
XLA Modules:
  0.0 583.8 jit_solution(14400713050944001544)
XLA Ops:
  10.4 47.9 %all-gather.5.cloned.1.call-done = bf16[512,2048]{1,0:T(8,128)(2,1)} async-done(((bf16[128,2048]{1,0:T(8,128)(2,1)}), bf16[512,2048]{1,0:T(8,128)(2,1)}) %all-gather.5.cloned.1.call-update) | async-done | bytes 2097168 | tf_op jit(solution)/shard_map/all_gather | solution.py:133
  58.3 2.2 fusion
  61.1 6.3 %fusion.33 = f32[3,512,512]{2,1,0:T(8,128)S(1)} fusion(bf16[3,2048,512]{2,1,0:T(8,128)(2,1)} %param.12, bf16[512,2048]{1,0:T(8,128)(2,1)S(1)} %multiply_convert_fusion.3), kind=kOutput, calls=%fused_computation.94 | convolution fusion | flops 3221225472 | bytes 11534336 | tf_op jit(solution)/shard_map/td,kde->kte/dot_general | solution.py:139
  72.6 2.6 convolution_convert_fusion.1
  75.3 45.0 %reduce-scatter.5.cloned.1.call-done = bf16[128,2048]{1,0:T(8,128)(2,1)} async-done(((bf16[512,2048]{1,0:T(8,128)(2,1)}), bf16[128,2048]{1,0:T(8,128)(2,1)}) %reduce-scatter.5.cloned.1.call-update) | async-done | bytes 524304 | tf_op jit(solution)/shard_map/reduce_scatter | solution.py:147
  121.8 2.2 multiply_convert_fusion.8
  124.0 2.0 copy.75
  126.7 42.7 %all-gather.7.cloned.1.call-done = bf16[512,2048]{1,0:T(8,128)(2,1)} async-done(((bf16[128,2048]{1,0:T(8,128)(2,1)}), bf16[512,2048]{1,0:T(8,128)(2,1)}) %all-gather.7.cloned.1.call-update) | async-done | bytes 2097168 | tf_op jit(solution)/shard_map/all_gather | solution.py:155
  169.4 15.0 %convolution_bitcast_fusion = f32[2,512,2048]{2,1,0:T(8,128)} fusion(bf16[2,2048,2048]{2,1,0:T(8,128)(2,1)} %param.14, bf16[512,2048]{1,0:T(8,128)(2,1)} %all-gather.7.cloned.1.call-done), kind=kOutput, calls=%fused_computation.2 | convolution fusion | flops 8589934592 | bytes 27262976 | tf_op jit(solution)/shard_map/td,kdf->ktf/dot_general | solution.py:156
  184.4 32.1 %all-gather.9.cloned.1.call-done = bf16[512,2048]{0,1:T(8,128)(2,1)} async-done(((bf16[128,2048]{0,1:T(8,128)(2,1)}), bf16[512,2048]{0,1:T(8,128)(2,1)}) %all-gather.9.cloned.1.call-update) | async-done | bytes 2097168 | tf_op jit(solution)/shard_map/all_gather | solution.py:134
  216.5 14.5 %multiply_convert_fusion.1 = (bf16[512,2048]{1,0:T(8,128)(2,1)}, bf16[512,2048]{1,0:T(8,128)(2,1)S(1)}, bf16[512,2048]{1,0:T(8,128)(2,1)}) fusion(f32[2,512,2048]{2,1,0:T(8,128)} %convolution_bitcast_fusion, bf16[512,2048]{0,1:T(8,128)(2,1)} %all-gather.9.cloned.1.call-done, bf16[2048,2048]{1,0:T(8,128)(2,1)} %param.15), kind=kOutput, calls=%fused_computation.24 | convolution fusion | flops 4310695936 | bytes 25165824 | tf_op jit(solution)/shard_map/td,fd->tf/dot_general | solution.py:168
  232.3 14.2 %bitcast_convert_fusion.1 = bf16[512,2048]{1,0:T(8,128)(2,1)} fusion(bf16[2,2048,2048]{2,1,0:T(8,128)(2,1)} %param.14, bf16[1,512,2048]{2,1,0:T(8,128)(2,1)S(1)} %bitcast.365, bf16[1,512,2048]{2,1,0:T(8,128)(2,1)} %bitcast.14), kind=kOutput, calls=%fused_computation.22 | convolution fusion | flops 8593080320 | bytes 23068672 | tf_op jit(solution)/shard_map/ktf,kdf->td/dot_general | solution.py:173
  246.6 42.2 %reduce-scatter.9.cloned.1.call-done = bf16[128,2048]{1,0:T(8,128)(2,1)} async-done(((bf16[512,2048]{1,0:T(8,128)(2,1)}), bf16[128,2048]{1,0:T(8,128)(2,1)}) %reduce-scatter.9.cloned.1.call-update) | async-done | bytes 524304 | tf_op jit(solution)/shard_map/reduce_scatter | solution.py:172
  290.7 2.8 fusion.205
  293.6 45.3 %all-gather.11.cloned.1.call-done = bf16[512,2048]{1,0:T(8,128)(2,1)} async-done(((bf16[128,2048]{1,0:T(8,128)(2,1)}), bf16[512,2048]{1,0:T(8,128)(2,1)}) %all-gather.11.cloned.1.call-update) | async-done | bytes 2097168 | tf_op jit(solution)/shard_map/all_gather | solution.py:211
  338.9 3.0 fusion.223
  341.9 2.6 fusion.122
  350.1 2.2 multiply_reduce_fusion.2
  353.9 8.3 %bitcast_convert_fusion = (bf16[512,2048]{1,0:T(8,128)(2,1)}, f32[512,2048,1]{1,0,2:T(8,128)}) fusion(bf16[3,2048,512]{2,1,0:T(8,128)(2,1)} %param.12, bf16[1,512,512]{2,1,0:T(8,128)(2,1)S(1)} %fusion.123, bf16[1,512,512]{2,1,0:T(8,128)(2,1)S(1)} %copy-done.16, bf16[1,512,512]{2,1,0:T(8,128)(2,1)S(1)} %get-tuple-element.66), kind=kOutput, calls=%fused_computation.20 | convolution fusion | flops 3223846912 | bytes 14155776 | tf_op jit(solution)/shard_map/kte,kde->td/dot_general | solution.py:234
  362.4 3.3 reshape.256
  365.7 5.7 constant_dynamic-slice_fusion.2
  373.1 3.3 reshape.254
  376.4 2.5 copy.94
  379.0 3.3 fusion.52
  384.3 2.7 fusion.55
  388.0 4.3 constant_dynamic-slice_fusion.6
  396.7 5.5 fusion.16
  402.8 6.6 %fusion.13 = bf16[2,256,2048]{2,1,0:T(8,128)(2,1)} fusion(bf16[512,2048]{1,0:T(8,128)(2,1)} %collective-permute-done.20, bf16[512,2048]{1,0:T(8,128)(2,1)} %get-tuple-element.53, s32[]{:T(128)S(6)} %select_n.177, bf16[512,2,2,256]{3,0,2,1:T(8,128)(2,1)S(1)} %bitcast.334, bf16[512,2,2,256]{3,0,2,1:T(8,128)(2,1)} %bitcast.70), kind=kOutput, calls=%fused_computation.70 | convolution fusion | flops 2159017984 | bytes 8388612 | tf_op jit(solution)/shard_map/t...d,tf->...df/dot_general | solution.py:202
  410.0 2.5 fusion.67
  414.0 3.2 fusion.66
  418.8 5.8 convolution_convert_fusion
  424.7 43.8 %collective-permute-done.31 = bf16[1024,256]{1,0:T(8,128)(2,1)} collective-permute-done((bf16[1024,256]{1,0:T(8,128)(2,1)S(1)}, bf16[1024,256]{1,0:T(8,128)(2,1)}, u32[]{:S(2)}, u32[]{:S(2)}) %collective-permute-start.31) | collective-permute-done | bytes 524320 | tf_op jit(solution)/shard_map/ppermute | solution.py:18
  468.5 2.7 fusion.58
  471.2 2.2 fusion.59
  476.1 4.2 fusion.24
  480.9 4.9 fusion.23
  487.2 4.7 reshape.255
  491.9 4.8 fusion.9
  496.8 6.5 %constant_dynamic-slice_fusion.4 = (bf16[512,4,1,256]{3,2,1,0:T(2,128)(2,1)S(1)}, bf16[512,4,1,256]{3,2,1,0:T(2,128)(2,1)S(1)}) fusion(bf16[512,4,2,256]{3,2,1,0:T(2,128)(2,1)} %reshape.255, s32[]{:T(128)S(6)} %select_n.168, s32[]{:T(128)S(6)} %select_n.167), kind=kLoop, calls=%fused_computation.258 | loop fusion | bytes 4194312 | tf_op jit(solution)/shard_map/jit(dynamic_index_in_dim)/dynamic_slice | solution.py:61
  508.9 3.6 fusion.22
  512.9 4.2 fusion.20
  517.5 2.0 collective-permute-start.6
  522.0 2.3 pad_maximum_fusion.2
  532.3 2.1 fusion.60
  535.3 2.0 fusion.63
  540.1 15.2 %collective-permute-done.16 = bf16[256,256]{1,0:T(8,128)(2,1)S(1)} collective-permute-done((bf16[256,256]{1,0:T(8,128)(2,1)S(1)}, bf16[256,256]{1,0:T(8,128)(2,1)S(1)}, u32[]{:S(2)}, u32[]{:S(2)}) %collective-permute-start.16) | collective-permute-done | bytes 131104 | tf_op jit(solution)/shard_map/ppermute | solution.py:18
  561.9 4.1 collective-permute-done.12
  573.1 3.7 multiply_add_fusion
  (216 shorter events, 73.9 us)
Async XLA Ops:
  7.2 65.4 %copy-start = (bf16[512,2048]{1,0:T(8,128)(2,1)S(1)}, bf16[512,2048]{1,0:T(8,128)(2,1)}, u32[]{:S(2)}) copy-start(bf16[512,2048]{1,0:T(8,128)(2,1)} %param.13) | copy-start | bytes 6291460
  7.2 51.1 %all-gather.5.cloned.1.call-start = ((), (), s32[]{:S(2)}) async-start(), calls=%async_computation.4 | async-start | bytes 2621440 | tf_op jit(solution)/shard_map/all_gather | solution.py:133
  7.9 112.4 %reduce-scatter.5.cloned.1.call-start = ((), (), s32[]{:S(2)}) async-start(), calls=%async_computation.5 | async-start | bytes 2621440 | tf_op jit(solution)/shard_map/reduce_scatter | solution.py:147
  10.4 50.7 %copy-start.26 = (f32[1,2048]{1,0:T(1,128)}, f32[1,2048]{1,0:T(1,128)S(1)}, u32[]{:S(2)}) copy-start(f32[1,2048]{1,0:T(1,128)S(1)} %get-tuple-element.73) | copy-start | bytes 24580
  67.6 2.6 collective-permute-start
  75.2 94.2 %all-gather.7.cloned.1.call-start = ((), (), s32[]{:S(2)}) async-start(), calls=%async_computation.6 | async-start | bytes 2621440 | tf_op jit(solution)/shard_map/all_gather | solution.py:155
  124.0 92.5 %all-gather.9.cloned.1.call-start = ((), (), s32[]{:S(2)}) async-start(), calls=%async_computation.8 | async-start | bytes 2621440 | tf_op jit(solution)/shard_map/all_gather | solution.py:134
  126.1 162.7 %reduce-scatter.9.cloned.1.call-start = ((), (), s32[]{:S(2)}) async-start(), calls=%async_computation.9 | async-start | bytes 2621440 | tf_op jit(solution)/shard_map/reduce_scatter | solution.py:172
  246.6 92.3 %all-gather.11.cloned.1.call-start = ((), (), s32[]{:S(2)}) async-start(), calls=%async_computation.10 | async-start | bytes 2621440 | tf_op jit(solution)/shard_map/all_gather | solution.py:211
  293.5 277.9 %reduce-scatter.11.cloned.1.call-start = ((), (), s32[]{:S(2)}) async-start(), calls=%async_computation.11 | async-start | bytes 2621440 | tf_op jit(solution)/shard_map/reduce_scatter | solution.py:235
  344.5 5.5 collective-permute-start.1
  348.3 30.6 %collective-permute-start.27 = (bf16[512,4,256]{2,0,1:T(8,128)(2,1)}, bf16[512,4,256]{2,0,1:T(8,128)(2,1)}, u32[]{:S(2)}, u32[]{:S(2)}) collective-permute-start(bf16[512,4,256]{2,0,1:T(8,128)(2,1)} %bitcast.340), channel_id=1, source_target_pairs={{0,4},{4,0},{8,12},{12,8},{16,20},{20,16},{24,28},{28,24},{1,5},{5... | collective-permute-start | bytes 3145736 | tf_op jit(solution)/shard_map/ppermute | solution.py:18
  349.4 46.7 %collective-permute-start.23 = (bf16[512,2048]{1,0:T(8,128)(2,1)}, bf16[512,2048]{1,0:T(8,128)(2,1)}, u32[]{:S(2)}, u32[]{:S(2)}) collective-permute-start(bf16[512,2048]{1,0:T(8,128)(2,1)} %copy-done.28), channel_id=1, source_target_pairs={{0,4},{4,0},{8,12},{12,8},{16,20},{20,16},{24,28},{28,24},{1,5},{5... | collective-permute-start | bytes 6291464 | tf_op jit(solution)/shard_map/ppermute | solution.py:18
  349.4 29.5 %collective-permute-start.26 = (bf16[512,2048]{1,0:T(8,128)(2,1)}, bf16[512,2048]{1,0:T(8,128)(2,1)}, u32[]{:S(2)}, u32[]{:S(2)}) collective-permute-start(bf16[512,2048]{1,0:T(8,128)(2,1)} %get-tuple-element.55), channel_id=1, source_target_pairs={{0,4},{4,0},{8,12},{12,8},{16,20},{20,16},{24,28},{28,24},{1,5},{5... | collective-permute-start | bytes 6291464 | tf_op jit(solution)/shard_map/ppermute | solution.py:18
  352.2 10.0 %copy-start.11 = (bf16[1,512,512]{2,1,0:T(8,128)(2,1)}, bf16[1,512,512]{2,1,0:T(8,128)(2,1)S(1)}, u32[]{:S(2)}) copy-start(bf16[1,512,512]{2,1,0:T(8,128)(2,1)S(1)} %get-tuple-element.66) | copy-start | bytes 1572868
  353.8 151.5 %copy-start.14 = (bf16[1,512,512]{2,1,0:T(8,128)(2,1)}, bf16[1,512,512]{2,1,0:T(8,128)(2,1)S(1)}, u32[]{:S(2)}) copy-start(bf16[1,512,512]{2,1,0:T(8,128)(2,1)S(1)} %fusion.123) | copy-start | bytes 1572868
  362.2 210.8 %reduce-scatter.7.cloned.1.call-start = ((), (), s32[]{:S(2)}) async-start(), calls=%async_computation.7 | async-start | bytes 2621440 | tf_op jit(solution)/shard_map/reduce_scatter | solution.py:160
  362.3 40.5 %collective-permute-start.20 = (bf16[512,2048]{1,0:T(8,128)(2,1)}, bf16[512,2048]{1,0:T(8,128)(2,1)}, u32[]{:S(2)}, u32[]{:S(2)}) collective-permute-start(bf16[512,2048]{1,0:T(8,128)(2,1)} %get-tuple-element.53), channel_id=1, source_target_pairs={{0,4},{4,0},{8,12},{12,8},{16,20},{20,16},{24,28},{28,24},{1,5},{5... | collective-permute-start | bytes 6291464 | tf_op jit(solution)/shard_map/ppermute | solution.py:18
  372.7 23.3 %collective-permute-start.19 = (bf16[512,4,256]{2,0,1:T(8,128)(2,1)}, bf16[512,4,256]{2,0,1:T(8,128)(2,1)}, u32[]{:S(2)}, u32[]{:S(2)}) collective-permute-start(bf16[512,4,256]{2,0,1:T(8,128)(2,1)} %bitcast.311), channel_id=1, source_target_pairs={{0,4},{4,0},{8,12},{12,8},{16,20},{20,16},{24,28},{28,24},{1,5},{5... | collective-permute-start | bytes 3145736 | tf_op jit(solution)/shard_map/ppermute | solution.py:18
  382.3 27.7 %collective-permute-start.30 = (bf16[2,1024,256]{2,1,0:T(8,128)(2,1)S(1)}, bf16[2,1024,256]{2,1,0:T(8,128)(2,1)S(1)}, u32[]{:S(2)}, u32[]{:S(2)}) collective-permute-start(bf16[2,1024,256]{2,1,0:T(8,128)(2,1)S(1)} %fusion.52), channel_id=1, source_target_pairs={{0,16},{4,20},{8,24},{12,28},{16,0},{20,4},{24,8},{28,12},{1,17},{... | collective-permute-start | bytes 3145736 | tf_op jit(solution)/shard_map/ppermute | solution.py:18
  386.9 27.1 %collective-permute-start.28 = (bf16[2,1024,256]{2,1,0:T(8,128)(2,1)S(1)}, bf16[2,1024,256]{2,1,0:T(8,128)(2,1)S(1)}, u32[]{:S(2)}, u32[]{:S(2)}) collective-permute-start(bf16[2,1024,256]{2,1,0:T(8,128)(2,1)S(1)} %fusion.55), channel_id=1, source_target_pairs={{0,8},{4,12},{8,0},{12,4},{16,24},{20,28},{24,16},{28,20},{1,9},{5... | collective-permute-start | bytes 3145736 | tf_op jit(solution)/shard_map/ppermute | solution.py:18
  396.0 136.3 %collective-permute-start.8 = (bf16[512,4,256]{2,0,1:T(8,128)(2,1)}, bf16[512,4,256]{2,0,1:T(8,128)(2,1)}, u32[]{:S(2)}, u32[]{:S(2)}) collective-permute-start(bf16[512,4,256]{2,0,1:T(8,128)(2,1)} %bitcast.313), channel_id=1, source_target_pairs={{0,4},{4,0},{8,12},{12,8},{16,20},{20,16},{24,28},{28,24},{1,5},{5... | collective-permute-start | bytes 3145736 | tf_op jit(solution)/shard_map/ppermute | solution.py:18
  402.2 72.7 %collective-permute-start.24 = (bf16[2,256,2048]{2,1,0:T(8,128)(2,1)}, bf16[2,256,2048]{2,1,0:T(8,128)(2,1)}, u32[]{:S(2)}, u32[]{:S(2)}) collective-permute-start(bf16[2,256,2048]{2,1,0:T(8,128)(2,1)} %fusion.16), channel_id=1, source_target_pairs={{0,16},{4,20},{8,24},{12,28},{16,0},{20,4},{24,8},{28,12},{1,17},{... | collective-permute-start | bytes 6291464 | tf_op jit(solution)/shard_map/ppermute | solution.py:18
  409.4 71.5 %collective-permute-start.21 = (bf16[2,256,2048]{2,1,0:T(8,128)(2,1)}, bf16[2,256,2048]{2,1,0:T(8,128)(2,1)}, u32[]{:S(2)}, u32[]{:S(2)}) collective-permute-start(bf16[2,256,2048]{2,1,0:T(8,128)(2,1)} %fusion.13), channel_id=1, source_target_pairs={{0,8},{4,12},{8,0},{12,4},{16,24},{20,28},{24,16},{28,20},{1,9},{5... | collective-permute-start | bytes 6291464 | tf_op jit(solution)/shard_map/ppermute | solution.py:18
  410.0 8.9 %slice-start = ((s8[8388608]{0:T(1024)(128)(4,1)}), s8[4194304]{0:T(1024)(128)(4,1)S(1)}, s32[]{:S(2)}) async-start(s8[8388608]{0:T(1024)(128)(4,1)} %bitcast.363), calls=%async_computation.12 | async-start | bytes 8388608
  412.5 56.0 %collective-permute-start.31 = (bf16[1024,256]{1,0:T(8,128)(2,1)S(1)}, bf16[1024,256]{1,0:T(8,128)(2,1)}, u32[]{:S(2)}, u32[]{:S(2)}) collective-permute-start(bf16[1024,256]{1,0:T(8,128)(2,1)S(1)} %fusion.67), channel_id=1, source_target_pairs={{0,8},{4,12},{8,0},{12,4},{16,24},{20,28},{24,16},{28,20},{1,9},{5... | collective-permute-start | bytes 1572872 | tf_op jit(solution)/shard_map/ppermute | solution.py:18
  417.3 53.9 %collective-permute-start.29 = (bf16[1024,256]{1,0:T(8,128)(2,1)}, bf16[1024,256]{1,0:T(8,128)(2,1)}, u32[]{:S(2)}, u32[]{:S(2)}) collective-permute-start(bf16[1024,256]{1,0:T(8,128)(2,1)} %fusion.66), channel_id=1, source_target_pairs={{0,16},{4,20},{8,24},{12,28},{16,0},{20,4},{24,8},{28,12},{1,17},{... | collective-permute-start | bytes 1572872 | tf_op jit(solution)/shard_map/ppermute | solution.py:18
  424.6 43.9 %copy-start.25 = (bf16[512,4,1,256]{3,0,1,2:T(8,128)(2,1)S(1)}, bf16[512,4,1,256]{3,0,1,2:T(8,128)(2,1)}, u32[]{:S(2)}) copy-start(bf16[512,4,1,256]{3,0,1,2:T(8,128)(2,1)} %copy.94) | copy-start | bytes 3145732
  424.6 46.5 %copy-start.33 = (bf16[512,2048]{1,0:T(8,128)(2,1)S(1)}, bf16[512,2048]{1,0:T(8,128)(2,1)}, u32[]{:S(2)}) copy-start(bf16[512,2048]{1,0:T(8,128)(2,1)} %get-tuple-element.55) | copy-start | bytes 6291460
  424.7 46.5 %copy-start.35 = (bf16[2,1024,256]{2,1,0:T(8,128)(2,1)S(1)}, bf16[2,1024,256]{2,1,0:T(8,128)(2,1)}, u32[]{:S(2)}) copy-start(bf16[2,1024,256]{2,1,0:T(8,128)(2,1)} %copy-done.34) | copy-start | bytes 3145732
  480.3 27.9 %collective-permute-start.25 = (bf16[256,2048]{1,0:T(8,128)(2,1)}, bf16[256,2048]{1,0:T(8,128)(2,1)}, u32[]{:S(2)}, u32[]{:S(2)}) collective-permute-start(bf16[256,2048]{1,0:T(8,128)(2,1)} %fusion.24), channel_id=1, source_target_pairs={{0,8},{4,12},{8,0},{12,4},{16,24},{20,28},{24,16},{28,20},{1,9},{5... | collective-permute-start | bytes 3145736 | tf_op jit(solution)/shard_map/ppermute | solution.py:18
  485.7 27.1 %collective-permute-start.22 = (bf16[256,2048]{1,0:T(8,128)(2,1)}, bf16[256,2048]{1,0:T(8,128)(2,1)}, u32[]{:S(2)}, u32[]{:S(2)}) collective-permute-start(bf16[256,2048]{1,0:T(8,128)(2,1)} %fusion.23), channel_id=1, source_target_pairs={{0,16},{4,20},{8,24},{12,28},{16,0},{20,4},{24,8},{28,12},{1,17},{... | collective-permute-start | bytes 3145736 | tf_op jit(solution)/shard_map/ppermute | solution.py:18
  496.7 7.6 %collective-permute-start.2 = (f32[5632]{0:T(1024)S(1)}, f32[5632]{0:T(1024)S(1)}, u32[]{:S(2)}, u32[]{:S(2)}) collective-permute-start(f32[5632]{0:T(1024)S(1)} %pad_maximum_fusion.16), channel_id=1, source_target_pairs={{0,4},{4,0},{8,12},{12,8},{16,20},{20,16},{24,28},{28,24},{1,5},{5... | collective-permute-start | bytes 67592 | tf_op jit(solution)/shard_map/ppermute | solution.py:18
  503.7 15.7 %collective-permute-start.14 = (bf16[512,4,256]{2,0,1:T(8,128)(2,1)S(1)}, bf16[512,4,256]{2,0,1:T(8,128)(2,1)S(1)}, u32[]{:S(2)}, u32[]{:S(2)}) collective-permute-start(bf16[512,4,256]{2,0,1:T(8,128)(2,1)S(1)} %bitcast.339), channel_id=1, source_target_pairs={{0,4},{4,0},{8,12},{12,8},{16,20},{20,16},{24,28},{28,24},{1,5},{5... | collective-permute-start | bytes 3145736 | tf_op jit(solution)/shard_map/ppermute | solution.py:18
  504.3 3.9 collective-permute-start.3
  508.2 22.3 %collective-permute-start.7 = (bf16[3,512,512]{2,1,0:T(8,128)(2,1)}, bf16[3,512,512]{2,1,0:T(8,128)(2,1)}, u32[]{:S(2)}, u32[]{:S(2)}) collective-permute-start(bf16[3,512,512]{2,1,0:T(8,128)(2,1)} %pad_maximum_fusion.6), channel_id=1, source_target_pairs={{0,4},{4,0},{8,12},{12,8},{16,20},{20,16},{24,28},{28,24},{1,5},{5... | collective-permute-start | bytes 4718600 | tf_op jit(solution)/shard_map/ppermute | solution.py:18
  508.2 4.3 collective-permute-start.4
  512.5 6.9 %collective-permute-start.13 = (bf16[512,512]{1,0:T(8,128)(2,1)S(1)}, bf16[512,512]{1,0:T(8,128)(2,1)S(1)}, u32[]{:S(2)}, u32[]{:S(2)}) collective-permute-start(bf16[512,512]{1,0:T(8,128)(2,1)S(1)} %copy-done.7), channel_id=1, source_target_pairs={{0,4},{4,0},{8,12},{12,8},{16,20},{20,16},{24,28},{28,24},{1,5},{5... | collective-permute-start | bytes 1572872 | tf_op jit(solution)/shard_map/ppermute | solution.py:18
  512.8 4.6 collective-permute-start.5
  517.5 7.5 %collective-permute-start.6 = (f32[4096]{0:T(1024)S(1)}, f32[4096]{0:T(1024)S(1)}, u32[]{:S(2)}, u32[]{:S(2)}) collective-permute-start(f32[4096]{0:T(1024)S(1)} %slice_add_fusion), channel_id=1, source_target_pairs={{0,2},{1,3},{2,0},{3,1},{4,6},{5,7},{6,4},{7,5},{8,10},{9,11},{10,... | collective-permute-start | bytes 49160 | tf_op jit(solution)/shard_map/ppermute | solution.py:18
  520.6 8.2 %collective-permute-start.17 = (bf16[2,256,256]{2,1,0:T(8,128)(2,1)}, bf16[2,256,256]{2,1,0:T(8,128)(2,1)S(1)}, u32[]{:S(2)}, u32[]{:S(2)}) collective-permute-start(bf16[2,256,256]{2,1,0:T(8,128)(2,1)} %fusion.87), channel_id=1, source_target_pairs={{0,16},{4,20},{8,24},{12,28},{16,0},{20,4},{24,8},{28,12},{1,17},{... | collective-permute-start | bytes 786440 | tf_op jit(solution)/shard_map/ppermute | solution.py:18
  526.0 12.7 %collective-permute-start.15 = (bf16[2,256,256]{2,1,0:T(8,128)(2,1)S(1)}, bf16[2,256,256]{2,1,0:T(8,128)(2,1)S(1)}, u32[]{:S(2)}, u32[]{:S(2)}) collective-permute-start(bf16[2,256,256]{2,1,0:T(8,128)(2,1)S(1)} %fusion.86), channel_id=1, source_target_pairs={{0,8},{4,12},{8,0},{12,4},{16,24},{20,28},{24,16},{28,20},{1,9},{5... | collective-permute-start | bytes 786440 | tf_op jit(solution)/shard_map/ppermute | solution.py:18
  529.1 10.6 %collective-permute-start.18 = (bf16[256,256]{1,0:T(8,128)(2,1)S(1)}, bf16[256,256]{1,0:T(8,128)(2,1)S(1)}, u32[]{:S(2)}, u32[]{:S(2)}) collective-permute-start(bf16[256,256]{1,0:T(8,128)(2,1)S(1)} %fusion.89), channel_id=1, source_target_pairs={{0,8},{4,12},{8,0},{12,4},{16,24},{20,28},{24,16},{28,20},{1,9},{5... | collective-permute-start | bytes 393224 | tf_op jit(solution)/shard_map/ppermute | solution.py:18
  534.4 21.3 %collective-permute-start.11 = (bf16[2,3,256,256]{2,3,1,0:T(8,128)(2,1)S(1)}, bf16[2,3,256,256]{2,3,1,0:T(8,128)(2,1)S(1)}, u32[]{:S(2)}, u32[]{:S(2)}) collective-permute-start(bf16[2,3,256,256]{2,3,1,0:T(8,128)(2,1)S(1)} %fusion.60), channel_id=1, source_target_pairs={{0,16},{4,20},{8,24},{12,28},{16,0},{20,4},{24,8},{28,12},{1,17},{... | collective-permute-start | bytes 2359304 | tf_op jit(solution)/shard_map/ppermute | solution.py:18
  537.3 20.7 %collective-permute-start.9 = (bf16[2,3,256,256]{2,3,1,0:T(8,128)(2,1)S(1)}, bf16[2,3,256,256]{2,3,1,0:T(8,128)(2,1)S(1)}, u32[]{:S(2)}, u32[]{:S(2)}) collective-permute-start(bf16[2,3,256,256]{2,3,1,0:T(8,128)(2,1)S(1)} %fusion.63), channel_id=1, source_target_pairs={{0,8},{4,12},{8,0},{12,4},{16,24},{20,28},{24,16},{28,20},{1,9},{5... | collective-permute-start | bytes 2359304 | tf_op jit(solution)/shard_map/ppermute | solution.py:18
  539.0 16.2 %collective-permute-start.16 = (bf16[256,256]{1,0:T(8,128)(2,1)S(1)}, bf16[256,256]{1,0:T(8,128)(2,1)S(1)}, u32[]{:S(2)}, u32[]{:S(2)}) collective-permute-start(bf16[256,256]{1,0:T(8,128)(2,1)S(1)} %fusion.88), channel_id=1, source_target_pairs={{0,16},{4,20},{8,24},{12,28},{16,0},{20,4},{24,8},{28,12},{1,17},{... | collective-permute-start | bytes 393224 | tf_op jit(solution)/shard_map/ppermute | solution.py:18
  557.2 8.7 %collective-permute-start.12 = (bf16[3,256,256]{1,2,0:T(8,128)(2,1)S(1)}, bf16[3,256,256]{1,2,0:T(8,128)(2,1)S(1)}, u32[]{:S(2)}, u32[]{:S(2)}) collective-permute-start(bf16[3,256,256]{1,2,0:T(8,128)(2,1)S(1)} %fusion.75), channel_id=1, source_target_pairs={{0,8},{4,12},{8,0},{12,4},{16,24},{20,28},{24,16},{28,20},{1,9},{5... | collective-permute-start | bytes 1179656 | tf_op jit(solution)/shard_map/ppermute | solution.py:18
  559.6 8.5 %collective-permute-start.10 = (bf16[3,256,256]{1,2,0:T(8,128)(2,1)S(1)}, bf16[3,256,256]{1,2,0:T(8,128)(2,1)S(1)}, u32[]{:S(2)}, u32[]{:S(2)}) collective-permute-start(bf16[3,256,256]{1,2,0:T(8,128)(2,1)S(1)} %fusion.74), channel_id=1, source_target_pairs={{0,16},{4,20},{8,24},{12,28},{16,0},{20,4},{24,8},{28,12},{1,17},{... | collective-permute-start | bytes 1179656 | tf_op jit(solution)/shard_map/ppermute | solution.py:18
  (31 other events, 111.1 us)
Sparse Core Ops, SparseCore 0:
  9.6 48.6 all-gather.4
  75.3 44.9 reduce-scatter.4
  124.1 45.2 all-gather.6
  171.5 44.9 all-gather.8
  246.7 42.0 reduce-scatter.8
  293.6 45.2 all-gather.10
  362.3 42.5 reduce-scatter.10
  424.8 41.3 reduce-scatter.6

commit v2 on v0

v2 whole, which is shorter than its diff:
```python
import functools

import jax
import jax.numpy as jnp
from jax import lax
from jax.experimental import pallas as pl
from jax.experimental.pallas import tpu as pltpu
from jax.sharding import PartitionSpec as P

EPS = 1e-05
BF = jnp.bfloat16
F32 = jnp.float32
MIB = 2**20
VMEM = 48


def params(mebibytes):
    return pltpu.CompilerParams(vmem_limit_bytes=mebibytes * MIB)


def cost():
    return pl.CostEstimate(flops=1024, bytes_accessed=1024, transcendentals=0)


def dot(a, b, dim_a, dim_b):
    return lax.dot_general(a, b, (((dim_a,), (dim_b,)), ((), ())), preferred_element_type=F32)


def after(value, *earlier):
    return lax.optimization_barrier((value,) + earlier)[0]


def passed_along(block, axis, distance):
    devices = range(lax.axis_size(axis))
    route = [(i - distance, i) for i in devices if i - distance in devices]
    return lax.ppermute(block, axis, route)


def turned(block, axis, distance):
    count = lax.axis_size(axis)
    return lax.ppermute(block, axis, [(i, (i + distance) % count) for i in range(count)])


def swapped(block, axis, bit):
    return lax.ppermute(block, axis, [(i, i ^ bit) for i in range(lax.axis_size(axis))])


def summed(block, axis, bit=1):
    while bit < lax.axis_size(axis):
        block = block + swapped(block, axis, bit)
        bit *= 2
    return block


def keep_masks(positions, starts):
    at_start = jnp.any(positions[..., None] == starts, axis=-1)
    prev_start = jnp.any((positions - 1)[..., None] == starts, axis=-1)
    keep_one = ((positions >= 1) & jnp.logical_not(at_start)).astype(F32)[..., None]
    keep_two = ((positions >= 2) & jnp.logical_not(at_start) & jnp.logical_not(prev_start)).astype(
        F32
    )[..., None]
    return (keep_one, keep_two)


def unit_rows(values):
    inv_scale = lax.rsqrt(jnp.mean(values * values, axis=-1, keepdims=True) + EPS)
    return (values * inv_scale, inv_scale)


def norm_back(grad_normed, unit_vals, inv_scale, gain_row):
    weighted = grad_normed * gain_row
    return inv_scale * (
        weighted - unit_vals * jnp.mean(weighted * unit_vals, axis=-1, keepdims=True)
    )


def group_bits():
    groups = lax.axis_size("seq") // 2
    bits = []
    while groups > 1:
        groups //= 2
        bits.append(groups)
    return bits


def ffn_body(count, joining, ids, *refs):
    normed = refs[:count]
    cots = refs[count : 2 * count]
    gate_up_w, down_w = refs[2 * count : 2 * count + 2]
    outs = refs[2 * count + 2 + joining :]
    hidden_ref, pair_ref = outs[:2]
    ffn_refs, grad_refs = outs[2 : 2 + count], outs[2 + count : 2 + 2 * count]
    normed_all, cot_all, ffn_acc, grad_acc = outs[2 + 2 * count :]
    step = pl.program_id(0)
    rows = normed[0].shape[0]

    @pl.when(step == 0)
    def _():
        for place in range(count):
            normed_all[pl.ds(place * rows, rows), :] = normed[place][...]
            cot_all[pl.ds(place * rows, rows), :] = cots[place][...]

    gate = dot(normed_all[...], gate_up_w[0], 1, 0)
    up = dot(normed_all[...], gate_up_w[1], 1, 0)
    grad_hidden = dot(cot_all[...], down_w[...], 1, 1)
    sig = jax.nn.sigmoid(gate)
    activated = gate * sig
    hidden = (activated * up).astype(BF)
    hidden_ref[0] = hidden
    grad_gate = (grad_hidden * up * sig * (1.0 + gate * (1.0 - sig))).astype(BF)
    grad_up = (grad_hidden * activated).astype(BF)
    pair_ref[0] = grad_gate
    pair_ref[1] = grad_up
    ffn_part = dot(hidden, down_w[...], 1, 0)
    grad_part = dot(grad_gate, gate_up_w[0], 1, 1) + dot(grad_up, gate_up_w[1], 1, 1)

    @pl.when(step == 0)
    def _():
        ffn_acc[...] = ffn_part
        grad_acc[...] = grad_part

    @pl.when(step > 0)
    def _():
        ffn_acc[...] += ffn_part
        grad_acc[...] += grad_part

    @pl.when(step == pl.num_programs(0) - 1)
    def _():
        for place in range(count):
            own = pl.ds(place * rows, rows)
            ffn_refs[place][...] = ffn_acc[own, :].astype(BF)
            grad_refs[place][...] = grad_acc[own, :].astype(BF)


def feed_forward(owner, normed, cots, gate_up_weight, down_weight, first, total, joined, tile=512):
    count = len(normed)
    rows, width = normed[0].shape
    units = down_weight.shape[0]
    here, all_rows = count * rows, total * rows
    place = first // count
    block = pl.BlockSpec((rows, width), lambda j, ids: (0, 0))
    anywhere = pl.BlockSpec(memory_space=pl.ANY)
    results = pl.pallas_call(
        functools.partial(ffn_body, count, len(joined)),
        grid_spec=pltpu.PrefetchScalarGridSpec(
            num_scalar_prefetch=1,
            grid=(units // tile,),
            in_specs=[block] * count
            + [
                pl.BlockSpec((rows, width), lambda j, ids, r=first + r: (ids[r], 0))
                for r in range(count)
            ]
            + [
                pl.BlockSpec((2, width, tile), lambda j, ids: (0, 0, j)),
                pl.BlockSpec((tile, width), lambda j, ids: (j, 0)),
            ]
            + [anywhere] * len(joined),
            out_specs=[
                pl.BlockSpec((1, here, tile), lambda j, ids: (0, place, j)),
                pl.BlockSpec((2, here, tile), lambda j, ids: (0, place, j)),
            ]
            + [block] * (2 * count),
            scratch_shapes=[
                pltpu.VMEM((here, width), BF),
                pltpu.VMEM((here, width), BF),
                pltpu.VMEM((here, width), F32),
                pltpu.VMEM((here, width), F32),
            ],
        ),
        out_shape=[
            jax.ShapeDtypeStruct((1, all_rows, units), BF),
            jax.ShapeDtypeStruct((2, all_rows, units), BF),
        ]
        + [jax.ShapeDtypeStruct((rows, width), BF)] * (2 * count),
        input_output_aliases={2 * count + 3 + k: k for k in range(len(joined))},
        compiler_params=params(VMEM),
        cost_estimate=cost(),
        name="feed_forward",
    )(owner, *normed, *([cots] * count), gate_up_weight, down_weight, *joined)
    return results[0], results[1], results[2 : 2 + count], results[2 + count :]


def slices_body(count, groups, part, apart, ids, *refs):
    ins, outs = refs[:-2], refs[-2:]
    rows = outs[0].shape[0] // count
    for r in range(count):
        here = pl.ds(r * rows, rows)
        if apart:
            source, there = ins[r], slice(None)
        else:
            source = ins[0]
            there = pl.ds(pl.multiple_of(ids[2 * groups + r] * rows, rows), rows)
        for half in range(2):
            for slot in range(groups):
                start = pl.multiple_of(ids[half * groups + slot] * part, part)
                outs[half][here, slot * part : (slot + 1) * part] = source[
                    there, pl.ds(start, part)
                ]


def own_slices(blocks, owner=None):
    seq = lax.axis_size("seq")
    groups = seq // 2
    place = lax.axis_index("seq")
    core, group = place % 2, place // 2
    chips = jnp.bitwise_xor(group, jnp.arange(groups, dtype=jnp.int32))
    mine, other = 2 * chips + core, 2 * chips + 1 - core
    apart = owner is None
    if apart:
        count = len(blocks)
        owner = jnp.zeros((count,), jnp.int32)
        rows = blocks[0].shape[0]
    else:
        count = owner.shape[0]
        rows = blocks.shape[0] // count
        blocks = [blocks]
    width = blocks[0].shape[1]
    part = width // seq
    if part % 128:
        if apart:
            full = jnp.concatenate(blocks, axis=0)
        else:
            full = jnp.concatenate(
                [
                    lax.dynamic_slice_in_dim(blocks[0], owner[r] * rows, rows, 0)
                    for r in range(count)
                ],
                axis=0,
            )
        full = full.reshape(count * rows, seq, part)
        picked = [
            jnp.take(full, ids, axis=1).reshape(count * rows, groups * part)
            for ids in (mine, other)
        ]
    else:
        ids = jnp.concatenate([mine, other, owner]).astype(jnp.int32)
        picked = pl.pallas_call(
            functools.partial(slices_body, count, groups, part, apart),
            in_specs=[pl.BlockSpec(memory_space=pltpu.SMEM)]
            + [pl.BlockSpec(memory_space=pltpu.VMEM)] * len(blocks),
            out_specs=[pl.BlockSpec(memory_space=pltpu.VMEM)] * 2,
            out_shape=[jax.ShapeDtypeStruct((count * rows, groups * part), BF)] * 2,
            compiler_params=params(VMEM),
            cost_estimate=cost(),
            name="own_slices",
        )(ids, *blocks)
    return picked[0], swapped(picked[1], "seq", 1)


def product_body(slots, part, tiles, tall, *refs):
    own, rec, units_own, units_rec = refs[:4]
    outs = refs[4:]
    step = pl.program_id(0)
    for half in range(2):

        @pl.when((step < tiles) if half == 0 else (step >= tiles))
        def _():
            for kind in range(2):
                out = outs[2 * half + kind]
                for place, slot in enumerate(slots[half][kind]):
                    columns = slice(slot * part, (slot + 1) * part)
                    if tall:
                        total = dot(units_own[0], own[:, columns], 0, 0) + dot(
                            units_rec[0], rec[:, columns], 0, 0
                        )
                    else:
                        total = dot(own[:, columns], units_own[0], 0, 0) + dot(
                            rec[:, columns], units_rec[0], 0, 0
                        )
                    out[place] = total.astype(BF)


class Joined:
    def __init__(self, lhs, units, orders, part, tall=False, piece=0, pieces=1):
        rows, slotted = lhs[0].shape
        groups = slotted // part
        kinds, _, wide = units[0].shape
        wide = wide // pieces
        tile = next(t for t in (512, 256, 128) if (kinds * wide // 2) % t == 0 and wide % t == 0)
        each = wide // tile
        tiles = kinds * each // 2
        slots = tuple(self.slots(order) for order in orders)
        whole = pl.BlockSpec((rows, slotted), lambda j: (0, 0))
        column = pl.BlockSpec((1, rows, tile), lambda j: (j // each, 0, piece * each + j % each))
        here = groups // 2
        shapes, specs = [], []
        for half in range(2):
            for kind in range(2):

                def at(j, half=half):
                    return (
                        jnp.minimum(j, tiles - 1) if half == 0 else jnp.maximum(j - tiles, 0)
                    )

                if tall:
                    shape, block = (here, tiles * tile, part), (here, tile, part)
                    specs.append(pl.BlockSpec(block, lambda j, at=at: (0, at(j), 0)))
                else:
                    shape, block = (here, part, tiles * tile), (here, part, tile)
                    specs.append(pl.BlockSpec(block, lambda j, at=at: (0, 0, at(j))))
                shapes.append(jax.ShapeDtypeStruct(shape, BF))
        outs = pl.pallas_call(
            functools.partial(product_body, slots, part, tiles, tall),
            grid=(2 * tiles,),
            in_specs=[whole, whole, column, column],
            out_specs=specs,
            out_shape=shapes,
            compiler_params=params(VMEM),
            cost_estimate=cost(),
            name="product",
        )(*lhs, *units)
        self.orders, self.tall = orders, tall
        self.sent = [outs[0], outs[2]]
        self.kept = [[outs[1]], [outs[3]]]
        self.made = outs[0]
        self.done = 0

    def slots(self, order):
        slots = [0]
        for bit in reversed(order):
            slots = slots + [slot + bit for slot in slots]
        half = len(slots) // 2
        return tuple(slots[half:]), tuple(slots[:half])

    def send(self, *earlier):
        self.arrived = []
        for half in range(2):
            bit = 2 * self.orders[half][self.done]
            sent = after(self.sent[half], *earlier) if earlier else self.sent[half]
            arrived = swapped(sent, "seq", bit)
            self.arrived.append(arrived)
            self.kept[half].append(arrived)
        self.done += 1

    def add(self, *earlier):
        kept = [list(arrays) for arrays in self.kept]
        if earlier:
            kept[0][0] = after(kept[0][0], *earlier)
        left = len(self.orders[0]) - self.done
        self.sent = upper_sums(kept, 2 ** (left - 1))
        self.made = self.sent[0]

    def finish(self, *earlier):
        while self.done < len(self.orders[0]):
            self.add(*earlier)
            self.send()
        kept = [list(arrays) for arrays in self.kept]
        if earlier:
            kept[0][0] = after(kept[0][0], *earlier)
        return kept


def sums_body(counts, tiles, *refs):
    ins, outs = refs[: sum(counts)], refs[sum(counts) :]
    step = pl.program_id(0)
    start = 0
    for source, count in enumerate(counts):
        arrays = ins[start : start + count]
        start += count
        out = outs[source] if len(outs) > 1 else outs[0]

        @pl.when(step // tiles == source)
        def _():
            total = arrays[0][...].astype(F32)
            for array in arrays[1:]:
                total = total + array[...].astype(F32)
            out[...] = total.reshape(out.shape).astype(out.dtype)


def source_tile(step, source, tiles):
    return jnp.clip(step - source * tiles, 0, tiles - 1)


def upper_sums(sources, here):
    _, rows, columns = sources[0][0].shape
    tiles = 2
    block = (here, rows // tiles, columns)
    in_specs, arrays = [], []
    for source, parts in enumerate(sources):
        for array in parts:
            in_specs.append(
                pl.BlockSpec(block, lambda j, s=source: (1, source_tile(j, s, tiles), 0))
            )
            arrays.append(array)
    return pl.pallas_call(
        functools.partial(sums_body, [len(parts) for parts in sources], tiles),
        grid=(len(sources) * tiles,),
        in_specs=in_specs,
        out_specs=[
            pl.BlockSpec(block, lambda j, s=source: (0, source_tile(j, s, tiles), 0))
            for source in range(len(sources))
        ],
        out_shape=[jax.ShapeDtypeStruct((here, rows, columns), BF)] * len(sources),
        compiler_params=params(VMEM),
        cost_estimate=cost(),
        name="upper_sums",
    )(*arrays)


def final_sums(sources, tall, shape):
    _, rows, columns = sources[0][0].shape
    if tall:
        tile = min(512, rows)
        tiles = rows // tile
        block, out_block = (1, tile, columns), (tile, columns)
        out_spec = pl.BlockSpec(out_block, lambda j: (j, 0))

        def at(j, s):
            return (0, source_tile(j, s, tiles), 0)
    else:
        tile = next(t for t in (512, 256, 128) if columns % t == 0 and shape[2] % t == 0)
        tiles = columns // tile
        each = shape[2] // tile
        block, out_block = (1, rows, tile), (1, rows, tile)
        out_spec = pl.BlockSpec(out_block, lambda j: (j // each, 0, j % each))

        def at(j, s):
            return (0, 0, source_tile(j, s, tiles))

    in_specs, arrays = [], []
    for source, parts in enumerate(sources):
        for array in parts:
            in_specs.append(pl.BlockSpec(block, lambda j, s=source: at(j, s)))
            arrays.append(array)
    return pl.pallas_call(
        functools.partial(sums_body, [len(parts) for parts in sources], tiles),
        grid=(len(sources) * tiles,),
        in_specs=in_specs,
        out_specs=out_spec,
        out_shape=jax.ShapeDtypeStruct(shape, F32),
        compiler_params=params(VMEM),
        cost_estimate=cost(),
        name="final_sums",
    )(*arrays)


def ring_body(a, b, out):
    out[...] = (a[...].astype(F32) + b[...].astype(F32)).astype(BF)


def ring_sum(arrived, own):
    rows, width = own.shape
    spec = pl.BlockSpec((rows // 2, width), lambda j: (j, 0))
    return pl.pallas_call(
        ring_body,
        grid=(2,),
        in_specs=[spec, spec],
        out_specs=spec,
        out_shape=jax.ShapeDtypeStruct((rows, width), BF),
        compiler_params=params(VMEM),
        cost_estimate=cost(),
        name="ring_sum",
    )(arrived, own)


def back_body(count, *refs):
    grads, weights = refs[:2]
    toks = refs[2 : 2 + count]
    scale_ref = refs[2 + count]
    outs = refs[3 + count : 3 + 2 * count]
    gains_ref = refs[3 + 2 * count]
    rows = toks[0].shape[0]
    total = dot(grads[0], weights[0], 1, 1)
    for kind in range(1, grads.shape[0]):
        total = total + dot(grads[kind], weights[kind], 1, 1)
    gains = None
    for place in range(count):
        here = total[place * rows : (place + 1) * rows]
        outs[place][...] = here.astype(BF)
        unit = toks[place][...].astype(F32) * scale_ref[pl.ds(place * rows, rows), :]
        part = jnp.sum(here * unit, axis=0, keepdims=True)
        gains = part if gains is None else gains + part
    gains_ref[...] = gains


def mixer_back(grads, weights, toks, scale, tile=512):
    kinds, all_rows, chans = grads.shape
    width = weights.shape[1]
    count = len(toks)
    rows = all_rows // count
    block = pl.BlockSpec((rows, tile), lambda j: (0, j))
    results = pl.pallas_call(
        functools.partial(back_body, count),
        grid=(width // tile,),
        in_specs=[
            pl.BlockSpec((kinds, all_rows, chans), lambda j: (0, 0, 0)),
            pl.BlockSpec((kinds, tile, chans), lambda j: (0, j, 0)),
        ]
        + [block] * count
        + [pl.BlockSpec((all_rows, 1), lambda j: (0, 0))],
        out_specs=[block] * count + [pl.BlockSpec((1, tile), lambda j: (0, j))],
        out_shape=[jax.ShapeDtypeStruct((rows, width), BF)] * count
        + [jax.ShapeDtypeStruct((1, width), F32)],
        compiler_params=params(VMEM),
        cost_estimate=cost(),
        name="mixer_back",
    )(grads, weights, *toks, scale)
    return results[:count], results[count][0]


def full_others(others):
    seq = lax.axis_size("seq")
    stacked = jnp.stack(others, axis=1)
    stacked = stacked.reshape((seq,) + stacked.shape[2:])
    slots = jnp.bitwise_xor(lax.axis_index("seq"), jnp.arange(seq, dtype=jnp.int32))
    full = jnp.transpose(jnp.take(stacked, slots, axis=0), (1, 2, 0, 3))
    return full.reshape(full.shape[:2] + (-1,))


def plane_ids():
    place = lax.axis_index("seq")
    groups = lax.axis_size("seq") // 2
    chips = jnp.bitwise_xor(place // 2, jnp.arange(groups, dtype=jnp.int32))
    return jnp.concatenate([chips, (place % 2)[None]]).astype(jnp.int32)


def core_columns(ids, groups, kind, part, base=0):
    core = ids[groups]
    offset = jnp.where(core == kind, 0, part)
    return pl.ds(pl.multiple_of(base + offset, part), part)


def mixer_body(count, ids, *refs):
    gated = refs[:count]
    own_w, same_w, cross_w, rows_ref, gain_ref, state_ref, normed_ref, scale_ref = refs[count:]
    step = pl.program_id(0)
    part = same_w.shape[3]
    groups = pl.num_programs(0)
    base = pl.multiple_of(step * 2 * part, 2 * part)
    for kind, other_w in enumerate((same_w, cross_w)):
        inner = core_columns(ids, groups, kind, part)
        total = dot(gated[0][...], own_w[:, inner], 1, 0)
        for place in range(1, count):
            total = total + dot(gated[place][...], other_w[0, count - 1 - place], 1, 0)
        columns = core_columns(ids, groups, kind, part, base)
        state_ref[:, columns] = total + rows_ref[:, columns].astype(F32)

    @pl.when(step == groups - 1)
    def _():
        state = state_ref[...]
        scale = lax.rsqrt(jnp.mean(state * state, axis=-1, keepdims=True) + EPS)
        normed_ref[...] = (state * scale * gain_ref[...]).astype(BF)
        scale_ref[...] = scale


def mixer_rows(gated, own_w, others, input_rows, gain):
    count = len(gated)
    rows, width = input_rows.shape
    chans = gated[0].shape[1]
    groups, _, _, part = others[0].shape
    if part % 128:
        full = full_others(others)
        total = dot(gated[0], own_w, 1, 0)
        for r in range(1, count):
            total = total + dot(gated[r], full[count - 1 - r], 1, 0)
        state = input_rows.astype(F32) + total
        unit, scale = unit_rows(state)
        return state, (unit * gain).astype(BF), scale
    full_rows = pl.BlockSpec((rows, width), lambda t, ids: (0, 0))
    weights = pl.BlockSpec((1, count - 1, chans, part), lambda t, ids: (ids[t], 0, 0, 0))
    return pl.pallas_call(
        functools.partial(mixer_body, count),
        grid_spec=pltpu.PrefetchScalarGridSpec(
            num_scalar_prefetch=1,
            grid=(groups,),
            in_specs=[pl.BlockSpec((rows, chans), lambda t, ids: (0, 0))] * count
            + [
                pl.BlockSpec((chans, 2 * part), lambda t, ids: (0, t)),
                weights,
                weights,
                full_rows,
                pl.BlockSpec((1, width), lambda t, ids: (0, 0)),
            ],
            out_specs=[full_rows, full_rows, pl.BlockSpec((rows, 1), lambda t, ids: (0, 0))],
        ),
        out_shape=[
            jax.ShapeDtypeStruct((rows, width), F32),
            jax.ShapeDtypeStruct((rows, width), BF),
            jax.ShapeDtypeStruct((rows, 1), F32),
        ],
        compiler_params=params(VMEM),
        cost_estimate=cost(),
        name="mixer_rows",
    )(plane_ids(), *gated, own_w, *others, input_rows, gain.reshape(1, width))


def gated_body(count, ids, *refs):
    own_w, same_w, cross_w, arrived, part_own, state_ref, scale_ref, cot_ref, gain_ref = refs[:9]
    outs = refs[9 : 9 + count]
    grad_ref, mix_ref, gains_ref = refs[9 + count : 12 + count]
    accs = refs[12 + count :]
    step = pl.program_id(0)
    part = same_w.shape[3]
    groups = pl.num_programs(0)

    @pl.when(step == 0)
    def _():
        grad_normed = arrived[...].astype(F32) + part_own[...].astype(F32)
        unit = state_ref[...] * scale_ref[...]
        weighted = grad_normed * gain_ref[...]
        grad = cot_ref[...].astype(F32) + scale_ref[...] * (
            weighted - unit * jnp.mean(weighted * unit, axis=-1, keepdims=True)
        )
        grad_ref[...] = grad
        mix_ref[...] = grad.astype(BF)
        gains_ref[...] = jnp.sum(grad_normed * unit, axis=0, keepdims=True)
        for acc in accs:
            acc[...] = jnp.zeros_like(acc)

    base = pl.multiple_of(step * 2 * part, 2 * part)
    mix = [
        mix_ref[:, core_columns(ids, groups, kind, part, base)] for kind in range(2)
    ]
    accs[0][...] += dot(mix_ref[:, pl.ds(base, 2 * part)], own_w[...], 1, 1)
    for place in range(1, count):
        accs[place][...] += dot(mix[0], same_w[0, count - 1 - place], 1, 1) + dot(
            mix[1], cross_w[0, count - 1 - place], 1, 1
        )

    @pl.when(step == groups - 1)
    def _():
        for out, acc in zip(outs, accs):
            out[...] = acc[...].astype(BF)


def gated_rows(arrived, part_own, state, scale, cot, gain, own_w, others):
    rows, width = state.shape
    chans = own_w.shape[0]
    groups, less, _, part = others[0].shape
    count = less + 1
    if part % 128:
        full = full_others(others)
        grad_normed = arrived.astype(F32) + part_own.astype(F32)
        unit = state * scale
        grad = cot.astype(F32) + norm_back(grad_normed, unit, scale, gain)
        mix = grad.astype(BF)
        outs = [dot(mix, own_w, 1, 1).astype(BF)] + [
            dot(mix, full[count - 1 - r], 1, 1).astype(BF) for r in range(1, count)
        ]
        return outs, grad, mix, jnp.sum(grad_normed * unit, axis=0)
    full_rows = pl.BlockSpec((rows, width), lambda t, ids: (0, 0))
    one_row = pl.BlockSpec((1, width), lambda t, ids: (0, 0))
    weights = pl.BlockSpec((1, less, chans, part), lambda t, ids: (ids[t], 0, 0, 0))
    results = pl.pallas_call(
        functools.partial(gated_body, count),
        grid_spec=pltpu.PrefetchScalarGridSpec(
            num_scalar_prefetch=1,
            grid=(groups,),
            in_specs=[
                pl.BlockSpec((chans, 2 * part), lambda t, ids: (0, t)),
                weights,
                weights,
                full_rows,
                full_rows,
                full_rows,
                pl.BlockSpec((rows, 1), lambda t, ids: (0, 0)),
                full_rows,
                one_row,
            ],
            out_specs=[pl.BlockSpec((rows, chans), lambda t, ids: (0, 0))] * count
            + [full_rows, full_rows, one_row],
            scratch_shapes=[pltpu.VMEM((rows, chans), F32)] * count,
        ),
        out_shape=[jax.ShapeDtypeStruct((rows, chans), BF)] * count
        + [
            jax.ShapeDtypeStruct((rows, width), F32),
            jax.ShapeDtypeStruct((rows, width), BF),
            jax.ShapeDtypeStruct((1, width), F32),
        ],
        compiler_params=params(VMEM),
        cost_estimate=cost(),
        name="gated_rows",
    )(plane_ids(), own_w, *others, arrived, part_own, state, scale, cot, gain.reshape(1, width))
    return results[:count], results[count], results[count + 1], results[count + 2][0]


def on_device(
    tokens,
    norm_gains,
    conv_weight,
    in_weight,
    out_weight,
    gate_up_weight,
    down_weight,
    starts,
    cotangent,
):
    shard_rows, width = tokens.shape
    chan_count = lax.axis_size("chan")
    seq_count = lax.axis_size("seq")
    seq_rows = shard_rows * chan_count
    chan_cols = conv_weight.shape[1]
    chan_index = lax.axis_index("chan")
    seq_index = lax.axis_index("seq")
    relative = jnp.arange(chan_count, dtype=jnp.int32)
    owner = (chan_index - relative) % chan_count
    positions = (
        seq_index * seq_rows
        + owner[:, None] * shard_rows
        + jnp.arange(shard_rows, dtype=jnp.int32)[None, :]
    )
    keep_one, keep_two = keep_masks(positions, starts)
    next_one, unused_one = keep_masks(positions + 1, starts)
    unused_two, next_two = keep_masks(positions + 2, starts)
    gain_one = norm_gains[0].astype(F32)
    gain_two = norm_gains[1].astype(F32)
    conv_taps = conv_weight.astype(F32)
    bits = group_bits()
    orders = (bits[::-1], bits)

    part = width // seq_count
    w_own = lax.dynamic_slice_in_dim(out_weight, seq_index * part, part, 1)
    w_one = turned(w_own, "chan", 1)
    w_three = turned(w_own, "chan", 3)
    tok_one = turned(tokens, "chan", 1)
    tok_three = turned(tokens, "chan", 3)
    w_two = turned(w_one, "chan", 1)
    tok_two = turned(after(tok_one, w_three), "chan", 1)
    others = jnp.stack([w_one, w_two, w_three])[None]
    halves = [others[:, :, : chan_cols // 2], others[:, :, chan_cols // 2 :]]
    for place, order in enumerate(orders):
        held = halves[place]
        for bit in order:
            held = jnp.concatenate([held, swapped(held, "seq", 2 * bit)], axis=0)
        split = held.reshape((2,) * len(order) + held.shape[1:])
        axes = [len(order) - 1 - order.index(bit) for bit in bits]
        held = jnp.transpose(split, (*axes, *range(len(order), split.ndim))).reshape(held.shape)
        halves[place] = held
    held = jnp.concatenate(halves, axis=2)
    others = (held, swapped(held, "seq", 1))

    tok_blocks = [tokens, tok_one, tok_two, tok_three]
    inputs_all = jnp.concatenate(tok_blocks, axis=0).astype(F32)
    unit_all, scale_all = unit_rows(inputs_all)
    normed_one = (unit_all * gain_one).astype(BF)
    projected = jnp.einsum("td,kde->kte", normed_one, in_weight, preferred_element_type=F32)
    projected = projected.reshape(3, chan_count, shard_rows, chan_cols)

    grad_out = lax.all_gather(after(cotangent, tok_two, tok_three), "chan", axis=0, tiled=True)

    def at_edge(edge_rows, device):
        return lax.dynamic_index_in_dim(edge_rows, (chan_index - device) % chan_count, 0, False)

    def is_owner(device):
        return (owner == device)[:, None, None]

    mixed_in = (projected[0] * projected[2]).astype(BF)
    ends = mixed_in[:, shard_rows - 2 :]
    rim_rows = passed_along(at_edge(ends, chan_count - 1), "seq", 1)
    before = jnp.where(is_owner(0), rim_rows[None], jnp.roll(ends, -1, axis=0))
    extended = jnp.concatenate([before, mixed_in], axis=1).astype(F32)
    lag_one = keep_one * extended[:, 1 : shard_rows + 1]
    lag_two = keep_two * extended[:, 0:shard_rows]
    conv_out = conv_taps[0] * extended[:, 2:] + conv_taps[1] * lag_one + conv_taps[2] * lag_two
    gated_mix = (projected[1] * conv_out).astype(BF)

    gated_rows_own = [gated_mix[0]] + [
        turned(gated_mix[r], "chan", -r) for r in range(1, chan_count)
    ]
    state_own, normed_two_own, scale_two = mixer_rows(
        gated_rows_own, out_weight, others, tokens, gain_two
    )
    n_one = turned(normed_two_own, "chan", 1)
    normed_one_slices = own_slices(
        [
            after(normed_one[r * shard_rows : (r + 1) * shard_rows], normed_two_own)
            for r in range(chan_count)
        ]
    )
    n_two = turned(n_one, "chan", 1)
    n_three = turned(after(normed_two_own, n_one), "chan", 3)
    hidden, grad_pair, ffn_parts, grad_two_parts = feed_forward(
        owner,
        [after(normed_two_own, normed_one_slices[0]), n_one],
        grad_out,
        gate_up_weight,
        down_weight,
        0,
        chan_count,
        (),
    )
    cot_slices = own_slices(after(grad_out, hidden), owner)
    run = turned(grad_two_parts[1], "chan", 1)
    hidden, grad_pair, ffn_more, grad_more = feed_forward(
        owner,
        [after(n_two, cot_slices[0]), n_three],
        grad_out,
        gate_up_weight,
        down_weight,
        2,
        chan_count,
        (hidden, grad_pair),
    )
    ffn_parts = list(ffn_parts) + list(ffn_more)
    grad_two_parts = list(grad_two_parts) + list(grad_more)

    total = ring_sum(run, grad_two_parts[2])
    hidden_rec = swapped(after(hidden, total), "seq", 1)
    pair_rec = swapped(after(grad_pair, total), "seq", 1)
    run = turned(total, "chan", 1)
    normed_two_slices = own_slices([normed_two_own, n_one, n_two, after(n_three, total)])
    down = Joined(
        (after(cot_slices[0], normed_two_slices[0]), cot_slices[1]),
        (hidden, hidden_rec),
        orders,
        part,
        tall=True,
    )
    down.send()
    total = ring_sum(after(run, down.made), grad_two_parts[3])
    run = turned(total, "chan", 1)
    gate_up_a = Joined(
        (after(normed_two_slices[0], total), normed_two_slices[1]),
        (grad_pair, pair_rec),
        orders,
        part,
        False,
        0,
        2,
    )
    gate_up_a.send()
    run = after(run, gate_up_a.made, *down.arrived)

    grad_gated_rows, grad_state_own, grad_mix_own, gain_two_part = gated_rows(
        run,
        grad_two_parts[0],
        state_own,
        scale_two,
        cotangent,
        gain_two,
        out_weight,
        others,
    )
    gg = [grad_gated_rows[0]] + [
        turned(grad_gated_rows[r], "chan", r) for r in range(1, chan_count)
    ]
    grad_mix = lax.all_gather(after(grad_mix_own, *gg), "chan", axis=0, tiled=True)
    ffn_run = turned(after(ffn_parts[1], *gg), "chan", 1)
    grad_gated = jnp.stack(gg).astype(F32)

    grad_conv = (grad_gated * projected[1]).astype(BF)
    grad_c = grad_gated * conv_out
    heads = after(grad_conv[:, :2], *gate_up_a.arrived)
    rim_back = passed_along(at_edge(heads, 0), "seq", -1)
    behind = jnp.where(is_owner(chan_count - 1), rim_back[None], jnp.roll(heads, 1, axis=0))
    ext_back = jnp.concatenate([grad_conv, behind], axis=1).astype(F32)
    grad_here = ext_back[:, :shard_rows]
    grad_mixed = (
        conv_taps[0] * grad_here
        + conv_taps[1] * next_one * ext_back[:, 1 : shard_rows + 1]
        + conv_taps[2] * next_two * ext_back[:, 2:]
    )
    tap_part = jnp.stack(
        [
            jnp.sum(grad_here * extended[:, 2:], axis=(0, 1)),
            jnp.sum(grad_here * lag_one, axis=(0, 1)),
            jnp.sum(grad_here * lag_two, axis=(0, 1)),
        ]
    )
    grad_triple = jnp.stack(
        [
            v.astype(BF).reshape(seq_rows, chan_cols)
            for v in (grad_mixed * projected[2], grad_c, grad_mixed * projected[0])
        ]
    )
    grad_one_parts, gain_one_part = mixer_back(grad_triple, in_weight, tok_blocks, scale_all)
    run = turned(grad_one_parts[1], "chan", 1)
    triple_rec = swapped(after(grad_triple, grad_one_parts[1]), "seq", 1)
    small = jnp.concatenate([gain_one_part, gain_two_part, tap_part.reshape(-1)])
    small_rec = swapped(small, "seq", 1)
    gate_up_b = Joined(
        (after(normed_two_slices[0], grad_one_parts[1], small), normed_two_slices[1]),
        (grad_pair, pair_rec),
        orders,
        part,
        False,
        1,
        2,
    )
    small = small + after(small_rec, gate_up_b.made)
    small_rec = swapped(small, "seq", 2)
    down.add(small)
    small = summed(small + after(small_rec, down.made), "seq", 4)
    gate_up_b.send(small)
    down.send(small)
    total = ring_sum(after(run, small), grad_one_parts[2])
    run = turned(total, "chan", 1)
    into = Joined(
        (after(normed_one_slices[0], total), normed_one_slices[1]),
        (grad_triple, triple_rec),
        orders,
        part,
    )
    gate_up_a.add(into.made)
    into.send(gate_up_a.made)
    gate_up_a.send()
    total = ring_sum(after(run, gate_up_a.made), grad_one_parts[3])
    run = turned(total, "chan", 1)
    mix_slices = own_slices(after(grad_mix, total), owner)
    gated_all = gated_mix.reshape(1, seq_rows, chan_cols)
    outward = Joined(
        mix_slices, (gated_all, swapped(gated_all, "seq", 1)), orders, part, tall=True
    )
    outward.send()
    small_rec = swapped(after(small[: 2 * width], outward.made), "chan", 1)
    gate_up_b.add(outward.made)
    gate_up_b.send()
    run = after(run, gate_up_b.made)
    ffn_sum = ring_sum(after(ffn_run, gate_up_b.made), ffn_parts[2])
    ffn_run = turned(ffn_sum, "chan", 1)
    down_grad = final_sums(down.finish(ffn_sum), True, (hidden.shape[2], part))
    into.add(down_grad)
    into.send()
    gains = small[: 2 * width] + after(small_rec, into.made)
    small_rec = swapped(gains, "chan", 2)
    ffn_sum = ring_sum(after(ffn_run, into.made), ffn_parts[3])
    ffn_run = turned(ffn_sum, "chan", 1)
    first, third = gate_up_a.finish(ffn_sum)
    second, fourth = gate_up_b.finish()
    gate_up_grad = final_sums(
        [first, second, third, fourth], False, (2, part, hidden.shape[2])
    )
    outward.add(gate_up_grad)
    outward.send()
    gains = gains + after(small_rec, outward.made)
    in_grad = final_sums(into.finish(outward.made), False, (3, part, chan_cols))
    out_grad = final_sums(outward.finish(in_grad), True, (chan_cols, part))

    grad_one_own = run.astype(F32) + grad_one_parts[0].astype(F32)
    input_grad = grad_state_own + norm_back(
        grad_one_own, unit_all[:shard_rows], scale_all[:shard_rows], gain_one
    )
    block_output = (state_own + (ffn_run.astype(F32) + ffn_parts[0].astype(F32))).astype(BF)
    gains_grad = gains.reshape(2, width)
    conv_grad = small[2 * width :].reshape(3, chan_cols)
    return (
        block_output,
        input_grad,
        gains_grad,
        conv_grad,
        in_grad,
        out_grad,
        gate_up_grad,
        down_grad,
    )


def solution(mesh):
    placed = (
        P(("seq", "chan"), None),
        P(),
        P(None, "chan"),
        P(None, None, "chan"),
        P("chan", None),
        P(None, None, "chan"),
        P("chan", None),
        P(),
        P(("seq", "chan"), None),
    )
    return jax.shard_map(
        on_device,
        mesh=mesh,
        in_specs=placed,
        out_specs=(
            P(("seq", "chan"), None),
            P(("seq", "chan"), None),
            P(),
            P(None, "chan"),
            P(None, "seq", "chan"),
            P("chan", "seq"),
            P(None, "seq", "chan"),
            P("chan", "seq"),
        ),
        check_vma=False,
    )
```

time: 1150 us -> 459 us (0.40)
  waiting for transfers between devices: 916 us -> 160 us
  Pallas kernels: 0 us -> 129 us
  matrix products: 110 us -> 3.42 us
  starting transfers between devices: 4.21 us -> 72.5 us
  blocking collectives: 41.5 us -> 0 us
  local copies, waits for them, and re-layouts: 25.9 us -> 38.8 us
    reduce_scatter x6 -> x0, waiting for transfers between devices: 511 us -> none  [the longest x1 206 us: on_device(): lax.psum_scatter(grad_gate_up, 'seq', scatter_dimension=1, tiled=True)]
    psum x2 -> x0, waiting for transfers between devices: 300 us -> none  [the longest x1 157 us: on_device(): lax.psum(jnp.dot(gated_mix, out_weight, preferred_element_type=jnp.float3...]
    ppermute x0 -> x62, waiting for transfers between devices: none -> 157 us  [the longest x24 108 us: turned(): lax.ppermute(block, axis, [(i, (i + distance) % count) for i in range(cou...]
    pallas_call x0 -> x29, Pallas kernels: none -> 129 us  [the longest x2 43.3 us: feed_forward(): pl.pallas_call(functools.partial(ffn_body, count, len(joined)), grid_spec...]
    dot_general x12 -> x1, matrix products: 110 us -> 3.42 us  [on_device(): jnp.einsum('td,kde->kte', normed_one, in_weight, preferred_element_type=F32)]
    all_gather x3 -> x2, waiting for transfers between devices: 101 us -> 0.02 us  [the longest x1 0.02 us: on_device(): lax.all_gather(after(grad_mix_own, *gg), 'chan', axis=0, tiled=True)]
    ppermute x0 -> x62, starting transfers between devices: none -> 68.7 us  [the longest x38 35.4 us: swapped(): lax.ppermute(block, axis, [(i, i ^ bit) for i in range(lax.axis_size(axis...]
    psum x1 -> x0, blocking collectives: 41.5 us -> none  [on_device(): lax.psum((jnp.stack([gain_one_part, gain_two_part]), padded_taps.reshape(...]
  transfers between devices with their start and end apart: 13 -> 66, of which waited for: 13 -> 23; matrix products, arithmetic and copies ran while one was open for 10% -> 8% of each run, Pallas kernels for 0% -> 28%
where the time goes in v2:
time: 459 us; the launch traced here: 451 us
  waiting for transfers between devices  160 us (35%)
  Pallas kernels  129 us (28%)
  starting transfers between devices  72.5 us (16%)
  local copies, waits for them, and re-layouts  38.8 us (8%)
  other arithmetic  32.3 us (7%)
  between operations  15.6 us (3%)
    ppermute x24, waiting for transfers between devices, turned(): lax.ppermute(block, axis, [(i, (i + distance) % count) for i in range(cou...  108 us
    ppermute x38, waiting for transfers between devices, swapped(): lax.ppermute(block, axis, [(i, i ^ bit) for i in range(lax.axis_size(axis...  49.6 us
    pallas_call x2, Pallas kernels, feed_forward(): pl.pallas_call(functools.partial(ffn_body, count, len(joined)), grid_spec...  43.3 us
    ppermute x38, starting transfers between devices, swapped(): lax.ppermute(block, axis, [(i, i ^ bit) for i in range(lax.axis_size(axis...  35.4 us
    unnamed x198, local copies, waits for them, and re-layouts  34.8 us
    ppermute x24, starting transfers between devices, turned(): lax.ppermute(block, axis, [(i, (i + distance) % count) for i in range(cou...  33.4 us
    pallas_call x5, Pallas kernels, __init__(): pl.pallas_call(functools.partial(product_body, slots, part, tiles, tall),...  33.3 us
    pallas_call x4, Pallas kernels, final_sums(): pl.pallas_call(functools.partial(sums_body, [len(parts) for parts in sour...  14.9 us
  transfers between devices with their start and end apart: 66, of which 23 were waited for; matrix products, arithmetic and copies ran while one was open for 8% of the time, Pallas kernels for 28%

profile of v2, /device:TPU:0, one launch (start us, length us, event | category | flops | bytes accessed | tf_op | source)
XLA Modules:
  0.0 450.9 jit_solution(9991756837435419652)
XLA Ops:
  7.2 5.1 %collective-permute-start.3 = (bf16[128,2048]{1,0:T(8,128)(2,1)}, bf16[128,2048]{1,0:T(8,128)(2,1)S(1)}, u32[]{:S(2)}, u32[]{:S(2)}) collective-permute-start(bf16[128,2048]{1,0:T(8,128)(2,1)} %refs_2_.1), channel_id=1, source_target_pairs={{0,3},{1,0},{2,1},{3,2},{4,7},{5,4},{6,5},{7,6},{8,11},{9,8},{10,9... | collective-permute-start | bytes 1572872 | tf_op jit(solution)/shard_map/ppermute | solution.py:41
  13.3 3.9 collective-permute-start.1
  18.0 29.1 %collective-permute-done.8 = bf16[512,256]{1,0:T(8,128)(2,1)S(1)} collective-permute-done((bf16[512,256]{1,0:T(8,128)(2,1)S(1)}, bf16[512,256]{1,0:T(8,128)(2,1)S(1)}, u32[]{:S(2)}, u32[]{:S(2)}) %collective-permute-start.8) | collective-permute-done | bytes 262176 | tf_op jit(solution)/shard_map/ppermute | solution.py:41
  49.6 6.5 %collective-permute-done.9 = bf16[512,256]{1,0:T(8,128)(2,1)S(1)} collective-permute-done((bf16[512,256]{1,0:T(8,128)(2,1)S(1)}, bf16[512,256]{1,0:T(8,128)(2,1)S(1)}, u32[]{:S(2)}, u32[]{:S(2)}) %collective-permute-start.9) | collective-permute-done | bytes 262176 | tf_op jit(solution)/shard_map/ppermute | solution.py:41
  59.6 5.9 %collective-permute-done.12 = bf16[1,3,256,256]{3,2,1,0:T(8,128)(2,1)} collective-permute-done((bf16[1,3,256,256]{3,2,1,0:T(8,128)(2,1)S(1)}, bf16[1,3,256,256]{3,2,1,0:T(8,128)(2,1)}, u32[]{:S(2)}, u32[]{:S(2)}) %collective-permute-start.12) | collective-permute-done | bytes 393248 | tf_op jit(solution)/shard_map/ppermute | solution.py:45
  65.5 1.9 pad_maximum_fusion.5
  68.9 1.9 pad_maximum_fusion.4
  73.2 11.1 %collective-permute-done.13 = bf16[2,3,256,256]{3,2,1,0:T(8,128)(2,1)} collective-permute-done((bf16[2,3,256,256]{3,2,1,0:T(8,128)(2,1)}, bf16[2,3,256,256]{3,2,1,0:T(8,128)(2,1)}, u32[]{:S(2)}, u32[]{:S(2)}) %collective-permute-start.13) | collective-permute-done | bytes 786464 | tf_op jit(solution)/shard_map/ppermute | solution.py:45
  87.5 3.2 pad_maximum_fusion.refs_5_.refs_1_
  90.8 4.6 %convert_multiply_fusion = (f32[512,2048]{1,0:T(8,128)}, bf16[512,2048]{1,0:T(8,128)(2,1)S(1)}) fusion(f32[512]{0:T(512)S(1)} %add_rsqrt_fusion, bf16[128,2048]{1,0:T(8,128)(2,1)S(1)} %collective-permute-done.3.refs_5_, bf16[128,2048]{1,0:T(8,128)(2,1)S(1)} %collective-permute-done.2.refs_4_, bf16[128,2048]{1,0:T(8,128)(2,1)S(1)} %collective-permute-done.refs_3_, ...), kind=kLoop, calls=%fused_computation | loop fusion | flops 11534336 | bytes 8398848 | tf_op jit(solution)/shard_map/mul | solution.py:67
  96.7 3.4 fusion.3
  102.7 2.4 collective-permute-start.4
  106.2 3.2 multiply_convert_fusion.3
  111.8 4.5 %collective-permute-done.5.refs_1_ = bf16[128,512]{1,0:T(8,128)(2,1)S(1)} collective-permute-done((bf16[128,512]{1,0:T(8,128)(2,1)S(1)}, bf16[128,512]{1,0:T(8,128)(2,1)S(1)}, u32[]{:S(2)}, u32[]{:S(2)}) %collective-permute-start.5) | collective-permute-done | bytes 131104 | tf_op jit(solution)/shard_map/ppermute | solution.py:41
  116.3 9.6 %collective-permute-done.6.refs_2_ = bf16[128,512]{1,0:T(8,128)(2,1)S(1)} collective-permute-done((bf16[128,512]{1,0:T(8,128)(2,1)S(1)}, bf16[128,512]{1,0:T(8,128)(2,1)S(1)}, u32[]{:S(2)}, u32[]{:S(2)}) %collective-permute-start.6) | collective-permute-done | bytes 131104 | tf_op jit(solution)/shard_map/ppermute | solution.py:41
  125.9 6.0 %mixer_rows.1 = (f32[128,2048]{1,0:T(8,128)S(1)}, bf16[128,2048]{1,0:T(8,128)(2,1)}, f32[128,1]{1,0:T(8,128)S(1)}) custom-call(s32[5]{0:T(128)S(1)} %pad_add_fusion.ids, bf16[128,512]{1,0:T(8,128)(2,1)S(1)} %get-tuple-element.265.refs_0_, bf16[128,512]{1,0:T(8,128)(2,1)S(1)} %collective-permute-done.5.refs_1_, ...), custom_call_target="tpu_custom_call" | custom-call | flops 1024 | bytes 1024 | tf_op jit(solution)/shard_map/mixer_rows/pallas_call | solution.py:561
  135.9 12.7 %collective-permute-done.15.refs_1_ = bf16[128,2048]{1,0:T(8,128)(2,1)S(1)} collective-permute-done((bf16[128,2048]{1,0:T(8,128)(2,1)}, bf16[128,2048]{1,0:T(8,128)(2,1)S(1)}, u32[]{:S(2)}, u32[]{:S(2)}) %collective-permute-start.15) | collective-permute-done | bytes 524320 | tf_op jit(solution)/shard_map/ppermute | solution.py:41
  148.7 4.0 collective-permute-start.18
  152.6 22.5 %feed_forward.2 = (bf16[1,512,2048]{2,1,0:T(8,128)(2,1)S(1)}, bf16[2,512,2048]{2,1,0:T(8,128)(2,1)}, bf16[128,2048]{1,0:T(8,128)(2,1)S(1)}, bf16[128,2048]{1,0:T...) custom-call(s32[4]{0:T(128)S(1)} %and_select_fusion.ids, ...), custom_call_target="tpu_custom_call" | custom-call | flops 1024 | bytes 1024 | tf_op jit(solution)/shard_map/feed_forward/pallas_call | solution.py:143
  176.8 20.8 %feed_forward.3 = (bf16[1,512,2048]{2,1,0:T(8,128)(2,1)S(1)}, bf16[2,512,2048]{2,1,0:T(8,128)(2,1)}, bf16[128,2048]{1,0:T(8,128)(2,1)S(1)}, bf16[128,2048]{1,0:T...) custom-call(s32[4]{0:T(128)S(1)} %and_select_fusion.ids, ...), custom_call_target="tpu_custom_call", output_to_operand_aliasing={{0}: (7, {}), {1}: (8, {})} | custom-call | flops 1024 | bytes 1024 | tf_op jit(solution)/shard_map/feed_forward/pallas_call | solution.py:143
  202.1 8.3 %collective-permute-done.20.refs_1_ = bf16[512,1024]{1,0:T(8,128)(2,1)S(1)} collective-permute-done((bf16[512,1024]{1,0:T(8,128)(2,1)S(1)}, bf16[512,1024]{1,0:T(8,128)(2,1)S(1)}, u32[]{:S(2)}, u32[]{:S(2)}) %collective-permute-start.20) | collective-permute-done | bytes 1048608 | tf_op jit(solution)/shard_map/ppermute | solution.py:45
  211.7 7.4 %product.5 = (bf16[2,1024,256]{2,1,0:T(8,128)(2,1)S(1)}, bf16[2,1024,256]{2,1,0:T(8,128)(2,1)S(1)}, bf16[2,1024,256]{2,1,0:T(8,128)(2,1)S(1)}, bf16[2,1024,256]{2,1,0:T(8,128)(2,1)S(1)}) custom-call(bf16[512,1024]{1,0:T(8,128)(2,1)S(1)} %get-tuple-element.143.refs_0_, bf16[512,1024]{1,0:T(8,128)(2,1)} %copy-done.95, bf16[1,512,2048]{2,1,0:T(8,128)(2,1)} %copy-done.3, ...), custom_call_target="tpu_custom_call" | custom-call | flops 1024 | bytes 1024 | tf_op jit(solution)/shard_map/product/pallas_call | solution.py:302
  223.7 8.0 %product.6 = (bf16[2,256,1024]{2,1,0:T(8,128)(2,1)}, bf16[2,256,1024]{2,1,0:T(8,128)(2,1)S(1)}, bf16[2,256,1024]{2,1,0:T(8,128)(2,1)}, bf16[2,256,1024]{2,1,0:T(8,128)(2,1)S(1)}) custom-call(bf16[512,1024]{1,0:T(8,128)(2,1)S(1)} %get-tuple-element.169.refs_0_, bf16[512,1024]{1,0:T(8,128)(2,1)} %copy-done.92, ...), custom_call_target="tpu_custom_call" | custom-call | flops 1024 | bytes 1024 | tf_op jit(solution)/shard_map/product/pallas_call | solution.py:302
  235.3 14.9 %collective-permute-done.22.refs_3_ = bf16[128,2048]{1,0:T(8,128)(2,1)S(1)} collective-permute-done((bf16[128,2048]{1,0:T(8,128)(2,1)S(1)}, bf16[128,2048]{1,0:T(8,128)(2,1)S(1)}, u32[]{:S(2)}, u32[]{:S(2)}) %collective-permute-start.22) | collective-permute-done | bytes 524320 | tf_op jit(solution)/shard_map/ppermute | solution.py:41
  250.2 8.1 %gated_rows.1 = (bf16[128,512]{1,0:T(8,128)(2,1)S(1)}, bf16[128,512]{1,0:T(8,128)(2,1)}, bf16[128,512]{1,0:T(8,128)(2,1)}, bf16[128,512]{1,0:T(8,128)(2,1)}, f32...) custom-call(s32[5]{0:T(128)S(1)} %pad_add_fusion.ids, bf16[512,2048]{1,0:T(8,128)(2,1)} %refs_0_.1, ...), custom_call_target="tpu_custom_call" | custom-call | flops 1024 | bytes 1024 | tf_op jit(solution)/shard_map/gated_rows/pallas_call | solution.py:644
  261.9 2.0 collective-permute-start.29
  263.9 4.6 %collective-permute-done.27 = bf16[128,512]{1,0:T(8,128)(2,1)S(1)} collective-permute-done((bf16[128,512]{1,0:T(8,128)(2,1)}, bf16[128,512]{1,0:T(8,128)(2,1)S(1)}, u32[]{:S(2)}, u32[]{:S(2)}) %collective-permute-start.27) | collective-permute-done | bytes 131104 | tf_op jit(solution)/shard_map/ppermute | solution.py:41
  268.5 3.2 collective-permute-done.28
  271.8 2.8 fusion.7
  280.0 2.2 multiply_reduce_fusion.3
  283.5 7.4 %mixer_back.1 = (bf16[128,2048]{1,0:T(8,128)(2,1)S(1)}, bf16[128,2048]{1,0:T(8,128)(2,1)}, bf16[128,2048]{1,0:T(8,128)(2,1)S(1)}, bf16[128,2048]{1,0:T(8,128)(2,1)S(1)}, f32[1,2048]{1,0:T(1,128)S(1)}) custom-call(bf16[3,512,512]{2,1,0:T(8,128)(2,1)S(1)} %pad_maximum_fusion.3.refs_0_.refs_2_, bf16[3,2048,512]{2,1,0:T(8,128)(2,1)} %refs_1_.1, ...), custom_call_target="tpu_custom_call" | custom-call | flops 1024 | bytes 1024 | tf_op jit(solution)/shard_map/mixer_back/pallas_call | solution.py:482
  295.1 2.6 collective-permute-start.34
  299.3 8.3 %product.7 = (bf16[2,256,1024]{2,1,0:T(8,128)(2,1)}, bf16[2,256,1024]{2,1,0:T(8,128)(2,1)S(1)}, bf16[2,256,1024]{2,1,0:T(8,128)(2,1)}, bf16[2,256,1024]{2,1,0:T(8,128)(2,1)S(1)}) custom-call(bf16[512,1024]{1,0:T(8,128)(2,1)S(1)} %copy-done.25, bf16[512,1024]{1,0:T(8,128)(2,1)} %copy-done.92, bf16[2,512,2048]{2,1,0:T(8,128)(2,1)} %get-tuple-element.153.refs_2_, ...), custom_call_target="tpu_custom_call" | custom-call | flops 1024 | bytes 1024 | tf_op jit(solution)/shard_map/product/pallas_call | solution.py:302
  313.3 3.0 collective-permute-done.37
  316.3 7.0 %collective-permute-done.34.a = bf16[128,2048]{1,0:T(8,128)(2,1)} collective-permute-done((bf16[128,2048]{1,0:T(8,128)(2,1)}, bf16[128,2048]{1,0:T(8,128)(2,1)}, u32[]{:S(2)}, u32[]{:S(2)}) %collective-permute-start.34) | collective-permute-done | bytes 524320 | tf_op jit(solution)/shard_map/ppermute | solution.py:41
  324.6 3.1 collective-permute-start.38
  330.7 7.0 %product.8 = (bf16[2,256,768]{2,1,0:T(8,128)(2,1)S(1)}, bf16[2,256,768]{2,1,0:T(8,128)(2,1)S(1)}, bf16[2,256,768]{2,1,0:T(8,128)(2,1)S(1)}, bf16[2,256,768]{2,1,0:T(8,128)(2,1)S(1)}) custom-call(bf16[512,1024]{1,0:T(8,128)(2,1)S(1)} %copy-done.52, bf16[512,1024]{1,0:T(8,128)(2,1)} %collective-permute-done.39.refs_1_, bf16[3,512,512]{2,1,0:T(8,128)(2,1)} %copy-done.1, ...), custom_call_target="tpu_custom_call" | custom-call | flops 1024 | bytes 1024 | tf_op jit(solution)/shard_map/product/pallas_call | solution.py:302
  347.8 14.2 %collective-permute-done.30.a = bf16[128,2048]{1,0:T(8,128)(2,1)S(1)} collective-permute-done((bf16[128,2048]{1,0:T(8,128)(2,1)}, bf16[128,2048]{1,0:T(8,128)(2,1)S(1)}, u32[]{:S(2)}, u32[]{:S(2)}) %collective-permute-start.30) | collective-permute-done | bytes 524320 | tf_op jit(solution)/shard_map/ppermute | solution.py:41
  363.4 2.6 collective-permute-done.46.refs_2_
  366.8 2.5 collective-permute-start.51
  371.8 2.6 product.9
  376.6 2.4 upper_sums.7
  385.8 13.8 %collective-permute-done.54.refs_2_ = bf16[1,256,1024]{2,1,0:T(8,128)(2,1)} collective-permute-done((bf16[1,256,1024]{2,1,0:T(8,128)(2,1)}, bf16[1,256,1024]{2,1,0:T(8,128)(2,1)}, u32[]{:S(2)}, u32[]{:S(2)}) %collective-permute-start.54) | collective-permute-done | bytes 524320 | tf_op jit(solution)/shard_map/ppermute | solution.py:45
  413.6 2.3 upper_sums.8
  422.5 7.4 %final_sums.5 = f32[2,256,2048]{2,1,0:T(8,128)} custom-call(bf16[2,256,1024]{2,1,0:T(8,128)(2,1)S(1)} %copy-done.12, bf16[2,256,1024]{2,1,0:T(8,128)(2,1)S(1)} %copy-done.17, bf16[1,256,1024]{2,1,0:T(8,128)(2,1)} %collective-permute-done.54.refs_2_, bf16[2,256,1024]{2,1,0:T(8,128)(2,1)S(1)} %copy-done.21, ...), custom_call_target="tpu_custom_call" | custom-call | flops 1024 | bytes 1024 | tf_op jit(solution)/shard_map/final_sums/pallas_call | solution.py:425
  432.7 2.7 multiply_add_fusion
  435.4 4.7 %final_sums.6 = f32[3,256,512]{2,1,0:T(8,128)} custom-call(bf16[2,256,768]{2,1,0:T(8,128)(2,1)S(1)} %copy-done.42, bf16[2,256,768]{2,1,0:T(8,128)(2,1)} %collective-permute-done.48.refs_1_, bf16[1,256,768]{2,1,0:T(8,128)(2,1)S(1)} %collective-permute-done.60.refs_2_, bf16[2,256,768]{2,1,0:T(8,128)(2,1)S(1)} %copy-done.44, ...), custom_call_target="tpu_custom_call" | custom-call | flops 1024 | bytes 1024 | tf_op jit(solution)/shard_map/final_sums/pallas_call | solution.py:425
  441.6 2.0 add_convert_fusion
  (378 shorter events, 115.8 us)
Async XLA Ops:
  7.2 145.5 %all-gather.3.cloned.1.call-start = ((), (), s32[]{:S(2)}) async-start(), calls=%async_computation | async-start | bytes 2621440 | tf_op jit(solution)/shard_map/all_gather | solution.py:739
  7.2 65.2 %collective-permute-start.3 = (bf16[128,2048]{1,0:T(8,128)(2,1)}, bf16[128,2048]{1,0:T(8,128)(2,1)S(1)}, u32[]{:S(2)}, u32[]{:S(2)}) collective-permute-start(bf16[128,2048]{1,0:T(8,128)(2,1)} %refs_2_.1), channel_id=1, source_target_pairs={{0,3},{1,0},{2,1},{3,2},{4,7},{5,4},{6,5},{7,6},{8,11},{9,8},{10,9... | collective-permute-start | bytes 1572872 | tf_op jit(solution)/shard_map/ppermute | solution.py:41
  12.3 47.1 %collective-permute-start = (bf16[128,2048]{1,0:T(8,128)(2,1)}, bf16[128,2048]{1,0:T(8,128)(2,1)S(1)}, u32[]{:S(2)}, u32[]{:S(2)}) collective-permute-start(bf16[128,2048]{1,0:T(8,128)(2,1)} %refs_2_.1), channel_id=1, source_target_pairs={{0,1},{1,2},{2,3},{3,0},{4,5},{5,6},{6,7},{7,4},{8,9},{9,10},{10,1... | collective-permute-start | bytes 1572872 | tf_op jit(solution)/shard_map/ppermute | solution.py:41
  13.3 36.3 %collective-permute-start.1 = (bf16[512,256]{1,0:T(8,128)(2,1)S(1)}, bf16[512,256]{1,0:T(8,128)(2,1)S(1)}, u32[]{:S(2)}, u32[]{:S(2)}) collective-permute-start(bf16[512,256]{1,0:T(8,128)(2,1)S(1)} %constant_dynamic-slice_fusion), channel_id=1, source_target_pairs={{0,3},{1,0},{2,1},{3,2},{4,7},{5,4},{6,5},{7,6},{8,11},{9,8},{10,9... | collective-permute-start | bytes 786440 | tf_op jit(solution)/shard_map/ppermute | solution.py:41
  17.2 30.0 %collective-permute-start.8 = (bf16[512,256]{1,0:T(8,128)(2,1)S(1)}, bf16[512,256]{1,0:T(8,128)(2,1)S(1)}, u32[]{:S(2)}, u32[]{:S(2)}) collective-permute-start(bf16[512,256]{1,0:T(8,128)(2,1)S(1)} %constant_dynamic-slice_fusion), channel_id=1, source_target_pairs={{0,1},{1,2},{2,3},{3,0},{4,5},{5,6},{6,7},{7,4},{8,9},{9,10},{10,1... | collective-permute-start | bytes 786440 | tf_op jit(solution)/shard_map/ppermute | solution.py:41
  67.4 16.9 %collective-permute-start.13 = (bf16[2,3,256,256]{3,2,1,0:T(8,128)(2,1)}, bf16[2,3,256,256]{3,2,1,0:T(8,128)(2,1)}, u32[]{:S(2)}, u32[]{:S(2)}) collective-permute-start(bf16[2,3,256,256]{3,2,1,0:T(8,128)(2,1)} %pad_maximum_fusion.5), channel_id=1, source_target_pairs={{0,8},{4,12},{8,0},{12,4},{16,24},{20,28},{24,16},{28,20},{1,9},{5... | collective-permute-start | bytes 2359304 | tf_op jit(solution)/shard_map/ppermute | solution.py:45
  70.9 16.6 %collective-permute-start.11 = (bf16[2,3,256,256]{3,2,1,0:T(8,128)(2,1)}, bf16[2,3,256,256]{3,2,1,0:T(8,128)(2,1)}, u32[]{:S(2)}, u32[]{:S(2)}) collective-permute-start(bf16[2,3,256,256]{3,2,1,0:T(8,128)(2,1)} %pad_maximum_fusion.4), channel_id=1, source_target_pairs={{0,16},{4,20},{8,24},{12,28},{16,0},{20,4},{24,8},{28,12},{1,17},{... | collective-permute-start | bytes 2359304 | tf_op jit(solution)/shard_map/ppermute | solution.py:45
  72.6 270.2 %all-gather.5.cloned.1.call-start = ((), (), s32[]{:S(2)}) async-start(), calls=%async_computation.1 | async-start | bytes 2621440 | tf_op jit(solution)/shard_map/all_gather | solution.py:837
  90.7 35.2 %collective-permute-start.14 = (bf16[4,3,512,256]{3,2,1,0:T(8,128)(2,1)}, bf16[4,3,512,256]{3,2,1,0:T(8,128)(2,1)}, u32[]{:S(2)}, u32[]{:S(2)}) collective-permute-start(bf16[4,3,512,256]{3,2,1,0:T(8,128)(2,1)} %pad_maximum_fusion.refs_5_.refs_1_), channel_id=1, source_target_pairs={{0,4},{4,0},{8,12},{12,8},{16,20},{20,16},{24,28},{28,24},{1,5},{5... | collective-permute-start | bytes 9437192 | tf_op jit(solution)/shard_map/ppermute | solution.py:45
  109.5 16.4 %collective-permute-start.6 = (bf16[128,512]{1,0:T(8,128)(2,1)S(1)}, bf16[128,512]{1,0:T(8,128)(2,1)S(1)}, u32[]{:S(2)}, u32[]{:S(2)}) collective-permute-start(bf16[128,512]{1,0:T(8,128)(2,1)S(1)} %get-tuple-element.263), channel_id=1, source_target_pairs={{0,2},{1,3},{2,0},{3,1},{4,6},{5,7},{6,4},{7,5},{8,10},{9,11},{10,... | collective-permute-start | bytes 393224 | tf_op jit(solution)/shard_map/ppermute | solution.py:41
  110.9 15.0 %collective-permute-start.7 = (bf16[128,512]{1,0:T(8,128)(2,1)S(1)}, bf16[128,512]{1,0:T(8,128)(2,1)S(1)}, u32[]{:S(2)}, u32[]{:S(2)}) collective-permute-start(bf16[128,512]{1,0:T(8,128)(2,1)S(1)} %get-tuple-element.262), channel_id=1, source_target_pairs={{0,1},{1,2},{2,3},{3,0},{4,5},{5,6},{6,7},{7,4},{8,9},{9,10},{10,1... | collective-permute-start | bytes 393224 | tf_op jit(solution)/shard_map/ppermute | solution.py:41
  132.9 15.8 %collective-permute-start.15 = (bf16[128,2048]{1,0:T(8,128)(2,1)}, bf16[128,2048]{1,0:T(8,128)(2,1)S(1)}, u32[]{:S(2)}, u32[]{:S(2)}) collective-permute-start(bf16[128,2048]{1,0:T(8,128)(2,1)} %get-tuple-element.138.refs_0_), channel_id=1, source_target_pairs={{0,1},{1,2},{2,3},{3,0},{4,5},{5,6},{6,7},{7,4},{8,9},{9,10},{10,1... | collective-permute-start | bytes 1572872 | tf_op jit(solution)/shard_map/ppermute | solution.py:41
  148.7 28.2 %collective-permute-start.17 = (bf16[128,2048]{1,0:T(8,128)(2,1)S(1)}, bf16[128,2048]{1,0:T(8,128)(2,1)S(1)}, u32[]{:S(2)}, u32[]{:S(2)}) collective-permute-start(bf16[128,2048]{1,0:T(8,128)(2,1)S(1)} %collective-permute-done.15.refs_1_), channel_id=1, source_target_pairs={{0,1},{1,2},{2,3},{3,0},{4,5},{5,6},{6,7},{7,4},{8,9},{9,10},{10,1... | collective-permute-start | bytes 1572872 | tf_op jit(solution)/shard_map/ppermute | solution.py:41
  148.7 28.2 %collective-permute-start.18 = (bf16[128,2048]{1,0:T(8,128)(2,1)}, bf16[128,2048]{1,0:T(8,128)(2,1)S(1)}, u32[]{:S(2)}, u32[]{:S(2)}) collective-permute-start(bf16[128,2048]{1,0:T(8,128)(2,1)} %get-tuple-element.138.refs_0_), channel_id=1, source_target_pairs={{0,3},{1,0},{2,1},{3,2},{4,7},{5,4},{6,5},{7,6},{8,11},{9,8},{10,9... | collective-permute-start | bytes 1572872 | tf_op jit(solution)/shard_map/ppermute | solution.py:41
  175.2 24.1 %collective-permute-start.16 = (bf16[128,2048]{1,0:T(8,128)(2,1)S(1)}, bf16[128,2048]{1,0:T(8,128)(2,1)S(1)}, u32[]{:S(2)}, u32[]{:S(2)}) collective-permute-start(bf16[128,2048]{1,0:T(8,128)(2,1)S(1)} %get-tuple-element.133), channel_id=1, source_target_pairs={{0,1},{1,2},{2,3},{3,0},{4,5},{5,6},{6,7},{7,4},{8,9},{9,10},{10,1... | collective-permute-start | bytes 1572872 | tf_op jit(solution)/shard_map/ppermute | solution.py:41
  199.4 23.3 %collective-permute-start.24 = (bf16[2,512,2048]{2,1,0:T(8,128)(2,1)}, bf16[2,512,2048]{2,1,0:T(8,128)(2,1)}, u32[]{:S(2)}, u32[]{:S(2)}) collective-permute-start(bf16[2,512,2048]{2,1,0:T(8,128)(2,1)} %get-tuple-element.153.refs_2_), channel_id=1, source_target_pairs={{0,4},{4,0},{8,12},{12,8},{16,20},{20,16},{24,28},{28,24},{1,5},{5... | collective-permute-start | bytes 12582920 | tf_op jit(solution)/shard_map/ppermute | solution.py:45
  201.4 21.3 %collective-permute-start.23 = (bf16[512,1024]{1,0:T(8,128)(2,1)S(1)}, bf16[512,1024]{1,0:T(8,128)(2,1)S(1)}, u32[]{:S(2)}, u32[]{:S(2)}) collective-permute-start(bf16[512,1024]{1,0:T(8,128)(2,1)S(1)} %get-tuple-element.151), channel_id=1, source_target_pairs={{0,4},{4,0},{8,12},{12,8},{16,20},{20,16},{24,28},{28,24},{1,5},{5... | collective-permute-start | bytes 3145736 | tf_op jit(solution)/shard_map/ppermute | solution.py:45
  201.9 20.6 %collective-permute-start.19 = (bf16[128,2048]{1,0:T(8,128)(2,1)S(1)}, bf16[128,2048]{1,0:T(8,128)(2,1)S(1)}, u32[]{:S(2)}, u32[]{:S(2)}) collective-permute-start(bf16[128,2048]{1,0:T(8,128)(2,1)S(1)} %ring_sum.6), channel_id=1, source_target_pairs={{0,1},{1,2},{2,3},{3,0},{4,5},{5,6},{6,7},{7,4},{8,9},{9,10},{10,1... | collective-permute-start | bytes 1572872 | tf_op jit(solution)/shard_map/ppermute | solution.py:41
  220.1 30.1 %collective-permute-start.25 = (bf16[2,1024,256]{2,1,0:T(8,128)(2,1)S(1)}, bf16[2,1024,256]{2,1,0:T(8,128)(2,1)S(1)}, u32[]{:S(2)}, u32[]{:S(2)}) collective-permute-start(bf16[2,1024,256]{2,1,0:T(8,128)(2,1)S(1)} %get-tuple-element.147), channel_id=1, source_target_pairs={{0,8},{4,12},{8,0},{12,4},{16,24},{20,28},{24,16},{28,20},{1,9},{5... | collective-permute-start | bytes 3145736 | tf_op jit(solution)/shard_map/ppermute | solution.py:45
  221.6 28.5 %collective-permute-start.26 = (bf16[2,1024,256]{2,1,0:T(8,128)(2,1)S(1)}, bf16[2,1024,256]{2,1,0:T(8,128)(2,1)S(1)}, u32[]{:S(2)}, u32[]{:S(2)}) collective-permute-start(bf16[2,1024,256]{2,1,0:T(8,128)(2,1)S(1)} %get-tuple-element.155), channel_id=1, source_target_pairs={{0,16},{4,20},{8,24},{12,28},{16,0},{20,4},{24,8},{28,12},{1,17},{... | collective-permute-start | bytes 3145736 | tf_op jit(solution)/shard_map/ppermute | solution.py:45
  233.6 40.9 %collective-permute-start.31 = (bf16[2,256,1024]{2,1,0:T(8,128)(2,1)}, bf16[2,256,1024]{2,1,0:T(8,128)(2,1)S(1)}, u32[]{:S(2)}, u32[]{:S(2)}) collective-permute-start(bf16[2,256,1024]{2,1,0:T(8,128)(2,1)} %get-tuple-element.154), channel_id=1, source_target_pairs={{0,8},{4,12},{8,0},{12,4},{16,24},{20,28},{24,16},{28,20},{1,9},{5... | collective-permute-start | bytes 3145736 | tf_op jit(solution)/shard_map/ppermute | solution.py:45
  234.3 40.3 %collective-permute-start.32 = (bf16[2,256,1024]{2,1,0:T(8,128)(2,1)}, bf16[2,256,1024]{2,1,0:T(8,128)(2,1)S(1)}, u32[]{:S(2)}, u32[]{:S(2)}) collective-permute-start(bf16[2,256,1024]{2,1,0:T(8,128)(2,1)} %get-tuple-element.164), channel_id=1, source_target_pairs={{0,16},{4,20},{8,24},{12,28},{16,0},{20,4},{24,8},{28,12},{1,17},{... | collective-permute-start | bytes 3145736 | tf_op jit(solution)/shard_map/ppermute | solution.py:45
  235.3 14.9 %collective-permute-start.22 = (bf16[128,2048]{1,0:T(8,128)(2,1)S(1)}, bf16[128,2048]{1,0:T(8,128)(2,1)S(1)}, u32[]{:S(2)}, u32[]{:S(2)}) collective-permute-start(bf16[128,2048]{1,0:T(8,128)(2,1)S(1)} %ring_sum.7), channel_id=1, source_target_pairs={{0,1},{1,2},{2,3},{3,0},{4,5},{5,6},{6,7},{7,4},{8,9},{9,10},{10,1... | collective-permute-start | bytes 1572872 | tf_op jit(solution)/shard_map/ppermute | solution.py:41
  293.3 37.4 %collective-permute-start.40 = (bf16[3,512,512]{2,1,0:T(8,128)(2,1)S(1)}, bf16[3,512,512]{2,1,0:T(8,128)(2,1)}, u32[]{:S(2)}, u32[]{:S(2)}) collective-permute-start(bf16[3,512,512]{2,1,0:T(8,128)(2,1)S(1)} %pad_maximum_fusion.3.refs_0_.refs_2_), channel_id=1, source_target_pairs={{0,4},{4,0},{8,12},{12,8},{16,20},{20,16},{24,28},{28,24},{1,5},{5... | collective-permute-start | bytes 4718600 | tf_op jit(solution)/shard_map/ppermute | solution.py:45
  295.1 34.1 %collective-permute-start.39 = (bf16[512,1024]{1,0:T(8,128)(2,1)}, bf16[512,1024]{1,0:T(8,128)(2,1)}, u32[]{:S(2)}, u32[]{:S(2)}) collective-permute-start(bf16[512,1024]{1,0:T(8,128)(2,1)} %get-tuple-element.184), channel_id=1, source_target_pairs={{0,4},{4,0},{8,12},{12,8},{16,20},{20,16},{24,28},{28,24},{1,5},{5... | collective-permute-start | bytes 3145736 | tf_op jit(solution)/shard_map/ppermute | solution.py:45
  295.1 28.2 %collective-permute-start.34 = (bf16[128,2048]{1,0:T(8,128)(2,1)}, bf16[128,2048]{1,0:T(8,128)(2,1)}, u32[]{:S(2)}, u32[]{:S(2)}) collective-permute-start(bf16[128,2048]{1,0:T(8,128)(2,1)} %get-tuple-element.166), channel_id=1, source_target_pairs={{0,1},{1,2},{2,3},{3,0},{4,5},{5,6},{6,7},{7,4},{8,9},{9,10},{10,1... | collective-permute-start | bytes 1572872 | tf_op jit(solution)/shard_map/ppermute | solution.py:41
  324.6 18.0 %collective-permute-start.38 = (bf16[128,2048]{1,0:T(8,128)(2,1)S(1)}, bf16[128,2048]{1,0:T(8,128)(2,1)S(1)}, u32[]{:S(2)}, u32[]{:S(2)}) collective-permute-start(bf16[128,2048]{1,0:T(8,128)(2,1)S(1)} %ring_sum.8), channel_id=1, source_target_pairs={{0,1},{1,2},{2,3},{3,0},{4,5},{5,6},{6,7},{7,4},{8,9},{9,10},{10,1... | collective-permute-start | bytes 1572872 | tf_op jit(solution)/shard_map/ppermute | solution.py:41
  327.7 19.5 %collective-permute-start.42 = (bf16[1,512,512]{2,1,0:T(8,128)(2,1)S(1)}, bf16[1,512,512]{2,1,0:T(8,128)(2,1)}, u32[]{:S(2)}, u32[]{:S(2)}) collective-permute-start(bf16[1,512,512]{2,1,0:T(8,128)(2,1)S(1)} %bitcast.51), channel_id=1, source_target_pairs={{0,4},{4,0},{8,12},{12,8},{16,20},{20,16},{24,28},{28,24},{1,5},{5... | collective-permute-start | bytes 1572872 | tf_op jit(solution)/shard_map/ppermute | solution.py:45
  327.7 41.6 %collective-permute-start.43 = (bf16[2,256,1024]{2,1,0:T(8,128)(2,1)}, bf16[2,256,1024]{2,1,0:T(8,128)(2,1)}, u32[]{:S(2)}, u32[]{:S(2)}) collective-permute-start(bf16[2,256,1024]{2,1,0:T(8,128)(2,1)} %get-tuple-element.197), channel_id=1, source_target_pairs={{0,8},{4,12},{8,0},{12,4},{16,24},{20,28},{24,16},{28,20},{1,9},{5... | collective-permute-start | bytes 3145736 | tf_op jit(solution)/shard_map/ppermute | solution.py:45
  329.3 40.5 %collective-permute-start.44 = (bf16[2,256,1024]{2,1,0:T(8,128)(2,1)}, bf16[2,256,1024]{2,1,0:T(8,128)(2,1)}, u32[]{:S(2)}, u32[]{:S(2)}) collective-permute-start(bf16[2,256,1024]{2,1,0:T(8,128)(2,1)} %get-tuple-element.200), channel_id=1, source_target_pairs={{0,16},{4,20},{8,24},{12,28},{16,0},{20,4},{24,8},{28,12},{1,17},{... | collective-permute-start | bytes 3145736 | tf_op jit(solution)/shard_map/ppermute | solution.py:45
  345.6 25.7 %collective-permute-start.41 = (bf16[512,1024]{1,0:T(8,128)(2,1)S(1)}, bf16[512,1024]{1,0:T(8,128)(2,1)S(1)}, u32[]{:S(2)}, u32[]{:S(2)}) collective-permute-start(bf16[512,1024]{1,0:T(8,128)(2,1)S(1)} %get-tuple-element.194), channel_id=1, source_target_pairs={{0,4},{4,0},{8,12},{12,8},{16,20},{20,16},{24,28},{28,24},{1,5},{5... | collective-permute-start | bytes 3145736 | tf_op jit(solution)/shard_map/ppermute | solution.py:45
  345.6 16.3 %collective-permute-start.30 = (bf16[128,2048]{1,0:T(8,128)(2,1)}, bf16[128,2048]{1,0:T(8,128)(2,1)S(1)}, u32[]{:S(2)}, u32[]{:S(2)}) collective-permute-start(bf16[128,2048]{1,0:T(8,128)(2,1)} %copy-done.75), channel_id=1, source_target_pairs={{0,1},{1,2},{2,3},{3,0},{4,5},{5,6},{6,7},{7,4},{8,9},{9,10},{10,1... | collective-permute-start | bytes 1572872 | tf_op jit(solution)/shard_map/ppermute | solution.py:41
  347.2 18.8 %collective-permute-start.46 = (bf16[1,1024,256]{2,1,0:T(8,128)(2,1)}, bf16[1,1024,256]{2,1,0:T(8,128)(2,1)S(1)}, u32[]{:S(2)}, u32[]{:S(2)}) collective-permute-start(bf16[1,1024,256]{2,1,0:T(8,128)(2,1)} %copy-done.79), channel_id=1, source_target_pairs={{0,16},{4,20},{8,24},{12,28},{16,0},{20,4},{24,8},{28,12},{1,17},{... | collective-permute-start | bytes 1572872 | tf_op jit(solution)/shard_map/ppermute | solution.py:45
  362.0 18.6 %collective-permute-start.47 = (bf16[1,1024,256]{2,1,0:T(8,128)(2,1)}, bf16[1,1024,256]{2,1,0:T(8,128)(2,1)S(1)}, u32[]{:S(2)}, u32[]{:S(2)}) collective-permute-start(bf16[1,1024,256]{2,1,0:T(8,128)(2,1)} %copy-done.76), channel_id=1, source_target_pairs={{0,8},{4,12},{8,0},{12,4},{16,24},{20,28},{24,16},{28,20},{1,9},{5... | collective-permute-start | bytes 1572872 | tf_op jit(solution)/shard_map/ppermute | solution.py:45
  366.8 17.0 %collective-permute-start.51 = (bf16[128,2048]{1,0:T(8,128)(2,1)}, bf16[128,2048]{1,0:T(8,128)(2,1)}, u32[]{:S(2)}, u32[]{:S(2)}) collective-permute-start(bf16[128,2048]{1,0:T(8,128)(2,1)} %copy-done.69), channel_id=1, source_target_pairs={{0,1},{1,2},{2,3},{3,0},{4,5},{5,6},{6,7},{7,4},{8,9},{9,10},{10,1... | collective-permute-start | bytes 1572872 | tf_op jit(solution)/shard_map/ppermute | solution.py:41
  369.3 31.9 %collective-permute-start.48 = (bf16[2,256,768]{2,1,0:T(8,128)(2,1)}, bf16[2,256,768]{2,1,0:T(8,128)(2,1)}, u32[]{:S(2)}, u32[]{:S(2)}) collective-permute-start(bf16[2,256,768]{2,1,0:T(8,128)(2,1)} %copy-done.74), channel_id=1, source_target_pairs={{0,8},{4,12},{8,0},{12,4},{16,24},{20,28},{24,16},{28,20},{1,9},{5... | collective-permute-start | bytes 2359304 | tf_op jit(solution)/shard_map/ppermute | solution.py:45
  369.7 32.8 %collective-permute-start.49 = (bf16[2,256,768]{2,1,0:T(8,128)(2,1)}, bf16[2,256,768]{2,1,0:T(8,128)(2,1)}, u32[]{:S(2)}, u32[]{:S(2)}) collective-permute-start(bf16[2,256,768]{2,1,0:T(8,128)(2,1)} %copy-done.73), channel_id=1, source_target_pairs={{0,16},{4,20},{8,24},{12,28},{16,0},{20,4},{24,8},{28,12},{1,17},{... | collective-permute-start | bytes 2359304 | tf_op jit(solution)/shard_map/ppermute | solution.py:45
  371.3 28.3 %collective-permute-start.54 = (bf16[1,256,1024]{2,1,0:T(8,128)(2,1)}, bf16[1,256,1024]{2,1,0:T(8,128)(2,1)}, u32[]{:S(2)}, u32[]{:S(2)}) collective-permute-start(bf16[1,256,1024]{2,1,0:T(8,128)(2,1)} %copy-done.77), channel_id=1, source_target_pairs={{0,16},{4,20},{8,24},{12,28},{16,0},{20,4},{24,8},{28,12},{1,17},{... | collective-permute-start | bytes 1572872 | tf_op jit(solution)/shard_map/ppermute | solution.py:45
  381.3 34.6 %collective-permute-start.56 = (bf16[1,256,1024]{2,1,0:T(8,128)(2,1)}, bf16[1,256,1024]{2,1,0:T(8,128)(2,1)}, u32[]{:S(2)}, u32[]{:S(2)}) collective-permute-start(bf16[1,256,1024]{2,1,0:T(8,128)(2,1)} %get-tuple-element.225), channel_id=1, source_target_pairs={{0,8},{4,12},{8,0},{12,4},{16,24},{20,28},{24,16},{28,20},{1,9},{5... | collective-permute-start | bytes 1572872 | tf_op jit(solution)/shard_map/ppermute | solution.py:45
  383.8 33.4 %collective-permute-start.45 = (bf16[128,2048]{1,0:T(8,128)(2,1)}, bf16[128,2048]{1,0:T(8,128)(2,1)}, u32[]{:S(2)}, u32[]{:S(2)}) collective-permute-start(bf16[128,2048]{1,0:T(8,128)(2,1)} %ring_sum.10), channel_id=1, source_target_pairs={{0,1},{1,2},{2,3},{3,0},{4,5},{5,6},{6,7},{7,4},{8,9},{9,10},{10,1... | collective-permute-start | bytes 1572872 | tf_op jit(solution)/shard_map/ppermute | solution.py:41
  399.6 20.9 %collective-permute-start.55 = (bf16[1,256,1024]{2,1,0:T(8,128)(2,1)}, bf16[1,256,1024]{2,1,0:T(8,128)(2,1)S(1)}, u32[]{:S(2)}, u32[]{:S(2)}) collective-permute-start(bf16[1,256,1024]{2,1,0:T(8,128)(2,1)} %copy-done.80), channel_id=1, source_target_pairs={{0,16},{4,20},{8,24},{12,28},{16,0},{20,4},{24,8},{28,12},{1,17},{... | collective-permute-start | bytes 1572872 | tf_op jit(solution)/shard_map/ppermute | solution.py:45
  401.1 15.4 %collective-permute-start.52 = (f32[4096]{0:T(1024)S(1)}, f32[4096]{0:T(1024)S(1)}, u32[]{:S(2)}, u32[]{:S(2)}) collective-permute-start(f32[4096]{0:T(1024)S(1)} %slice.192), channel_id=1, source_target_pairs={{0,1},{1,0},{2,3},{3,2},{4,5},{5,4},{6,7},{7,6},{8,9},{9,8},{10,11... | collective-permute-start | bytes 49160 | tf_op jit(solution)/shard_map/ppermute | solution.py:45
  402.5 19.5 %collective-permute-start.57 = (bf16[1,256,1024]{2,1,0:T(8,128)(2,1)}, bf16[1,256,1024]{2,1,0:T(8,128)(2,1)S(1)}, u32[]{:S(2)}, u32[]{:S(2)}) collective-permute-start(bf16[1,256,1024]{2,1,0:T(8,128)(2,1)} %copy-done.78), channel_id=1, source_target_pairs={{0,8},{4,12},{8,0},{12,4},{16,24},{20,28},{24,16},{28,20},{1,9},{5... | collective-permute-start | bytes 1572872 | tf_op jit(solution)/shard_map/ppermute | solution.py:45
  416.0 13.9 %collective-permute-start.58 = (bf16[2,256,256]{2,1,0:T(8,128)(2,1)S(1)}, bf16[2,256,256]{2,1,0:T(8,128)(2,1)S(1)}, u32[]{:S(2)}, u32[]{:S(2)}) collective-permute-start(bf16[2,256,256]{2,1,0:T(8,128)(2,1)S(1)} %copy-done.84), channel_id=1, source_target_pairs={{0,8},{4,12},{8,0},{12,4},{16,24},{20,28},{24,16},{28,20},{1,9},{5... | collective-permute-start | bytes 786440 | tf_op jit(solution)/shard_map/ppermute | solution.py:45
  416.6 14.6 %collective-permute-start.59 = (bf16[2,256,256]{2,1,0:T(8,128)(2,1)S(1)}, bf16[2,256,256]{2,1,0:T(8,128)(2,1)S(1)}, u32[]{:S(2)}, u32[]{:S(2)}) collective-permute-start(bf16[2,256,256]{2,1,0:T(8,128)(2,1)S(1)} %copy-done.82), channel_id=1, source_target_pairs={{0,16},{4,20},{8,24},{12,28},{16,0},{20,4},{24,8},{28,12},{1,17},{... | collective-permute-start | bytes 786440 | tf_op jit(solution)/shard_map/ppermute | solution.py:45
  417.1 14.9 %collective-permute-start.60 = (bf16[1,256,768]{2,1,0:T(8,128)(2,1)S(1)}, bf16[1,256,768]{2,1,0:T(8,128)(2,1)S(1)}, u32[]{:S(2)}, u32[]{:S(2)}) collective-permute-start(bf16[1,256,768]{2,1,0:T(8,128)(2,1)S(1)} %get-tuple-element.214), channel_id=1, source_target_pairs={{0,16},{4,20},{8,24},{12,28},{16,0},{20,4},{24,8},{28,12},{1,17},{... | collective-permute-start | bytes 1179656 | tf_op jit(solution)/shard_map/ppermute | solution.py:45
  420.5 14.9 %collective-permute-start.61 = (bf16[1,256,768]{2,1,0:T(8,128)(2,1)S(1)}, bf16[1,256,768]{2,1,0:T(8,128)(2,1)S(1)}, u32[]{:S(2)}, u32[]{:S(2)}) collective-permute-start(bf16[1,256,768]{2,1,0:T(8,128)(2,1)S(1)} %get-tuple-element.233), channel_id=1, source_target_pairs={{0,8},{4,12},{8,0},{12,4},{16,24},{20,28},{24,16},{28,20},{1,9},{5... | collective-permute-start | bytes 1179656 | tf_op jit(solution)/shard_map/ppermute | solution.py:45
  422.0 18.1 %collective-permute-start.53 = (f32[4096]{0:T(1024)S(1)}, f32[4096]{0:T(1024)S(1)}, u32[]{:S(2)}, u32[]{:S(2)}) collective-permute-start(f32[4096]{0:T(1024)S(1)} %slice_add_fusion), channel_id=1, source_target_pairs={{0,2},{1,3},{2,0},{3,1},{4,6},{5,7},{6,4},{7,5},{8,10},{9,11},{10,... | collective-permute-start | bytes 49160 | tf_op jit(solution)/shard_map/ppermute | solution.py:45
  (117 other events, 946.0 us)
Sparse Core Ops, SparseCore 0:
  72.8 43.7 all-gather.2
  271.9 56.5 all-gather.4

commit v3 on v2

--- a/solution.py
+++ b/solution.py
@@ -83,11 +83,11 @@
     return bits
 
 
-def ffn_body(count, joining, ids, *refs):
+def ffn_body(count, ids, *refs):
     normed = refs[:count]
     cots = refs[count : 2 * count]
     gate_up_w, down_w = refs[2 * count : 2 * count + 2]
-    outs = refs[2 * count + 2 + joining :]
+    outs = refs[2 * count + 2 :]
     hidden_ref, pair_ref = outs[:2]
     ffn_refs, grad_refs = outs[2 : 2 + count], outs[2 + count : 2 + 2 * count]
     normed_all, cot_all, ffn_acc, grad_acc = outs[2 + 2 * count :]
@@ -132,16 +132,14 @@
             grad_refs[place][...] = grad_acc[own, :].astype(BF)
 
 
-def feed_forward(owner, normed, cots, gate_up_weight, down_weight, first, total, joined, tile=512):
+def feed_forward(owner, normed, cots, gate_up_weight, down_weight, first, tile=512):
     count = len(normed)
     rows, width = normed[0].shape
     units = down_weight.shape[0]
-    here, all_rows = count * rows, total * rows
-    place = first // count
+    here = count * rows
     block = pl.BlockSpec((rows, width), lambda j, ids: (0, 0))
-    anywhere = pl.BlockSpec(memory_space=pl.ANY)
     results = pl.pallas_call(
-        functools.partial(ffn_body, count, len(joined)),
+        functools.partial(ffn_body, count),
         grid_spec=pltpu.PrefetchScalarGridSpec(
             num_scalar_prefetch=1,
             grid=(units // tile,),
@@ -153,11 +151,10 @@
             + [
                 pl.BlockSpec((2, width, tile), lambda j, ids: (0, 0, j)),
                 pl.BlockSpec((tile, width), lambda j, ids: (j, 0)),
-            ]
-            + [anywhere] * len(joined),
+            ],
             out_specs=[
-                pl.BlockSpec((1, here, tile), lambda j, ids: (0, place, j)),
-                pl.BlockSpec((2, here, tile), lambda j, ids: (0, place, j)),
+                pl.BlockSpec((1, here, tile), lambda j, ids: (0, 0, j)),
+                pl.BlockSpec((2, here, tile), lambda j, ids: (0, 0, j)),
             ]
             + [block] * (2 * count),
             scratch_shapes=[
@@ -168,15 +165,14 @@
             ],
         ),
         out_shape=[
-            jax.ShapeDtypeStruct((1, all_rows, units), BF),
-            jax.ShapeDtypeStruct((2, all_rows, units), BF),
+            jax.ShapeDtypeStruct((1, here, units), BF),
+            jax.ShapeDtypeStruct((2, here, units), BF),
         ]
         + [jax.ShapeDtypeStruct((rows, width), BF)] * (2 * count),
-        input_output_aliases={2 * count + 3 + k: k for k in range(len(joined))},
         compiler_params=params(VMEM),
         cost_estimate=cost(),
         name="feed_forward",
-    )(owner, *normed, *([cots] * count), gate_up_weight, down_weight, *joined)
+    )(owner, *normed, *([cots] * count), gate_up_weight, down_weight)
     return results[0], results[1], results[2 : 2 + count], results[2 + count :]
 
 
@@ -198,12 +194,14 @@
                 ]
 
 
-def own_slices(blocks, owner=None):
+def own_slices(blocks, owner=None, relative=True):
     seq = lax.axis_size("seq")
     groups = seq // 2
     place = lax.axis_index("seq")
     core, group = place % 2, place // 2
-    chips = jnp.bitwise_xor(group, jnp.arange(groups, dtype=jnp.int32))
+    chips = jnp.arange(groups, dtype=jnp.int32)
+    if relative:
+        chips = jnp.bitwise_xor(group, chips)
     mine, other = 2 * chips + core, 2 * chips + 1 - core
     apart = owner is None
     if apart:
@@ -247,9 +245,20 @@
     return picked[0], swapped(picked[1], "seq", 1)
 
 
-def product_body(slots, part, tiles, tall, *refs):
-    own, rec, units_own, units_rec = refs[:4]
-    outs = refs[4:]
+def rows_dot(lhs, columns, units, swap):
+    total, start = None, 0
+    for piece in units:
+        here = lhs[start : start + piece.shape[1], columns]
+        start += piece.shape[1]
+        part = dot(piece[0], here, 0, 0) if swap else dot(here, piece[0], 0, 0)
+        total = part if total is None else total + part
+    return total
+
+
+def product_body(slots, part, tiles, tall, pieces, *refs):
+    own, rec = refs[:2]
+    units_own, units_rec = refs[2 : 2 + pieces], refs[2 + pieces : 2 + 2 * pieces]
+    outs = refs[2 + 2 * pieces :]
     step = pl.program_id(0)
     for half in range(2):
 
@@ -259,29 +268,26 @@
                 out = outs[2 * half + kind]
                 for place, slot in enumerate(slots[half][kind]):
                     columns = slice(slot * part, (slot + 1) * part)
-                    if tall:
-                        total = dot(units_own[0], own[:, columns], 0, 0) + dot(
-                            units_rec[0], rec[:, columns], 0, 0
-                        )
-                    else:
-                        total = dot(own[:, columns], units_own[0], 0, 0) + dot(
-                            rec[:, columns], units_rec[0], 0, 0
-                        )
-                    out[place] = total.astype(BF)
+                    out[place] = (
+                        rows_dot(own, columns, units_own, tall)
+                        + rows_dot(rec, columns, units_rec, tall)
+                    ).astype(BF)
 
 
 class Joined:
-    def __init__(self, lhs, units, orders, part, tall=False, piece=0, pieces=1):
+    def __init__(self, lhs, units, orders, part, tall=False):
         rows, slotted = lhs[0].shape
         groups = slotted // part
-        kinds, _, wide = units[0].shape
-        wide = wide // pieces
+        kinds, _, wide = units[0][0].shape
         tile = next(t for t in (512, 256, 128) if (kinds * wide // 2) % t == 0 and wide % t == 0)
         each = wide // tile
         tiles = kinds * each // 2
         slots = tuple(self.slots(order) for order in orders)
         whole = pl.BlockSpec((rows, slotted), lambda j: (0, 0))
-        column = pl.BlockSpec((1, rows, tile), lambda j: (j // each, 0, piece * each + j % each))
+        columns = [
+            pl.BlockSpec((1, piece.shape[1], tile), lambda j: (j // each, 0, j % each))
+            for piece in (*units[0], *units[1])
+        ]
         here = groups // 2
         shapes, specs = [], []
         for half in range(2):
@@ -300,15 +306,15 @@
                     specs.append(pl.BlockSpec(block, lambda j, at=at: (0, 0, at(j))))
                 shapes.append(jax.ShapeDtypeStruct(shape, BF))
         outs = pl.pallas_call(
-            functools.partial(product_body, slots, part, tiles, tall),
+            functools.partial(product_body, slots, part, tiles, tall, len(units[0])),
             grid=(2 * tiles,),
-            in_specs=[whole, whole, column, column],
+            in_specs=[whole, whole, *columns],
             out_specs=specs,
             out_shape=shapes,
-            compiler_params=params(VMEM),
+            compiler_params=params(58),
             cost_estimate=cost(),
             name="product",
-        )(*lhs, *units)
+        )(*lhs, *units[0], *units[1])
         self.orders, self.tall = orders, tall
         self.sent = [outs[0], outs[2]]
         self.kept = [[outs[1]], [outs[3]]]
@@ -348,6 +354,50 @@
         if earlier:
             kept[0][0] = after(kept[0][0], *earlier)
         return kept
+
+
+def whole_body(part, pieces, own, rec, *refs):
+    units_own, units_rec, out = refs[:pieces], refs[pieces : 2 * pieces], refs[2 * pieces]
+    for slot in range(out.shape[0]):
+        columns = slice(slot * part, (slot + 1) * part)
+        out[slot, 0] = (
+            rows_dot(own, columns, units_own, False) + rows_dot(rec, columns, units_rec, False)
+        ).astype(BF)
+
+
+def whole_product(lhs, units, part):
+    rows, slotted = lhs[0].shape
+    groups = slotted // part
+    kinds, _, wide = units[0][0].shape
+    tile = min(512, wide)
+    each = wide // tile
+    whole = pl.BlockSpec((rows, slotted), lambda j: (0, 0))
+    columns = [
+        pl.BlockSpec((1, piece.shape[1], tile), lambda j: (j // each, 0, j % each))
+        for piece in (*units[0], *units[1])
+    ]
+    return pl.pallas_call(
+        functools.partial(whole_body, part, len(units[0])),
+        grid=(kinds * each,),
+        in_specs=[whole, whole, *columns],
+        out_specs=pl.BlockSpec(
+            (groups, 1, part, tile), lambda j: (0, j // each, 0, j % each)
+        ),
+        out_shape=jax.ShapeDtypeStruct((groups, kinds, part, wide), BF),
+        compiler_params=params(58),
+        cost_estimate=cost(),
+        name="whole_product",
+    )(*lhs, *units[0], *units[1])
+
+
+def plane_sum(products):
+    groups = products.shape[0]
+    flat = products.reshape(-1, products.shape[-1])
+    members = [[2 * group + core for group in range(groups)] for core in range(2)]
+    mine = lax.psum_scatter(
+        flat, "seq", scatter_dimension=0, axis_index_groups=members, tiled=True
+    )
+    return mine.reshape(products.shape[1:])
 
 
 def sums_body(counts, tiles, *refs):
@@ -391,22 +441,23 @@
             for source in range(len(sources))
         ],
         out_shape=[jax.ShapeDtypeStruct((here, rows, columns), BF)] * len(sources),
-        compiler_params=params(VMEM),
+        compiler_params=params(58),
         cost_estimate=cost(),
         name="upper_sums",
     )(*arrays)
 
 
 def final_sums(sources, tall, shape):
-    _, rows, columns = sources[0][0].shape
+    sources = [[part if isinstance(part, tuple) else (part, 0) for part in parts] for parts in sources]
+    _, rows, columns = sources[0][0][0].shape
     if tall:
         tile = min(512, rows)
         tiles = rows // tile
         block, out_block = (1, tile, columns), (tile, columns)
         out_spec = pl.BlockSpec(out_block, lambda j: (j, 0))
 
-        def at(j, s):
-            return (0, source_tile(j, s, tiles), 0)
+        def at(j, s, slot):
+            return (slot, source_tile(j, s, tiles), 0)
     else:
         tile = next(t for t in (512, 256, 128) if columns % t == 0 and shape[2] % t == 0)
         tiles = columns // tile
@@ -414,13 +465,13 @@
         block, out_block = (1, rows, tile), (1, rows, tile)
         out_spec = pl.BlockSpec(out_block, lambda j: (j // each, 0, j % each))
 
-        def at(j, s):
-            return (0, 0, source_tile(j, s, tiles))
+        def at(j, s, slot):
+            return (slot, 0, source_tile(j, s, tiles))
 
     in_specs, arrays = [], []
     for source, parts in enumerate(sources):
-        for array in parts:
-            in_specs.append(pl.BlockSpec(block, lambda j, s=source: at(j, s)))
+        for array, slot in parts:
+            in_specs.append(pl.BlockSpec(block, lambda j, s=source, slot=slot: at(j, s, slot)))
             arrays.append(array)
     return pl.pallas_call(
         functools.partial(sums_body, [len(parts) for parts in sources], tiles),
@@ -428,7 +479,7 @@
         in_specs=in_specs,
         out_specs=out_spec,
         out_shape=jax.ShapeDtypeStruct(shape, F32),
-        compiler_params=params(VMEM),
+        compiler_params=params(58),
         cost_estimate=cost(),
         name="final_sums",
     )(*arrays)
@@ -451,6 +502,230 @@
         cost_estimate=cost(),
         name="ring_sum",
     )(arrived, own)
+
+
+def rows_body(count, rows, ids, gated, *refs):
+    mixes, out, mix_all = refs[:count], refs[count], refs[count + 1]
+
+    @pl.when(pl.program_id(0) == 0)
+    def _():
+        for place in range(count):
+            there = pl.ds(pl.multiple_of(ids[place] * rows, rows), rows)
+            mix_all[there, :] = mixes[place][...]
+
+    out[0] = dot(gated[...], mix_all[...], 0, 0).astype(BF)
+
+
+def rows_product(gated_plane, mixes, count):
+    rows, part = mixes[0].shape
+    chans = gated_plane.shape[1] // count
+    ids = jnp.bitwise_xor(
+        lax.axis_index("seq"), jnp.arange(len(mixes), dtype=jnp.int32)
+    ).astype(jnp.int32)
+    all_rows = rows * len(mixes)
+    return pl.pallas_call(
+        functools.partial(rows_body, len(mixes), rows),
+        grid_spec=pltpu.PrefetchScalarGridSpec(
+            num_scalar_prefetch=1,
+            grid=(count,),
+            in_specs=[pl.BlockSpec((all_rows, chans), lambda r, ids: (0, r))]
+            + [pl.BlockSpec((rows, part), lambda r, ids: (0, 0))] * len(mixes),
+            out_specs=pl.BlockSpec((1, chans, part), lambda r, ids: (r, 0, 0)),
+            scratch_shapes=[pltpu.VMEM((all_rows, part), BF)],
+        ),
+        out_shape=jax.ShapeDtypeStruct((count, chans, part), BF),
+        compiler_params=params(60),
+        cost_estimate=cost(),
+        name="rows_product",
+    )(ids, gated_plane, *mixes)
+
+
+def spread_body(slots, part, ids, rows_ref, *outs):
+    for slot in range(slots):
+        start = pl.multiple_of(ids[slot] * part, part)
+        outs[slot][...] = rows_ref[:, pl.ds(start, part)]
+
+
+def spread_slices(rows):
+    seq = lax.axis_size("seq")
+    part = rows.shape[1] // seq
+    ids = jnp.bitwise_xor(lax.axis_index("seq"), jnp.arange(seq, dtype=jnp.int32))
+    ids = ids.astype(jnp.int32)
+    if part % 128:
+        slices = [lax.dynamic_slice_in_dim(rows, ids[q] * part, part, 1) for q in range(seq)]
+    else:
+        slices = pl.pallas_call(
+            functools.partial(spread_body, seq, part),
+            in_specs=[
+                pl.BlockSpec(memory_space=pltpu.SMEM),
+                pl.BlockSpec(memory_space=pltpu.VMEM),
+            ],
+            out_specs=[pl.BlockSpec(memory_space=pltpu.VMEM)] * seq,
+            out_shape=[jax.ShapeDtypeStruct((rows.shape[0], part), BF)] * seq,
+            compiler_params=params(VMEM),
+            cost_estimate=cost(),
+            name="spread_slices",
+        )(ids, rows)
+    return slices
+
+
+def project_body(count, *refs):
+    toks = refs[:count]
+    gain_ref, weights, first_ref, second_ref, third_ref, mixed, normed, scale_ref = refs[count:]
+    rows = toks[0].shape[0]
+
+    @pl.when(pl.program_id(0) == 0)
+    def _():
+        for place in range(count):
+            here = pl.ds(place * rows, rows)
+            values = toks[place][...].astype(F32)
+            scale = lax.rsqrt(jnp.mean(values * values, axis=-1, keepdims=True) + EPS)
+            normed[here, :] = (values * scale * gain_ref[...]).astype(BF)
+            scale_ref[here, :] = scale
+
+    first = dot(normed[...], weights[0], 1, 0)
+    third = dot(normed[...], weights[2], 1, 0)
+    first_ref[...] = first
+    second_ref[...] = dot(normed[...], weights[1], 1, 0)
+    third_ref[...] = third
+    mixed[...] = (first * third).astype(BF)
+
+
+def in_projection(toks, gain, weights, tile=256):
+    count = len(toks)
+    rows, width = toks[0].shape
+    kinds, _, chans = weights.shape
+    all_rows = count * rows
+    block = pl.BlockSpec((rows, width), lambda j: (0, 0))
+    return pl.pallas_call(
+        functools.partial(project_body, count),
+        grid=(chans // tile,),
+        in_specs=[block] * count
+        + [
+            pl.BlockSpec((1, width), lambda j: (0, 0)),
+            pl.BlockSpec((kinds, width, tile), lambda j: (0, 0, j)),
+        ],
+        out_specs=[
+            *([pl.BlockSpec((all_rows, tile), lambda j: (0, j))] * (kinds + 1)),
+            pl.BlockSpec((all_rows, width), lambda j: (0, 0)),
+            pl.BlockSpec((all_rows, 1), lambda j: (0, 0)),
+        ],
+        out_shape=[
+            *([jax.ShapeDtypeStruct((all_rows, chans), F32)] * kinds),
+            jax.ShapeDtypeStruct((all_rows, chans), BF),
+            jax.ShapeDtypeStruct((all_rows, width), BF),
+            jax.ShapeDtypeStruct((all_rows, 1), F32),
+        ],
+        compiler_params=params(VMEM),
+        cost_estimate=cost(),
+        name="in_projection",
+    )(*toks, gain.reshape(1, width), weights)
+
+
+def shifted(values, steps, edge):
+    rows = values.shape[0]
+    moved = pltpu.roll(values, steps % rows, 0)
+    place = lax.broadcasted_iota(jnp.int32, values.shape, 0)
+    for k in range(abs(steps)):
+        at = k if steps > 0 else rows - 1 - k
+        row = edge[k : k + 1] if steps > 0 else edge[abs(steps) - 1 - k : abs(steps) - k]
+        moved = jnp.where(place == at, row, moved)
+    return moved
+
+
+def conv_body(count, second, mixed, before, taps, masks, conv_ref, *gated):
+    rows = second.shape[0] // count
+    for place in range(count):
+        here = pl.ds(place * rows, rows)
+        values = mixed[here, :].astype(F32)
+        edge = before[place]
+        lag_one = masks[here, 0:1] * shifted(values, 1, edge[1:2])
+        lag_two = masks[here, 1:2] * shifted(values, 2, edge)
+        conv = taps[0:1, :] * values + taps[1:2, :] * lag_one + taps[2:3, :] * lag_two
+        conv_ref[here, :] = conv
+        gated[place][...] = (second[here, :] * conv).astype(BF)
+
+
+def conv_forward(second, mixed, before, taps, masks, count, tile=128):
+    all_rows, chans = mixed.shape
+    rows = all_rows // count
+    wide = pl.BlockSpec((all_rows, tile), lambda j: (0, j))
+    results = pl.pallas_call(
+        functools.partial(conv_body, count),
+        grid=(chans // tile,),
+        in_specs=[
+            wide,
+            wide,
+            pl.BlockSpec((count, 2, tile), lambda j: (0, 0, j)),
+            pl.BlockSpec((3, tile), lambda j: (0, j)),
+            pl.BlockSpec(masks.shape, lambda j: (0, 0)),
+        ],
+        out_specs=[wide] + [pl.BlockSpec((rows, tile), lambda j: (0, j))] * count,
+        out_shape=[jax.ShapeDtypeStruct((all_rows, chans), F32)]
+        + [jax.ShapeDtypeStruct((rows, chans), BF)] * count,
+        compiler_params=params(60),
+        cost_estimate=cost(),
+        name="conv_forward",
+    )(second, mixed, before, taps, masks)
+    return results[0], results[1:]
+
+
+def conv_back_body(count, *refs):
+    grads = refs[:count]
+    first, second, third, conv, mixed, before, behind, taps = refs[count : count + 8]
+    masks, triple, tap_ref = refs[count + 8 :]
+    rows = grads[0].shape[0]
+    sums = [None] * 3
+    for place in range(count):
+        here = pl.ds(place * rows, rows)
+        grad = grads[place][...].astype(F32)
+        grad_conv = (grad * second[here, :]).astype(BF).astype(F32)
+        edge = behind[place]
+        grad_mixed = (
+            taps[0:1, :] * grad_conv
+            + taps[1:2, :] * masks[here, 2:3] * shifted(grad_conv, -1, edge[0:1])
+            + taps[2:3, :] * masks[here, 3:4] * shifted(grad_conv, -2, edge)
+        )
+        triple[0, here, :] = (grad_mixed * third[here, :]).astype(BF)
+        triple[1, here, :] = (grad * conv[here, :]).astype(BF)
+        triple[2, here, :] = (grad_mixed * first[here, :]).astype(BF)
+        values = mixed[here, :].astype(F32)
+        lags = before[place]
+        for tap, lagged in enumerate(
+            (
+                values,
+                masks[here, 0:1] * shifted(values, 1, lags[1:2]),
+                masks[here, 1:2] * shifted(values, 2, lags),
+            )
+        ):
+            part = jnp.sum(grad_conv * lagged, axis=0, keepdims=True)
+            sums[tap] = part if sums[tap] is None else sums[tap] + part
+    tap_ref[...] = jnp.concatenate(sums, axis=0)
+
+
+def conv_backward(grads, first, second, third, conv, mixed, before, behind, taps, masks, tile=128):
+    count = len(grads)
+    all_rows, chans = mixed.shape
+    rows = all_rows // count
+    wide = pl.BlockSpec((all_rows, tile), lambda j: (0, j))
+    edge = pl.BlockSpec((count, 2, tile), lambda j: (0, 0, j))
+    three = pl.BlockSpec((3, tile), lambda j: (0, j))
+    return pl.pallas_call(
+        functools.partial(conv_back_body, count),
+        grid=(chans // tile,),
+        in_specs=[pl.BlockSpec((rows, tile), lambda j: (0, j))] * count
+        + [wide] * 5
+        + [edge, edge, three]
+        + [pl.BlockSpec(masks.shape, lambda j: (0, 0))],
+        out_specs=[pl.BlockSpec((3, all_rows, tile), lambda j: (0, 0, j)), three],
+        out_shape=[
+            jax.ShapeDtypeStruct((3, all_rows, chans), BF),
+            jax.ShapeDtypeStruct((3, chans), F32),
+        ],
+        compiler_params=params(60),
+        cost_estimate=cost(),
+        name="conv_backward",
+    )(*grads, first, second, third, conv, mixed, before, behind, taps, masks)
 
 
 def back_body(count, *refs):
@@ -491,7 +766,7 @@
         out_specs=[block] * count + [pl.BlockSpec((1, tile), lambda j: (0, j))],
         out_shape=[jax.ShapeDtypeStruct((rows, width), BF)] * count
         + [jax.ShapeDtypeStruct((1, width), F32)],
-        compiler_params=params(VMEM),
+        compiler_params=params(60),
         cost_estimate=cost(),
         name="mixer_back",
     )(grads, weights, *toks, scale)
@@ -578,7 +853,7 @@
             jax.ShapeDtypeStruct((rows, width), BF),
             jax.ShapeDtypeStruct((rows, 1), F32),
         ],
-        compiler_params=params(VMEM),
+        compiler_params=params(60),
         cost_estimate=cost(),
         name="mixer_rows",
     )(plane_ids(), *gated, own_w, *others, input_rows, gain.reshape(1, width))
@@ -667,7 +942,7 @@
             jax.ShapeDtypeStruct((rows, width), BF),
             jax.ShapeDtypeStruct((1, width), F32),
         ],
-        compiler_params=params(VMEM),
+        compiler_params=params(60),
         cost_estimate=cost(),
         name="gated_rows",
     )(plane_ids(), own_w, *others, arrived, part_own, state, scale, cot, gain.reshape(1, width))
@@ -713,52 +988,67 @@
     w_one = turned(w_own, "chan", 1)
     w_three = turned(w_own, "chan", 3)
     tok_one = turned(tokens, "chan", 1)
-    tok_three = turned(tokens, "chan", 3)
-    w_two = turned(w_one, "chan", 1)
-    tok_two = turned(after(tok_one, w_three), "chan", 1)
+    w_two = turned(after(w_one, w_three), "chan", 1)
+    tok_three = turned(after(tokens, w_three), "chan", 3)
     others = jnp.stack([w_one, w_two, w_three])[None]
     halves = [others[:, :, : chan_cols // 2], others[:, :, chan_cols // 2 :]]
+    first_arrived = [
+        swapped(half, "seq", 2 * order[0]) for half, order in zip(halves, orders)
+    ]
+    tok_two = turned(after(tok_one, w_two), "chan", 1)
+    second_arrived = []
     for place, order in enumerate(orders):
-        held = halves[place]
-        for bit in order:
+        held = jnp.concatenate([halves[place], first_arrived[place]], axis=0)
+        for bit in order[1:-1]:
             held = jnp.concatenate([held, swapped(held, "seq", 2 * bit)], axis=0)
+        halves[place] = held
+        second_arrived.append(swapped(held, "seq", 2 * order[-1]))
+    grad_out = lax.all_gather(after(cotangent, tok_two, tok_three), "chan", axis=0, tiled=True)
+    tok_blocks = [tokens, tok_one, tok_two, tok_three]
+    for place, order in enumerate(orders):
+        held = jnp.concatenate([halves[place], second_arrived[place]], axis=0)
         split = held.reshape((2,) * len(order) + held.shape[1:])
         axes = [len(order) - 1 - order.index(bit) for bit in bits]
         held = jnp.transpose(split, (*axes, *range(len(order), split.ndim))).reshape(held.shape)
         halves[place] = held
     held = jnp.concatenate(halves, axis=2)
     others = (held, swapped(held, "seq", 1))
-
-    tok_blocks = [tokens, tok_one, tok_two, tok_three]
-    inputs_all = jnp.concatenate(tok_blocks, axis=0).astype(F32)
-    unit_all, scale_all = unit_rows(inputs_all)
-    normed_one = (unit_all * gain_one).astype(BF)
-    projected = jnp.einsum("td,kde->kte", normed_one, in_weight, preferred_element_type=F32)
-    projected = projected.reshape(3, chan_count, shard_rows, chan_cols)
-
-    grad_out = lax.all_gather(after(cotangent, tok_two, tok_three), "chan", axis=0, tiled=True)
-
+    masks = jnp.concatenate(
+        [
+            mask.reshape(seq_rows, 1)
+            for mask in (keep_one, keep_two, next_one, next_two)
+        ]
+        + [jnp.zeros((seq_rows, 124), F32)],
+        axis=1,
+    )
+    *projected, mixed_in, normed_one, scale_all = in_projection(
+        [after(tokens, held, masks)] + tok_blocks[1:], gain_one, in_weight
+    )
     def at_edge(edge_rows, device):
         return lax.dynamic_index_in_dim(edge_rows, (chan_index - device) % chan_count, 0, False)
 
     def is_owner(device):
         return (owner == device)[:, None, None]
 
-    mixed_in = (projected[0] * projected[2]).astype(BF)
-    ends = mixed_in[:, shard_rows - 2 :]
+    ends = jnp.stack(
+        [mixed_in[(r + 1) * shard_rows - 2 : (r + 1) * shard_rows] for r in range(chan_count)]
+    )
     rim_rows = passed_along(at_edge(ends, chan_count - 1), "seq", 1)
-    before = jnp.where(is_owner(0), rim_rows[None], jnp.roll(ends, -1, axis=0))
-    extended = jnp.concatenate([before, mixed_in], axis=1).astype(F32)
-    lag_one = keep_one * extended[:, 1 : shard_rows + 1]
-    lag_two = keep_two * extended[:, 0:shard_rows]
-    conv_out = conv_taps[0] * extended[:, 2:] + conv_taps[1] * lag_one + conv_taps[2] * lag_two
-    gated_mix = (projected[1] * conv_out).astype(BF)
-
+    before = jnp.where(is_owner(0), rim_rows[None], jnp.roll(ends, -1, axis=0)).astype(F32)
+    conv_out, gated_mix = conv_forward(
+        projected[1], mixed_in, before, conv_taps, masks, chan_count
+    )
     gated_rows_own = [gated_mix[0]] + [
         turned(gated_mix[r], "chan", -r) for r in range(1, chan_count)
     ]
     state_own, normed_two_own, scale_two = mixer_rows(
         gated_rows_own, out_weight, others, tokens, gain_two
+    )
+    gated_plane = lax.all_gather(
+        jnp.concatenate([after(gated_rows_own[0], normed_two_own)] + gated_rows_own[1:], axis=1),
+        "seq",
+        axis=0,
+        tiled=True,
     )
     n_one = turned(normed_two_own, "chan", 1)
     normed_one_slices = own_slices(
@@ -769,57 +1059,65 @@
     )
     n_two = turned(n_one, "chan", 1)
     n_three = turned(after(normed_two_own, n_one), "chan", 3)
-    hidden, grad_pair, ffn_parts, grad_two_parts = feed_forward(
+    hidden_a, pair_a, ffn_parts, grad_two_parts = feed_forward(
         owner,
         [after(normed_two_own, normed_one_slices[0]), n_one],
         grad_out,
         gate_up_weight,
         down_weight,
         0,
-        chan_count,
-        (),
-    )
-    cot_slices = own_slices(after(grad_out, hidden), owner)
+    )
+    ffn_parts, grad_two_parts, hidden_a, pair_a = [
+        after(value, n_two, n_three)
+        if not isinstance(value, (list, tuple))
+        else [after(one, n_two, n_three) for one in value]
+        for value in (ffn_parts, grad_two_parts, hidden_a, pair_a)
+    ]
+    cot_slices = own_slices(after(grad_out, hidden_a), owner)
     run = turned(grad_two_parts[1], "chan", 1)
-    hidden, grad_pair, ffn_more, grad_more = feed_forward(
+    ffn_one = turned(ffn_parts[1], "chan", -1)
+    hidden_a_rec = swapped(hidden_a, "seq", 1)
+    pair_a_rec = swapped(pair_a, "seq", 1)
+    hidden_b, pair_b, ffn_more, grad_more = feed_forward(
         owner,
         [after(n_two, cot_slices[0]), n_three],
         grad_out,
         gate_up_weight,
         down_weight,
         2,
-        chan_count,
-        (hidden, grad_pair),
     )
     ffn_parts = list(ffn_parts) + list(ffn_more)
     grad_two_parts = list(grad_two_parts) + list(grad_more)
 
     total = ring_sum(run, grad_two_parts[2])
-    hidden_rec = swapped(after(hidden, total), "seq", 1)
-    pair_rec = swapped(after(grad_pair, total), "seq", 1)
+    hidden_b, pair_b = [
+        after(units, total, ffn_one, hidden_a_rec, pair_a_rec) for units in (hidden_b, pair_b)
+    ]
+    hidden_b_rec = swapped(hidden_b, "seq", 1)
+    pair_b_rec = swapped(pair_b, "seq", 1)
     run = turned(total, "chan", 1)
-    normed_two_slices = own_slices([normed_two_own, n_one, n_two, after(n_three, total)])
+    normed_two_slices = own_slices(
+        [normed_two_own, n_one, n_two, after(n_three, total)], None, False
+    )
     down = Joined(
         (after(cot_slices[0], normed_two_slices[0]), cot_slices[1]),
-        (hidden, hidden_rec),
+        ([hidden_a, hidden_b], [hidden_a_rec, hidden_b_rec]),
         orders,
         part,
         tall=True,
     )
-    down.send()
     total = ring_sum(after(run, down.made), grad_two_parts[3])
+    down.send(total)
     run = turned(total, "chan", 1)
-    gate_up_a = Joined(
+    gate_up = whole_product(
         (after(normed_two_slices[0], total), normed_two_slices[1]),
-        (grad_pair, pair_rec),
-        orders,
+        ([pair_a, pair_b], [pair_a_rec, pair_b_rec]),
         part,
-        False,
-        0,
-        2,
-    )
-    gate_up_a.send()
-    run = after(run, gate_up_a.made, *down.arrived)
+    )
+    ffn_three = turned(after(ffn_parts[3], total), "chan", -3)
+    run = after(run, gate_up, ffn_three, *down.arrived)
+    gate_up_mine = plane_sum(after(gate_up, gated_plane, run))
+    ffn_two = turned(after(ffn_parts[2], run), "chan", -1)
 
     grad_gated_rows, grad_state_own, grad_mix_own, gain_two_part = gated_rows(
         run,
@@ -831,106 +1129,86 @@
         out_weight,
         others,
     )
+    grad_gated_rows = list(grad_gated_rows)
+    grad_gated_rows[1:] = [
+        after(rows, ffn_two) for rows in grad_gated_rows[1:]
+    ]
     gg = [grad_gated_rows[0]] + [
         turned(grad_gated_rows[r], "chan", r) for r in range(1, chan_count)
     ]
-    grad_mix = lax.all_gather(after(grad_mix_own, *gg), "chan", axis=0, tiled=True)
-    ffn_run = turned(after(ffn_parts[1], *gg), "chan", 1)
-    grad_gated = jnp.stack(gg).astype(F32)
-
-    grad_conv = (grad_gated * projected[1]).astype(BF)
-    grad_c = grad_gated * conv_out
-    heads = after(grad_conv[:, :2], *gate_up_a.arrived)
+    mixes = spread_slices(after(grad_mix_own, *grad_gated_rows[1:]))
+    mixes = [mixes[0]] + [swapped(mixes[q], "seq", q) for q in range(1, seq_count)]
+    down.add(*grad_gated_rows[1:])
+    ffn_two = turned(after(ffn_two, *gg), "chan", -1)
+    heads = jnp.stack(
+        [
+            (
+                gg[r][:2].astype(F32) * projected[1][r * shard_rows : r * shard_rows + 2]
+            ).astype(BF)
+            for r in range(chan_count)
+        ]
+    )
+    heads = after(heads, down.made)
     rim_back = passed_along(at_edge(heads, 0), "seq", -1)
+    rim_back = after(rim_back, *mixes)
     behind = jnp.where(is_owner(chan_count - 1), rim_back[None], jnp.roll(heads, 1, axis=0))
-    ext_back = jnp.concatenate([grad_conv, behind], axis=1).astype(F32)
-    grad_here = ext_back[:, :shard_rows]
-    grad_mixed = (
-        conv_taps[0] * grad_here
-        + conv_taps[1] * next_one * ext_back[:, 1 : shard_rows + 1]
-        + conv_taps[2] * next_two * ext_back[:, 2:]
-    )
-    tap_part = jnp.stack(
-        [
-            jnp.sum(grad_here * extended[:, 2:], axis=(0, 1)),
-            jnp.sum(grad_here * lag_one, axis=(0, 1)),
-            jnp.sum(grad_here * lag_two, axis=(0, 1)),
-        ]
-    )
-    grad_triple = jnp.stack(
-        [
-            v.astype(BF).reshape(seq_rows, chan_cols)
-            for v in (grad_mixed * projected[2], grad_c, grad_mixed * projected[0])
-        ]
+    down.send(rim_back)
+    grad_triple, tap_part = conv_backward(
+        gg, *projected, conv_out, mixed_in, before, behind.astype(F32), conv_taps, masks
     )
     grad_one_parts, gain_one_part = mixer_back(grad_triple, in_weight, tok_blocks, scale_all)
+    grad_one_parts = [after(rows, ffn_two, *down.arrived) for rows in grad_one_parts]
     run = turned(grad_one_parts[1], "chan", 1)
+    small = after(
+        jnp.concatenate([gain_one_part, gain_two_part, tap_part.reshape(-1)]), grad_one_parts[1]
+    )
+    small_rec = swapped(small, "seq", 1)
     triple_rec = swapped(after(grad_triple, grad_one_parts[1]), "seq", 1)
-    small = jnp.concatenate([gain_one_part, gain_two_part, tap_part.reshape(-1)])
-    small_rec = swapped(small, "seq", 1)
-    gate_up_b = Joined(
-        (after(normed_two_slices[0], grad_one_parts[1], small), normed_two_slices[1]),
-        (grad_pair, pair_rec),
+    out_parts = rows_product(
+        after(gated_plane, grad_one_parts[1]), mixes, chan_count
+    )
+    out_run = turned(out_parts[3], "chan", 1)
+    into = Joined(
+        (after(normed_one_slices[0], out_parts), normed_one_slices[1]),
+        ([grad_triple], [triple_rec]),
         orders,
         part,
-        False,
-        1,
-        2,
-    )
-    small = small + after(small_rec, gate_up_b.made)
+    )
+    small = small + after(small_rec, into.made)
     small_rec = swapped(small, "seq", 2)
-    down.add(small)
-    small = summed(small + after(small_rec, down.made), "seq", 4)
-    gate_up_b.send(small)
-    down.send(small)
+    small = small + small_rec
+    into.send(small)
     total = ring_sum(after(run, small), grad_one_parts[2])
     run = turned(total, "chan", 1)
-    into = Joined(
-        (after(normed_one_slices[0], total), normed_one_slices[1]),
-        (grad_triple, triple_rec),
-        orders,
-        part,
-    )
-    gate_up_a.add(into.made)
-    into.send(gate_up_a.made)
-    gate_up_a.send()
-    total = ring_sum(after(run, gate_up_a.made), grad_one_parts[3])
+    small_rec = swapped(after(small, total), "seq", 4)
+    total = ring_sum(run, grad_one_parts[3])
+    out_total = ring_sum(after(out_run, total), out_parts[2])
     run = turned(total, "chan", 1)
-    mix_slices = own_slices(after(grad_mix, total), owner)
-    gated_all = gated_mix.reshape(1, seq_rows, chan_cols)
-    outward = Joined(
-        mix_slices, (gated_all, swapped(gated_all, "seq", 1)), orders, part, tall=True
-    )
-    outward.send()
-    small_rec = swapped(after(small[: 2 * width], outward.made), "chan", 1)
-    gate_up_b.add(outward.made)
-    gate_up_b.send()
-    run = after(run, gate_up_b.made)
-    ffn_sum = ring_sum(after(ffn_run, gate_up_b.made), ffn_parts[2])
-    ffn_run = turned(ffn_sum, "chan", 1)
-    down_grad = final_sums(down.finish(ffn_sum), True, (hidden.shape[2], part))
+    out_run = turned(out_total, "chan", 1)
+    down_grad = final_sums(down.finish(total), True, (hidden_a.shape[2], part))
     into.add(down_grad)
-    into.send()
-    gains = small[: 2 * width] + after(small_rec, into.made)
-    small_rec = swapped(gains, "chan", 2)
-    ffn_sum = ring_sum(after(ffn_run, into.made), ffn_parts[3])
-    ffn_run = turned(ffn_sum, "chan", 1)
-    first, third = gate_up_a.finish(ffn_sum)
-    second, fourth = gate_up_b.finish()
+    run = after(run, into.made)
+    into.send(run)
+    out_total = ring_sum(after(out_run, run), out_parts[1])
+    out_run = turned(out_total, "chan", 1)
+    small = small + after(small_rec, run)
+    if seq_count > 8:
+        small = summed(small, "seq", 8)
+    gains = small[: 2 * width]
+    gains_rec = swapped(gains, "chan", 1)
     gate_up_grad = final_sums(
-        [first, second, third, fourth], False, (2, part, hidden.shape[2])
-    )
-    outward.add(gate_up_grad)
-    outward.send()
-    gains = gains + after(small_rec, outward.made)
-    in_grad = final_sums(into.finish(outward.made), False, (3, part, chan_cols))
-    out_grad = final_sums(outward.finish(in_grad), True, (chan_cols, part))
+        [[(gate_up_mine, 0)], [(gate_up_mine, 1)]], False, (2, part, hidden_a.shape[2])
+    )
+    gains = gains + after(gains_rec, gate_up_grad)
+    gains = gains + swapped(gains, "chan", 2)
+    in_grad = final_sums(into.finish(gate_up_grad), False, (3, part, chan_cols))
+    out_grad = out_run.astype(F32) + out_parts[0].astype(F32)
 
     grad_one_own = run.astype(F32) + grad_one_parts[0].astype(F32)
     input_grad = grad_state_own + norm_back(
-        grad_one_own, unit_all[:shard_rows], scale_all[:shard_rows], gain_one
-    )
-    block_output = (state_own + (ffn_run.astype(F32) + ffn_parts[0].astype(F32))).astype(BF)
+        grad_one_own, tokens.astype(F32) * scale_all[:shard_rows], scale_all[:shard_rows], gain_one
+    )
+    block_output = (state_own + ((ffn_one.astype(F32) + ffn_two.astype(F32)) + (ffn_three.astype(F32) + ffn_parts[0].astype(F32)))).astype(BF)
     gains_grad = gains.reshape(2, width)
     conv_grad = small[2 * width :].reshape(3, chan_cols)
     return (

time: 459 us -> 417 us (0.908); the launches traced: 451 us -> 415 us
  Pallas kernels: 129 us -> 153 us
  local copies, waits for them, and re-layouts: 38.8 us -> 21 us
  other arithmetic: 32.3 us -> 15.3 us
  starting transfers between devices: 72.5 us -> 61 us
  waiting for transfers between devices: 160 us -> 150 us
    ppermute x38 -> x33, waiting for transfers between devices: 49.6 us -> 24.5 us  [swapped(): lax.ppermute(block, axis, [(i, i ^ bit) for i in range(lax.axis_size(axis...]
    pallas_call x7 -> x10, Pallas kernels: 76.6 us -> 100 us  [the longest x2 43.3 us: feed_forward(): pl.pallas_call(functools.partial(ffn_body, count), grid_spec=pltpu.Prefet...]
    unnamed x198 -> x134, local copies, waits for them, and re-layouts: 34.8 us -> 13.6 us
    ppermute x24 -> x28, waiting for transfers between devices: 108 us -> 125 us  [turned(): lax.ppermute(block, axis, [(i, (i + distance) % count) for i in range(cou...]
    ppermute x38 -> x33, starting transfers between devices: 35.4 us -> 28.5 us  [swapped(): lax.ppermute(block, axis, [(i, i ^ bit) for i in range(lax.axis_size(axis...]
    convert_element_type x8 -> x5, other arithmetic: 9.88 us -> 3.21 us  [the longest x1 1.17 us: on_device(): (state_own + (ffn_one.astype(F32) + ffn_two.astype(F32) + (ffn_three.asty...]
    mul x1 -> x0, other arithmetic: 4.6 us -> none  [unit_rows(): return (values * inv_scale, inv_scale)]
    ppermute x24 -> x28, starting transfers between devices: 33.4 us -> 29.7 us  [turned(): lax.ppermute(block, axis, [(i, (i + distance) % count) for i in range(cou...]
  transfers between devices with their start and end apart: 66 -> 66, of which waited for: 23 -> 28; matrix products, arithmetic and copies ran while one was open for 8% -> 5% of each run, Pallas kernels for 28% -> 37%
where the time goes in v3:
time: 417 us; the launch traced here: 415 us
  Pallas kernels  153 us (37%)
  waiting for transfers between devices  150 us (36%)
  starting transfers between devices  61 us (15%)
  local copies, waits for them, and re-layouts  21 us (5%)
  other arithmetic  15.3 us (4%)
  between operations  14.7 us (4%)
    ppermute x28, waiting for transfers between devices, turned(): lax.ppermute(block, axis, [(i, (i + distance) % count) for i in range(cou...  125 us
    pallas_call x2, Pallas kernels, feed_forward(): pl.pallas_call(functools.partial(ffn_body, count), grid_spec=pltpu.Prefet...  43.3 us
    ppermute x28, starting transfers between devices, turned(): lax.ppermute(block, axis, [(i, (i + distance) % count) for i in range(cou...  29.7 us
    ppermute x33, starting transfers between devices, swapped(): lax.ppermute(block, axis, [(i, i ^ bit) for i in range(lax.axis_size(axis...  28.5 us
    ppermute x33, waiting for transfers between devices, swapped(): lax.ppermute(block, axis, [(i, i ^ bit) for i in range(lax.axis_size(axis...  24.5 us
    pallas_call x2, Pallas kernels, __init__(): pl.pallas_call(functools.partial(product_body, slots, part, tiles, tall,...  18.2 us
    pallas_call x3, Pallas kernels, final_sums(): pl.pallas_call(functools.partial(sums_body, [len(parts) for parts in sour...  15.6 us
    pallas_call x1, Pallas kernels, whole_product(): pl.pallas_call(functools.partial(whole_body, part, len(units[0])), grid=(...  14.5 us
  transfers between devices with their start and end apart: 66, of which 28 were waited for; matrix products, arithmetic and copies ran while one was open for 5% of the time, Pallas kernels for 37%

profile of v3, /device:TPU:0, one launch (start us, length us, event | category | flops | bytes accessed | tf_op | source)
XLA Modules:
  0.0 415.2 jit_solution(14757368088026803398)
XLA Ops:
  8.2 5.1 %collective-permute-start.1 = (bf16[512,256]{1,0:T(8,128)(2,1)S(1)}, bf16[512,256]{1,0:T(8,128)(2,1)S(1)}, u32[]{:S(2)}, u32[]{:S(2)}) collective-permute-start(bf16[512,256]{1,0:T(8,128)(2,1)S(1)} %constant_dynamic-slice_fusion), channel_id=1, source_target_pairs={{0,3},{1,0},{2,1},{3,2},{4,7},{5,4},{6,5},{7,6},{8,11},{9,8},{10,9... | collective-permute-start | bytes 786440 | tf_op jit(solution)/shard_map/ppermute | solution.py:41
  13.3 6.7 %collective-permute-done.1 = bf16[512,256]{1,0:T(8,128)(2,1)S(1)} collective-permute-done((bf16[512,256]{1,0:T(8,128)(2,1)S(1)}, bf16[512,256]{1,0:T(8,128)(2,1)S(1)}, u32[]{:S(2)}, u32[]{:S(2)}) %collective-permute-start.1) | collective-permute-done | bytes 262176 | tf_op jit(solution)/shard_map/ppermute | solution.py:41
  20.0 5.4 %collective-permute-done = bf16[512,256]{1,0:T(8,128)(2,1)S(1)} collective-permute-done((bf16[512,256]{1,0:T(8,128)(2,1)S(1)}, bf16[512,256]{1,0:T(8,128)(2,1)S(1)}, u32[]{:S(2)}, u32[]{:S(2)}) %collective-permute-start) | collective-permute-done | bytes 262176 | tf_op jit(solution)/shard_map/ppermute | solution.py:41
  27.0 7.3 %collective-permute-done.2 = bf16[512,256]{1,0:T(8,128)(2,1)S(1)} collective-permute-done((bf16[512,256]{1,0:T(8,128)(2,1)S(1)}, bf16[512,256]{1,0:T(8,128)(2,1)S(1)}, u32[]{:S(2)}, u32[]{:S(2)}) %collective-permute-start.2) | collective-permute-done | bytes 262176 | tf_op jit(solution)/shard_map/ppermute | solution.py:41
  37.6 6.0 %collective-permute-done.5 = bf16[1,3,256,256]{3,2,1,0:T(8,128)(2,1)S(1)} collective-permute-done((bf16[1,3,256,256]{3,2,1,0:T(8,128)(2,1)S(1)}, bf16[1,3,256,256]{3,2,1,0:T(8,128)(2,1)S(1)}, u32[]{:S(2)}, u32[]{:S(2)}) %collective-permute-start.5) | collective-permute-done | bytes 393248 | tf_op jit(solution)/shard_map/ppermute | solution.py:45
  47.0 3.8 collective-permute-start.9
  50.8 12.8 %collective-permute-done.7.refs_1_.refs_3_ = bf16[128,2048]{1,0:T(8,128)(2,1)S(1)} collective-permute-done((bf16[128,2048]{1,0:T(8,128)(2,1)S(1)}, bf16[128,2048]{1,0:T(8,128)(2,1)S(1)}, u32[]{:S(2)}, u32[]{:S(2)}) %collective-permute-start.7) | collective-permute-done | bytes 524320 | tf_op jit(solution)/shard_map/ppermute | solution.py:41
  63.6 2.1 collective-permute-start.8
  66.1 2.0 pad_maximum_fusion.refs_5_.refs_1_
  68.0 3.1 collective-permute-done.9.refs_3_.refs_5_
  71.2 10.5 %collective-permute-done.8.refs_2_.refs_4_ = bf16[128,2048]{1,0:T(8,128)(2,1)S(1)} collective-permute-done((bf16[128,2048]{1,0:T(8,128)(2,1)S(1)}, bf16[128,2048]{1,0:T(8,128)(2,1)S(1)}, u32[]{:S(2)}, u32[]{:S(2)}) %collective-permute-start.8) | collective-permute-done | bytes 524320 | tf_op jit(solution)/shard_map/ppermute | solution.py:41
  84.4 8.1 %in_projection.1 = (f32[512,512]{1,0:T(8,128)S(1)}, f32[512,512]{1,0:T(8,128)S(1)}, f32[512,512]{1,0:T(8,128)S(1)}, bf16[512,512]{1,0:T(8,128)(2,1)S(1)}, bf16[5...) custom-call(bf16[128,2048]{1,0:T(8,128)(2,1)S(1)} %copy-done.1, bf16[128,2048]{1,0:T(8,128)(2,1)S(1)} %collective-permute-done.7.refs_1_.refs_3_, ...), custom_call_target="tpu_custom_call" | custom-call | flops 1024 | bytes 1024 | tf_op jit(solution)/shard_map/in_projection/pallas_call | solution.py:600
  98.3 4.3 %conv_forward.1 = (f32[512,512]{1,0:T(8,128)}, bf16[128,512]{1,0:T(8,128)(2,1)}, bf16[128,512]{1,0:T(8,128)(2,1)}, bf16[128,512]{1,0:T(8,128)(2,1)}, bf16[128,512]{1,0:T(8,128)(2,1)}) custom-call(f32[512,512]{1,0:T(8,128)} %copy-done.3, bf16[512,512]{1,0:T(8,128)(2,1)} %copy-done.4, f32[4,2,512]{2,1,0:T(2,128)} %fusion.before.refs_9_, ...), custom_call_target="tpu_custom_call" | custom-call | flops 1024 | bytes 1024 | tf_op jit(solution)/shard_map/conv_forward/pallas_call | solution.py:653
  102.8 1.9 collective-permute-start.13
  105.4 8.2 %collective-permute-done.11.refs_1_ = bf16[128,512]{1,0:T(8,128)(2,1)S(1)} collective-permute-done((bf16[128,512]{1,0:T(8,128)(2,1)}, bf16[128,512]{1,0:T(8,128)(2,1)S(1)}, u32[]{:S(2)}, u32[]{:S(2)}) %collective-permute-start.11) | collective-permute-done | bytes 131104 | tf_op jit(solution)/shard_map/ppermute | solution.py:41
  113.6 15.8 %collective-permute-done.12.refs_2_ = bf16[128,512]{1,0:T(8,128)(2,1)S(1)} collective-permute-done((bf16[128,512]{1,0:T(8,128)(2,1)}, bf16[128,512]{1,0:T(8,128)(2,1)S(1)}, u32[]{:S(2)}, u32[]{:S(2)}) %collective-permute-start.12) | collective-permute-done | bytes 131104 | tf_op jit(solution)/shard_map/ppermute | solution.py:41
  130.2 7.6 %mixer_rows.1 = (f32[128,2048]{1,0:T(8,128)}, bf16[128,2048]{1,0:T(8,128)(2,1)}, f32[128,1]{1,0:T(8,128)}) custom-call(s32[5]{0:T(128)} %pad_add_fusion.2.ids, bf16[128,512]{1,0:T(8,128)(2,1)} %get-tuple-element.237.refs_0_, bf16[128,512]{1,0:T(8,128)(2,1)} %copy-done.37, bf16[128,512]{1,0:T(8,128)(2,1)} %copy-done.38, bf16[128,512]{1,0:T(8,128)(2,1)} %copy-done.39, ...), custom_call_target="tpu_custom_call" | custom-call | flops 1024 | bytes 1024 | tf_op jit(solution)/shard_map/mixer_rows/pallas_call | solution.py:836
  137.8 1.9 pad_maximum_fusion.4
  141.1 14.8 %collective-permute-done.15.refs_1_ = bf16[128,2048]{1,0:T(8,128)(2,1)S(1)} collective-permute-done((bf16[128,2048]{1,0:T(8,128)(2,1)}, bf16[128,2048]{1,0:T(8,128)(2,1)S(1)}, u32[]{:S(2)}, u32[]{:S(2)}) %collective-permute-start.15) | collective-permute-done | bytes 524320 | tf_op jit(solution)/shard_map/ppermute | solution.py:41
  162.7 22.5 %feed_forward.2 = (bf16[1,256,2048]{2,1,0:T(8,128)(2,1)S(1)}, bf16[2,256,2048]{2,1,0:T(8,128)(2,1)}, bf16[128,2048]{1,0:T(8,128)(2,1)S(1)}, bf16[128,2048]{1,0:T...) custom-call(s32[4]{0:T(128)S(1)} %and_select_fusion.ids, bf16[128,2048]{1,0:T(8,128)(2,1)S(1)} %copy-done.5, ...), custom_call_target="tpu_custom_call" | custom-call | flops 1024 | bytes 1024 | tf_op jit(solution)/shard_map/feed_forward/pallas_call | solution.py:141
  185.9 3.8 collective-permute-start.18
  191.5 20.8 %feed_forward.3 = (bf16[1,256,2048]{2,1,0:T(8,128)(2,1)S(1)}, bf16[2,256,2048]{2,1,0:T(8,128)(2,1)}, bf16[128,2048]{1,0:T(8,128)(2,1)S(1)}, bf16[128,2048]{1,0:T...) custom-call(s32[4]{0:T(128)S(1)} %and_select_fusion.ids, ...), custom_call_target="tpu_custom_call" | custom-call | flops 1024 | bytes 1024 | tf_op jit(solution)/shard_map/feed_forward/pallas_call | solution.py:141
  217.7 9.1 %product.2 = (bf16[2,1024,256]{2,1,0:T(8,128)(2,1)}, bf16[2,1024,256]{2,1,0:T(8,128)(2,1)}, bf16[2,1024,256]{2,1,0:T(8,128)(2,1)}, bf16[2,1024,256]{2,1,0:T(8,128)(2,1)}) custom-call(bf16[512,1024]{1,0:T(8,128)(2,1)} %copy-done.14, bf16[512,1024]{1,0:T(8,128)(2,1)} %copy-done.35, bf16[1,256,2048]{2,1,0:T(8,128)(2,1)} %copy-done.13, ...), custom_call_target="tpu_custom_call" | custom-call | flops 1024 | bytes 1024 | tf_op jit(solution)/shard_map/product/pallas_call | solution.py:308
  226.8 2.4 collective-permute-done.20.a
  230.7 14.5 %whole_product.1 = bf16[4,2,256,2048]{3,2,1,0:T(8,128)(2,1)} custom-call(bf16[512,1024]{1,0:T(8,128)(2,1)} %copy-done.10, bf16[512,1024]{1,0:T(8,128)(2,1)} %collective-permute-done.26.rec, bf16[2,256,2048]{2,1,0:T(8,128)(2,1)} %get-tuple-element.177.refs_0_, bf16[2,256,2048]{2,1,0:T(8,128)(2,1)} %get-tuple-element.185.refs_1_, ...), custom_call_target="tpu_custom_call" | custom-call | flops 1024 | bytes 1024 | tf_op jit(solution)/shard_map/whole_product/pallas_call | solution.py:379
  245.2 2.1 collective-permute-done.28
  247.3 9.6 %collective-permute-done.25.refs_3_ = bf16[128,2048]{1,0:T(8,128)(2,1)S(1)} collective-permute-done((bf16[128,2048]{1,0:T(8,128)(2,1)S(1)}, bf16[128,2048]{1,0:T(8,128)(2,1)S(1)}, u32[]{:S(2)}, u32[]{:S(2)}) %collective-permute-start.25) | collective-permute-done | bytes 524320 | tf_op jit(solution)/shard_map/ppermute | solution.py:41
  258.4 9.5 %gated_rows.1 = (bf16[128,512]{1,0:T(8,128)(2,1)}, bf16[128,512]{1,0:T(8,128)(2,1)}, bf16[128,512]{1,0:T(8,128)(2,1)}, bf16[128,512]{1,0:T(8,128)(2,1)}, f32[128...) custom-call(s32[5]{0:T(128)} %pad_add_fusion.2.ids, bf16[512,2048]{1,0:T(8,128)(2,1)} %refs_0_.2, ...), custom_call_target="tpu_custom_call" | custom-call | flops 1024 | bytes 1024 | tf_op jit(solution)/shard_map/gated_rows/pallas_call | solution.py:919
  267.9 2.8 collective-permute-done.31
  270.8 2.4 collective-permute-start.34
  277.0 4.0 upper_sums.2
  286.6 2.0 collective-permute-start.43
  289.9 2.0 collective-permute-start.35
  292.8 2.5 collective-permute-done.43.refs_7_
  298.8 5.5 %conv_backward.1 = (bf16[3,512,512]{2,1,0:T(8,128)(2,1)}, f32[3,512]{1,0:T(4,128)}) custom-call(bf16[128,512]{1,0:T(8,128)(2,1)} %get-tuple-element.196.refs_0_, bf16[128,512]{1,0:T(8,128)(2,1)} %copy-done.54, bf16[128,512]{1,0:T(8,128)(2,1)} %copy-done.53, bf16[128,512]{1,0:T(8,128)(2,1)} %copy-done.52, f32[512,512]{1,0:T(8,128)} %copy-done.11, ...), custom_call_target="tpu_custom_call" | custom-call | flops 1024 | bytes 1024 | tf_op jit(solution)/shard_map/conv_backward/pallas_call | solution.py:713
  304.4 7.8 %mixer_back.1 = (bf16[128,2048]{1,0:T(8,128)(2,1)}, bf16[128,2048]{1,0:T(8,128)(2,1)}, bf16[128,2048]{1,0:T(8,128)(2,1)}, bf16[128,2048]{1,0:T(8,128)(2,1)}, f32[1,2048]{1,0:T(1,128)}) custom-call(bf16[3,512,512]{2,1,0:T(8,128)(2,1)} %get-tuple-element.241.refs_0_.refs_2_, bf16[3,2048,512]{2,1,0:T(8,128)(2,1)} %refs_1_.1, bf16[128,2048]{1,0:T(8,128)(2,1)} %refs_2_.1, ...), custom_call_target="tpu_custom_call" | custom-call | flops 1024 | bytes 1024 | tf_op jit(solution)/shard_map/mixer_back/pallas_call | solution.py:757
  312.2 9.7 %collective-permute-done.45.refs_5_ = bf16[1,1024,256]{2,1,0:T(8,128)(2,1)S(1)} collective-permute-done((bf16[1,1024,256]{2,1,0:T(8,128)(2,1)}, bf16[1,1024,256]{2,1,0:T(8,128)(2,1)S(1)}, u32[]{:S(2)}, u32[]{:S(2)}) %collective-permute-start.45) | collective-permute-done | bytes 524320 | tf_op jit(solution)/shard_map/ppermute | solution.py:45
  325.5 5.7 %rows_product.1 = bf16[4,512,256]{2,1,0:T(8,128)(2,1)} custom-call(s32[8]{0:T(128)} %copy-done.22, bf16[1024,2048]{1,0:T(8,128)(2,1)} %all-gather.5.cloned.1.call-done.gated, bf16[128,256]{1,0:T(8,128)(2,1)} %copy-done.21, bf16[128,256]{1,0:T(8,128)(2,1)} %copy-done.55, bf16[128,256]{1,0:T(8,128)(2,1)} %copy-done.56, bf16[128,256]{1,0:T(8,128)(2,1)} %copy-done.57, ...), custom_call_target="tpu_custom_call" | custom-call | flops 1024 | bytes 1024 | tf_op jit(solution)/shard_map/rows_product/pallas_call | solution.py:526
  331.3 9.1 %product.3 = (bf16[2,256,768]{2,1,0:T(8,128)(2,1)}, bf16[2,256,768]{2,1,0:T(8,128)(2,1)}, bf16[2,256,768]{2,1,0:T(8,128)(2,1)}, bf16[2,256,768]{2,1,0:T(8,128)(2,1)}) custom-call(bf16[512,1024]{1,0:T(8,128)(2,1)} %copy-done.9, bf16[512,1024]{1,0:T(8,128)(2,1)} %collective-permute-done.48.refs_1_, bf16[3,512,512]{2,1,0:T(8,128)(2,1)} %get-tuple-element.241.refs_0_.refs_2_, ...), custom_call_target="tpu_custom_call" | custom-call | flops 1024 | bytes 1024 | tf_op jit(solution)/shard_map/product/pallas_call | solution.py:308
  341.6 3.4 collective-permute-done.50
  351.0 11.4 %collective-permute-done.51.a = bf16[128,2048]{1,0:T(8,128)(2,1)S(1)} collective-permute-done((bf16[128,2048]{1,0:T(8,128)(2,1)S(1)}, bf16[128,2048]{1,0:T(8,128)(2,1)S(1)}, u32[]{:S(2)}, u32[]{:S(2)}) %collective-permute-start.51) | collective-permute-done | bytes 524320 | tf_op jit(solution)/shard_map/ppermute | solution.py:41
  362.7 5.4 %collective-permute-done.60.a = bf16[512,256]{1,0:T(8,128)(2,1)S(1)} collective-permute-done((bf16[512,256]{1,0:T(8,128)(2,1)S(1)}, bf16[512,256]{1,0:T(8,128)(2,1)S(1)}, u32[]{:S(2)}, u32[]{:S(2)}) %collective-permute-start.60) | collective-permute-done | bytes 262176 | tf_op jit(solution)/shard_map/ppermute | solution.py:41
  369.4 4.4 %final_sums.3 = f32[2048,256]{1,0:T(8,128)} custom-call(bf16[2,1024,256]{2,1,0:T(8,128)(2,1)} %get-tuple-element.250.refs_0_, bf16[2,1024,256]{2,1,0:T(8,128)(2,1)} %collective-permute-done.29.refs_1_, bf16[1,1024,256]{2,1,0:T(8,128)(2,1)} %copy-done.41, bf16[2,1024,256]{2,1,0:T(8,128)(2,1)} %get-tuple-element.213.refs_2_.refs_3_, ...), custom_call_target="tpu_custom_call" | custom-call | flops 1024 | bytes 1024 | tf_op jit(solution)/shard_map/final_sums/pallas_call | solution.py:476
  374.1 4.0 upper_sums.3
  379.3 4.3 %collective-permute-done.61.a = bf16[512,256]{1,0:T(8,128)(2,1)S(1)} collective-permute-done((bf16[512,256]{1,0:T(8,128)(2,1)S(1)}, bf16[512,256]{1,0:T(8,128)(2,1)S(1)}, u32[]{:S(2)}, u32[]{:S(2)}) %collective-permute-start.61) | collective-permute-done | bytes 262176 | tf_op jit(solution)/shard_map/ppermute | solution.py:41
  390.1 6.2 %final_sums.4 = f32[2,256,2048]{2,1,0:T(8,128)} custom-call(bf16[2,256,2048]{2,1,0:T(8,128)(2,1)} %bitcast.53, bf16[2,256,2048]{2,1,0:T(8,128)(2,1)} %bitcast.54), custom_call_target="tpu_custom_call" | custom-call | flops 1024 | bytes 1024 | tf_op jit(solution)/shard_map/final_sums/pallas_call | solution.py:476
  397.0 4.3 %collective-permute-start.57 = (f32[4096]{0:T(1024)S(1)}, f32[4096]{0:T(1024)S(1)}, u32[]{:S(2)}, u32[]{:S(2)}) collective-permute-start(f32[4096]{0:T(1024)S(1)} %slice_add_fusion), channel_id=1, source_target_pairs={{0,2},{1,3},{2,0},{3,1},{4,6},{5,7},{6,4},{7,5},{8,10},{9,11},{10,... | collective-permute-start | bytes 49160 | tf_op jit(solution)/shard_map/ppermute | solution.py:45
  402.9 5.1 %final_sums.5 = f32[3,256,512]{2,1,0:T(8,128)} custom-call(bf16[2,256,768]{2,1,0:T(8,128)(2,1)} %get-tuple-element.264.refs_0_, bf16[2,256,768]{2,1,0:T(8,128)(2,1)} %collective-permute-done.53.refs_1_, bf16[1,256,768]{2,1,0:T(8,128)(2,1)} %collective-permute-done.58.refs_2_, bf16[2,256,768]{2,1,0:T(8,128)(2,1)} %get-tuple-element.253.refs_2_.refs_3_, ...), custom_call_target="tpu_custom_call" | custom-call | flops 1024 | bytes 1024 | tf_op jit(solution)/shard_map/final_sums/pallas_call | solution.py:476
  (306 shorter events, 76.5 us)
Async XLA Ops:
  7.2 155.6 %all-gather.3.cloned.1.call-start = ((), (), s32[]{:S(2)}) async-start(), calls=%async_computation.1 | async-start | bytes 2621440 | tf_op jit(solution)/shard_map/all_gather | solution.py:1006
  8.2 11.8 %collective-permute-start.1 = (bf16[512,256]{1,0:T(8,128)(2,1)S(1)}, bf16[512,256]{1,0:T(8,128)(2,1)S(1)}, u32[]{:S(2)}, u32[]{:S(2)}) collective-permute-start(bf16[512,256]{1,0:T(8,128)(2,1)S(1)} %constant_dynamic-slice_fusion), channel_id=1, source_target_pairs={{0,3},{1,0},{2,1},{3,2},{4,7},{5,4},{6,5},{7,6},{8,11},{9,8},{10,9... | collective-permute-start | bytes 786440 | tf_op jit(solution)/shard_map/ppermute | solution.py:41
  13.3 12.1 %collective-permute-start = (bf16[512,256]{1,0:T(8,128)(2,1)S(1)}, bf16[512,256]{1,0:T(8,128)(2,1)S(1)}, u32[]{:S(2)}, u32[]{:S(2)}) collective-permute-start(bf16[512,256]{1,0:T(8,128)(2,1)S(1)} %constant_dynamic-slice_fusion), channel_id=1, source_target_pairs={{0,1},{1,2},{2,3},{3,0},{4,5},{5,6},{6,7},{7,4},{8,9},{9,10},{10,1... | collective-permute-start | bytes 786440 | tf_op jit(solution)/shard_map/ppermute | solution.py:41
  43.7 22.0 %collective-permute-start.6 = (bf16[2,3,256,256]{3,2,1,0:T(8,128)(2,1)S(1)}, bf16[2,3,256,256]{3,2,1,0:T(8,128)(2,1)S(1)}, u32[]{:S(2)}, u32[]{:S(2)}) collective-permute-start(bf16[2,3,256,256]{3,2,1,0:T(8,128)(2,1)S(1)} %pad_maximum_fusion.3), channel_id=1, source_target_pairs={{0,8},{4,12},{8,0},{12,4},{16,24},{20,28},{24,16},{28,20},{1,9},{5... | collective-permute-start | bytes 2359304 | tf_op jit(solution)/shard_map/ppermute | solution.py:45
  46.3 19.8 %collective-permute-start.4 = (bf16[2,3,256,256]{3,2,1,0:T(8,128)(2,1)S(1)}, bf16[2,3,256,256]{3,2,1,0:T(8,128)(2,1)S(1)}, u32[]{:S(2)}, u32[]{:S(2)}) collective-permute-start(bf16[2,3,256,256]{3,2,1,0:T(8,128)(2,1)S(1)} %pad_maximum_fusion.2), channel_id=1, source_target_pairs={{0,16},{4,20},{8,24},{12,28},{16,0},{20,4},{24,8},{28,12},{1,17},{... | collective-permute-start | bytes 2359304 | tf_op jit(solution)/shard_map/ppermute | solution.py:45
  47.0 16.7 %collective-permute-start.7 = (bf16[128,2048]{1,0:T(8,128)(2,1)S(1)}, bf16[128,2048]{1,0:T(8,128)(2,1)S(1)}, u32[]{:S(2)}, u32[]{:S(2)}) collective-permute-start(bf16[128,2048]{1,0:T(8,128)(2,1)S(1)} %copy-done.1), channel_id=1, source_target_pairs={{0,1},{1,2},{2,3},{3,0},{4,5},{5,6},{6,7},{7,4},{8,9},{9,10},{10,1... | collective-permute-start | bytes 1572872 | tf_op jit(solution)/shard_map/ppermute | solution.py:41
  47.0 24.2 %collective-permute-start.9 = (bf16[128,2048]{1,0:T(8,128)(2,1)S(1)}, bf16[128,2048]{1,0:T(8,128)(2,1)S(1)}, u32[]{:S(2)}, u32[]{:S(2)}) collective-permute-start(bf16[128,2048]{1,0:T(8,128)(2,1)S(1)} %copy-done.1), channel_id=1, source_target_pairs={{0,3},{1,0},{2,1},{3,2},{4,7},{5,4},{6,5},{7,6},{8,11},{9,8},{10,9... | collective-permute-start | bytes 1572872 | tf_op jit(solution)/shard_map/ppermute | solution.py:41
  63.6 18.0 %collective-permute-start.8 = (bf16[128,2048]{1,0:T(8,128)(2,1)S(1)}, bf16[128,2048]{1,0:T(8,128)(2,1)S(1)}, u32[]{:S(2)}, u32[]{:S(2)}) collective-permute-start(bf16[128,2048]{1,0:T(8,128)(2,1)S(1)} %collective-permute-done.7.refs_1_.refs_3_), channel_id=1, source_target_pairs={{0,1},{1,2},{2,3},{3,0},{4,5},{5,6},{6,7},{7,4},{8,9},{9,10},{10,1... | collective-permute-start | bytes 1572872 | tf_op jit(solution)/shard_map/ppermute | solution.py:41
  68.0 61.4 %collective-permute-start.14 = (bf16[4,3,512,256]{3,2,1,0:T(8,128)(2,1)}, bf16[4,3,512,256]{3,2,1,0:T(8,128)(2,1)}, u32[]{:S(2)}, u32[]{:S(2)}) collective-permute-start(bf16[4,3,512,256]{3,2,1,0:T(8,128)(2,1)} %pad_maximum_fusion.refs_5_.refs_1_), channel_id=1, source_target_pairs={{0,4},{4,0},{8,12},{12,8},{16,20},{20,16},{24,28},{28,24},{1,5},{5... | collective-permute-start | bytes 9437192 | tf_op jit(solution)/shard_map/ppermute | solution.py:45
  81.7 175.3 %all-gather.5.cloned.1.call-start = ((), (), s32[]{:S(2)}) async-start(), calls=%async_computation.2 | async-start | bytes 4718592 | tf_op jit(solution)/shard_map/all_gather | solution.py:1047
  102.7 10.9 %collective-permute-start.11 = (bf16[128,512]{1,0:T(8,128)(2,1)}, bf16[128,512]{1,0:T(8,128)(2,1)S(1)}, u32[]{:S(2)}, u32[]{:S(2)}) collective-permute-start(bf16[128,512]{1,0:T(8,128)(2,1)} %get-tuple-element.146), channel_id=1, source_target_pairs={{0,3},{1,0},{2,1},{3,2},{4,7},{5,4},{6,5},{7,6},{8,11},{9,8},{10,9... | collective-permute-start | bytes 393224 | tf_op jit(solution)/shard_map/ppermute | solution.py:41
  102.7 26.7 %collective-permute-start.12 = (bf16[128,512]{1,0:T(8,128)(2,1)}, bf16[128,512]{1,0:T(8,128)(2,1)S(1)}, u32[]{:S(2)}, u32[]{:S(2)}) collective-permute-start(bf16[128,512]{1,0:T(8,128)(2,1)} %get-tuple-element.147), channel_id=1, source_target_pairs={{0,2},{1,3},{2,0},{3,1},{4,6},{5,7},{6,4},{7,5},{8,10},{9,11},{10,... | collective-permute-start | bytes 393224 | tf_op jit(solution)/shard_map/ppermute | solution.py:41
  102.8 26.6 %collective-permute-start.13 = (bf16[128,512]{1,0:T(8,128)(2,1)}, bf16[128,512]{1,0:T(8,128)(2,1)S(1)}, u32[]{:S(2)}, u32[]{:S(2)}) collective-permute-start(bf16[128,512]{1,0:T(8,128)(2,1)} %get-tuple-element.148), channel_id=1, source_target_pairs={{0,1},{1,2},{2,3},{3,0},{4,5},{5,6},{6,7},{7,4},{8,9},{9,10},{10,1... | collective-permute-start | bytes 393224 | tf_op jit(solution)/shard_map/ppermute | solution.py:41
  139.6 250.5 %reduce-scatter.2.cloned.1.call-start = ((), (), s32[]{:S(2)}) async-start(), calls=%async_computation.3 | async-start | bytes 10485760 | tf_op jit(solution)/shard_map/reduce_scatter | solution.py:397
  139.7 16.3 %collective-permute-start.15 = (bf16[128,2048]{1,0:T(8,128)(2,1)}, bf16[128,2048]{1,0:T(8,128)(2,1)S(1)}, u32[]{:S(2)}, u32[]{:S(2)}) collective-permute-start(bf16[128,2048]{1,0:T(8,128)(2,1)} %get-tuple-element.160.refs_0_), channel_id=1, source_target_pairs={{0,1},{1,2},{2,3},{3,0},{4,5},{5,6},{6,7},{7,4},{8,9},{9,10},{10,1... | collective-permute-start | bytes 1572872 | tf_op jit(solution)/shard_map/ppermute | solution.py:41
  156.0 29.3 %collective-permute-start.17 = (bf16[128,2048]{1,0:T(8,128)(2,1)}, bf16[128,2048]{1,0:T(8,128)(2,1)S(1)}, u32[]{:S(2)}, u32[]{:S(2)}) collective-permute-start(bf16[128,2048]{1,0:T(8,128)(2,1)} %get-tuple-element.160.refs_0_), channel_id=1, source_target_pairs={{0,3},{1,0},{2,1},{3,2},{4,7},{5,4},{6,5},{7,6},{8,11},{9,8},{10,9... | collective-permute-start | bytes 1572872 | tf_op jit(solution)/shard_map/ppermute | solution.py:41
  156.9 28.4 %collective-permute-start.16 = (bf16[128,2048]{1,0:T(8,128)(2,1)S(1)}, bf16[128,2048]{1,0:T(8,128)(2,1)S(1)}, u32[]{:S(2)}, u32[]{:S(2)}) collective-permute-start(bf16[128,2048]{1,0:T(8,128)(2,1)S(1)} %collective-permute-done.15.refs_1_), channel_id=1, source_target_pairs={{0,1},{1,2},{2,3},{3,0},{4,5},{5,6},{6,7},{7,4},{8,9},{9,10},{10,1... | collective-permute-start | bytes 1572872 | tf_op jit(solution)/shard_map/ppermute | solution.py:41
  185.3 27.2 %collective-permute-start.23 = (bf16[2,256,2048]{2,1,0:T(8,128)(2,1)}, bf16[2,256,2048]{2,1,0:T(8,128)(2,1)S(1)}, u32[]{:S(2)}, u32[]{:S(2)}) collective-permute-start(bf16[2,256,2048]{2,1,0:T(8,128)(2,1)} %get-tuple-element.177.refs_0_), channel_id=1, source_target_pairs={{0,4},{4,0},{8,12},{12,8},{16,20},{20,16},{24,28},{28,24},{1,5},{5... | collective-permute-start | bytes 6291464 | tf_op jit(solution)/shard_map/ppermute | solution.py:45
  185.4 27.1 %collective-permute-start.22 = (bf16[1,256,2048]{2,1,0:T(8,128)(2,1)S(1)}, bf16[1,256,2048]{2,1,0:T(8,128)(2,1)}, u32[]{:S(2)}, u32[]{:S(2)}) collective-permute-start(bf16[1,256,2048]{2,1,0:T(8,128)(2,1)S(1)} %get-tuple-element.163.refs_2_), channel_id=1, source_target_pairs={{0,4},{4,0},{8,12},{12,8},{16,20},{20,16},{24,28},{28,24},{1,5},{5... | collective-permute-start | bytes 3145736 | tf_op jit(solution)/shard_map/ppermute | solution.py:45
  185.8 26.4 %collective-permute-start.19 = (bf16[128,2048]{1,0:T(8,128)(2,1)S(1)}, bf16[128,2048]{1,0:T(8,128)(2,1)S(1)}, u32[]{:S(2)}, u32[]{:S(2)}) collective-permute-start(bf16[128,2048]{1,0:T(8,128)(2,1)S(1)} %get-tuple-element.169), channel_id=1, source_target_pairs={{0,1},{1,2},{2,3},{3,0},{4,5},{5,6},{6,7},{7,4},{8,9},{9,10},{10,1... | collective-permute-start | bytes 1572872 | tf_op jit(solution)/shard_map/ppermute | solution.py:41
  185.9 26.6 %collective-permute-start.18 = (bf16[128,2048]{1,0:T(8,128)(2,1)S(1)}, bf16[128,2048]{1,0:T(8,128)(2,1)S(1)}, u32[]{:S(2)}, u32[]{:S(2)}) collective-permute-start(bf16[128,2048]{1,0:T(8,128)(2,1)S(1)} %get-tuple-element.161), channel_id=1, source_target_pairs={{0,3},{1,0},{2,1},{3,2},{4,7},{5,4},{6,5},{7,6},{8,11},{9,8},{10,9... | collective-permute-start | bytes 1572872 | tf_op jit(solution)/shard_map/ppermute | solution.py:41
  191.5 25.3 %collective-permute-start.21 = (bf16[512,1024]{1,0:T(8,128)(2,1)S(1)}, bf16[512,1024]{1,0:T(8,128)(2,1)S(1)}, u32[]{:S(2)}, u32[]{:S(2)}) collective-permute-start(bf16[512,1024]{1,0:T(8,128)(2,1)S(1)} %get-tuple-element.174), channel_id=1, source_target_pairs={{0,4},{4,0},{8,12},{12,8},{16,20},{20,16},{24,28},{28,24},{1,5},{5... | collective-permute-start | bytes 3145736 | tf_op jit(solution)/shard_map/ppermute | solution.py:45
  213.1 17.7 %collective-permute-start.27 = (bf16[2,256,2048]{2,1,0:T(8,128)(2,1)}, bf16[2,256,2048]{2,1,0:T(8,128)(2,1)}, u32[]{:S(2)}, u32[]{:S(2)}) collective-permute-start(bf16[2,256,2048]{2,1,0:T(8,128)(2,1)} %get-tuple-element.185.refs_1_), channel_id=1, source_target_pairs={{0,4},{4,0},{8,12},{12,8},{16,20},{20,16},{24,28},{28,24},{1,5},{5... | collective-permute-start | bytes 6291464 | tf_op jit(solution)/shard_map/ppermute | solution.py:45
  213.1 16.1 %collective-permute-start.20 = (bf16[128,2048]{1,0:T(8,128)(2,1)S(1)}, bf16[128,2048]{1,0:T(8,128)(2,1)S(1)}, u32[]{:S(2)}, u32[]{:S(2)}) collective-permute-start(bf16[128,2048]{1,0:T(8,128)(2,1)S(1)} %ring_sum.6), channel_id=1, source_target_pairs={{0,1},{1,2},{2,3},{3,0},{4,5},{5,6},{6,7},{7,4},{8,9},{9,10},{10,1... | collective-permute-start | bytes 1572872 | tf_op jit(solution)/shard_map/ppermute | solution.py:41
  216.2 14.4 %collective-permute-start.26 = (bf16[512,1024]{1,0:T(8,128)(2,1)}, bf16[512,1024]{1,0:T(8,128)(2,1)}, u32[]{:S(2)}, u32[]{:S(2)}) collective-permute-start(bf16[512,1024]{1,0:T(8,128)(2,1)} %get-tuple-element.183), channel_id=1, source_target_pairs={{0,4},{4,0},{8,12},{12,8},{16,20},{20,16},{24,28},{28,24},{1,5},{5... | collective-permute-start | bytes 3145736 | tf_op jit(solution)/shard_map/ppermute | solution.py:45
  229.4 27.5 %collective-permute-start.30 = (bf16[2,1024,256]{2,1,0:T(8,128)(2,1)}, bf16[2,1024,256]{2,1,0:T(8,128)(2,1)S(1)}, u32[]{:S(2)}, u32[]{:S(2)}) collective-permute-start(bf16[2,1024,256]{2,1,0:T(8,128)(2,1)} %get-tuple-element.190), channel_id=1, source_target_pairs={{0,16},{4,20},{8,24},{12,28},{16,0},{20,4},{24,8},{28,12},{1,17},{... | collective-permute-start | bytes 3145736 | tf_op jit(solution)/shard_map/ppermute | solution.py:45
  229.4 27.5 %collective-permute-start.29 = (bf16[2,1024,256]{2,1,0:T(8,128)(2,1)}, bf16[2,1024,256]{2,1,0:T(8,128)(2,1)}, u32[]{:S(2)}, u32[]{:S(2)}) collective-permute-start(bf16[2,1024,256]{2,1,0:T(8,128)(2,1)} %get-tuple-element.188), channel_id=1, source_target_pairs={{0,8},{4,12},{8,0},{12,4},{16,24},{20,28},{24,16},{28,20},{1,9},{5... | collective-permute-start | bytes 3145736 | tf_op jit(solution)/shard_map/ppermute | solution.py:45
  230.6 16.7 %collective-permute-start.28 = (bf16[128,2048]{1,0:T(8,128)(2,1)S(1)}, bf16[128,2048]{1,0:T(8,128)(2,1)S(1)}, u32[]{:S(2)}, u32[]{:S(2)}) collective-permute-start(bf16[128,2048]{1,0:T(8,128)(2,1)S(1)} %copy-done.28), channel_id=1, source_target_pairs={{0,1},{1,2},{2,3},{3,0},{4,5},{5,6},{6,7},{7,4},{8,9},{9,10},{10,1... | collective-permute-start | bytes 1572872 | tf_op jit(solution)/shard_map/ppermute | solution.py:41
  230.7 26.2 %collective-permute-start.25 = (bf16[128,2048]{1,0:T(8,128)(2,1)S(1)}, bf16[128,2048]{1,0:T(8,128)(2,1)S(1)}, u32[]{:S(2)}, u32[]{:S(2)}) collective-permute-start(bf16[128,2048]{1,0:T(8,128)(2,1)S(1)} %ring_sum.7), channel_id=1, source_target_pairs={{0,1},{1,2},{2,3},{3,0},{4,5},{5,6},{6,7},{7,4},{8,9},{9,10},{10,1... | collective-permute-start | bytes 1572872 | tf_op jit(solution)/shard_map/ppermute | solution.py:41
  258.4 12.4 %collective-permute-start.31 = (bf16[128,2048]{1,0:T(8,128)(2,1)S(1)}, bf16[128,2048]{1,0:T(8,128)(2,1)}, u32[]{:S(2)}, u32[]{:S(2)}) collective-permute-start(bf16[128,2048]{1,0:T(8,128)(2,1)S(1)} %copy-done.26), channel_id=1, source_target_pairs={{0,3},{1,0},{2,1},{3,2},{4,7},{5,4},{6,5},{7,6},{8,11},{9,8},{10,9... | collective-permute-start | bytes 1572872 | tf_op jit(solution)/shard_map/ppermute | solution.py:41
  273.2 11.5 %collective-permute-start.32 = (bf16[128,512]{1,0:T(8,128)(2,1)}, bf16[128,512]{1,0:T(8,128)(2,1)S(1)}, u32[]{:S(2)}, u32[]{:S(2)}) collective-permute-start(bf16[128,512]{1,0:T(8,128)(2,1)} %get-tuple-element.198), channel_id=1, source_target_pairs={{0,1},{1,2},{2,3},{3,0},{4,5},{5,6},{6,7},{7,4},{8,9},{9,10},{10,1... | collective-permute-start | bytes 393224 | tf_op jit(solution)/shard_map/ppermute | solution.py:41
  276.0 10.5 %collective-permute-start.38 = (bf16[128,256]{1,0:T(8,128)(2,1)S(1)}, bf16[128,256]{1,0:T(8,128)(2,1)S(1)}, u32[]{:S(2)}, u32[]{:S(2)}) collective-permute-start(bf16[128,256]{1,0:T(8,128)(2,1)S(1)} %get-tuple-element.220), channel_id=1, source_target_pairs={{0,8},{4,12},{8,0},{12,4},{16,24},{20,28},{24,16},{28,20},{1,9},{5... | collective-permute-start | bytes 196616 | tf_op jit(solution)/shard_map/ppermute | solution.py:45
  289.9 22.2 %collective-permute-start.35 = (bf16[128,2048]{1,0:T(8,128)(2,1)}, bf16[128,2048]{1,0:T(8,128)(2,1)S(1)}, u32[]{:S(2)}, u32[]{:S(2)}) collective-permute-start(bf16[128,2048]{1,0:T(8,128)(2,1)} %collective-permute-done.31), channel_id=1, source_target_pairs={{0,3},{1,0},{2,1},{3,2},{4,7},{5,4},{6,5},{7,6},{8,11},{9,8},{10,9... | collective-permute-start | bytes 1572872 | tf_op jit(solution)/shard_map/ppermute | solution.py:41
  295.9 25.9 %collective-permute-start.45 = (bf16[1,1024,256]{2,1,0:T(8,128)(2,1)}, bf16[1,1024,256]{2,1,0:T(8,128)(2,1)S(1)}, u32[]{:S(2)}, u32[]{:S(2)}) collective-permute-start(bf16[1,1024,256]{2,1,0:T(8,128)(2,1)} %get-tuple-element.231), channel_id=1, source_target_pairs={{0,8},{4,12},{8,0},{12,4},{16,24},{20,28},{24,16},{28,20},{1,9},{5... | collective-permute-start | bytes 1572872 | tf_op jit(solution)/shard_map/ppermute | solution.py:45
  296.8 25.8 %collective-permute-start.44 = (bf16[1,1024,256]{2,1,0:T(8,128)(2,1)}, bf16[1,1024,256]{2,1,0:T(8,128)(2,1)S(1)}, u32[]{:S(2)}, u32[]{:S(2)}) collective-permute-start(bf16[1,1024,256]{2,1,0:T(8,128)(2,1)} %get-tuple-element.229), channel_id=1, source_target_pairs={{0,16},{4,20},{8,24},{12,28},{16,0},{20,4},{24,8},{28,12},{1,17},{... | collective-permute-start | bytes 1572872 | tf_op jit(solution)/shard_map/ppermute | solution.py:45
  323.1 22.4 %collective-permute-start.46 = (bf16[128,2048]{1,0:T(8,128)(2,1)}, bf16[128,2048]{1,0:T(8,128)(2,1)S(1)}, u32[]{:S(2)}, u32[]{:S(2)}) collective-permute-start(bf16[128,2048]{1,0:T(8,128)(2,1)} %get-tuple-element.232), channel_id=1, source_target_pairs={{0,1},{1,2},{2,3},{3,0},{4,5},{5,6},{6,7},{7,4},{8,9},{9,10},{10,1... | collective-permute-start | bytes 1572872 | tf_op jit(solution)/shard_map/ppermute | solution.py:41
  325.5 14.9 %collective-permute-start.47 = (f32[5632]{0:T(1024)S(1)}, f32[5632]{0:T(1024)S(1)}, u32[]{:S(2)}, u32[]{:S(2)}) collective-permute-start(f32[5632]{0:T(1024)S(1)} %pad_maximum_fusion.5), channel_id=1, source_target_pairs={{0,4},{4,0},{8,12},{12,8},{16,20},{20,16},{24,28},{28,24},{1,5},{5... | collective-permute-start | bytes 67592 | tf_op jit(solution)/shard_map/ppermute | solution.py:45
  345.8 16.7 %collective-permute-start.51 = (bf16[128,2048]{1,0:T(8,128)(2,1)S(1)}, bf16[128,2048]{1,0:T(8,128)(2,1)S(1)}, u32[]{:S(2)}, u32[]{:S(2)}) collective-permute-start(bf16[128,2048]{1,0:T(8,128)(2,1)S(1)} %ring_sum.8), channel_id=1, source_target_pairs={{0,1},{1,2},{2,3},{3,0},{4,5},{5,6},{6,7},{7,4},{8,9},{9,10},{10,1... | collective-permute-start | bytes 1572872 | tf_op jit(solution)/shard_map/ppermute | solution.py:41
  345.9 22.2 %collective-permute-start.60 = (bf16[512,256]{1,0:T(8,128)(2,1)S(1)}, bf16[512,256]{1,0:T(8,128)(2,1)S(1)}, u32[]{:S(2)}, u32[]{:S(2)}) collective-permute-start(bf16[512,256]{1,0:T(8,128)(2,1)S(1)} %get-tuple-element.280), channel_id=1, source_target_pairs={{0,1},{1,2},{2,3},{3,0},{4,5},{5,6},{6,7},{7,4},{8,9},{9,10},{10,1... | collective-permute-start | bytes 786440 | tf_op jit(solution)/shard_map/ppermute | solution.py:41
  346.7 27.1 %collective-permute-start.54 = (bf16[2,256,768]{2,1,0:T(8,128)(2,1)}, bf16[2,256,768]{2,1,0:T(8,128)(2,1)}, u32[]{:S(2)}, u32[]{:S(2)}) collective-permute-start(bf16[2,256,768]{2,1,0:T(8,128)(2,1)} %get-tuple-element.255), channel_id=1, source_target_pairs={{0,16},{4,20},{8,24},{12,28},{16,0},{20,4},{24,8},{28,12},{1,17},{... | collective-permute-start | bytes 2359304 | tf_op jit(solution)/shard_map/ppermute | solution.py:45
  348.1 26.0 %collective-permute-start.53 = (bf16[2,256,768]{2,1,0:T(8,128)(2,1)}, bf16[2,256,768]{2,1,0:T(8,128)(2,1)}, u32[]{:S(2)}, u32[]{:S(2)}) collective-permute-start(bf16[2,256,768]{2,1,0:T(8,128)(2,1)} %get-tuple-element.252), channel_id=1, source_target_pairs={{0,8},{4,12},{8,0},{12,4},{16,24},{20,28},{24,16},{28,20},{1,9},{5... | collective-permute-start | bytes 2359304 | tf_op jit(solution)/shard_map/ppermute | solution.py:45
  350.2 36.2 %collective-permute-start.55 = (f32[5632]{0:T(1024)}, f32[5632]{0:T(1024)}, u32[]{:S(2)}, u32[]{:S(2)}) collective-permute-start(f32[5632]{0:T(1024)} %add.227), channel_id=1, source_target_pairs={{0,16},{4,20},{8,24},{12,28},{16,0},{20,4},{24,8},{28,12},{1,17},{... | collective-permute-start | bytes 67592 | tf_op jit(solution)/shard_map/ppermute | solution.py:45
  362.6 16.7 %collective-permute-start.52 = (bf16[128,2048]{1,0:T(8,128)(2,1)S(1)}, bf16[128,2048]{1,0:T(8,128)(2,1)S(1)}, u32[]{:S(2)}, u32[]{:S(2)}) collective-permute-start(bf16[128,2048]{1,0:T(8,128)(2,1)S(1)} %ring_sum.9), channel_id=1, source_target_pairs={{0,1},{1,2},{2,3},{3,0},{4,5},{5,6},{6,7},{7,4},{8,9},{9,10},{10,1... | collective-permute-start | bytes 1572872 | tf_op jit(solution)/shard_map/ppermute | solution.py:41
  368.1 15.5 %collective-permute-start.61 = (bf16[512,256]{1,0:T(8,128)(2,1)S(1)}, bf16[512,256]{1,0:T(8,128)(2,1)S(1)}, u32[]{:S(2)}, u32[]{:S(2)}) collective-permute-start(bf16[512,256]{1,0:T(8,128)(2,1)S(1)} %ring_sum.10), channel_id=1, source_target_pairs={{0,1},{1,2},{2,3},{3,0},{4,5},{5,6},{6,7},{7,4},{8,9},{9,10},{10,1... | collective-permute-start | bytes 786440 | tf_op jit(solution)/shard_map/ppermute | solution.py:41
  383.7 17.6 %collective-permute-start.62 = (bf16[512,256]{1,0:T(8,128)(2,1)S(1)}, bf16[512,256]{1,0:T(8,128)(2,1)S(1)}, u32[]{:S(2)}, u32[]{:S(2)}) collective-permute-start(bf16[512,256]{1,0:T(8,128)(2,1)S(1)} %ring_sum.11), channel_id=1, source_target_pairs={{0,1},{1,2},{2,3},{3,0},{4,5},{5,6},{6,7},{7,4},{8,9},{9,10},{10,1... | collective-permute-start | bytes 786440 | tf_op jit(solution)/shard_map/ppermute | solution.py:41
  383.8 18.4 %collective-permute-start.59 = (bf16[1,256,768]{2,1,0:T(8,128)(2,1)}, bf16[1,256,768]{2,1,0:T(8,128)(2,1)S(1)}, u32[]{:S(2)}, u32[]{:S(2)}) collective-permute-start(bf16[1,256,768]{2,1,0:T(8,128)(2,1)} %get-tuple-element.267), channel_id=1, source_target_pairs={{0,8},{4,12},{8,0},{12,4},{16,24},{20,28},{24,16},{28,20},{1,9},{5... | collective-permute-start | bytes 1179656 | tf_op jit(solution)/shard_map/ppermute | solution.py:45
  385.3 16.9 %collective-permute-start.58 = (bf16[1,256,768]{2,1,0:T(8,128)(2,1)}, bf16[1,256,768]{2,1,0:T(8,128)(2,1)}, u32[]{:S(2)}, u32[]{:S(2)}) collective-permute-start(bf16[1,256,768]{2,1,0:T(8,128)(2,1)} %get-tuple-element.265), channel_id=1, source_target_pairs={{0,16},{4,20},{8,24},{12,28},{16,0},{20,4},{24,8},{28,12},{1,17},{... | collective-permute-start | bytes 1179656 | tf_op jit(solution)/shard_map/ppermute | solution.py:45
  397.0 11.0 %collective-permute-start.57 = (f32[4096]{0:T(1024)S(1)}, f32[4096]{0:T(1024)S(1)}, u32[]{:S(2)}, u32[]{:S(2)}) collective-permute-start(f32[4096]{0:T(1024)S(1)} %slice_add_fusion), channel_id=1, source_target_pairs={{0,2},{1,3},{2,0},{3,1},{4,6},{5,7},{6,4},{7,5},{8,10},{9,11},{10,... | collective-permute-start | bytes 49160 | tf_op jit(solution)/shard_map/ppermute | solution.py:45
  (85 other events, 851.1 us)
Sparse Core Ops, SparseCore 0:
  81.8 53.8 all-gather.2
  139.8 37.0 all-gather.4
  257.1 108.4 reduce-scatter.1

commit v4 on v3

--- a/solution.py
+++ b/solution.py
@@ -459,7 +459,9 @@
         def at(j, s, slot):
             return (slot, source_tile(j, s, tiles), 0)
     else:
-        tile = next(t for t in (512, 256, 128) if columns % t == 0 and shape[2] % t == 0)
+        tile = next(
+            t for t in (2048, 1024, 512, 256, 128) if columns % t == 0 and shape[2] % t == 0
+        )
         tiles = columns // tile
         each = shape[2] // tile
         block, out_block = (1, rows, tile), (1, rows, tile)
@@ -482,6 +484,43 @@
         compiler_params=params(58),
         cost_estimate=cost(),
         name="final_sums",
+    )(*arrays)
+
+
+def triple_body(counts, *refs):
+    out = refs[-1]
+    kinds, _, wide = out.shape
+    start = 0
+    column = 0
+    for count in counts:
+        arrays = refs[start : start + count]
+        start += count
+        width = arrays[0].shape[2]
+        done = 0
+        while done < width:
+            kind, at = column // wide, column % wide
+            step = min(width - done, wide - at)
+            total = arrays[0][0, :, done : done + step].astype(F32)
+            for array in arrays[1:]:
+                total = total + array[0, :, done : done + step].astype(F32)
+            out[kind, :, at : at + step] = total
+            done += step
+            column += step
+
+
+def triple_sums(sources, shape):
+    arrays = [array for parts in sources for array in parts]
+    return pl.pallas_call(
+        functools.partial(triple_body, [len(parts) for parts in sources]),
+        grid=(1,),
+        in_specs=[
+            pl.BlockSpec((1,) + array.shape[1:], lambda j: (0, 0, 0)) for array in arrays
+        ],
+        out_specs=pl.BlockSpec(shape, lambda j: (0, 0, 0)),
+        out_shape=jax.ShapeDtypeStruct(shape, F32),
+        compiler_params=params(VMEM),
+        cost_estimate=cost(),
+        name="triple_sums",
     )(*arrays)
 
 
@@ -616,7 +655,7 @@
             jax.ShapeDtypeStruct((all_rows, width), BF),
             jax.ShapeDtypeStruct((all_rows, 1), F32),
         ],
-        compiler_params=params(VMEM),
+        compiler_params=params(60),
         cost_estimate=cost(),
         name="in_projection",
     )(*toks, gain.reshape(1, width), weights)
@@ -646,7 +685,7 @@
         gated[place][...] = (second[here, :] * conv).astype(BF)
 
 
-def conv_forward(second, mixed, before, taps, masks, count, tile=128):
+def conv_forward(second, mixed, before, taps, masks, count, tile=256):
     all_rows, chans = mixed.shape
     rows = all_rows // count
     wide = pl.BlockSpec((all_rows, tile), lambda j: (0, j))
@@ -797,7 +836,8 @@
 
 def mixer_body(count, ids, *refs):
     gated = refs[:count]
-    own_w, same_w, cross_w, rows_ref, gain_ref, state_ref, normed_ref, scale_ref = refs[count:]
+    own_w, same_w, cross_w, rows_ref, gain_ref = refs[count : count + 5]
+    state_ref, normed_ref, scale_ref, joined_ref = refs[count + 5 :]
     step = pl.program_id(0)
     part = same_w.shape[3]
     groups = pl.num_programs(0)
@@ -816,6 +856,9 @@
         scale = lax.rsqrt(jnp.mean(state * state, axis=-1, keepdims=True) + EPS)
         normed_ref[...] = (state * scale * gain_ref[...]).astype(BF)
         scale_ref[...] = scale
+        chans = gated[0].shape[1]
+        for place in range(count):
+            joined_ref[:, place * chans : (place + 1) * chans] = gated[place][...]
 
 
 def mixer_rows(gated, own_w, others, input_rows, gain):
@@ -830,7 +873,7 @@
             total = total + dot(gated[r], full[count - 1 - r], 1, 0)
         state = input_rows.astype(F32) + total
         unit, scale = unit_rows(state)
-        return state, (unit * gain).astype(BF), scale
+        return state, (unit * gain).astype(BF), scale, jnp.concatenate(gated, axis=1)
     full_rows = pl.BlockSpec((rows, width), lambda t, ids: (0, 0))
     weights = pl.BlockSpec((1, count - 1, chans, part), lambda t, ids: (ids[t], 0, 0, 0))
     return pl.pallas_call(
@@ -846,14 +889,20 @@
                 full_rows,
                 pl.BlockSpec((1, width), lambda t, ids: (0, 0)),
             ],
-            out_specs=[full_rows, full_rows, pl.BlockSpec((rows, 1), lambda t, ids: (0, 0))],
+            out_specs=[
+                full_rows,
+                full_rows,
+                pl.BlockSpec((rows, 1), lambda t, ids: (0, 0)),
+                pl.BlockSpec((rows, count * chans), lambda t, ids: (0, 0)),
+            ],
         ),
         out_shape=[
             jax.ShapeDtypeStruct((rows, width), F32),
             jax.ShapeDtypeStruct((rows, width), BF),
             jax.ShapeDtypeStruct((rows, 1), F32),
+            jax.ShapeDtypeStruct((rows, count * chans), BF),
         ],
-        compiler_params=params(60),
+        compiler_params=params(VMEM),
         cost_estimate=cost(),
         name="mixer_rows",
     )(plane_ids(), *gated, own_w, *others, input_rows, gain.reshape(1, width))
@@ -988,8 +1037,8 @@
     w_one = turned(w_own, "chan", 1)
     w_three = turned(w_own, "chan", 3)
     tok_one = turned(tokens, "chan", 1)
-    w_two = turned(after(w_one, w_three), "chan", 1)
-    tok_three = turned(after(tokens, w_three), "chan", 3)
+    w_two = turned(after(w_one, w_three, tok_one), "chan", 1)
+    tok_three = turned(after(tokens, w_three, tok_one), "chan", 3)
     others = jnp.stack([w_one, w_two, w_three])[None]
     halves = [others[:, :, : chan_cols // 2], others[:, :, chan_cols // 2 :]]
     first_arrived = [
@@ -998,7 +1047,9 @@
     tok_two = turned(after(tok_one, w_two), "chan", 1)
     second_arrived = []
     for place, order in enumerate(orders):
-        held = jnp.concatenate([halves[place], first_arrived[place]], axis=0)
+        held = jnp.concatenate(
+            [halves[place], after(first_arrived[place], tok_three)], axis=0
+        )
         for bit in order[1:-1]:
             held = jnp.concatenate([held, swapped(held, "seq", 2 * bit)], axis=0)
         halves[place] = held
@@ -1006,7 +1057,7 @@
     grad_out = lax.all_gather(after(cotangent, tok_two, tok_three), "chan", axis=0, tiled=True)
     tok_blocks = [tokens, tok_one, tok_two, tok_three]
     for place, order in enumerate(orders):
-        held = jnp.concatenate([halves[place], second_arrived[place]], axis=0)
+        held = jnp.concatenate([halves[place], after(second_arrived[place], tok_two)], axis=0)
         split = held.reshape((2,) * len(order) + held.shape[1:])
         axes = [len(order) - 1 - order.index(bit) for bit in bits]
         held = jnp.transpose(split, (*axes, *range(len(order), split.ndim))).reshape(held.shape)
@@ -1024,6 +1075,7 @@
     *projected, mixed_in, normed_one, scale_all = in_projection(
         [after(tokens, held, masks)] + tok_blocks[1:], gain_one, in_weight
     )
+
     def at_edge(edge_rows, device):
         return lax.dynamic_index_in_dim(edge_rows, (chan_index - device) % chan_count, 0, False)
 
@@ -1041,27 +1093,26 @@
     gated_rows_own = [gated_mix[0]] + [
         turned(gated_mix[r], "chan", -r) for r in range(1, chan_count)
     ]
-    state_own, normed_two_own, scale_two = mixer_rows(
+    state_own, normed_two_own, scale_two, gated_joined = mixer_rows(
         gated_rows_own, out_weight, others, tokens, gain_two
     )
+    n_one = turned(normed_two_own, "chan", 1)
+    normed_one_slices = own_slices(
+        after(normed_one, normed_two_own), jnp.arange(chan_count, dtype=jnp.int32)
+    )
+    cot_slices = own_slices(after(grad_out, normed_two_own), owner)
+    n_one = after(n_one, normed_one_slices[0], cot_slices[0])
     gated_plane = lax.all_gather(
-        jnp.concatenate([after(gated_rows_own[0], normed_two_own)] + gated_rows_own[1:], axis=1),
+        after(gated_joined, n_one),
         "seq",
         axis=0,
         tiled=True,
-    )
-    n_one = turned(normed_two_own, "chan", 1)
-    normed_one_slices = own_slices(
-        [
-            after(normed_one[r * shard_rows : (r + 1) * shard_rows], normed_two_own)
-            for r in range(chan_count)
-        ]
     )
     n_two = turned(n_one, "chan", 1)
     n_three = turned(after(normed_two_own, n_one), "chan", 3)
     hidden_a, pair_a, ffn_parts, grad_two_parts = feed_forward(
         owner,
-        [after(normed_two_own, normed_one_slices[0]), n_one],
+        [normed_two_own, n_one],
         grad_out,
         gate_up_weight,
         down_weight,
@@ -1073,14 +1124,13 @@
         else [after(one, n_two, n_three) for one in value]
         for value in (ffn_parts, grad_two_parts, hidden_a, pair_a)
     ]
-    cot_slices = own_slices(after(grad_out, hidden_a), owner)
     run = turned(grad_two_parts[1], "chan", 1)
     ffn_one = turned(ffn_parts[1], "chan", -1)
     hidden_a_rec = swapped(hidden_a, "seq", 1)
     pair_a_rec = swapped(pair_a, "seq", 1)
     hidden_b, pair_b, ffn_more, grad_more = feed_forward(
         owner,
-        [after(n_two, cot_slices[0]), n_three],
+        [n_two, n_three],
         grad_out,
         gate_up_weight,
         down_weight,
@@ -1094,7 +1144,7 @@
         after(units, total, ffn_one, hidden_a_rec, pair_a_rec) for units in (hidden_b, pair_b)
     ]
     hidden_b_rec = swapped(hidden_b, "seq", 1)
-    pair_b_rec = swapped(pair_b, "seq", 1)
+    pair_b_rec = swapped(after(pair_b, hidden_b_rec), "seq", 1)
     run = turned(total, "chan", 1)
     normed_two_slices = own_slices(
         [normed_two_own, n_one, n_two, after(n_three, total)], None, False
@@ -1107,15 +1157,14 @@
         tall=True,
     )
     total = ring_sum(after(run, down.made), grad_two_parts[3])
-    down.send(total)
+    down.send()
     run = turned(total, "chan", 1)
     gate_up = whole_product(
         (after(normed_two_slices[0], total), normed_two_slices[1]),
         ([pair_a, pair_b], [pair_a_rec, pair_b_rec]),
         part,
     )
-    ffn_three = turned(after(ffn_parts[3], total), "chan", -3)
-    run = after(run, gate_up, ffn_three, *down.arrived)
+    run = after(run, gate_up, *down.arrived)
     gate_up_mine = plane_sum(after(gate_up, gated_plane, run))
     ffn_two = turned(after(ffn_parts[2], run), "chan", -1)
 
@@ -1138,8 +1187,8 @@
     ]
     mixes = spread_slices(after(grad_mix_own, *grad_gated_rows[1:]))
     mixes = [mixes[0]] + [swapped(mixes[q], "seq", q) for q in range(1, seq_count)]
-    down.add(*grad_gated_rows[1:])
     ffn_two = turned(after(ffn_two, *gg), "chan", -1)
+    ffn_three = turned(after(ffn_parts[3], *gg), "chan", -3)
     heads = jnp.stack(
         [
             (
@@ -1148,60 +1197,60 @@
             for r in range(chan_count)
         ]
     )
-    heads = after(heads, down.made)
     rim_back = passed_along(at_edge(heads, 0), "seq", -1)
     rim_back = after(rim_back, *mixes)
     behind = jnp.where(is_owner(chan_count - 1), rim_back[None], jnp.roll(heads, 1, axis=0))
-    down.send(rim_back)
     grad_triple, tap_part = conv_backward(
         gg, *projected, conv_out, mixed_in, before, behind.astype(F32), conv_taps, masks
     )
     grad_one_parts, gain_one_part = mixer_back(grad_triple, in_weight, tok_blocks, scale_all)
-    grad_one_parts = [after(rows, ffn_two, *down.arrived) for rows in grad_one_parts]
+    grad_one_parts = [after(rows, ffn_two, ffn_three) for rows in grad_one_parts]
     run = turned(grad_one_parts[1], "chan", 1)
     small = after(
         jnp.concatenate([gain_one_part, gain_two_part, tap_part.reshape(-1)]), grad_one_parts[1]
     )
     small_rec = swapped(small, "seq", 1)
     triple_rec = swapped(after(grad_triple, grad_one_parts[1]), "seq", 1)
-    out_parts = rows_product(
-        after(gated_plane, grad_one_parts[1]), mixes, chan_count
-    )
-    out_run = turned(out_parts[3], "chan", 1)
     into = Joined(
-        (after(normed_one_slices[0], out_parts), normed_one_slices[1]),
+        (after(normed_one_slices[0], grad_one_parts[1]), normed_one_slices[1]),
         ([grad_triple], [triple_rec]),
         orders,
         part,
     )
+    small = small + small_rec
+    small_rec = swapped(small, "seq", 2)
     small = small + after(small_rec, into.made)
-    small_rec = swapped(small, "seq", 2)
-    small = small + small_rec
     into.send(small)
     total = ring_sum(after(run, small), grad_one_parts[2])
     run = turned(total, "chan", 1)
     small_rec = swapped(after(small, total), "seq", 4)
-    total = ring_sum(run, grad_one_parts[3])
+    out_parts = rows_product(after(gated_plane, total), mixes, chan_count)
+    out_run = turned(out_parts[3], "chan", 1)
+    down.add(out_parts)
+    total = ring_sum(after(run, down.made, out_run), grad_one_parts[3])
     out_total = ring_sum(after(out_run, total), out_parts[2])
     run = turned(total, "chan", 1)
     out_run = turned(out_total, "chan", 1)
-    down_grad = final_sums(down.finish(total), True, (hidden_a.shape[2], part))
-    into.add(down_grad)
-    run = after(run, into.made)
-    into.send(run)
-    out_total = ring_sum(after(out_run, run), out_parts[1])
+    down.send(total)
+    into.add(out_total)
+    into.send()
+    gate_up_grad = final_sums(
+        [[(after(gate_up_mine, into.made), 0)], [(gate_up_mine, 1)]],
+        False,
+        (2, part, hidden_a.shape[2]),
+    )
+    run = after(run, gate_up_grad)
+    out_total = ring_sum(after(out_run, gate_up_grad), out_parts[1])
     out_run = turned(out_total, "chan", 1)
-    small = small + after(small_rec, run)
+    small = small + after(small_rec, out_total)
     if seq_count > 8:
         small = summed(small, "seq", 8)
     gains = small[: 2 * width]
     gains_rec = swapped(gains, "chan", 1)
-    gate_up_grad = final_sums(
-        [[(gate_up_mine, 0)], [(gate_up_mine, 1)]], False, (2, part, hidden_a.shape[2])
-    )
-    gains = gains + after(gains_rec, gate_up_grad)
+    down_grad = final_sums(down.finish(out_total), True, (hidden_a.shape[2], part))
+    gains = gains + after(gains_rec, down_grad)
     gains = gains + swapped(gains, "chan", 2)
-    in_grad = final_sums(into.finish(gate_up_grad), False, (3, part, chan_cols))
+    in_grad = triple_sums(into.finish(down_grad), (3, part, chan_cols))
     out_grad = out_run.astype(F32) + out_parts[0].astype(F32)
 
     grad_one_own = run.astype(F32) + grad_one_parts[0].astype(F32)

time: 417 us -> 393 us (0.942)
  waiting for transfers between devices: 150 us -> 120 us
  starting transfers between devices: 61 us -> 75.9 us
  Pallas kernels: 153 us -> 141 us
  local copies, waits for them, and re-layouts: 21 us -> 25.8 us
    ppermute x28, waiting for transfers between devices: 125 us -> 92 us  [turned(): lax.ppermute(block, axis, [(i, (i + distance) % count) for i in range(cou...]
    ppermute x28, starting transfers between devices: 29.7 us -> 39.9 us  [turned(): lax.ppermute(block, axis, [(i, (i + distance) % count) for i in range(cou...]
    pallas_call x3 -> x2, Pallas kernels: 15.6 us -> 8.24 us  [final_sums(): pl.pallas_call(functools.partial(sums_body, [len(parts) for parts in sour...]
    unnamed x134 -> x138, local copies, waits for them, and re-layouts: 13.6 us -> 18.8 us
  transfers between devices with their start and end apart: 66 -> 66, of which waited for: 28 -> 27; matrix products, arithmetic and copies ran while one was open for 5% -> 4% of each run, Pallas kernels for 37% -> 36%
where the time goes in v4:
time: 393 us; the launch traced here: 391 us
  Pallas kernels  141 us (36%)
  waiting for transfers between devices  120 us (31%)
  starting transfers between devices  75.9 us (19%)
  local copies, waits for them, and re-layouts  25.8 us (7%)
  between operations  14.6 us (4%)
  other arithmetic  13 us (3%)
    ppermute x28, waiting for transfers between devices, turned(): lax.ppermute(block, axis, [(i, (i + distance) % count) for i in range(cou...  92 us
    pallas_call x2, Pallas kernels, feed_forward(): pl.pallas_call(functools.partial(ffn_body, count), grid_spec=pltpu.Prefet...  41.5 us
    ppermute x28, starting transfers between devices, turned(): lax.ppermute(block, axis, [(i, (i + distance) % count) for i in range(cou...  39.9 us
    ppermute x33, starting transfers between devices, swapped(): lax.ppermute(block, axis, [(i, i ^ bit) for i in range(lax.axis_size(axis...  32 us
    ppermute x33, waiting for transfers between devices, swapped(): lax.ppermute(block, axis, [(i, i ^ bit) for i in range(lax.axis_size(axis...  27.9 us
    unnamed x138, local copies, waits for them, and re-layouts  18.8 us
    pallas_call x2, Pallas kernels, __init__(): pl.pallas_call(functools.partial(product_body, slots, part, tiles, tall,...  17.5 us
    pallas_call x1, Pallas kernels, whole_product(): pl.pallas_call(functools.partial(whole_body, part, len(units[0])), grid=(...  14.4 us
  transfers between devices with their start and end apart: 66, of which 27 were waited for; matrix products, arithmetic and copies ran while one was open for 4% of the time, Pallas kernels for 36%

profile of v4, /device:TPU:0, one launch (start us, length us, event | category | flops | bytes accessed | tf_op | source)
XLA Modules:
  0.0 391.0 jit_solution(1160078688366733901)
XLA Ops:
  7.2 3.1 collective-permute-start.2
  11.3 2.1 collective-permute-start.1
  13.4 17.5 %collective-permute-done.1 = bf16[512,256]{1,0:T(8,128)(2,1)S(1)} collective-permute-done((bf16[512,256]{1,0:T(8,128)(2,1)S(1)}, bf16[512,256]{1,0:T(8,128)(2,1)S(1)}, u32[]{:S(2)}, u32[]{:S(2)}) %collective-permute-start.1) | collective-permute-done | bytes 262176 | tf_op jit(solution)/shard_map/ppermute | solution.py:41
  30.9 4.9 %collective-permute-done = bf16[512,256]{1,0:T(8,128)(2,1)S(1)} collective-permute-done((bf16[512,256]{1,0:T(8,128)(2,1)S(1)}, bf16[512,256]{1,0:T(8,128)(2,1)S(1)}, u32[]{:S(2)}, u32[]{:S(2)}) %collective-permute-start) | collective-permute-done | bytes 262176 | tf_op jit(solution)/shard_map/ppermute | solution.py:41
  35.7 3.8 collective-permute-start.5
  39.6 7.2 %collective-permute-done.3 = bf16[512,256]{1,0:T(8,128)(2,1)S(1)} collective-permute-done((bf16[512,256]{1,0:T(8,128)(2,1)S(1)}, bf16[512,256]{1,0:T(8,128)(2,1)S(1)}, u32[]{:S(2)}, u32[]{:S(2)}) %collective-permute-start.3) | collective-permute-done | bytes 262176 | tf_op jit(solution)/shard_map/ppermute | solution.py:41
  50.0 4.7 %collective-permute-done.5.refs_3_.refs_5_ = bf16[128,2048]{1,0:T(8,128)(2,1)S(1)} collective-permute-done((bf16[128,2048]{1,0:T(8,128)(2,1)}, bf16[128,2048]{1,0:T(8,128)(2,1)S(1)}, u32[]{:S(2)}, u32[]{:S(2)}) %collective-permute-start.5) | collective-permute-done | bytes 524320 | tf_op jit(solution)/shard_map/ppermute | solution.py:41
  58.6 12.6 %collective-permute-done.7.refs_2_.refs_4_ = bf16[128,2048]{1,0:T(8,128)(2,1)S(1)} collective-permute-done((bf16[128,2048]{1,0:T(8,128)(2,1)S(1)}, bf16[128,2048]{1,0:T(8,128)(2,1)S(1)}, u32[]{:S(2)}, u32[]{:S(2)}) %collective-permute-start.7) | collective-permute-done | bytes 524320 | tf_op jit(solution)/shard_map/ppermute | solution.py:41
  73.8 1.9 pad_maximum_fusion.refs_5_.refs_1_
  78.5 8.9 %in_projection.1 = (f32[512,512]{1,0:T(8,128)}, f32[512,512]{1,0:T(8,128)}, f32[512,512]{1,0:T(8,128)}, bf16[512,512]{1,0:T(8,128)(2,1)}, bf16[512,2048]{1,0:T(8,128)(2,1)}, /*index=5*/f32[512,1]{1,0:T(8,128)}) custom-call(bf16[128,2048]{1,0:T(8,128)(2,1)} %refs_2_.1, bf16[128,2048]{1,0:T(8,128)(2,1)} %copy-done.39, bf16[128,2048]{1,0:T(8,128)(2,1)} %copy-done.41, ...), custom_call_target="tpu_custom_call" | custom-call | flops 1024 | bytes 1024 | tf_op jit(solution)/shard_map/in_projection/pallas_call | solution.py:639
  88.2 2.4 collective-permute-start.10
  92.1 2.9 conv_forward.1
  99.1 7.8 %collective-permute-done.11.refs_1_ = bf16[128,512]{1,0:T(8,128)(2,1)S(1)} collective-permute-done((bf16[128,512]{1,0:T(8,128)(2,1)}, bf16[128,512]{1,0:T(8,128)(2,1)S(1)}, u32[]{:S(2)}, u32[]{:S(2)}) %collective-permute-start.11) | collective-permute-done | bytes 131104 | tf_op jit(solution)/shard_map/ppermute | solution.py:41
  106.9 16.8 %collective-permute-done.12.refs_2_ = bf16[128,512]{1,0:T(8,128)(2,1)S(1)} collective-permute-done((bf16[128,512]{1,0:T(8,128)(2,1)}, bf16[128,512]{1,0:T(8,128)(2,1)S(1)}, u32[]{:S(2)}, u32[]{:S(2)}) %collective-permute-start.12) | collective-permute-done | bytes 131104 | tf_op jit(solution)/shard_map/ppermute | solution.py:41
  124.6 6.0 %mixer_rows.1 = (f32[128,2048]{1,0:T(8,128)S(1)}, bf16[128,2048]{1,0:T(8,128)(2,1)S(1)}, f32[128,1]{1,0:T(8,128)S(1)}, bf16[128,2048]{1,0:T(8,128)(2,1)}) custom-call(s32[5]{0:T(128)S(1)} %pad_add_fusion.ids, bf16[128,512]{1,0:T(8,128)(2,1)S(1)} %copy-done.24, bf16[128,512]{1,0:T(8,128)(2,1)S(1)} %collective-permute-done.11.refs_1_, ...), custom_call_target="tpu_custom_call" | custom-call | flops 1024 | bytes 1024 | tf_op jit(solution)/shard_map/mixer_rows/pallas_call | solution.py:879
  141.6 6.5 %collective-permute-done.15.refs_1_ = bf16[128,2048]{1,0:T(8,128)(2,1)S(1)} collective-permute-done((bf16[128,2048]{1,0:T(8,128)(2,1)S(1)}, bf16[128,2048]{1,0:T(8,128)(2,1)S(1)}, u32[]{:S(2)}, u32[]{:S(2)}) %collective-permute-start.15) | collective-permute-done | bytes 524320 | tf_op jit(solution)/shard_map/ppermute | solution.py:41
  150.3 20.7 %feed_forward.2 = (bf16[1,256,2048]{2,1,0:T(8,128)(2,1)S(1)}, bf16[2,256,2048]{2,1,0:T(8,128)(2,1)}, bf16[128,2048]{1,0:T(8,128)(2,1)S(1)}, bf16[128,2048]{1,0:T...) custom-call(s32[4]{0:T(128)S(1)} %and_select_fusion.ids, ...), custom_call_target="tpu_custom_call" | custom-call | flops 1024 | bytes 1024 | tf_op jit(solution)/shard_map/feed_forward/pallas_call | solution.py:141
  173.7 3.4 collective-permute-start.18
  177.1 20.8 %feed_forward.3 = (bf16[1,256,2048]{2,1,0:T(8,128)(2,1)S(1)}, bf16[2,256,2048]{2,1,0:T(8,128)(2,1)}, bf16[128,2048]{1,0:T(8,128)(2,1)S(1)}, bf16[128,2048]{1,0:T...) custom-call(s32[4]{0:T(128)S(1)} %and_select_fusion.ids, ...), custom_call_target="tpu_custom_call" | custom-call | flops 1024 | bytes 1024 | tf_op jit(solution)/shard_map/feed_forward/pallas_call | solution.py:141
  200.4 3.0 collective-permute-done.24.refs_5_
  206.4 9.0 %product.2 = (bf16[2,1024,256]{2,1,0:T(8,128)(2,1)}, bf16[2,1024,256]{2,1,0:T(8,128)(2,1)}, bf16[2,1024,256]{2,1,0:T(8,128)(2,1)}, bf16[2,1024,256]{2,1,0:T(8,128)(2,1)}) custom-call(bf16[512,1024]{1,0:T(8,128)(2,1)} %copy-done.15, bf16[512,1024]{1,0:T(8,128)(2,1)} %collective-permute-done.21.refs_1_, bf16[1,256,2048]{2,1,0:T(8,128)(2,1)} %copy-done.16, ...), custom_call_target="tpu_custom_call" | custom-call | flops 1024 | bytes 1024 | tf_op jit(solution)/shard_map/product/pallas_call | solution.py:308
  216.5 4.8 %collective-permute-start.29 = (bf16[2,1024,256]{2,1,0:T(8,128)(2,1)}, bf16[2,1024,256]{2,1,0:T(8,128)(2,1)}, u32[]{:S(2)}, u32[]{:S(2)}) collective-permute-start(bf16[2,1024,256]{2,1,0:T(8,128)(2,1)} %get-tuple-element.186), channel_id=1, source_target_pairs={{0,16},{4,20},{8,24},{12,28},{16,0},{20,4},{24,8},{28,12},{1,17},{... | collective-permute-start | bytes 3145736 | tf_op jit(solution)/shard_map/ppermute | solution.py:45
  221.5 2.5 collective-permute-start.25
  225.0 14.4 %whole_product.1 = bf16[4,2,256,2048]{3,2,1,0:T(8,128)(2,1)} custom-call(bf16[512,1024]{1,0:T(8,128)(2,1)} %copy-done.14, bf16[512,1024]{1,0:T(8,128)(2,1)} %copy-done.43, bf16[2,256,2048]{2,1,0:T(8,128)(2,1)} %get-tuple-element.176.refs_0_, bf16[2,256,2048]{2,1,0:T(8,128)(2,1)} %get-tuple-element.185.refs_1_, bf16[2,256,2048]{2,1,0:T(8,128)(2,1)} %copy-done.38, ...), custom_call_target="tpu_custom_call" | custom-call | flops 1024 | bytes 1024 | tf_op jit(solution)/shard_map/whole_product/pallas_call | solution.py:379
  241.3 4.1 %collective-permute-done.29.refs_3_.refs_4_ = bf16[2,1024,256]{2,1,0:T(8,128)(2,1)} collective-permute-done((bf16[2,1024,256]{2,1,0:T(8,128)(2,1)}, bf16[2,1024,256]{2,1,0:T(8,128)(2,1)}, u32[]{:S(2)}, u32[]{:S(2)}) %collective-permute-start.29) | collective-permute-done | bytes 1048608 | tf_op jit(solution)/shard_map/ppermute | solution.py:45
  246.4 3.2 collective-permute-start.30
  249.7 9.7 %gated_rows.1 = (bf16[128,512]{1,0:T(8,128)(2,1)}, bf16[128,512]{1,0:T(8,128)(2,1)}, bf16[128,512]{1,0:T(8,128)(2,1)}, bf16[128,512]{1,0:T(8,128)(2,1)}, f32[128...) custom-call(s32[5]{0:T(128)} %copy-done.28, bf16[512,2048]{1,0:T(8,128)(2,1)} %refs_0_.2, ...), custom_call_target="tpu_custom_call" | custom-call | flops 1024 | bytes 1024 | tf_op jit(solution)/shard_map/gated_rows/pallas_call | solution.py:968
  260.9 4.3 %collective-permute-start.33 = (bf16[128,512]{1,0:T(8,128)(2,1)}, bf16[128,512]{1,0:T(8,128)(2,1)S(1)}, u32[]{:S(2)}, u32[]{:S(2)}) collective-permute-start(bf16[128,512]{1,0:T(8,128)(2,1)} %get-tuple-element.198), channel_id=1, source_target_pairs={{0,3},{1,0},{2,1},{3,2},{4,7},{5,4},{6,5},{7,6},{8,11},{9,8},{10,9... | collective-permute-start | bytes 393224 | tf_op jit(solution)/shard_map/ppermute | solution.py:41
  269.9 5.7 %collective-permute-done.32.refs_2_ = bf16[128,512]{1,0:T(8,128)(2,1)S(1)} collective-permute-done((bf16[128,512]{1,0:T(8,128)(2,1)}, bf16[128,512]{1,0:T(8,128)(2,1)S(1)}, u32[]{:S(2)}, u32[]{:S(2)}) %collective-permute-start.32) | collective-permute-done | bytes 131104 | tf_op jit(solution)/shard_map/ppermute | solution.py:41
  281.6 3.0 collective-permute-done.40.refs_4_
  284.7 2.5 collective-permute-done.41.refs_5_
  288.8 2.2 collective-permute-done.43.refs_7_
  291.8 5.3 %conv_backward.1 = (bf16[3,512,512]{2,1,0:T(8,128)(2,1)}, f32[3,512]{1,0:T(4,128)}) custom-call(bf16[128,512]{1,0:T(8,128)(2,1)} %get-tuple-element.192.refs_0_, bf16[128,512]{1,0:T(8,128)(2,1)} %copy-done.53, bf16[128,512]{1,0:T(8,128)(2,1)} %copy-done.52, bf16[128,512]{1,0:T(8,128)(2,1)} %copy-done.51, f32[512,512]{1,0:T(8,128)} %get-tuple-element.206.refs_4_, ...), custom_call_target="tpu_custom_call" | custom-call | flops 1024 | bytes 1024 | tf_op jit(solution)/shard_map/conv_backward/pallas_call | solution.py:752
  297.3 7.9 %mixer_back.1 = (bf16[128,2048]{1,0:T(8,128)(2,1)}, bf16[128,2048]{1,0:T(8,128)(2,1)}, bf16[128,2048]{1,0:T(8,128)(2,1)}, bf16[128,2048]{1,0:T(8,128)(2,1)}, f32[1,2048]{1,0:T(1,128)}) custom-call(bf16[3,512,512]{2,1,0:T(8,128)(2,1)} %get-tuple-element.229.refs_0_.refs_2_, bf16[3,2048,512]{2,1,0:T(8,128)(2,1)} %refs_1_.1, bf16[128,2048]{1,0:T(8,128)(2,1)} %refs_2_.1, ...), custom_call_target="tpu_custom_call" | custom-call | flops 1024 | bytes 1024 | tf_op jit(solution)/shard_map/mixer_back/pallas_call | solution.py:796
  305.2 2.9 collective-permute-start.48
  310.1 2.6 collective-permute-done.45
  312.7 2.4 collective-permute-start.46
  316.1 8.5 %product.3 = (bf16[2,256,768]{2,1,0:T(8,128)(2,1)}, bf16[2,256,768]{2,1,0:T(8,128)(2,1)}, bf16[2,256,768]{2,1,0:T(8,128)(2,1)}, bf16[2,256,768]{2,1,0:T(8,128)(2,1)}) custom-call(bf16[512,1024]{1,0:T(8,128)(2,1)} %copy-done.13, bf16[512,1024]{1,0:T(8,128)(2,1)} %copy-done.44, bf16[3,512,512]{2,1,0:T(8,128)(2,1)} %get-tuple-element.229.refs_0_.refs_2_, ...), custom_call_target="tpu_custom_call" | custom-call | flops 1024 | bytes 1024 | tf_op jit(solution)/shard_map/product/pallas_call | solution.py:308
  326.9 5.9 %rows_product.1 = bf16[4,512,256]{2,1,0:T(8,128)(2,1)} custom-call(s32[8]{0:T(128)} %copy-done.29, bf16[1024,2048]{1,0:T(8,128)(2,1)} %all-gather.5.cloned.1.call-done.gated, bf16[128,256]{1,0:T(8,128)(2,1)} %copy-done.27, bf16[128,256]{1,0:T(8,128)(2,1)} %copy-done.55, bf16[128,256]{1,0:T(8,128)(2,1)} %copy-done.56, bf16[128,256]{1,0:T(8,128)(2,1)} %copy-done.57, ...), custom_call_target="tpu_custom_call" | custom-call | flops 1024 | bytes 1024 | tf_op jit(solution)/shard_map/rows_product/pallas_call | solution.py:565
  334.0 2.1 collective-permute-start.50
  337.9 4.0 %upper_sums.2 = (bf16[1,1024,256]{2,1,0:T(8,128)(2,1)}, bf16[1,1024,256]{2,1,0:T(8,128)(2,1)}) custom-call(bf16[2,1024,256]{2,1,0:T(8,128)(2,1)} %get-tuple-element.261.refs_0_, bf16[2,1024,256]{2,1,0:T(8,128)(2,1)} %collective-permute-done.28.refs_1_, bf16[2,1024,256]{2,1,0:T(8,128)(2,1)} %get-tuple-element.240.refs_2_.refs_3_, ...), custom_call_target="tpu_custom_call" | custom-call | flops 1024 | bytes 1024 | tf_op jit(solution)/shard_map/upper_sums/pallas_call | solution.py:435
  341.9 5.5 %collective-permute-done.50.a = bf16[512,256]{1,0:T(8,128)(2,1)S(1)} collective-permute-done((bf16[512,256]{1,0:T(8,128)(2,1)S(1)}, bf16[512,256]{1,0:T(8,128)(2,1)S(1)}, u32[]{:S(2)}, u32[]{:S(2)}) %collective-permute-start.50) | collective-permute-done | bytes 262176 | tf_op jit(solution)/shard_map/ppermute | solution.py:41
  348.6 5.8 %collective-permute-done.53.refs_3_.refs_4_ = bf16[2,256,768]{2,1,0:T(8,128)(2,1)S(1)} collective-permute-done((bf16[2,256,768]{2,1,0:T(8,128)(2,1)}, bf16[2,256,768]{2,1,0:T(8,128)(2,1)S(1)}, u32[]{:S(2)}, u32[]{:S(2)}) %collective-permute-start.53) | collective-permute-done | bytes 786464 | tf_op jit(solution)/shard_map/ppermute | solution.py:45
  356.5 2.4 add_convert_fusion
  358.9 3.8 upper_sums.3
  362.8 3.8 final_sums.2
  370.9 2.0 collective-permute-start.62
  372.9 4.4 %final_sums.3 = f32[2048,256]{1,0:T(8,128)} custom-call(bf16[2,1024,256]{2,1,0:T(8,128)(2,1)} %get-tuple-element.261.refs_0_, bf16[2,1024,256]{2,1,0:T(8,128)(2,1)} %collective-permute-done.28.refs_1_, bf16[1,1024,256]{2,1,0:T(8,128)(2,1)} %collective-permute-done.57.refs_2_, bf16[2,1024,256]{2,1,0:T(8,128)(2,1)} %get-tuple-element.240.refs_2_.refs_3_, ...), custom_call_target="tpu_custom_call" | custom-call | flops 1024 | bytes 1024 | tf_op jit(solution)/shard_map/final_sums/pallas_call | solution.py:478
  (308 shorter events, 84.2 us)
Async XLA Ops:
  7.2 125.7 %all-gather.3.cloned.1.call-start = ((), (), s32[]{:S(2)}) async-start(), calls=%async_computation.1 | async-start | bytes 2621440 | tf_op jit(solution)/shard_map/all_gather | solution.py:1057
  7.2 28.5 %collective-permute-start.2 = (bf16[128,2048]{1,0:T(8,128)(2,1)}, bf16[128,2048]{1,0:T(8,128)(2,1)S(1)}, u32[]{:S(2)}, u32[]{:S(2)}) collective-permute-start(bf16[128,2048]{1,0:T(8,128)(2,1)} %refs_2_.1), channel_id=1, source_target_pairs={{0,1},{1,2},{2,3},{3,0},{4,5},{5,6},{6,7},{7,4},{8,9},{9,10},{10,1... | collective-permute-start | bytes 1572872 | tf_op jit(solution)/shard_map/ppermute | solution.py:41
  11.3 19.6 %collective-permute-start.1 = (bf16[512,256]{1,0:T(8,128)(2,1)S(1)}, bf16[512,256]{1,0:T(8,128)(2,1)S(1)}, u32[]{:S(2)}, u32[]{:S(2)}) collective-permute-start(bf16[512,256]{1,0:T(8,128)(2,1)S(1)} %constant_dynamic-slice_fusion), channel_id=1, source_target_pairs={{0,3},{1,0},{2,1},{3,2},{4,7},{5,4},{6,5},{7,6},{8,11},{9,8},{10,9... | collective-permute-start | bytes 786440 | tf_op jit(solution)/shard_map/ppermute | solution.py:41
  13.4 22.4 %collective-permute-start = (bf16[512,256]{1,0:T(8,128)(2,1)S(1)}, bf16[512,256]{1,0:T(8,128)(2,1)S(1)}, u32[]{:S(2)}, u32[]{:S(2)}) collective-permute-start(bf16[512,256]{1,0:T(8,128)(2,1)S(1)} %constant_dynamic-slice_fusion), channel_id=1, source_target_pairs={{0,1},{1,2},{2,3},{3,0},{4,5},{5,6},{6,7},{7,4},{8,9},{9,10},{10,1... | collective-permute-start | bytes 786440 | tf_op jit(solution)/shard_map/ppermute | solution.py:41
  35.7 11.0 %collective-permute-start.3 = (bf16[512,256]{1,0:T(8,128)(2,1)S(1)}, bf16[512,256]{1,0:T(8,128)(2,1)S(1)}, u32[]{:S(2)}, u32[]{:S(2)}) collective-permute-start(bf16[512,256]{1,0:T(8,128)(2,1)S(1)} %collective-permute-done), channel_id=1, source_target_pairs={{0,1},{1,2},{2,3},{3,0},{4,5},{5,6},{6,7},{7,4},{8,9},{9,10},{10,1... | collective-permute-start | bytes 786440 | tf_op jit(solution)/shard_map/ppermute | solution.py:41
  35.7 19.0 %collective-permute-start.5 = (bf16[128,2048]{1,0:T(8,128)(2,1)}, bf16[128,2048]{1,0:T(8,128)(2,1)S(1)}, u32[]{:S(2)}, u32[]{:S(2)}) collective-permute-start(bf16[128,2048]{1,0:T(8,128)(2,1)} %refs_2_.1), channel_id=1, source_target_pairs={{0,3},{1,0},{2,1},{3,2},{4,7},{5,4},{6,5},{7,6},{8,11},{9,8},{10,9... | collective-permute-start | bytes 1572872 | tf_op jit(solution)/shard_map/ppermute | solution.py:41
  54.8 18.3 %collective-permute-start.9 = (bf16[2,3,256,256]{3,2,1,0:T(8,128)(2,1)S(1)}, bf16[2,3,256,256]{3,2,1,0:T(8,128)(2,1)S(1)}, u32[]{:S(2)}, u32[]{:S(2)}) collective-permute-start(bf16[2,3,256,256]{3,2,1,0:T(8,128)(2,1)S(1)} %pad_maximum_fusion.3), channel_id=1, source_target_pairs={{0,8},{4,12},{8,0},{12,4},{16,24},{20,28},{24,16},{28,20},{1,9},{5... | collective-permute-start | bytes 2359304 | tf_op jit(solution)/shard_map/ppermute | solution.py:45
  56.7 17.1 %collective-permute-start.6 = (bf16[2,3,256,256]{3,2,1,0:T(8,128)(2,1)S(1)}, bf16[2,3,256,256]{3,2,1,0:T(8,128)(2,1)S(1)}, u32[]{:S(2)}, u32[]{:S(2)}) collective-permute-start(bf16[2,3,256,256]{3,2,1,0:T(8,128)(2,1)S(1)} %pad_maximum_fusion.2), channel_id=1, source_target_pairs={{0,16},{4,20},{8,24},{12,28},{16,0},{20,4},{24,8},{28,12},{1,17},{... | collective-permute-start | bytes 2359304 | tf_op jit(solution)/shard_map/ppermute | solution.py:45
  58.1 13.2 %collective-permute-start.7 = (bf16[128,2048]{1,0:T(8,128)(2,1)S(1)}, bf16[128,2048]{1,0:T(8,128)(2,1)S(1)}, u32[]{:S(2)}, u32[]{:S(2)}) collective-permute-start(bf16[128,2048]{1,0:T(8,128)(2,1)S(1)} %collective-permute-done.2.refs_1_.refs_3_), channel_id=1, source_target_pairs={{0,1},{1,2},{2,3},{3,0},{4,5},{5,6},{6,7},{7,4},{8,9},{9,10},{10,1... | collective-permute-start | bytes 1572872 | tf_op jit(solution)/shard_map/ppermute | solution.py:41
  75.8 47.9 %collective-permute-start.14 = (bf16[4,3,512,256]{3,2,1,0:T(8,128)(2,1)}, bf16[4,3,512,256]{3,2,1,0:T(8,128)(2,1)}, u32[]{:S(2)}, u32[]{:S(2)}) collective-permute-start(bf16[4,3,512,256]{3,2,1,0:T(8,128)(2,1)} %pad_maximum_fusion.refs_5_.refs_1_), channel_id=1, source_target_pairs={{0,4},{4,0},{8,12},{12,8},{16,20},{20,16},{24,28},{28,24},{1,5},{5... | collective-permute-start | bytes 9437192 | tf_op jit(solution)/shard_map/ppermute | solution.py:45
  75.8 169.6 %all-gather.5.cloned.1.call-start = ((), (), s32[]{:S(2)}) async-start(), calls=%async_computation.2 | async-start | bytes 4718592 | tf_op jit(solution)/shard_map/all_gather | solution.py:1105
  95.1 11.8 %collective-permute-start.11 = (bf16[128,512]{1,0:T(8,128)(2,1)}, bf16[128,512]{1,0:T(8,128)(2,1)S(1)}, u32[]{:S(2)}, u32[]{:S(2)}) collective-permute-start(bf16[128,512]{1,0:T(8,128)(2,1)} %get-tuple-element.149), channel_id=1, source_target_pairs={{0,3},{1,0},{2,1},{3,2},{4,7},{5,4},{6,5},{7,6},{8,11},{9,8},{10,9... | collective-permute-start | bytes 393224 | tf_op jit(solution)/shard_map/ppermute | solution.py:41
  96.9 26.8 %collective-permute-start.12 = (bf16[128,512]{1,0:T(8,128)(2,1)}, bf16[128,512]{1,0:T(8,128)(2,1)S(1)}, u32[]{:S(2)}, u32[]{:S(2)}) collective-permute-start(bf16[128,512]{1,0:T(8,128)(2,1)} %get-tuple-element.150), channel_id=1, source_target_pairs={{0,2},{1,3},{2,0},{3,1},{4,6},{5,7},{6,4},{7,5},{8,10},{9,11},{10,... | collective-permute-start | bytes 393224 | tf_op jit(solution)/shard_map/ppermute | solution.py:41
  97.6 26.1 %collective-permute-start.13 = (bf16[128,512]{1,0:T(8,128)(2,1)}, bf16[128,512]{1,0:T(8,128)(2,1)S(1)}, u32[]{:S(2)}, u32[]{:S(2)}) collective-permute-start(bf16[128,512]{1,0:T(8,128)(2,1)} %get-tuple-element.151), channel_id=1, source_target_pairs={{0,1},{1,2},{2,3},{3,0},{4,5},{5,6},{6,7},{7,4},{8,9},{9,10},{10,1... | collective-permute-start | bytes 393224 | tf_op jit(solution)/shard_map/ppermute | solution.py:41
  132.3 15.8 %collective-permute-start.15 = (bf16[128,2048]{1,0:T(8,128)(2,1)S(1)}, bf16[128,2048]{1,0:T(8,128)(2,1)S(1)}, u32[]{:S(2)}, u32[]{:S(2)}) collective-permute-start(bf16[128,2048]{1,0:T(8,128)(2,1)S(1)} %get-tuple-element.162.refs_0_), channel_id=1, source_target_pairs={{0,1},{1,2},{2,3},{3,0},{4,5},{5,6},{6,7},{7,4},{8,9},{9,10},{10,1... | collective-permute-start | bytes 1572872 | tf_op jit(solution)/shard_map/ppermute | solution.py:41
  148.2 214.5 %reduce-scatter.2.cloned.1.call-start = ((), (), s32[]{:S(2)}) async-start(), calls=%async_computation.3 | async-start | bytes 10485760 | tf_op jit(solution)/shard_map/reduce_scatter | solution.py:397
  148.2 24.5 %collective-permute-start.17 = (bf16[128,2048]{1,0:T(8,128)(2,1)S(1)}, bf16[128,2048]{1,0:T(8,128)(2,1)S(1)}, u32[]{:S(2)}, u32[]{:S(2)}) collective-permute-start(bf16[128,2048]{1,0:T(8,128)(2,1)S(1)} %get-tuple-element.162.refs_0_), channel_id=1, source_target_pairs={{0,3},{1,0},{2,1},{3,2},{4,7},{5,4},{6,5},{7,6},{8,11},{9,8},{10,9... | collective-permute-start | bytes 1572872 | tf_op jit(solution)/shard_map/ppermute | solution.py:41
  148.4 24.3 %collective-permute-start.16 = (bf16[128,2048]{1,0:T(8,128)(2,1)S(1)}, bf16[128,2048]{1,0:T(8,128)(2,1)S(1)}, u32[]{:S(2)}, u32[]{:S(2)}) collective-permute-start(bf16[128,2048]{1,0:T(8,128)(2,1)S(1)} %collective-permute-done.15.refs_1_), channel_id=1, source_target_pairs={{0,1},{1,2},{2,3},{3,0},{4,5},{5,6},{6,7},{7,4},{8,9},{9,10},{10,1... | collective-permute-start | bytes 1572872 | tf_op jit(solution)/shard_map/ppermute | solution.py:41
  172.7 26.2 %collective-permute-start.23 = (bf16[2,256,2048]{2,1,0:T(8,128)(2,1)}, bf16[2,256,2048]{2,1,0:T(8,128)(2,1)S(1)}, u32[]{:S(2)}, u32[]{:S(2)}) collective-permute-start(bf16[2,256,2048]{2,1,0:T(8,128)(2,1)} %get-tuple-element.176.refs_0_), channel_id=1, source_target_pairs={{0,4},{4,0},{8,12},{12,8},{16,20},{20,16},{24,28},{28,24},{1,5},{5... | collective-permute-start | bytes 6291464 | tf_op jit(solution)/shard_map/ppermute | solution.py:45
  172.7 26.2 %collective-permute-start.22 = (bf16[1,256,2048]{2,1,0:T(8,128)(2,1)S(1)}, bf16[1,256,2048]{2,1,0:T(8,128)(2,1)S(1)}, u32[]{:S(2)}, u32[]{:S(2)}) collective-permute-start(bf16[1,256,2048]{2,1,0:T(8,128)(2,1)S(1)} %get-tuple-element.173.refs_2_), channel_id=1, source_target_pairs={{0,4},{4,0},{8,12},{12,8},{16,20},{20,16},{24,28},{28,24},{1,5},{5... | collective-permute-start | bytes 3145736 | tf_op jit(solution)/shard_map/ppermute | solution.py:45
  173.3 25.5 %collective-permute-start.19 = (bf16[128,2048]{1,0:T(8,128)(2,1)S(1)}, bf16[128,2048]{1,0:T(8,128)(2,1)S(1)}, u32[]{:S(2)}, u32[]{:S(2)}) collective-permute-start(bf16[128,2048]{1,0:T(8,128)(2,1)S(1)} %get-tuple-element.166), channel_id=1, source_target_pairs={{0,1},{1,2},{2,3},{3,0},{4,5},{5,6},{6,7},{7,4},{8,9},{9,10},{10,1... | collective-permute-start | bytes 1572872 | tf_op jit(solution)/shard_map/ppermute | solution.py:41
  173.7 25.2 %collective-permute-start.18 = (bf16[128,2048]{1,0:T(8,128)(2,1)S(1)}, bf16[128,2048]{1,0:T(8,128)(2,1)S(1)}, u32[]{:S(2)}, u32[]{:S(2)}) collective-permute-start(bf16[128,2048]{1,0:T(8,128)(2,1)S(1)} %get-tuple-element.163), channel_id=1, source_target_pairs={{0,3},{1,0},{2,1},{3,2},{4,7},{5,4},{6,5},{7,6},{8,11},{9,8},{10,9... | collective-permute-start | bytes 1572872 | tf_op jit(solution)/shard_map/ppermute | solution.py:41
  203.4 20.6 %collective-permute-start.27 = (bf16[2,256,2048]{2,1,0:T(8,128)(2,1)}, bf16[2,256,2048]{2,1,0:T(8,128)(2,1)}, u32[]{:S(2)}, u32[]{:S(2)}) collective-permute-start(bf16[2,256,2048]{2,1,0:T(8,128)(2,1)} %get-tuple-element.185.refs_1_), channel_id=1, source_target_pairs={{0,4},{4,0},{8,12},{12,8},{16,20},{20,16},{24,28},{28,24},{1,5},{5... | collective-permute-start | bytes 6291464 | tf_op jit(solution)/shard_map/ppermute | solution.py:45
  203.6 17.7 %collective-permute-start.20 = (bf16[128,2048]{1,0:T(8,128)(2,1)S(1)}, bf16[128,2048]{1,0:T(8,128)(2,1)S(1)}, u32[]{:S(2)}, u32[]{:S(2)}) collective-permute-start(bf16[128,2048]{1,0:T(8,128)(2,1)S(1)} %ring_sum.6), channel_id=1, source_target_pairs={{0,1},{1,2},{2,3},{3,0},{4,5},{5,6},{6,7},{7,4},{8,9},{9,10},{10,1... | collective-permute-start | bytes 1572872 | tf_op jit(solution)/shard_map/ppermute | solution.py:41
  206.3 17.7 %collective-permute-start.26 = (bf16[512,1024]{1,0:T(8,128)(2,1)S(1)}, bf16[512,1024]{1,0:T(8,128)(2,1)S(1)}, u32[]{:S(2)}, u32[]{:S(2)}) collective-permute-start(bf16[512,1024]{1,0:T(8,128)(2,1)S(1)} %get-tuple-element.182), channel_id=1, source_target_pairs={{0,4},{4,0},{8,12},{12,8},{16,20},{20,16},{24,28},{28,24},{1,5},{5... | collective-permute-start | bytes 3145736 | tf_op jit(solution)/shard_map/ppermute | solution.py:45
  215.4 25.8 %collective-permute-start.28 = (bf16[2,1024,256]{2,1,0:T(8,128)(2,1)}, bf16[2,1024,256]{2,1,0:T(8,128)(2,1)}, u32[]{:S(2)}, u32[]{:S(2)}) collective-permute-start(bf16[2,1024,256]{2,1,0:T(8,128)(2,1)} %get-tuple-element.178), channel_id=1, source_target_pairs={{0,8},{4,12},{8,0},{12,4},{16,24},{20,28},{24,16},{28,20},{1,9},{5... | collective-permute-start | bytes 3145736 | tf_op jit(solution)/shard_map/ppermute | solution.py:45
  216.5 28.9 %collective-permute-start.29 = (bf16[2,1024,256]{2,1,0:T(8,128)(2,1)}, bf16[2,1024,256]{2,1,0:T(8,128)(2,1)}, u32[]{:S(2)}, u32[]{:S(2)}) collective-permute-start(bf16[2,1024,256]{2,1,0:T(8,128)(2,1)} %get-tuple-element.186), channel_id=1, source_target_pairs={{0,16},{4,20},{8,24},{12,28},{16,0},{20,4},{24,8},{28,12},{1,17},{... | collective-permute-start | bytes 3145736 | tf_op jit(solution)/shard_map/ppermute | solution.py:45
  221.5 18.0 %collective-permute-start.25 = (bf16[128,2048]{1,0:T(8,128)(2,1)S(1)}, bf16[128,2048]{1,0:T(8,128)(2,1)S(1)}, u32[]{:S(2)}, u32[]{:S(2)}) collective-permute-start(bf16[128,2048]{1,0:T(8,128)(2,1)S(1)} %ring_sum.7), channel_id=1, source_target_pairs={{0,1},{1,2},{2,3},{3,0},{4,5},{5,6},{6,7},{7,4},{8,9},{9,10},{10,1... | collective-permute-start | bytes 1572872 | tf_op jit(solution)/shard_map/ppermute | solution.py:41
  246.4 14.4 %collective-permute-start.30 = (bf16[128,2048]{1,0:T(8,128)(2,1)S(1)}, bf16[128,2048]{1,0:T(8,128)(2,1)S(1)}, u32[]{:S(2)}, u32[]{:S(2)}) collective-permute-start(bf16[128,2048]{1,0:T(8,128)(2,1)S(1)} %copy-done.37), channel_id=1, source_target_pairs={{0,3},{1,0},{2,1},{3,2},{4,7},{5,4},{6,5},{7,6},{8,11},{9,8},{10,9... | collective-permute-start | bytes 1572872 | tf_op jit(solution)/shard_map/ppermute | solution.py:41
  268.0 10.5 %collective-permute-start.37 = (bf16[128,256]{1,0:T(8,128)(2,1)S(1)}, bf16[128,256]{1,0:T(8,128)(2,1)S(1)}, u32[]{:S(2)}, u32[]{:S(2)}) collective-permute-start(bf16[128,256]{1,0:T(8,128)(2,1)S(1)} %get-tuple-element.212), channel_id=1, source_target_pairs={{0,4},{4,0},{8,12},{12,8},{16,20},{20,16},{24,28},{28,24},{1,5},{5... | collective-permute-start | bytes 196616 | tf_op jit(solution)/shard_map/ppermute | solution.py:45
  268.0 12.1 %collective-permute-start.38 = (bf16[128,256]{1,0:T(8,128)(2,1)S(1)}, bf16[128,256]{1,0:T(8,128)(2,1)S(1)}, u32[]{:S(2)}, u32[]{:S(2)}) collective-permute-start(bf16[128,256]{1,0:T(8,128)(2,1)S(1)} %get-tuple-element.213), channel_id=1, source_target_pairs={{0,8},{4,12},{8,0},{12,4},{16,24},{20,28},{24,16},{28,20},{1,9},{5... | collective-permute-start | bytes 196616 | tf_op jit(solution)/shard_map/ppermute | solution.py:45
  269.5 10.7 %collective-permute-start.39 = (bf16[128,256]{1,0:T(8,128)(2,1)S(1)}, bf16[128,256]{1,0:T(8,128)(2,1)S(1)}, u32[]{:S(2)}, u32[]{:S(2)}) collective-permute-start(bf16[128,256]{1,0:T(8,128)(2,1)S(1)} %get-tuple-element.214), channel_id=1, source_target_pairs={{0,12},{4,8},{8,4},{12,0},{16,28},{20,24},{24,20},{28,16},{1,13},{... | collective-permute-start | bytes 196616 | tf_op jit(solution)/shard_map/ppermute | solution.py:45
  275.6 29.6 %collective-permute-start.34 = (bf16[128,2048]{1,0:T(8,128)(2,1)S(1)}, bf16[128,2048]{1,0:T(8,128)(2,1)}, u32[]{:S(2)}, u32[]{:S(2)}) collective-permute-start(bf16[128,2048]{1,0:T(8,128)(2,1)S(1)} %collective-permute-done.30), channel_id=1, source_target_pairs={{0,3},{1,0},{2,1},{3,2},{4,7},{5,4},{6,5},{7,6},{8,11},{9,8},{10,9... | collective-permute-start | bytes 1572872 | tf_op jit(solution)/shard_map/ppermute | solution.py:41
  277.4 27.8 %collective-permute-start.35 = (bf16[128,2048]{1,0:T(8,128)(2,1)S(1)}, bf16[128,2048]{1,0:T(8,128)(2,1)}, u32[]{:S(2)}, u32[]{:S(2)}) collective-permute-start(bf16[128,2048]{1,0:T(8,128)(2,1)S(1)} %copy-done.35), channel_id=1, source_target_pairs={{0,1},{1,2},{2,3},{3,0},{4,5},{5,6},{6,7},{7,4},{8,9},{9,10},{10,1... | collective-permute-start | bytes 1572872 | tf_op jit(solution)/shard_map/ppermute | solution.py:41
  308.2 18.2 %collective-permute-start.44 = (bf16[128,2048]{1,0:T(8,128)(2,1)}, bf16[128,2048]{1,0:T(8,128)(2,1)S(1)}, u32[]{:S(2)}, u32[]{:S(2)}) collective-permute-start(bf16[128,2048]{1,0:T(8,128)(2,1)} %get-tuple-element.222), channel_id=1, source_target_pairs={{0,1},{1,2},{2,3},{3,0},{4,5},{5,6},{6,7},{7,4},{8,9},{9,10},{10,1... | collective-permute-start | bytes 1572872 | tf_op jit(solution)/shard_map/ppermute | solution.py:41
  312.7 11.9 %collective-permute-start.46 = (f32[5632]{0:T(1024)S(1)}, f32[5632]{0:T(1024)S(1)}, u32[]{:S(2)}, u32[]{:S(2)}) collective-permute-start(f32[5632]{0:T(1024)S(1)} %add.226), channel_id=1, source_target_pairs={{0,8},{4,12},{8,0},{12,4},{16,24},{20,28},{24,16},{28,20},{1,9},{5... | collective-permute-start | bytes 67592 | tf_op jit(solution)/shard_map/ppermute | solution.py:45
  324.6 29.8 %collective-permute-start.53 = (bf16[2,256,768]{2,1,0:T(8,128)(2,1)}, bf16[2,256,768]{2,1,0:T(8,128)(2,1)S(1)}, u32[]{:S(2)}, u32[]{:S(2)}) collective-permute-start(bf16[2,256,768]{2,1,0:T(8,128)(2,1)} %get-tuple-element.252), channel_id=1, source_target_pairs={{0,16},{4,20},{8,24},{12,28},{16,0},{20,4},{24,8},{28,12},{1,17},{... | collective-permute-start | bytes 2359304 | tf_op jit(solution)/shard_map/ppermute | solution.py:45
  324.7 31.1 %collective-permute-start.52 = (bf16[2,256,768]{2,1,0:T(8,128)(2,1)}, bf16[2,256,768]{2,1,0:T(8,128)(2,1)S(1)}, u32[]{:S(2)}, u32[]{:S(2)}) collective-permute-start(bf16[2,256,768]{2,1,0:T(8,128)(2,1)} %get-tuple-element.249), channel_id=1, source_target_pairs={{0,8},{4,12},{8,0},{12,4},{16,24},{20,28},{24,16},{28,20},{1,9},{5... | collective-permute-start | bytes 2359304 | tf_op jit(solution)/shard_map/ppermute | solution.py:45
  326.5 20.9 %collective-permute-start.49 = (bf16[128,2048]{1,0:T(8,128)(2,1)S(1)}, bf16[128,2048]{1,0:T(8,128)(2,1)S(1)}, u32[]{:S(2)}, u32[]{:S(2)}) collective-permute-start(bf16[128,2048]{1,0:T(8,128)(2,1)S(1)} %ring_sum.8), channel_id=1, source_target_pairs={{0,1},{1,2},{2,3},{3,0},{4,5},{5,6},{6,7},{7,4},{8,9},{9,10},{10,1... | collective-permute-start | bytes 1572872 | tf_op jit(solution)/shard_map/ppermute | solution.py:41
  334.0 13.5 %collective-permute-start.50 = (bf16[512,256]{1,0:T(8,128)(2,1)S(1)}, bf16[512,256]{1,0:T(8,128)(2,1)S(1)}, u32[]{:S(2)}, u32[]{:S(2)}) collective-permute-start(bf16[512,256]{1,0:T(8,128)(2,1)S(1)} %get-tuple-element.274), channel_id=1, source_target_pairs={{0,1},{1,2},{2,3},{3,0},{4,5},{5,6},{6,7},{7,4},{8,9},{9,10},{10,1... | collective-permute-start | bytes 786440 | tf_op jit(solution)/shard_map/ppermute | solution.py:41
  337.1 31.8 %collective-permute-start.54 = (f32[5632]{0:T(1024)S(1)}, f32[5632]{0:T(1024)S(1)}, u32[]{:S(2)}, u32[]{:S(2)}) collective-permute-start(f32[5632]{0:T(1024)S(1)} %add.227), channel_id=1, source_target_pairs={{0,16},{4,20},{8,24},{12,28},{16,0},{20,4},{24,8},{28,12},{1,17},{... | collective-permute-start | bytes 67592 | tf_op jit(solution)/shard_map/ppermute | solution.py:45
  347.6 22.7 %collective-permute-start.51 = (bf16[128,2048]{1,0:T(8,128)(2,1)S(1)}, bf16[128,2048]{1,0:T(8,128)(2,1)S(1)}, u32[]{:S(2)}, u32[]{:S(2)}) collective-permute-start(bf16[128,2048]{1,0:T(8,128)(2,1)S(1)} %ring_sum.9), channel_id=1, source_target_pairs={{0,1},{1,2},{2,3},{3,0},{4,5},{5,6},{6,7},{7,4},{8,9},{9,10},{10,1... | collective-permute-start | bytes 1572872 | tf_op jit(solution)/shard_map/ppermute | solution.py:41
  347.8 19.8 %collective-permute-start.55 = (bf16[512,256]{1,0:T(8,128)(2,1)S(1)}, bf16[512,256]{1,0:T(8,128)(2,1)S(1)}, u32[]{:S(2)}, u32[]{:S(2)}) collective-permute-start(bf16[512,256]{1,0:T(8,128)(2,1)S(1)} %ring_sum.10), channel_id=1, source_target_pairs={{0,1},{1,2},{2,3},{3,0},{4,5},{5,6},{6,7},{7,4},{8,9},{9,10},{10,1... | collective-permute-start | bytes 786440 | tf_op jit(solution)/shard_map/ppermute | solution.py:41
  354.5 16.4 %collective-permute-start.58 = (bf16[1,1024,256]{2,1,0:T(8,128)(2,1)}, bf16[1,1024,256]{2,1,0:T(8,128)(2,1)}, u32[]{:S(2)}, u32[]{:S(2)}) collective-permute-start(bf16[1,1024,256]{2,1,0:T(8,128)(2,1)} %get-tuple-element.264), channel_id=1, source_target_pairs={{0,8},{4,12},{8,0},{12,4},{16,24},{20,28},{24,16},{28,20},{1,9},{5... | collective-permute-start | bytes 1572872 | tf_op jit(solution)/shard_map/ppermute | solution.py:45
  355.8 17.0 %collective-permute-start.57 = (bf16[1,1024,256]{2,1,0:T(8,128)(2,1)}, bf16[1,1024,256]{2,1,0:T(8,128)(2,1)}, u32[]{:S(2)}, u32[]{:S(2)}) collective-permute-start(bf16[1,1024,256]{2,1,0:T(8,128)(2,1)} %get-tuple-element.262), channel_id=1, source_target_pairs={{0,16},{4,20},{8,24},{12,28},{16,0},{20,4},{24,8},{28,12},{1,17},{... | collective-permute-start | bytes 1572872 | tf_op jit(solution)/shard_map/ppermute | solution.py:45
  367.6 12.2 %collective-permute-start.60 = (bf16[1,256,768]{2,1,0:T(8,128)(2,1)S(1)}, bf16[1,256,768]{2,1,0:T(8,128)(2,1)S(1)}, u32[]{:S(2)}, u32[]{:S(2)}) collective-permute-start(bf16[1,256,768]{2,1,0:T(8,128)(2,1)S(1)} %copy-done.68), channel_id=1, source_target_pairs={{0,16},{4,20},{8,24},{12,28},{16,0},{20,4},{24,8},{28,12},{1,17},{... | collective-permute-start | bytes 1179656 | tf_op jit(solution)/shard_map/ppermute | solution.py:45
  368.8 11.0 %collective-permute-start.61 = (bf16[1,256,768]{2,1,0:T(8,128)(2,1)S(1)}, bf16[1,256,768]{2,1,0:T(8,128)(2,1)S(1)}, u32[]{:S(2)}, u32[]{:S(2)}) collective-permute-start(bf16[1,256,768]{2,1,0:T(8,128)(2,1)S(1)} %copy-done.67), channel_id=1, source_target_pairs={{0,8},{4,12},{8,0},{12,4},{16,24},{20,28},{24,16},{28,20},{1,9},{5... | collective-permute-start | bytes 1179656 | tf_op jit(solution)/shard_map/ppermute | solution.py:45
  370.9 11.8 %collective-permute-start.62 = (bf16[512,256]{1,0:T(8,128)(2,1)S(1)}, bf16[512,256]{1,0:T(8,128)(2,1)S(1)}, u32[]{:S(2)}, u32[]{:S(2)}) collective-permute-start(bf16[512,256]{1,0:T(8,128)(2,1)S(1)} %ring_sum.11), channel_id=1, source_target_pairs={{0,1},{1,2},{2,3},{3,0},{4,5},{5,6},{6,7},{7,4},{8,9},{9,10},{10,1... | collective-permute-start | bytes 786440 | tf_op jit(solution)/shard_map/ppermute | solution.py:41
  (87 other events, 814.0 us)
Sparse Core Ops, SparseCore 0:
  75.9 55.7 all-gather.2
  148.3 41.0 all-gather.4
  245.5 103.8 reduce-scatter.1

commit v5 on v4

--- a/solution.py
+++ b/solution.py
@@ -245,33 +245,62 @@
     return picked[0], swapped(picked[1], "seq", 1)
 
 
-def rows_dot(lhs, columns, units, swap):
+def turn_rows(lhs, turned_lhs, part):
+    for start in range(0, lhs.shape[1], part):
+        columns = slice(start, start + part)
+        turned_lhs[columns, :] = lhs[:, columns].astype(F32).T.astype(BF)
+
+
+def wide_dot(turned_lhs, columns, units):
     total, start = None, 0
     for piece in units:
-        here = lhs[start : start + piece.shape[1], columns]
-        start += piece.shape[1]
-        part = dot(piece[0], here, 0, 0) if swap else dot(here, piece[0], 0, 0)
+        end = start + piece.shape[1]
+        part = dot(turned_lhs[columns, start:end], piece[0], 1, 0)
         total = part if total is None else total + part
+        start = end
+    return total
+
+
+def tall_dot(lhs, units):
+    total, start = None, 0
+    for piece in units:
+        end = start + piece.shape[1]
+        part = dot(piece[0], lhs[start:end, :], 0, 0)
+        total = part if total is None else total + part
+        start = end
     return total
 
 
 def product_body(slots, part, tiles, tall, pieces, *refs):
     own, rec = refs[:2]
     units_own, units_rec = refs[2 : 2 + pieces], refs[2 + pieces : 2 + 2 * pieces]
-    outs = refs[2 + 2 * pieces :]
+    outs = refs[2 + 2 * pieces : 6 + 2 * pieces]
     step = pl.program_id(0)
+    if not tall:
+        own_t, rec_t = refs[6 + 2 * pieces :]
+
+        @pl.when(step == 0)
+        def _():
+            turn_rows(own, own_t, part)
+            turn_rows(rec, rec_t, part)
+
     for half in range(2):
 
         @pl.when((step < tiles) if half == 0 else (step >= tiles))
         def _():
+            if tall:
+                total = tall_dot(own, units_own) + tall_dot(rec, units_rec)
             for kind in range(2):
                 out = outs[2 * half + kind]
                 for place, slot in enumerate(slots[half][kind]):
                     columns = slice(slot * part, (slot + 1) * part)
-                    out[place] = (
-                        rows_dot(own, columns, units_own, tall)
-                        + rows_dot(rec, columns, units_rec, tall)
-                    ).astype(BF)
+                    if tall:
+                        out[place] = total[:, columns].astype(BF)
+                    else:
+                        out[place] = (
+                            wide_dot(own_t, columns, units_own)
+                            + wide_dot(rec_t, columns, units_rec)
+                        ).astype(BF)
 
 
 class Joined:
@@ -311,6 +340,7 @@
             in_specs=[whole, whole, *columns],
             out_specs=specs,
             out_shape=shapes,
+            scratch_shapes=[] if tall else [pltpu.VMEM((slotted, rows), BF)] * 2,
             compiler_params=params(58),
             cost_estimate=cost(),
             name="product",
@@ -357,11 +387,18 @@
 
 
 def whole_body(part, pieces, own, rec, *refs):
-    units_own, units_rec, out = refs[:pieces], refs[pieces : 2 * pieces], refs[2 * pieces]
+    units_own, units_rec = refs[:pieces], refs[pieces : 2 * pieces]
+    out, own_t, rec_t = refs[2 * pieces :]
+
+    @pl.when(pl.program_id(0) == 0)
+    def _():
+        turn_rows(own, own_t, part)
+        turn_rows(rec, rec_t, part)
+
     for slot in range(out.shape[0]):
         columns = slice(slot * part, (slot + 1) * part)
         out[slot, 0] = (
-            rows_dot(own, columns, units_own, False) + rows_dot(rec, columns, units_rec, False)
+            wide_dot(own_t, columns, units_own) + wide_dot(rec_t, columns, units_rec)
         ).astype(BF)
 
 
@@ -384,6 +421,7 @@
             (groups, 1, part, tile), lambda j: (0, j // each, 0, j % each)
         ),
         out_shape=jax.ShapeDtypeStruct((groups, kinds, part, wide), BF),
+        scratch_shapes=[pltpu.VMEM((slotted, rows), BF)] * 2,
         compiler_params=params(58),
         cost_estimate=cost(),
         name="whole_product",
@@ -1054,7 +1092,7 @@
             held = jnp.concatenate([held, swapped(held, "seq", 2 * bit)], axis=0)
         halves[place] = held
         second_arrived.append(swapped(held, "seq", 2 * order[-1]))
-    grad_out = lax.all_gather(after(cotangent, tok_two, tok_three), "chan", axis=0, tiled=True)
+    grad_out = lax.all_gather(after(cotangent, tok_three), "chan", axis=0, tiled=True)
     tok_blocks = [tokens, tok_one, tok_two, tok_three]
     for place, order in enumerate(orders):
         held = jnp.concatenate([halves[place], after(second_arrived[place], tok_two)], axis=0)
@@ -1090,6 +1128,7 @@
     conv_out, gated_mix = conv_forward(
         projected[1], mixed_in, before, conv_taps, masks, chan_count
     )
+    gated_mix = [after(rows, grad_out) for rows in gated_mix]
     gated_rows_own = [gated_mix[0]] + [
         turned(gated_mix[r], "chan", -r) for r in range(1, chan_count)
     ]

time: 393 us -> 386 us (0.982)
  starting transfers between devices: 75.9 us -> 70.4 us
  other arithmetic: 13 us -> 17.1 us
  waiting for transfers between devices: 120 us -> 116 us
    ppermute x28, waiting for transfers between devices: 92 us -> 80.1 us  [turned(): lax.ppermute(block, axis, [(i, (i + distance) % count) for i in range(cou...]
    all_gather x1, waiting for transfers between devices: 0.01 us -> 8.51 us  [on_device(): lax.all_gather(after(cotangent, tok_three), 'chan', axis=0, tiled=True)]
    ppermute x33, starting transfers between devices: 32 us -> 25.2 us  [swapped(): lax.ppermute(block, axis, [(i, i ^ bit) for i in range(lax.axis_size(axis...]
    unnamed x138 -> x130, local copies, waits for them, and re-layouts: 18.8 us -> 15 us
  transfers between devices with their start and end apart: 66 -> 66, of which waited for: 27 -> 24; matrix products, arithmetic and copies ran while one was open for 4% -> 6% of each run, Pallas kernels for 36% -> 36%
where the time goes in v5:
time: 386 us; the launch traced here: 384 us
  Pallas kernels  144 us (37%)
  waiting for transfers between devices  116 us (30%)
  starting transfers between devices  70.4 us (18%)
  local copies, waits for them, and re-layouts  22 us (6%)
  other arithmetic  17.1 us (4%)
  between operations  14.6 us (4%)
    ppermute x28, waiting for transfers between devices, turned(): lax.ppermute(block, axis, [(i, (i + distance) % count) for i in range(cou...  80.1 us
    pallas_call x2, Pallas kernels, feed_forward(): pl.pallas_call(functools.partial(ffn_body, count), grid_spec=pltpu.Prefet...  41.9 us
    ppermute x28, starting transfers between devices, turned(): lax.ppermute(block, axis, [(i, (i + distance) % count) for i in range(cou...  41.2 us
    ppermute x33, waiting for transfers between devices, swapped(): lax.ppermute(block, axis, [(i, i ^ bit) for i in range(lax.axis_size(axis...  27.4 us
    ppermute x33, starting transfers between devices, swapped(): lax.ppermute(block, axis, [(i, i ^ bit) for i in range(lax.axis_size(axis...  25.2 us
    pallas_call x2, Pallas kernels, __init__(): pl.pallas_call(functools.partial(product_body, slots, part, tiles, tall,...  17.8 us
    unnamed x130, local copies, waits for them, and re-layouts  15 us
    pallas_call x1, Pallas kernels, whole_product(): pl.pallas_call(functools.partial(whole_body, part, len(units[0])), grid=(...  14.9 us
  transfers between devices with their start and end apart: 66, of which 24 were waited for; matrix products, arithmetic and copies ran while one was open for 6% of the time, Pallas kernels for 36%

profile of v5, /device:TPU:0, one launch (start us, length us, event | category | flops | bytes accessed | tf_op | source)
XLA Modules:
  0.0 384.2 jit_solution(10055964701769953402)
XLA Ops:
  7.2 3.1 collective-permute-start.2
  11.3 2.1 collective-permute-start.1
  13.4 17.5 %collective-permute-done.1 = bf16[512,256]{1,0:T(8,128)(2,1)S(1)} collective-permute-done((bf16[512,256]{1,0:T(8,128)(2,1)S(1)}, bf16[512,256]{1,0:T(8,128)(2,1)S(1)}, u32[]{:S(2)}, u32[]{:S(2)}) %collective-permute-start.1) | collective-permute-done | bytes 262176 | tf_op jit(solution)/shard_map/ppermute | solution.py:41
  30.9 4.9 %collective-permute-done = bf16[512,256]{1,0:T(8,128)(2,1)S(1)} collective-permute-done((bf16[512,256]{1,0:T(8,128)(2,1)S(1)}, bf16[512,256]{1,0:T(8,128)(2,1)S(1)}, u32[]{:S(2)}, u32[]{:S(2)}) %collective-permute-start) | collective-permute-done | bytes 262176 | tf_op jit(solution)/shard_map/ppermute | solution.py:41
  35.7 3.8 collective-permute-start.5
  39.6 7.2 %collective-permute-done.3 = bf16[512,256]{1,0:T(8,128)(2,1)S(1)} collective-permute-done((bf16[512,256]{1,0:T(8,128)(2,1)S(1)}, bf16[512,256]{1,0:T(8,128)(2,1)S(1)}, u32[]{:S(2)}, u32[]{:S(2)}) %collective-permute-start.3) | collective-permute-done | bytes 262176 | tf_op jit(solution)/shard_map/ppermute | solution.py:41
  50.0 4.7 %collective-permute-done.5.refs_3_.refs_5_ = bf16[128,2048]{1,0:T(8,128)(2,1)S(1)} collective-permute-done((bf16[128,2048]{1,0:T(8,128)(2,1)}, bf16[128,2048]{1,0:T(8,128)(2,1)S(1)}, u32[]{:S(2)}, u32[]{:S(2)}) %collective-permute-start.5) | collective-permute-done | bytes 524320 | tf_op jit(solution)/shard_map/ppermute | solution.py:41
  60.4 15.0 %collective-permute-done.7.refs_2_.refs_4_ = bf16[128,2048]{1,0:T(8,128)(2,1)S(1)} collective-permute-done((bf16[128,2048]{1,0:T(8,128)(2,1)S(1)}, bf16[128,2048]{1,0:T(8,128)(2,1)S(1)}, u32[]{:S(2)}, u32[]{:S(2)}) %collective-permute-start.7) | collective-permute-done | bytes 524320 | tf_op jit(solution)/shard_map/ppermute | solution.py:41
  77.1 2.9 pad_maximum_fusion.refs_5_.refs_1_
  82.6 8.7 %in_projection.1 = (f32[512,512]{1,0:T(8,128)}, f32[512,512]{1,0:T(8,128)}, f32[512,512]{1,0:T(8,128)}, bf16[512,512]{1,0:T(8,128)(2,1)}, bf16[512,2048]{1,0:T(8,128)(2,1)}, /*index=5*/f32[512,1]{1,0:T(8,128)}) custom-call(bf16[128,2048]{1,0:T(8,128)(2,1)} %refs_2_.1, bf16[128,2048]{1,0:T(8,128)(2,1)} %copy-done.35, bf16[128,2048]{1,0:T(8,128)(2,1)} %copy-done.37, ...), custom_call_target="tpu_custom_call" | custom-call | flops 1024 | bytes 1024 | tf_op jit(solution)/shard_map/in_projection/pallas_call | solution.py:677
  92.2 2.4 collective-permute-start.10
  96.1 2.9 conv_forward.1
  99.0 8.5 %all-gather.3.cloned.1.call-done.refs_0_.refs_2_.refs_3_ = bf16[512,2048]{1,0:T(8,128)(2,1)} async-done(((bf16[128,2048]{1,0:T(8,128)(2,1)}), bf16[512,2048]{1,0:T(8,128)(2,1)}) %all-gather.3.cloned.1.call-update) | async-done | bytes 2097168 | tf_op jit(solution)/shard_map/all_gather | solution.py:1095
  109.0 2.4 collective-permute-start.11
  111.4 4.6 %collective-permute-done.13.refs_3_ = bf16[128,512]{1,0:T(8,128)(2,1)S(1)} collective-permute-done((bf16[128,512]{1,0:T(8,128)(2,1)}, bf16[128,512]{1,0:T(8,128)(2,1)S(1)}, u32[]{:S(2)}, u32[]{:S(2)}) %collective-permute-start.13) | collective-permute-done | bytes 131104 | tf_op jit(solution)/shard_map/ppermute | solution.py:41
  116.0 4.6 %collective-permute-done.12.refs_2_ = bf16[128,512]{1,0:T(8,128)(2,1)S(1)} collective-permute-done((bf16[128,512]{1,0:T(8,128)(2,1)}, bf16[128,512]{1,0:T(8,128)(2,1)S(1)}, u32[]{:S(2)}, u32[]{:S(2)}) %collective-permute-start.12) | collective-permute-done | bytes 131104 | tf_op jit(solution)/shard_map/ppermute | solution.py:41
  123.1 6.1 %mixer_rows.1 = (f32[128,2048]{1,0:T(8,128)S(1)}, bf16[128,2048]{1,0:T(8,128)(2,1)S(1)}, f32[128,1]{1,0:T(8,128)S(1)}, bf16[128,2048]{1,0:T(8,128)(2,1)}) custom-call(s32[5]{0:T(128)S(1)} %pad_add_fusion.ids, bf16[128,512]{1,0:T(8,128)(2,1)S(1)} %copy-done.24, bf16[128,512]{1,0:T(8,128)(2,1)S(1)} %collective-permute-done.11.refs_1_, ...), custom_call_target="tpu_custom_call" | custom-call | flops 1024 | bytes 1024 | tf_op jit(solution)/shard_map/mixer_rows/pallas_call | solution.py:917
  130.8 2.5 collective-permute-start.15
  137.0 7.9 %collective-permute-done.15.refs_1_ = bf16[128,2048]{1,0:T(8,128)(2,1)S(1)} collective-permute-done((bf16[128,2048]{1,0:T(8,128)(2,1)S(1)}, bf16[128,2048]{1,0:T(8,128)(2,1)S(1)}, u32[]{:S(2)}, u32[]{:S(2)}) %collective-permute-start.15) | collective-permute-done | bytes 524320 | tf_op jit(solution)/shard_map/ppermute | solution.py:41
  147.1 21.1 %feed_forward.2 = (bf16[1,256,2048]{2,1,0:T(8,128)(2,1)S(1)}, bf16[2,256,2048]{2,1,0:T(8,128)(2,1)}, bf16[128,2048]{1,0:T(8,128)(2,1)S(1)}, bf16[128,2048]{1,0:T...) custom-call(s32[4]{0:T(128)S(1)} %and_select_fusion.ids, ...), custom_call_target="tpu_custom_call" | custom-call | flops 1024 | bytes 1024 | tf_op jit(solution)/shard_map/feed_forward/pallas_call | solution.py:141
  171.7 2.5 collective-permute-start.18
  174.2 20.8 %feed_forward.3 = (bf16[1,256,2048]{2,1,0:T(8,128)(2,1)S(1)}, bf16[2,256,2048]{2,1,0:T(8,128)(2,1)}, bf16[128,2048]{1,0:T(8,128)(2,1)S(1)}, bf16[128,2048]{1,0:T...) custom-call(s32[4]{0:T(128)S(1)} %and_select_fusion.ids, ...), custom_call_target="tpu_custom_call" | custom-call | flops 1024 | bytes 1024 | tf_op jit(solution)/shard_map/feed_forward/pallas_call | solution.py:141
  197.1 2.8 collective-permute-done.24.refs_5_
  205.0 8.9 %product.2 = (bf16[2,1024,256]{2,1,0:T(8,128)(2,1)}, bf16[2,1024,256]{2,1,0:T(8,128)(2,1)}, bf16[2,1024,256]{2,1,0:T(8,128)(2,1)}, bf16[2,1024,256]{2,1,0:T(8,128)(2,1)}) custom-call(bf16[512,1024]{1,0:T(8,128)(2,1)} %copy-done.15, bf16[512,1024]{1,0:T(8,128)(2,1)} %collective-permute-done.21.refs_1_, bf16[1,256,2048]{2,1,0:T(8,128)(2,1)} %copy-done.16, ...), custom_call_target="tpu_custom_call" | custom-call | flops 1024 | bytes 1024 | tf_op jit(solution)/shard_map/product/pallas_call | solution.py:337
  217.9 14.9 %whole_product.1 = bf16[4,2,256,2048]{3,2,1,0:T(8,128)(2,1)} custom-call(bf16[512,1024]{1,0:T(8,128)(2,1)} %copy-done.14, bf16[512,1024]{1,0:T(8,128)(2,1)} %copy-done.39, bf16[2,256,2048]{2,1,0:T(8,128)(2,1)} %get-tuple-element.184.refs_0_, bf16[2,256,2048]{2,1,0:T(8,128)(2,1)} %get-tuple-element.193.refs_1_, bf16[2,256,2048]{2,1,0:T(8,128)(2,1)} %copy-done.34, ...), custom_call_target="tpu_custom_call" | custom-call | flops 1024 | bytes 1024 | tf_op jit(solution)/shard_map/whole_product/pallas_call | solution.py:416
  232.7 7.0 %collective-permute-done.28.refs_1_ = bf16[2,1024,256]{2,1,0:T(8,128)(2,1)} collective-permute-done((bf16[2,1024,256]{2,1,0:T(8,128)(2,1)}, bf16[2,1024,256]{2,1,0:T(8,128)(2,1)}, u32[]{:S(2)}, u32[]{:S(2)}) %collective-permute-start.28) | collective-permute-done | bytes 1048608 | tf_op jit(solution)/shard_map/ppermute | solution.py:45
  240.9 2.5 collective-permute-start.30
  243.4 10.1 %gated_rows.1 = (bf16[128,512]{1,0:T(8,128)(2,1)}, bf16[128,512]{1,0:T(8,128)(2,1)}, bf16[128,512]{1,0:T(8,128)(2,1)}, bf16[128,512]{1,0:T(8,128)(2,1)}, f32[128...) custom-call(s32[5]{0:T(128)} %copy-done.28, bf16[512,2048]{1,0:T(8,128)(2,1)} %refs_0_.2, ...), custom_call_target="tpu_custom_call" | custom-call | flops 1024 | bytes 1024 | tf_op jit(solution)/shard_map/gated_rows/pallas_call | solution.py:1006
  254.4 4.3 %collective-permute-start.33 = (bf16[128,512]{1,0:T(8,128)(2,1)}, bf16[128,512]{1,0:T(8,128)(2,1)S(1)}, u32[]{:S(2)}, u32[]{:S(2)}) collective-permute-start(bf16[128,512]{1,0:T(8,128)(2,1)} %get-tuple-element.206), channel_id=1, source_target_pairs={{0,3},{1,0},{2,1},{3,2},{4,7},{5,4},{6,5},{7,6},{8,11},{9,8},{10,9... | collective-permute-start | bytes 393224 | tf_op jit(solution)/shard_map/ppermute | solution.py:41
  263.4 5.0 %collective-permute-done.32.refs_2_ = bf16[128,512]{1,0:T(8,128)(2,1)S(1)} collective-permute-done((bf16[128,512]{1,0:T(8,128)(2,1)}, bf16[128,512]{1,0:T(8,128)(2,1)S(1)}, u32[]{:S(2)}, u32[]{:S(2)}) %collective-permute-start.32) | collective-permute-done | bytes 131104 | tf_op jit(solution)/shard_map/ppermute | solution.py:41
  268.4 2.2 collective-permute-start.34
  271.8 2.5 collective-permute-start.42
  274.3 4.6 %collective-permute-done.40.refs_4_ = bf16[128,256]{1,0:T(8,128)(2,1)S(1)} collective-permute-done((bf16[128,256]{1,0:T(8,128)(2,1)S(1)}, bf16[128,256]{1,0:T(8,128)(2,1)S(1)}, u32[]{:S(2)}, u32[]{:S(2)}) %collective-permute-start.40) | collective-permute-done | bytes 65568 | tf_op jit(solution)/shard_map/ppermute | solution.py:45
  280.4 4.4 %collective-permute-done.43.refs_7_ = bf16[128,256]{1,0:T(8,128)(2,1)S(1)} collective-permute-done((bf16[128,256]{1,0:T(8,128)(2,1)S(1)}, bf16[128,256]{1,0:T(8,128)(2,1)S(1)}, u32[]{:S(2)}, u32[]{:S(2)}) %collective-permute-start.43) | collective-permute-done | bytes 65568 | tf_op jit(solution)/shard_map/ppermute | solution.py:45
  285.5 5.7 %conv_backward.1 = (bf16[3,512,512]{2,1,0:T(8,128)(2,1)}, f32[3,512]{1,0:T(4,128)}) custom-call(bf16[128,512]{1,0:T(8,128)(2,1)} %get-tuple-element.200.refs_0_, bf16[128,512]{1,0:T(8,128)(2,1)} %copy-done.49, bf16[128,512]{1,0:T(8,128)(2,1)} %copy-done.48, bf16[128,512]{1,0:T(8,128)(2,1)} %copy-done.47, f32[512,512]{1,0:T(8,128)} %get-tuple-element.214.refs_4_, ...), custom_call_target="tpu_custom_call" | custom-call | flops 1024 | bytes 1024 | tf_op jit(solution)/shard_map/conv_backward/pallas_call | solution.py:790
  291.3 7.7 %mixer_back.1 = (bf16[128,2048]{1,0:T(8,128)(2,1)}, bf16[128,2048]{1,0:T(8,128)(2,1)}, bf16[128,2048]{1,0:T(8,128)(2,1)}, bf16[128,2048]{1,0:T(8,128)(2,1)}, f32[1,2048]{1,0:T(1,128)}) custom-call(bf16[3,512,512]{2,1,0:T(8,128)(2,1)} %get-tuple-element.237.refs_0_.refs_2_, bf16[3,2048,512]{2,1,0:T(8,128)(2,1)} %refs_1_.1, bf16[128,2048]{1,0:T(8,128)(2,1)} %refs_2_.1, ...), custom_call_target="tpu_custom_call" | custom-call | flops 1024 | bytes 1024 | tf_op jit(solution)/shard_map/mixer_back/pallas_call | solution.py:834
  299.1 2.4 collective-permute-start.48
  304.0 2.1 collective-permute-done.45
  309.1 8.9 %product.3 = (bf16[2,256,768]{2,1,0:T(8,128)(2,1)}, bf16[2,256,768]{2,1,0:T(8,128)(2,1)}, bf16[2,256,768]{2,1,0:T(8,128)(2,1)}, bf16[2,256,768]{2,1,0:T(8,128)(2,1)}) custom-call(bf16[512,1024]{1,0:T(8,128)(2,1)} %copy-done.13, bf16[512,1024]{1,0:T(8,128)(2,1)} %copy-done.40, bf16[3,512,512]{2,1,0:T(8,128)(2,1)} %get-tuple-element.237.refs_0_.refs_2_, ...), custom_call_target="tpu_custom_call" | custom-call | flops 1024 | bytes 1024 | tf_op jit(solution)/shard_map/product/pallas_call | solution.py:337
  320.3 5.7 %rows_product.1 = bf16[4,512,256]{2,1,0:T(8,128)(2,1)} custom-call(s32[8]{0:T(128)} %copy-done.29, bf16[1024,2048]{1,0:T(8,128)(2,1)} %all-gather.5.cloned.1.call-done.gated, bf16[128,256]{1,0:T(8,128)(2,1)} %copy-done.27, bf16[128,256]{1,0:T(8,128)(2,1)} %copy-done.51, bf16[128,256]{1,0:T(8,128)(2,1)} %copy-done.52, bf16[128,256]{1,0:T(8,128)(2,1)} %copy-done.53, ...), custom_call_target="tpu_custom_call" | custom-call | flops 1024 | bytes 1024 | tf_op jit(solution)/shard_map/rows_product/pallas_call | solution.py:603
  331.5 4.0 %upper_sums.2 = (bf16[1,1024,256]{2,1,0:T(8,128)(2,1)}, bf16[1,1024,256]{2,1,0:T(8,128)(2,1)}) custom-call(bf16[2,1024,256]{2,1,0:T(8,128)(2,1)} %get-tuple-element.269.refs_0_, bf16[2,1024,256]{2,1,0:T(8,128)(2,1)} %collective-permute-done.28.refs_1_, bf16[2,1024,256]{2,1,0:T(8,128)(2,1)} %get-tuple-element.248.refs_2_.refs_3_, ...), custom_call_target="tpu_custom_call" | custom-call | flops 1024 | bytes 1024 | tf_op jit(solution)/shard_map/upper_sums/pallas_call | solution.py:473
  335.5 4.3 %collective-permute-done.50.a = bf16[512,256]{1,0:T(8,128)(2,1)S(1)} collective-permute-done((bf16[512,256]{1,0:T(8,128)(2,1)S(1)}, bf16[512,256]{1,0:T(8,128)(2,1)S(1)}, u32[]{:S(2)}, u32[]{:S(2)}) %collective-permute-start.50) | collective-permute-done | bytes 262176 | tf_op jit(solution)/shard_map/ppermute | solution.py:41
  341.4 5.6 %collective-permute-done.53.refs_3_.refs_4_ = bf16[2,256,768]{2,1,0:T(8,128)(2,1)S(1)} collective-permute-done((bf16[2,256,768]{2,1,0:T(8,128)(2,1)}, bf16[2,256,768]{2,1,0:T(8,128)(2,1)S(1)}, u32[]{:S(2)}, u32[]{:S(2)}) %collective-permute-start.53) | collective-permute-done | bytes 786464 | tf_op jit(solution)/shard_map/ppermute | solution.py:45
  349.1 2.4 add_convert_fusion
  351.4 3.8 %upper_sums.3 = (bf16[1,256,768]{2,1,0:T(8,128)(2,1)}, bf16[1,256,768]{2,1,0:T(8,128)(2,1)}) custom-call(bf16[2,256,768]{2,1,0:T(8,128)(2,1)} %get-tuple-element.274.refs_0_, bf16[2,256,768]{2,1,0:T(8,128)(2,1)} %copy-done.10, bf16[2,256,768]{2,1,0:T(8,128)(2,1)} %get-tuple-element.258.refs_2_.refs_3_, bf16[2,256,768]{2,1,0:T(8,128)(2,1)} %copy-done.8), custom_call_target="tpu_custom_call" | custom-call | flops 1024 | bytes 1024 | tf_op jit(solution)/shard_map/upper_sums/pallas_call | solution.py:473
  355.3 3.8 final_sums.2
  363.9 2.0 collective-permute-start.62
  365.9 4.4 %final_sums.3 = f32[2048,256]{1,0:T(8,128)} custom-call(bf16[2,1024,256]{2,1,0:T(8,128)(2,1)} %get-tuple-element.269.refs_0_, bf16[2,1024,256]{2,1,0:T(8,128)(2,1)} %collective-permute-done.28.refs_1_, bf16[1,1024,256]{2,1,0:T(8,128)(2,1)} %collective-permute-done.57.refs_2_, bf16[2,1024,256]{2,1,0:T(8,128)(2,1)} %get-tuple-element.248.refs_2_.refs_3_, ...), custom_call_target="tpu_custom_call" | custom-call | flops 1024 | bytes 1024 | tf_op jit(solution)/shard_map/final_sums/pallas_call | solution.py:516
  (300 shorter events, 81.3 us)
Async XLA Ops:
  7.2 100.3 %all-gather.3.cloned.1.call-start = ((), (), s32[]{:S(2)}) async-start(), calls=%async_computation.1 | async-start | bytes 2621440 | tf_op jit(solution)/shard_map/all_gather | solution.py:1095
  7.2 28.5 %collective-permute-start.2 = (bf16[128,2048]{1,0:T(8,128)(2,1)}, bf16[128,2048]{1,0:T(8,128)(2,1)S(1)}, u32[]{:S(2)}, u32[]{:S(2)}) collective-permute-start(bf16[128,2048]{1,0:T(8,128)(2,1)} %refs_2_.1), channel_id=1, source_target_pairs={{0,1},{1,2},{2,3},{3,0},{4,5},{5,6},{6,7},{7,4},{8,9},{9,10},{10,1... | collective-permute-start | bytes 1572872 | tf_op jit(solution)/shard_map/ppermute | solution.py:41
  11.3 19.6 %collective-permute-start.1 = (bf16[512,256]{1,0:T(8,128)(2,1)S(1)}, bf16[512,256]{1,0:T(8,128)(2,1)S(1)}, u32[]{:S(2)}, u32[]{:S(2)}) collective-permute-start(bf16[512,256]{1,0:T(8,128)(2,1)S(1)} %constant_dynamic-slice_fusion), channel_id=1, source_target_pairs={{0,3},{1,0},{2,1},{3,2},{4,7},{5,4},{6,5},{7,6},{8,11},{9,8},{10,9... | collective-permute-start | bytes 786440 | tf_op jit(solution)/shard_map/ppermute | solution.py:41
  13.4 22.4 %collective-permute-start = (bf16[512,256]{1,0:T(8,128)(2,1)S(1)}, bf16[512,256]{1,0:T(8,128)(2,1)S(1)}, u32[]{:S(2)}, u32[]{:S(2)}) collective-permute-start(bf16[512,256]{1,0:T(8,128)(2,1)S(1)} %constant_dynamic-slice_fusion), channel_id=1, source_target_pairs={{0,1},{1,2},{2,3},{3,0},{4,5},{5,6},{6,7},{7,4},{8,9},{9,10},{10,1... | collective-permute-start | bytes 786440 | tf_op jit(solution)/shard_map/ppermute | solution.py:41
  35.7 11.0 %collective-permute-start.3 = (bf16[512,256]{1,0:T(8,128)(2,1)S(1)}, bf16[512,256]{1,0:T(8,128)(2,1)S(1)}, u32[]{:S(2)}, u32[]{:S(2)}) collective-permute-start(bf16[512,256]{1,0:T(8,128)(2,1)S(1)} %collective-permute-done), channel_id=1, source_target_pairs={{0,1},{1,2},{2,3},{3,0},{4,5},{5,6},{6,7},{7,4},{8,9},{9,10},{10,1... | collective-permute-start | bytes 786440 | tf_op jit(solution)/shard_map/ppermute | solution.py:41
  35.7 19.0 %collective-permute-start.5 = (bf16[128,2048]{1,0:T(8,128)(2,1)}, bf16[128,2048]{1,0:T(8,128)(2,1)S(1)}, u32[]{:S(2)}, u32[]{:S(2)}) collective-permute-start(bf16[128,2048]{1,0:T(8,128)(2,1)} %refs_2_.1), channel_id=1, source_target_pairs={{0,3},{1,0},{2,1},{3,2},{4,7},{5,4},{6,5},{7,6},{8,11},{9,8},{10,9... | collective-permute-start | bytes 1572872 | tf_op jit(solution)/shard_map/ppermute | solution.py:41
  55.8 19.7 %collective-permute-start.9 = (bf16[2,3,256,256]{3,2,1,0:T(8,128)(2,1)}, bf16[2,3,256,256]{3,2,1,0:T(8,128)(2,1)}, u32[]{:S(2)}, u32[]{:S(2)}) collective-permute-start(bf16[2,3,256,256]{3,2,1,0:T(8,128)(2,1)} %pad_maximum_fusion.3), channel_id=1, source_target_pairs={{0,8},{4,12},{8,0},{12,4},{16,24},{20,28},{24,16},{28,20},{1,9},{5... | collective-permute-start | bytes 2359304 | tf_op jit(solution)/shard_map/ppermute | solution.py:45
  58.2 18.9 %collective-permute-start.6 = (bf16[2,3,256,256]{3,2,1,0:T(8,128)(2,1)}, bf16[2,3,256,256]{3,2,1,0:T(8,128)(2,1)}, u32[]{:S(2)}, u32[]{:S(2)}) collective-permute-start(bf16[2,3,256,256]{3,2,1,0:T(8,128)(2,1)} %pad_maximum_fusion.2), channel_id=1, source_target_pairs={{0,16},{4,20},{8,24},{12,28},{16,0},{20,4},{24,8},{28,12},{1,17},{... | collective-permute-start | bytes 2359304 | tf_op jit(solution)/shard_map/ppermute | solution.py:45
  59.7 15.7 %collective-permute-start.7 = (bf16[128,2048]{1,0:T(8,128)(2,1)S(1)}, bf16[128,2048]{1,0:T(8,128)(2,1)S(1)}, u32[]{:S(2)}, u32[]{:S(2)}) collective-permute-start(bf16[128,2048]{1,0:T(8,128)(2,1)S(1)} %collective-permute-done.2.refs_1_.refs_3_), channel_id=1, source_target_pairs={{0,1},{1,2},{2,3},{3,0},{4,5},{5,6},{6,7},{7,4},{8,9},{9,10},{10,1... | collective-permute-start | bytes 1572872 | tf_op jit(solution)/shard_map/ppermute | solution.py:41
  60.3 179.5 %all-gather.5.cloned.1.call-start = ((), (), s32[]{:S(2)}) async-start(), calls=%async_computation.2 | async-start | bytes 4718592 | tf_op jit(solution)/shard_map/all_gather | solution.py:1144
  80.0 40.6 %collective-permute-start.14 = (bf16[4,3,512,256]{3,2,1,0:T(8,128)(2,1)}, bf16[4,3,512,256]{3,2,1,0:T(8,128)(2,1)}, u32[]{:S(2)}, u32[]{:S(2)}) collective-permute-start(bf16[4,3,512,256]{3,2,1,0:T(8,128)(2,1)} %pad_maximum_fusion.refs_5_.refs_1_), channel_id=1, source_target_pairs={{0,4},{4,0},{8,12},{12,8},{16,20},{20,16},{24,28},{28,24},{1,5},{5... | collective-permute-start | bytes 9437192 | tf_op jit(solution)/shard_map/ppermute | solution.py:45
  107.5 13.1 %collective-permute-start.12 = (bf16[128,512]{1,0:T(8,128)(2,1)}, bf16[128,512]{1,0:T(8,128)(2,1)S(1)}, u32[]{:S(2)}, u32[]{:S(2)}) collective-permute-start(bf16[128,512]{1,0:T(8,128)(2,1)} %get-tuple-element.158), channel_id=1, source_target_pairs={{0,2},{1,3},{2,0},{3,1},{4,6},{5,7},{6,4},{7,5},{8,10},{9,11},{10,... | collective-permute-start | bytes 393224 | tf_op jit(solution)/shard_map/ppermute | solution.py:41
  109.0 11.7 %collective-permute-start.11 = (bf16[128,512]{1,0:T(8,128)(2,1)}, bf16[128,512]{1,0:T(8,128)(2,1)S(1)}, u32[]{:S(2)}, u32[]{:S(2)}) collective-permute-start(bf16[128,512]{1,0:T(8,128)(2,1)} %get-tuple-element.156), channel_id=1, source_target_pairs={{0,3},{1,0},{2,1},{3,2},{4,7},{5,4},{6,5},{7,6},{8,11},{9,8},{10,9... | collective-permute-start | bytes 393224 | tf_op jit(solution)/shard_map/ppermute | solution.py:41
  130.8 14.1 %collective-permute-start.15 = (bf16[128,2048]{1,0:T(8,128)(2,1)S(1)}, bf16[128,2048]{1,0:T(8,128)(2,1)S(1)}, u32[]{:S(2)}, u32[]{:S(2)}) collective-permute-start(bf16[128,2048]{1,0:T(8,128)(2,1)S(1)} %get-tuple-element.170.refs_0_), channel_id=1, source_target_pairs={{0,1},{1,2},{2,3},{3,0},{4,5},{5,6},{6,7},{7,4},{8,9},{9,10},{10,1... | collective-permute-start | bytes 1572872 | tf_op jit(solution)/shard_map/ppermute | solution.py:41
  145.0 210.3 %reduce-scatter.2.cloned.1.call-start = ((), (), s32[]{:S(2)}) async-start(), calls=%async_computation.3 | async-start | bytes 10485760 | tf_op jit(solution)/shard_map/reduce_scatter | solution.py:435
  145.0 24.7 %collective-permute-start.17 = (bf16[128,2048]{1,0:T(8,128)(2,1)S(1)}, bf16[128,2048]{1,0:T(8,128)(2,1)S(1)}, u32[]{:S(2)}, u32[]{:S(2)}) collective-permute-start(bf16[128,2048]{1,0:T(8,128)(2,1)S(1)} %get-tuple-element.170.refs_0_), channel_id=1, source_target_pairs={{0,3},{1,0},{2,1},{3,2},{4,7},{5,4},{6,5},{7,6},{8,11},{9,8},{10,9... | collective-permute-start | bytes 1572872 | tf_op jit(solution)/shard_map/ppermute | solution.py:41
  146.8 23.0 %collective-permute-start.16 = (bf16[128,2048]{1,0:T(8,128)(2,1)S(1)}, bf16[128,2048]{1,0:T(8,128)(2,1)S(1)}, u32[]{:S(2)}, u32[]{:S(2)}) collective-permute-start(bf16[128,2048]{1,0:T(8,128)(2,1)S(1)} %collective-permute-done.15.refs_1_), channel_id=1, source_target_pairs={{0,1},{1,2},{2,3},{3,0},{4,5},{5,6},{6,7},{7,4},{8,9},{9,10},{10,1... | collective-permute-start | bytes 1572872 | tf_op jit(solution)/shard_map/ppermute | solution.py:41
  169.8 26.8 %collective-permute-start.23 = (bf16[2,256,2048]{2,1,0:T(8,128)(2,1)}, bf16[2,256,2048]{2,1,0:T(8,128)(2,1)S(1)}, u32[]{:S(2)}, u32[]{:S(2)}) collective-permute-start(bf16[2,256,2048]{2,1,0:T(8,128)(2,1)} %get-tuple-element.184.refs_0_), channel_id=1, source_target_pairs={{0,4},{4,0},{8,12},{12,8},{16,20},{20,16},{24,28},{28,24},{1,5},{5... | collective-permute-start | bytes 6291464 | tf_op jit(solution)/shard_map/ppermute | solution.py:45
  169.8 26.7 %collective-permute-start.22 = (bf16[1,256,2048]{2,1,0:T(8,128)(2,1)S(1)}, bf16[1,256,2048]{2,1,0:T(8,128)(2,1)S(1)}, u32[]{:S(2)}, u32[]{:S(2)}) collective-permute-start(bf16[1,256,2048]{2,1,0:T(8,128)(2,1)S(1)} %get-tuple-element.181.refs_2_), channel_id=1, source_target_pairs={{0,4},{4,0},{8,12},{12,8},{16,20},{20,16},{24,28},{28,24},{1,5},{5... | collective-permute-start | bytes 3145736 | tf_op jit(solution)/shard_map/ppermute | solution.py:45
  170.3 25.5 %collective-permute-start.19 = (bf16[128,2048]{1,0:T(8,128)(2,1)S(1)}, bf16[128,2048]{1,0:T(8,128)(2,1)S(1)}, u32[]{:S(2)}, u32[]{:S(2)}) collective-permute-start(bf16[128,2048]{1,0:T(8,128)(2,1)S(1)} %get-tuple-element.174), channel_id=1, source_target_pairs={{0,1},{1,2},{2,3},{3,0},{4,5},{5,6},{6,7},{7,4},{8,9},{9,10},{10,1... | collective-permute-start | bytes 1572872 | tf_op jit(solution)/shard_map/ppermute | solution.py:41
  171.7 24.9 %collective-permute-start.18 = (bf16[128,2048]{1,0:T(8,128)(2,1)S(1)}, bf16[128,2048]{1,0:T(8,128)(2,1)S(1)}, u32[]{:S(2)}, u32[]{:S(2)}) collective-permute-start(bf16[128,2048]{1,0:T(8,128)(2,1)S(1)} %get-tuple-element.171), channel_id=1, source_target_pairs={{0,3},{1,0},{2,1},{3,2},{4,7},{5,4},{6,5},{7,6},{8,11},{9,8},{10,9... | collective-permute-start | bytes 1572872 | tf_op jit(solution)/shard_map/ppermute | solution.py:41
  199.9 17.0 %collective-permute-start.27 = (bf16[2,256,2048]{2,1,0:T(8,128)(2,1)}, bf16[2,256,2048]{2,1,0:T(8,128)(2,1)}, u32[]{:S(2)}, u32[]{:S(2)}) collective-permute-start(bf16[2,256,2048]{2,1,0:T(8,128)(2,1)} %get-tuple-element.193.refs_1_), channel_id=1, source_target_pairs={{0,4},{4,0},{8,12},{12,8},{16,20},{20,16},{24,28},{28,24},{1,5},{5... | collective-permute-start | bytes 6291464 | tf_op jit(solution)/shard_map/ppermute | solution.py:45
  200.9 15.8 %collective-permute-start.20 = (bf16[128,2048]{1,0:T(8,128)(2,1)S(1)}, bf16[128,2048]{1,0:T(8,128)(2,1)S(1)}, u32[]{:S(2)}, u32[]{:S(2)}) collective-permute-start(bf16[128,2048]{1,0:T(8,128)(2,1)S(1)} %ring_sum.6), channel_id=1, source_target_pairs={{0,1},{1,2},{2,3},{3,0},{4,5},{5,6},{6,7},{7,4},{8,9},{9,10},{10,1... | collective-permute-start | bytes 1572872 | tf_op jit(solution)/shard_map/ppermute | solution.py:41
  205.0 11.9 %collective-permute-start.26 = (bf16[512,1024]{1,0:T(8,128)(2,1)}, bf16[512,1024]{1,0:T(8,128)(2,1)S(1)}, u32[]{:S(2)}, u32[]{:S(2)}) collective-permute-start(bf16[512,1024]{1,0:T(8,128)(2,1)} %get-tuple-element.190), channel_id=1, source_target_pairs={{0,4},{4,0},{8,12},{12,8},{16,20},{20,16},{24,28},{28,24},{1,5},{5... | collective-permute-start | bytes 3145736 | tf_op jit(solution)/shard_map/ppermute | solution.py:45
  213.9 25.9 %collective-permute-start.28 = (bf16[2,1024,256]{2,1,0:T(8,128)(2,1)}, bf16[2,1024,256]{2,1,0:T(8,128)(2,1)}, u32[]{:S(2)}, u32[]{:S(2)}) collective-permute-start(bf16[2,1024,256]{2,1,0:T(8,128)(2,1)} %get-tuple-element.186), channel_id=1, source_target_pairs={{0,8},{4,12},{8,0},{12,4},{16,24},{20,28},{24,16},{28,20},{1,9},{5... | collective-permute-start | bytes 3145736 | tf_op jit(solution)/shard_map/ppermute | solution.py:45
  214.3 25.6 %collective-permute-start.29 = (bf16[2,1024,256]{2,1,0:T(8,128)(2,1)}, bf16[2,1024,256]{2,1,0:T(8,128)(2,1)}, u32[]{:S(2)}, u32[]{:S(2)}) collective-permute-start(bf16[2,1024,256]{2,1,0:T(8,128)(2,1)} %get-tuple-element.194), channel_id=1, source_target_pairs={{0,16},{4,20},{8,24},{12,28},{16,0},{20,4},{24,8},{28,12},{1,17},{... | collective-permute-start | bytes 3145736 | tf_op jit(solution)/shard_map/ppermute | solution.py:45
  216.8 15.9 %collective-permute-start.25 = (bf16[128,2048]{1,0:T(8,128)(2,1)S(1)}, bf16[128,2048]{1,0:T(8,128)(2,1)S(1)}, u32[]{:S(2)}, u32[]{:S(2)}) collective-permute-start(bf16[128,2048]{1,0:T(8,128)(2,1)S(1)} %ring_sum.7), channel_id=1, source_target_pairs={{0,1},{1,2},{2,3},{3,0},{4,5},{5,6},{6,7},{7,4},{8,9},{9,10},{10,1... | collective-permute-start | bytes 1572872 | tf_op jit(solution)/shard_map/ppermute | solution.py:41
  240.9 13.5 %collective-permute-start.30 = (bf16[128,2048]{1,0:T(8,128)(2,1)S(1)}, bf16[128,2048]{1,0:T(8,128)(2,1)S(1)}, u32[]{:S(2)}, u32[]{:S(2)}) collective-permute-start(bf16[128,2048]{1,0:T(8,128)(2,1)S(1)} %copy-done.33), channel_id=1, source_target_pairs={{0,3},{1,0},{2,1},{3,2},{4,7},{5,4},{6,5},{7,6},{8,11},{9,8},{10,9... | collective-permute-start | bytes 1572872 | tf_op jit(solution)/shard_map/ppermute | solution.py:41
  258.7 9.7 %collective-permute-start.32 = (bf16[128,512]{1,0:T(8,128)(2,1)}, bf16[128,512]{1,0:T(8,128)(2,1)S(1)}, u32[]{:S(2)}, u32[]{:S(2)}) collective-permute-start(bf16[128,512]{1,0:T(8,128)(2,1)} %get-tuple-element.204), channel_id=1, source_target_pairs={{0,2},{1,3},{2,0},{3,1},{4,6},{5,7},{6,4},{7,5},{8,10},{9,11},{10,... | collective-permute-start | bytes 393224 | tf_op jit(solution)/shard_map/ppermute | solution.py:41
  258.7 9.7 %collective-permute-start.31 = (bf16[128,512]{1,0:T(8,128)(2,1)}, bf16[128,512]{1,0:T(8,128)(2,1)S(1)}, u32[]{:S(2)}, u32[]{:S(2)}) collective-permute-start(bf16[128,512]{1,0:T(8,128)(2,1)} %get-tuple-element.202), channel_id=1, source_target_pairs={{0,1},{1,2},{2,3},{3,0},{4,5},{5,6},{6,7},{7,4},{8,9},{9,10},{10,1... | collective-permute-start | bytes 393224 | tf_op jit(solution)/shard_map/ppermute | solution.py:41
  261.5 9.9 %collective-permute-start.37 = (bf16[128,256]{1,0:T(8,128)(2,1)S(1)}, bf16[128,256]{1,0:T(8,128)(2,1)S(1)}, u32[]{:S(2)}, u32[]{:S(2)}) collective-permute-start(bf16[128,256]{1,0:T(8,128)(2,1)S(1)} %get-tuple-element.220), channel_id=1, source_target_pairs={{0,4},{4,0},{8,12},{12,8},{16,20},{20,16},{24,28},{28,24},{1,5},{5... | collective-permute-start | bytes 196616 | tf_op jit(solution)/shard_map/ppermute | solution.py:45
  261.5 10.2 %collective-permute-start.38 = (bf16[128,256]{1,0:T(8,128)(2,1)S(1)}, bf16[128,256]{1,0:T(8,128)(2,1)S(1)}, u32[]{:S(2)}, u32[]{:S(2)}) collective-permute-start(bf16[128,256]{1,0:T(8,128)(2,1)S(1)} %get-tuple-element.221), channel_id=1, source_target_pairs={{0,8},{4,12},{8,0},{12,4},{16,24},{20,28},{24,16},{28,20},{1,9},{5... | collective-permute-start | bytes 196616 | tf_op jit(solution)/shard_map/ppermute | solution.py:45
  268.4 30.7 %collective-permute-start.34 = (bf16[128,2048]{1,0:T(8,128)(2,1)S(1)}, bf16[128,2048]{1,0:T(8,128)(2,1)}, u32[]{:S(2)}, u32[]{:S(2)}) collective-permute-start(bf16[128,2048]{1,0:T(8,128)(2,1)S(1)} %collective-permute-done.30), channel_id=1, source_target_pairs={{0,3},{1,0},{2,1},{3,2},{4,7},{5,4},{6,5},{7,6},{8,11},{9,8},{10,9... | collective-permute-start | bytes 1572872 | tf_op jit(solution)/shard_map/ppermute | solution.py:41
  270.7 28.4 %collective-permute-start.35 = (bf16[128,2048]{1,0:T(8,128)(2,1)S(1)}, bf16[128,2048]{1,0:T(8,128)(2,1)}, u32[]{:S(2)}, u32[]{:S(2)}) collective-permute-start(bf16[128,2048]{1,0:T(8,128)(2,1)S(1)} %get-tuple-element.209), channel_id=1, source_target_pairs={{0,1},{1,2},{2,3},{3,0},{4,5},{5,6},{6,7},{7,4},{8,9},{9,10},{10,1... | collective-permute-start | bytes 1572872 | tf_op jit(solution)/shard_map/ppermute | solution.py:41
  301.6 17.0 %collective-permute-start.44 = (bf16[128,2048]{1,0:T(8,128)(2,1)}, bf16[128,2048]{1,0:T(8,128)(2,1)S(1)}, u32[]{:S(2)}, u32[]{:S(2)}) collective-permute-start(bf16[128,2048]{1,0:T(8,128)(2,1)} %get-tuple-element.230), channel_id=1, source_target_pairs={{0,1},{1,2},{2,3},{3,0},{4,5},{5,6},{6,7},{7,4},{8,9},{9,10},{10,1... | collective-permute-start | bytes 1572872 | tf_op jit(solution)/shard_map/ppermute | solution.py:41
  306.1 11.8 %collective-permute-start.46 = (f32[5632]{0:T(1024)S(1)}, f32[5632]{0:T(1024)S(1)}, u32[]{:S(2)}, u32[]{:S(2)}) collective-permute-start(f32[5632]{0:T(1024)S(1)} %add.226), channel_id=1, source_target_pairs={{0,8},{4,12},{8,0},{12,4},{16,24},{20,28},{24,16},{28,20},{1,9},{5... | collective-permute-start | bytes 67592 | tf_op jit(solution)/shard_map/ppermute | solution.py:45
  318.0 29.1 %collective-permute-start.53 = (bf16[2,256,768]{2,1,0:T(8,128)(2,1)}, bf16[2,256,768]{2,1,0:T(8,128)(2,1)S(1)}, u32[]{:S(2)}, u32[]{:S(2)}) collective-permute-start(bf16[2,256,768]{2,1,0:T(8,128)(2,1)} %get-tuple-element.260), channel_id=1, source_target_pairs={{0,16},{4,20},{8,24},{12,28},{16,0},{20,4},{24,8},{28,12},{1,17},{... | collective-permute-start | bytes 2359304 | tf_op jit(solution)/shard_map/ppermute | solution.py:45
  318.0 30.4 %collective-permute-start.52 = (bf16[2,256,768]{2,1,0:T(8,128)(2,1)}, bf16[2,256,768]{2,1,0:T(8,128)(2,1)S(1)}, u32[]{:S(2)}, u32[]{:S(2)}) collective-permute-start(bf16[2,256,768]{2,1,0:T(8,128)(2,1)} %get-tuple-element.257), channel_id=1, source_target_pairs={{0,8},{4,12},{8,0},{12,4},{16,24},{20,28},{24,16},{28,20},{1,9},{5... | collective-permute-start | bytes 2359304 | tf_op jit(solution)/shard_map/ppermute | solution.py:45
  318.8 21.0 %collective-permute-start.49 = (bf16[128,2048]{1,0:T(8,128)(2,1)S(1)}, bf16[128,2048]{1,0:T(8,128)(2,1)S(1)}, u32[]{:S(2)}, u32[]{:S(2)}) collective-permute-start(bf16[128,2048]{1,0:T(8,128)(2,1)S(1)} %ring_sum.8), channel_id=1, source_target_pairs={{0,1},{1,2},{2,3},{3,0},{4,5},{5,6},{6,7},{7,4},{8,9},{9,10},{10,1... | collective-permute-start | bytes 1572872 | tf_op jit(solution)/shard_map/ppermute | solution.py:41
  327.2 12.6 %collective-permute-start.50 = (bf16[512,256]{1,0:T(8,128)(2,1)S(1)}, bf16[512,256]{1,0:T(8,128)(2,1)S(1)}, u32[]{:S(2)}, u32[]{:S(2)}) collective-permute-start(bf16[512,256]{1,0:T(8,128)(2,1)S(1)} %get-tuple-element.282), channel_id=1, source_target_pairs={{0,1},{1,2},{2,3},{3,0},{4,5},{5,6},{6,7},{7,4},{8,9},{9,10},{10,1... | collective-permute-start | bytes 786440 | tf_op jit(solution)/shard_map/ppermute | solution.py:41
  330.1 31.9 %collective-permute-start.54 = (f32[5632]{0:T(1024)S(1)}, f32[5632]{0:T(1024)S(1)}, u32[]{:S(2)}, u32[]{:S(2)}) collective-permute-start(f32[5632]{0:T(1024)S(1)} %add.227), channel_id=1, source_target_pairs={{0,16},{4,20},{8,24},{12,28},{16,0},{20,4},{24,8},{28,12},{1,17},{... | collective-permute-start | bytes 67592 | tf_op jit(solution)/shard_map/ppermute | solution.py:45
  339.9 23.4 %collective-permute-start.51 = (bf16[128,2048]{1,0:T(8,128)(2,1)S(1)}, bf16[128,2048]{1,0:T(8,128)(2,1)S(1)}, u32[]{:S(2)}, u32[]{:S(2)}) collective-permute-start(bf16[128,2048]{1,0:T(8,128)(2,1)S(1)} %ring_sum.9), channel_id=1, source_target_pairs={{0,1},{1,2},{2,3},{3,0},{4,5},{5,6},{6,7},{7,4},{8,9},{9,10},{10,1... | collective-permute-start | bytes 1572872 | tf_op jit(solution)/shard_map/ppermute | solution.py:41
  340.1 19.9 %collective-permute-start.55 = (bf16[512,256]{1,0:T(8,128)(2,1)S(1)}, bf16[512,256]{1,0:T(8,128)(2,1)S(1)}, u32[]{:S(2)}, u32[]{:S(2)}) collective-permute-start(bf16[512,256]{1,0:T(8,128)(2,1)S(1)} %ring_sum.10), channel_id=1, source_target_pairs={{0,1},{1,2},{2,3},{3,0},{4,5},{5,6},{6,7},{7,4},{8,9},{9,10},{10,1... | collective-permute-start | bytes 786440 | tf_op jit(solution)/shard_map/ppermute | solution.py:41
  347.0 16.9 %collective-permute-start.58 = (bf16[1,1024,256]{2,1,0:T(8,128)(2,1)}, bf16[1,1024,256]{2,1,0:T(8,128)(2,1)}, u32[]{:S(2)}, u32[]{:S(2)}) collective-permute-start(bf16[1,1024,256]{2,1,0:T(8,128)(2,1)} %get-tuple-element.272), channel_id=1, source_target_pairs={{0,8},{4,12},{8,0},{12,4},{16,24},{20,28},{24,16},{28,20},{1,9},{5... | collective-permute-start | bytes 1572872 | tf_op jit(solution)/shard_map/ppermute | solution.py:45
  348.4 17.5 %collective-permute-start.57 = (bf16[1,1024,256]{2,1,0:T(8,128)(2,1)}, bf16[1,1024,256]{2,1,0:T(8,128)(2,1)}, u32[]{:S(2)}, u32[]{:S(2)}) collective-permute-start(bf16[1,1024,256]{2,1,0:T(8,128)(2,1)} %get-tuple-element.270), channel_id=1, source_target_pairs={{0,16},{4,20},{8,24},{12,28},{16,0},{20,4},{24,8},{28,12},{1,17},{... | collective-permute-start | bytes 1572872 | tf_op jit(solution)/shard_map/ppermute | solution.py:45
  360.0 12.3 %collective-permute-start.60 = (bf16[1,256,768]{2,1,0:T(8,128)(2,1)S(1)}, bf16[1,256,768]{2,1,0:T(8,128)(2,1)S(1)}, u32[]{:S(2)}, u32[]{:S(2)}) collective-permute-start(bf16[1,256,768]{2,1,0:T(8,128)(2,1)S(1)} %copy-done.64), channel_id=1, source_target_pairs={{0,16},{4,20},{8,24},{12,28},{16,0},{20,4},{24,8},{28,12},{1,17},{... | collective-permute-start | bytes 1179656 | tf_op jit(solution)/shard_map/ppermute | solution.py:45
  362.0 10.3 %collective-permute-start.61 = (bf16[1,256,768]{2,1,0:T(8,128)(2,1)S(1)}, bf16[1,256,768]{2,1,0:T(8,128)(2,1)S(1)}, u32[]{:S(2)}, u32[]{:S(2)}) collective-permute-start(bf16[1,256,768]{2,1,0:T(8,128)(2,1)S(1)} %copy-done.63), channel_id=1, source_target_pairs={{0,8},{4,12},{8,0},{12,4},{16,24},{20,28},{24,16},{28,20},{1,9},{5... | collective-permute-start | bytes 1179656 | tf_op jit(solution)/shard_map/ppermute | solution.py:45
  363.9 12.0 %collective-permute-start.62 = (bf16[512,256]{1,0:T(8,128)(2,1)S(1)}, bf16[512,256]{1,0:T(8,128)(2,1)S(1)}, u32[]{:S(2)}, u32[]{:S(2)}) collective-permute-start(bf16[512,256]{1,0:T(8,128)(2,1)S(1)} %ring_sum.11), channel_id=1, source_target_pairs={{0,1},{1,2},{2,3},{3,0},{4,5},{5,6},{6,7},{7,4},{8,9},{9,10},{10,1... | collective-permute-start | bytes 786440 | tf_op jit(solution)/shard_map/ppermute | solution.py:41
  (83 other events, 736.0 us)
Sparse Core Ops, SparseCore 0:
  60.5 47.0 all-gather.2
  145.1 34.2 all-gather.4
  240.0 101.2 reduce-scatter.1

commit v6 on v5

--- a/solution.py
+++ b/solution.py
@@ -1185,17 +1185,17 @@
     hidden_b_rec = swapped(hidden_b, "seq", 1)
     pair_b_rec = swapped(after(pair_b, hidden_b_rec), "seq", 1)
     run = turned(total, "chan", 1)
-    normed_two_slices = own_slices(
-        [normed_two_own, n_one, n_two, after(n_three, total)], None, False
-    )
     down = Joined(
-        (after(cot_slices[0], normed_two_slices[0]), cot_slices[1]),
+        (after(cot_slices[0], total), cot_slices[1]),
         ([hidden_a, hidden_b], [hidden_a_rec, hidden_b_rec]),
         orders,
         part,
         tall=True,
     )
-    total = ring_sum(after(run, down.made), grad_two_parts[3])
+    normed_two_slices = own_slices(
+        [normed_two_own, n_one, n_two, after(n_three, down.made)], None, False
+    )
+    total = ring_sum(after(run, normed_two_slices[0]), grad_two_parts[3])
     down.send()
     run = turned(total, "chan", 1)
     gate_up = whole_product(
@@ -1237,10 +1237,9 @@
         ]
     )
     rim_back = passed_along(at_edge(heads, 0), "seq", -1)
-    rim_back = after(rim_back, *mixes)
     behind = jnp.where(is_owner(chan_count - 1), rim_back[None], jnp.roll(heads, 1, axis=0))
     grad_triple, tap_part = conv_backward(
-        gg, *projected, conv_out, mixed_in, before, behind.astype(F32), conv_taps, masks
+        gg, *projected, conv_out, mixed_in, before, after(behind.astype(F32), *mixes), conv_taps, masks
     )
     grad_one_parts, gain_one_part = mixer_back(grad_triple, in_weight, tok_blocks, scale_all)
     grad_one_parts = [after(rows, ffn_two, ffn_three) for rows in grad_one_parts]

time: 386 us -> 383 us (level)
  waiting for transfers between devices: 116 us -> 111 us
    unnamed x130 -> x138, local copies, waits for them, and re-layouts: 15 us -> 16.4 us
where the time goes in v6:
time: 383 us; the launch traced here: 382 us
  Pallas kernels  143 us (37%)
  waiting for transfers between devices  111 us (29%)
  starting transfers between devices  72.1 us (19%)
  local copies, waits for them, and re-layouts  23.3 us (6%)
  other arithmetic  17.1 us (4%)
  between operations  14.6 us (4%)
    ppermute x28, waiting for transfers between devices, turned(): lax.ppermute(block, axis, [(i, (i + distance) % count) for i in range(cou...  78.1 us
    pallas_call x2, Pallas kernels, feed_forward(): pl.pallas_call(functools.partial(ffn_body, count), grid_spec=pltpu.Prefet...  41.9 us
    ppermute x28, starting transfers between devices, turned(): lax.ppermute(block, axis, [(i, (i + distance) % count) for i in range(cou...  39.2 us
    ppermute x33, starting transfers between devices, swapped(): lax.ppermute(block, axis, [(i, i ^ bit) for i in range(lax.axis_size(axis...  28.8 us
    ppermute x33, waiting for transfers between devices, swapped(): lax.ppermute(block, axis, [(i, i ^ bit) for i in range(lax.axis_size(axis...  24.5 us
    pallas_call x2, Pallas kernels, __init__(): pl.pallas_call(functools.partial(product_body, slots, part, tiles, tall,...  17.7 us
    unnamed x138, local copies, waits for them, and re-layouts  16.4 us
    pallas_call x1, Pallas kernels, whole_product(): pl.pallas_call(functools.partial(whole_body, part, len(units[0])), grid=(...  14.9 us
  transfers between devices with their start and end apart: 66, of which 24 were waited for; matrix products, arithmetic and copies ran while one was open for 6% of the time, Pallas kernels for 36%

profile of v6, /device:TPU:0, one launch (start us, length us, event | category | flops | bytes accessed | tf_op | source)
XLA Modules:
  0.0 381.7 jit_solution(10323585796159237946)
XLA Ops:
  7.2 3.1 collective-permute-start.2
  11.3 2.1 collective-permute-start.1
  13.4 17.5 %collective-permute-done.1 = bf16[512,256]{1,0:T(8,128)(2,1)S(1)} collective-permute-done((bf16[512,256]{1,0:T(8,128)(2,1)S(1)}, bf16[512,256]{1,0:T(8,128)(2,1)S(1)}, u32[]{:S(2)}, u32[]{:S(2)}) %collective-permute-start.1) | collective-permute-done | bytes 262176 | tf_op jit(solution)/shard_map/ppermute | solution.py:41
  30.9 4.9 %collective-permute-done = bf16[512,256]{1,0:T(8,128)(2,1)S(1)} collective-permute-done((bf16[512,256]{1,0:T(8,128)(2,1)S(1)}, bf16[512,256]{1,0:T(8,128)(2,1)S(1)}, u32[]{:S(2)}, u32[]{:S(2)}) %collective-permute-start) | collective-permute-done | bytes 262176 | tf_op jit(solution)/shard_map/ppermute | solution.py:41
  35.7 3.8 %collective-permute-start.5 = (bf16[128,2048]{1,0:T(8,128)(2,1)}, bf16[128,2048]{1,0:T(8,128)(2,1)S(1)}, u32[]{:S(2)}, u32[]{:S(2)}) collective-permute-start(bf16[128,2048]{1,0:T(8,128)(2,1)} %refs_2_.1), channel_id=1, source_target_pairs={{0,3},{1,0},{2,1},{3,2},{4,7},{5,4},{6,5},{7,6},{8,11},{9,8},{10,9... | collective-permute-start | bytes 1572872 | tf_op jit(solution)/shard_map/ppermute | solution.py:41
  39.6 7.2 %collective-permute-done.3 = bf16[512,256]{1,0:T(8,128)(2,1)S(1)} collective-permute-done((bf16[512,256]{1,0:T(8,128)(2,1)S(1)}, bf16[512,256]{1,0:T(8,128)(2,1)S(1)}, u32[]{:S(2)}, u32[]{:S(2)}) %collective-permute-start.3) | collective-permute-done | bytes 262176 | tf_op jit(solution)/shard_map/ppermute | solution.py:41
  50.0 4.7 %collective-permute-done.5.refs_3_.refs_5_ = bf16[128,2048]{1,0:T(8,128)(2,1)S(1)} collective-permute-done((bf16[128,2048]{1,0:T(8,128)(2,1)}, bf16[128,2048]{1,0:T(8,128)(2,1)S(1)}, u32[]{:S(2)}, u32[]{:S(2)}) %collective-permute-start.5) | collective-permute-done | bytes 524320 | tf_op jit(solution)/shard_map/ppermute | solution.py:41
  60.4 15.1 %collective-permute-done.7.refs_2_.refs_4_ = bf16[128,2048]{1,0:T(8,128)(2,1)S(1)} collective-permute-done((bf16[128,2048]{1,0:T(8,128)(2,1)S(1)}, bf16[128,2048]{1,0:T(8,128)(2,1)S(1)}, u32[]{:S(2)}, u32[]{:S(2)}) %collective-permute-start.7) | collective-permute-done | bytes 524320 | tf_op jit(solution)/shard_map/ppermute | solution.py:41
  77.2 2.9 pad_maximum_fusion.refs_5_.refs_1_
  82.7 8.7 %in_projection.1 = (f32[512,512]{1,0:T(8,128)}, f32[512,512]{1,0:T(8,128)}, f32[512,512]{1,0:T(8,128)}, bf16[512,512]{1,0:T(8,128)(2,1)}, bf16[512,2048]{1,0:T(8,128)(2,1)}, /*index=5*/f32[512,1]{1,0:T(8,128)}) custom-call(bf16[128,2048]{1,0:T(8,128)(2,1)} %refs_2_.1, bf16[128,2048]{1,0:T(8,128)(2,1)} %copy-done.39, bf16[128,2048]{1,0:T(8,128)(2,1)} %copy-done.41, ...), custom_call_target="tpu_custom_call" | custom-call | flops 1024 | bytes 1024 | tf_op jit(solution)/shard_map/in_projection/pallas_call | solution.py:677
  92.3 2.4 collective-permute-start.10
  96.2 2.9 conv_forward.1
  99.1 8.4 %all-gather.3.cloned.1.call-done.refs_0_.refs_2_.refs_3_ = bf16[512,2048]{1,0:T(8,128)(2,1)} async-done(((bf16[128,2048]{1,0:T(8,128)(2,1)}), bf16[512,2048]{1,0:T(8,128)(2,1)}) %all-gather.3.cloned.1.call-update) | async-done | bytes 2097168 | tf_op jit(solution)/shard_map/all_gather | solution.py:1095
  109.0 2.4 collective-permute-start.11
  111.5 4.6 %collective-permute-done.13.refs_3_ = bf16[128,512]{1,0:T(8,128)(2,1)S(1)} collective-permute-done((bf16[128,512]{1,0:T(8,128)(2,1)}, bf16[128,512]{1,0:T(8,128)(2,1)S(1)}, u32[]{:S(2)}, u32[]{:S(2)}) %collective-permute-start.13) | collective-permute-done | bytes 131104 | tf_op jit(solution)/shard_map/ppermute | solution.py:41
  116.1 4.6 %collective-permute-done.12.refs_2_ = bf16[128,512]{1,0:T(8,128)(2,1)S(1)} collective-permute-done((bf16[128,512]{1,0:T(8,128)(2,1)}, bf16[128,512]{1,0:T(8,128)(2,1)S(1)}, u32[]{:S(2)}, u32[]{:S(2)}) %collective-permute-start.12) | collective-permute-done | bytes 131104 | tf_op jit(solution)/shard_map/ppermute | solution.py:41
  123.2 6.1 %mixer_rows.1 = (f32[128,2048]{1,0:T(8,128)S(1)}, bf16[128,2048]{1,0:T(8,128)(2,1)S(1)}, f32[128,1]{1,0:T(8,128)S(1)}, bf16[128,2048]{1,0:T(8,128)(2,1)}) custom-call(s32[5]{0:T(128)S(1)} %pad_add_fusion.ids, bf16[128,512]{1,0:T(8,128)(2,1)S(1)} %copy-done.24, bf16[128,512]{1,0:T(8,128)(2,1)S(1)} %collective-permute-done.11.refs_1_, ...), custom_call_target="tpu_custom_call" | custom-call | flops 1024 | bytes 1024 | tf_op jit(solution)/shard_map/mixer_rows/pallas_call | solution.py:917
  130.9 2.5 collective-permute-start.15
  139.2 5.8 %collective-permute-done.15.refs_1_ = bf16[128,2048]{1,0:T(8,128)(2,1)S(1)} collective-permute-done((bf16[128,2048]{1,0:T(8,128)(2,1)S(1)}, bf16[128,2048]{1,0:T(8,128)(2,1)S(1)}, u32[]{:S(2)}, u32[]{:S(2)}) %collective-permute-start.15) | collective-permute-done | bytes 524320 | tf_op jit(solution)/shard_map/ppermute | solution.py:41
  145.1 1.8 collective-permute-start.17
  147.2 21.1 %feed_forward.2 = (bf16[1,256,2048]{2,1,0:T(8,128)(2,1)S(1)}, bf16[2,256,2048]{2,1,0:T(8,128)(2,1)}, bf16[128,2048]{1,0:T(8,128)(2,1)S(1)}, bf16[128,2048]{1,0:T...) custom-call(s32[4]{0:T(128)S(1)} %and_select_fusion.ids, ...), custom_call_target="tpu_custom_call" | custom-call | flops 1024 | bytes 1024 | tf_op jit(solution)/shard_map/feed_forward/pallas_call | solution.py:141
  171.8 2.5 collective-permute-start.18
  174.3 20.8 %feed_forward.3 = (bf16[1,256,2048]{2,1,0:T(8,128)(2,1)S(1)}, bf16[2,256,2048]{2,1,0:T(8,128)(2,1)}, bf16[128,2048]{1,0:T(8,128)(2,1)S(1)}, bf16[128,2048]{1,0:T...) custom-call(s32[4]{0:T(128)S(1)} %and_select_fusion.ids, ...), custom_call_target="tpu_custom_call" | custom-call | flops 1024 | bytes 1024 | tf_op jit(solution)/shard_map/feed_forward/pallas_call | solution.py:141
  197.3 2.8 collective-permute-done.24.refs_5_
  201.6 8.9 %product.2 = (bf16[2,1024,256]{2,1,0:T(8,128)(2,1)}, bf16[2,1024,256]{2,1,0:T(8,128)(2,1)}, bf16[2,1024,256]{2,1,0:T(8,128)(2,1)}, bf16[2,1024,256]{2,1,0:T(8,128)(2,1)}) custom-call(bf16[512,1024]{1,0:T(8,128)(2,1)} %copy-done.15, bf16[512,1024]{1,0:T(8,128)(2,1)} %collective-permute-done.21.refs_1_, bf16[1,256,2048]{2,1,0:T(8,128)(2,1)} %copy-done.16, ...), custom_call_target="tpu_custom_call" | custom-call | flops 1024 | bytes 1024 | tf_op jit(solution)/shard_map/product/pallas_call | solution.py:337
  213.1 3.1 collective-permute-done.20.a
  217.5 14.9 %whole_product.1 = bf16[4,2,256,2048]{3,2,1,0:T(8,128)(2,1)} custom-call(bf16[512,1024]{1,0:T(8,128)(2,1)} %copy-done.14, bf16[512,1024]{1,0:T(8,128)(2,1)} %copy-done.44, bf16[2,256,2048]{2,1,0:T(8,128)(2,1)} %get-tuple-element.182.refs_0_, bf16[2,256,2048]{2,1,0:T(8,128)(2,1)} %get-tuple-element.193.refs_1_, bf16[2,256,2048]{2,1,0:T(8,128)(2,1)} %copy-done.38, ...), custom_call_target="tpu_custom_call" | custom-call | flops 1024 | bytes 1024 | tf_op jit(solution)/shard_map/whole_product/pallas_call | solution.py:416
  232.4 5.8 %collective-permute-done.28.refs_1_ = bf16[2,1024,256]{2,1,0:T(8,128)(2,1)} collective-permute-done((bf16[2,1024,256]{2,1,0:T(8,128)(2,1)}, bf16[2,1024,256]{2,1,0:T(8,128)(2,1)}, u32[]{:S(2)}, u32[]{:S(2)}) %collective-permute-start.28) | collective-permute-done | bytes 1048608 | tf_op jit(solution)/shard_map/ppermute | solution.py:45
  239.3 2.5 collective-permute-start.30
  241.9 10.3 %gated_rows.1 = (bf16[128,512]{1,0:T(8,128)(2,1)}, bf16[128,512]{1,0:T(8,128)(2,1)}, bf16[128,512]{1,0:T(8,128)(2,1)}, bf16[128,512]{1,0:T(8,128)(2,1)}, f32[128...) custom-call(s32[5]{0:T(128)} %copy-done.28, bf16[512,2048]{1,0:T(8,128)(2,1)} %refs_0_.2, ...), custom_call_target="tpu_custom_call" | custom-call | flops 1024 | bytes 1024 | tf_op jit(solution)/shard_map/gated_rows/pallas_call | solution.py:1006
  252.8 4.3 %collective-permute-start.33 = (bf16[128,512]{1,0:T(8,128)(2,1)}, bf16[128,512]{1,0:T(8,128)(2,1)S(1)}, u32[]{:S(2)}, u32[]{:S(2)}) collective-permute-start(bf16[128,512]{1,0:T(8,128)(2,1)} %get-tuple-element.206), channel_id=1, source_target_pairs={{0,3},{1,0},{2,1},{3,2},{4,7},{5,4},{6,5},{7,6},{8,11},{9,8},{10,9... | collective-permute-start | bytes 393224 | tf_op jit(solution)/shard_map/ppermute | solution.py:41
  261.8 5.0 %collective-permute-done.32.refs_2_ = bf16[128,512]{1,0:T(8,128)(2,1)S(1)} collective-permute-done((bf16[128,512]{1,0:T(8,128)(2,1)}, bf16[128,512]{1,0:T(8,128)(2,1)S(1)}, u32[]{:S(2)}, u32[]{:S(2)}) %collective-permute-start.32) | collective-permute-done | bytes 131104 | tf_op jit(solution)/shard_map/ppermute | solution.py:41
  266.8 2.3 collective-permute-start.34
  271.7 2.6 collective-permute-start.41
  277.3 1.8 collective-permute-done.41.refs_5_
  279.1 3.7 collective-permute-done.42.refs_6_
  283.2 5.6 %conv_backward.1 = (bf16[3,512,512]{2,1,0:T(8,128)(2,1)}, f32[3,512]{1,0:T(4,128)}) custom-call(bf16[128,512]{1,0:T(8,128)(2,1)} %get-tuple-element.200.refs_0_, bf16[128,512]{1,0:T(8,128)(2,1)} %copy-done.55, bf16[128,512]{1,0:T(8,128)(2,1)} %copy-done.54, bf16[128,512]{1,0:T(8,128)(2,1)} %copy-done.53, f32[512,512]{1,0:T(8,128)} %get-tuple-element.214.refs_4_, ...), custom_call_target="tpu_custom_call" | custom-call | flops 1024 | bytes 1024 | tf_op jit(solution)/shard_map/conv_backward/pallas_call | solution.py:790
  288.9 7.9 %mixer_back.1 = (bf16[128,2048]{1,0:T(8,128)(2,1)}, bf16[128,2048]{1,0:T(8,128)(2,1)}, bf16[128,2048]{1,0:T(8,128)(2,1)}, bf16[128,2048]{1,0:T(8,128)(2,1)}, f32[1,2048]{1,0:T(1,128)}) custom-call(bf16[3,512,512]{2,1,0:T(8,128)(2,1)} %get-tuple-element.237.refs_0_.refs_2_, bf16[3,2048,512]{2,1,0:T(8,128)(2,1)} %refs_1_.1, bf16[128,2048]{1,0:T(8,128)(2,1)} %refs_2_.1, ...), custom_call_target="tpu_custom_call" | custom-call | flops 1024 | bytes 1024 | tf_op jit(solution)/shard_map/mixer_back/pallas_call | solution.py:834
  305.2 8.8 %product.3 = (bf16[2,256,768]{2,1,0:T(8,128)(2,1)}, bf16[2,256,768]{2,1,0:T(8,128)(2,1)}, bf16[2,256,768]{2,1,0:T(8,128)(2,1)}, bf16[2,256,768]{2,1,0:T(8,128)(2,1)}) custom-call(bf16[512,1024]{1,0:T(8,128)(2,1)} %copy-done.13, bf16[512,1024]{1,0:T(8,128)(2,1)} %copy-done.43, bf16[3,512,512]{2,1,0:T(8,128)(2,1)} %get-tuple-element.237.refs_0_.refs_2_, ...), custom_call_target="tpu_custom_call" | custom-call | flops 1024 | bytes 1024 | tf_op jit(solution)/shard_map/product/pallas_call | solution.py:337
  317.7 5.9 %rows_product.1 = bf16[4,512,256]{2,1,0:T(8,128)(2,1)} custom-call(s32[8]{0:T(128)} %copy-done.29, bf16[1024,2048]{1,0:T(8,128)(2,1)} %all-gather.5.cloned.1.call-done.gated, bf16[128,256]{1,0:T(8,128)(2,1)} %copy-done.27, bf16[128,256]{1,0:T(8,128)(2,1)} %copy-done.57, bf16[128,256]{1,0:T(8,128)(2,1)} %copy-done.58, bf16[128,256]{1,0:T(8,128)(2,1)} %copy-done.59, ...), custom_call_target="tpu_custom_call" | custom-call | flops 1024 | bytes 1024 | tf_op jit(solution)/shard_map/rows_product/pallas_call | solution.py:603
  328.6 4.0 %upper_sums.2 = (bf16[1,1024,256]{2,1,0:T(8,128)(2,1)}, bf16[1,1024,256]{2,1,0:T(8,128)(2,1)}) custom-call(bf16[2,1024,256]{2,1,0:T(8,128)(2,1)} %get-tuple-element.269.refs_0_, bf16[2,1024,256]{2,1,0:T(8,128)(2,1)} %collective-permute-done.28.refs_1_, bf16[2,1024,256]{2,1,0:T(8,128)(2,1)} %get-tuple-element.248.refs_2_.refs_3_, ...), custom_call_target="tpu_custom_call" | custom-call | flops 1024 | bytes 1024 | tf_op jit(solution)/shard_map/upper_sums/pallas_call | solution.py:473
  332.6 4.4 %collective-permute-done.50.a = bf16[512,256]{1,0:T(8,128)(2,1)S(1)} collective-permute-done((bf16[512,256]{1,0:T(8,128)(2,1)S(1)}, bf16[512,256]{1,0:T(8,128)(2,1)S(1)}, u32[]{:S(2)}, u32[]{:S(2)}) %collective-permute-start.50) | collective-permute-done | bytes 262176 | tf_op jit(solution)/shard_map/ppermute | solution.py:41
  338.6 6.9 %collective-permute-done.53.refs_3_.refs_4_ = bf16[2,256,768]{2,1,0:T(8,128)(2,1)S(1)} collective-permute-done((bf16[2,256,768]{2,1,0:T(8,128)(2,1)}, bf16[2,256,768]{2,1,0:T(8,128)(2,1)S(1)}, u32[]{:S(2)}, u32[]{:S(2)}) %collective-permute-start.53) | collective-permute-done | bytes 786464 | tf_op jit(solution)/shard_map/ppermute | solution.py:45
  347.5 2.4 add_convert_fusion
  349.9 3.8 %upper_sums.3 = (bf16[1,256,768]{2,1,0:T(8,128)(2,1)}, bf16[1,256,768]{2,1,0:T(8,128)(2,1)}) custom-call(bf16[2,256,768]{2,1,0:T(8,128)(2,1)} %get-tuple-element.274.refs_0_, bf16[2,256,768]{2,1,0:T(8,128)(2,1)} %copy-done.10, bf16[2,256,768]{2,1,0:T(8,128)(2,1)} %get-tuple-element.258.refs_2_.refs_3_, bf16[2,256,768]{2,1,0:T(8,128)(2,1)} %copy-done.8), custom_call_target="tpu_custom_call" | custom-call | flops 1024 | bytes 1024 | tf_op jit(solution)/shard_map/upper_sums/pallas_call | solution.py:473
  353.7 3.8 final_sums.2
  362.3 4.4 %final_sums.3 = f32[2048,256]{1,0:T(8,128)} custom-call(bf16[2,1024,256]{2,1,0:T(8,128)(2,1)} %get-tuple-element.269.refs_0_, bf16[2,1024,256]{2,1,0:T(8,128)(2,1)} %collective-permute-done.28.refs_1_, bf16[1,1024,256]{2,1,0:T(8,128)(2,1)} %collective-permute-done.57.refs_2_, bf16[2,1024,256]{2,1,0:T(8,128)(2,1)} %get-tuple-element.248.refs_2_.refs_3_, ...), custom_call_target="tpu_custom_call" | custom-call | flops 1024 | bytes 1024 | tf_op jit(solution)/shard_map/final_sums/pallas_call | solution.py:516
  366.8 2.5 collective-permute-start.59
  (308 shorter events, 82.8 us)
Async XLA Ops:
  7.2 100.4 %all-gather.3.cloned.1.call-start = ((), (), s32[]{:S(2)}) async-start(), calls=%async_computation.1 | async-start | bytes 2621440 | tf_op jit(solution)/shard_map/all_gather | solution.py:1095
  7.2 28.5 %collective-permute-start.2 = (bf16[128,2048]{1,0:T(8,128)(2,1)}, bf16[128,2048]{1,0:T(8,128)(2,1)S(1)}, u32[]{:S(2)}, u32[]{:S(2)}) collective-permute-start(bf16[128,2048]{1,0:T(8,128)(2,1)} %refs_2_.1), channel_id=1, source_target_pairs={{0,1},{1,2},{2,3},{3,0},{4,5},{5,6},{6,7},{7,4},{8,9},{9,10},{10,1... | collective-permute-start | bytes 1572872 | tf_op jit(solution)/shard_map/ppermute | solution.py:41
  11.3 19.6 %collective-permute-start.1 = (bf16[512,256]{1,0:T(8,128)(2,1)S(1)}, bf16[512,256]{1,0:T(8,128)(2,1)S(1)}, u32[]{:S(2)}, u32[]{:S(2)}) collective-permute-start(bf16[512,256]{1,0:T(8,128)(2,1)S(1)} %constant_dynamic-slice_fusion), channel_id=1, source_target_pairs={{0,3},{1,0},{2,1},{3,2},{4,7},{5,4},{6,5},{7,6},{8,11},{9,8},{10,9... | collective-permute-start | bytes 786440 | tf_op jit(solution)/shard_map/ppermute | solution.py:41
  13.4 22.4 %collective-permute-start = (bf16[512,256]{1,0:T(8,128)(2,1)S(1)}, bf16[512,256]{1,0:T(8,128)(2,1)S(1)}, u32[]{:S(2)}, u32[]{:S(2)}) collective-permute-start(bf16[512,256]{1,0:T(8,128)(2,1)S(1)} %constant_dynamic-slice_fusion), channel_id=1, source_target_pairs={{0,1},{1,2},{2,3},{3,0},{4,5},{5,6},{6,7},{7,4},{8,9},{9,10},{10,1... | collective-permute-start | bytes 786440 | tf_op jit(solution)/shard_map/ppermute | solution.py:41
  35.7 11.0 %collective-permute-start.3 = (bf16[512,256]{1,0:T(8,128)(2,1)S(1)}, bf16[512,256]{1,0:T(8,128)(2,1)S(1)}, u32[]{:S(2)}, u32[]{:S(2)}) collective-permute-start(bf16[512,256]{1,0:T(8,128)(2,1)S(1)} %collective-permute-done), channel_id=1, source_target_pairs={{0,1},{1,2},{2,3},{3,0},{4,5},{5,6},{6,7},{7,4},{8,9},{9,10},{10,1... | collective-permute-start | bytes 786440 | tf_op jit(solution)/shard_map/ppermute | solution.py:41
  35.7 19.0 %collective-permute-start.5 = (bf16[128,2048]{1,0:T(8,128)(2,1)}, bf16[128,2048]{1,0:T(8,128)(2,1)S(1)}, u32[]{:S(2)}, u32[]{:S(2)}) collective-permute-start(bf16[128,2048]{1,0:T(8,128)(2,1)} %refs_2_.1), channel_id=1, source_target_pairs={{0,3},{1,0},{2,1},{3,2},{4,7},{5,4},{6,5},{7,6},{8,11},{9,8},{10,9... | collective-permute-start | bytes 1572872 | tf_op jit(solution)/shard_map/ppermute | solution.py:41
  55.8 19.8 %collective-permute-start.9 = (bf16[2,3,256,256]{3,2,1,0:T(8,128)(2,1)}, bf16[2,3,256,256]{3,2,1,0:T(8,128)(2,1)}, u32[]{:S(2)}, u32[]{:S(2)}) collective-permute-start(bf16[2,3,256,256]{3,2,1,0:T(8,128)(2,1)} %pad_maximum_fusion.3), channel_id=1, source_target_pairs={{0,8},{4,12},{8,0},{12,4},{16,24},{20,28},{24,16},{28,20},{1,9},{5... | collective-permute-start | bytes 2359304 | tf_op jit(solution)/shard_map/ppermute | solution.py:45
  58.2 19.0 %collective-permute-start.6 = (bf16[2,3,256,256]{3,2,1,0:T(8,128)(2,1)}, bf16[2,3,256,256]{3,2,1,0:T(8,128)(2,1)}, u32[]{:S(2)}, u32[]{:S(2)}) collective-permute-start(bf16[2,3,256,256]{3,2,1,0:T(8,128)(2,1)} %pad_maximum_fusion.2), channel_id=1, source_target_pairs={{0,16},{4,20},{8,24},{12,28},{16,0},{20,4},{24,8},{28,12},{1,17},{... | collective-permute-start | bytes 2359304 | tf_op jit(solution)/shard_map/ppermute | solution.py:45
  59.7 15.8 %collective-permute-start.7 = (bf16[128,2048]{1,0:T(8,128)(2,1)S(1)}, bf16[128,2048]{1,0:T(8,128)(2,1)S(1)}, u32[]{:S(2)}, u32[]{:S(2)}) collective-permute-start(bf16[128,2048]{1,0:T(8,128)(2,1)S(1)} %collective-permute-done.2.refs_1_.refs_3_), channel_id=1, source_target_pairs={{0,1},{1,2},{2,3},{3,0},{4,5},{5,6},{6,7},{7,4},{8,9},{9,10},{10,1... | collective-permute-start | bytes 1572872 | tf_op jit(solution)/shard_map/ppermute | solution.py:41
  60.4 177.9 %all-gather.5.cloned.1.call-start = ((), (), s32[]{:S(2)}) async-start(), calls=%async_computation.2 | async-start | bytes 4718592 | tf_op jit(solution)/shard_map/all_gather | solution.py:1144
  80.1 40.6 %collective-permute-start.14 = (bf16[4,3,512,256]{3,2,1,0:T(8,128)(2,1)}, bf16[4,3,512,256]{3,2,1,0:T(8,128)(2,1)}, u32[]{:S(2)}, u32[]{:S(2)}) collective-permute-start(bf16[4,3,512,256]{3,2,1,0:T(8,128)(2,1)} %pad_maximum_fusion.refs_5_.refs_1_), channel_id=1, source_target_pairs={{0,4},{4,0},{8,12},{12,8},{16,20},{20,16},{24,28},{28,24},{1,5},{5... | collective-permute-start | bytes 9437192 | tf_op jit(solution)/shard_map/ppermute | solution.py:45
  107.6 13.1 %collective-permute-start.12 = (bf16[128,512]{1,0:T(8,128)(2,1)}, bf16[128,512]{1,0:T(8,128)(2,1)S(1)}, u32[]{:S(2)}, u32[]{:S(2)}) collective-permute-start(bf16[128,512]{1,0:T(8,128)(2,1)} %get-tuple-element.158), channel_id=1, source_target_pairs={{0,2},{1,3},{2,0},{3,1},{4,6},{5,7},{6,4},{7,5},{8,10},{9,11},{10,... | collective-permute-start | bytes 393224 | tf_op jit(solution)/shard_map/ppermute | solution.py:41
  109.0 11.7 %collective-permute-start.11 = (bf16[128,512]{1,0:T(8,128)(2,1)}, bf16[128,512]{1,0:T(8,128)(2,1)S(1)}, u32[]{:S(2)}, u32[]{:S(2)}) collective-permute-start(bf16[128,512]{1,0:T(8,128)(2,1)} %get-tuple-element.156), channel_id=1, source_target_pairs={{0,3},{1,0},{2,1},{3,2},{4,7},{5,4},{6,5},{7,6},{8,11},{9,8},{10,9... | collective-permute-start | bytes 393224 | tf_op jit(solution)/shard_map/ppermute | solution.py:41
  130.9 14.1 %collective-permute-start.15 = (bf16[128,2048]{1,0:T(8,128)(2,1)S(1)}, bf16[128,2048]{1,0:T(8,128)(2,1)S(1)}, u32[]{:S(2)}, u32[]{:S(2)}) collective-permute-start(bf16[128,2048]{1,0:T(8,128)(2,1)S(1)} %get-tuple-element.170.refs_0_), channel_id=1, source_target_pairs={{0,1},{1,2},{2,3},{3,0},{4,5},{5,6},{6,7},{7,4},{8,9},{9,10},{10,1... | collective-permute-start | bytes 1572872 | tf_op jit(solution)/shard_map/ppermute | solution.py:41
  145.0 208.7 %reduce-scatter.2.cloned.1.call-start = ((), (), s32[]{:S(2)}) async-start(), calls=%async_computation.3 | async-start | bytes 10485760 | tf_op jit(solution)/shard_map/reduce_scatter | solution.py:435
  145.1 24.8 %collective-permute-start.17 = (bf16[128,2048]{1,0:T(8,128)(2,1)S(1)}, bf16[128,2048]{1,0:T(8,128)(2,1)S(1)}, u32[]{:S(2)}, u32[]{:S(2)}) collective-permute-start(bf16[128,2048]{1,0:T(8,128)(2,1)S(1)} %get-tuple-element.170.refs_0_), channel_id=1, source_target_pairs={{0,3},{1,0},{2,1},{3,2},{4,7},{5,4},{6,5},{7,6},{8,11},{9,8},{10,9... | collective-permute-start | bytes 1572872 | tf_op jit(solution)/shard_map/ppermute | solution.py:41
  146.9 23.0 %collective-permute-start.16 = (bf16[128,2048]{1,0:T(8,128)(2,1)S(1)}, bf16[128,2048]{1,0:T(8,128)(2,1)S(1)}, u32[]{:S(2)}, u32[]{:S(2)}) collective-permute-start(bf16[128,2048]{1,0:T(8,128)(2,1)S(1)} %collective-permute-done.15.refs_1_), channel_id=1, source_target_pairs={{0,1},{1,2},{2,3},{3,0},{4,5},{5,6},{6,7},{7,4},{8,9},{9,10},{10,1... | collective-permute-start | bytes 1572872 | tf_op jit(solution)/shard_map/ppermute | solution.py:41
  169.9 26.8 %collective-permute-start.23 = (bf16[2,256,2048]{2,1,0:T(8,128)(2,1)}, bf16[2,256,2048]{2,1,0:T(8,128)(2,1)S(1)}, u32[]{:S(2)}, u32[]{:S(2)}) collective-permute-start(bf16[2,256,2048]{2,1,0:T(8,128)(2,1)} %get-tuple-element.182.refs_0_), channel_id=1, source_target_pairs={{0,4},{4,0},{8,12},{12,8},{16,20},{20,16},{24,28},{28,24},{1,5},{5... | collective-permute-start | bytes 6291464 | tf_op jit(solution)/shard_map/ppermute | solution.py:45
  169.9 26.7 %collective-permute-start.22 = (bf16[1,256,2048]{2,1,0:T(8,128)(2,1)S(1)}, bf16[1,256,2048]{2,1,0:T(8,128)(2,1)S(1)}, u32[]{:S(2)}, u32[]{:S(2)}) collective-permute-start(bf16[1,256,2048]{2,1,0:T(8,128)(2,1)S(1)} %get-tuple-element.179.refs_2_), channel_id=1, source_target_pairs={{0,4},{4,0},{8,12},{12,8},{16,20},{20,16},{24,28},{28,24},{1,5},{5... | collective-permute-start | bytes 3145736 | tf_op jit(solution)/shard_map/ppermute | solution.py:45
  170.4 25.5 %collective-permute-start.19 = (bf16[128,2048]{1,0:T(8,128)(2,1)S(1)}, bf16[128,2048]{1,0:T(8,128)(2,1)S(1)}, u32[]{:S(2)}, u32[]{:S(2)}) collective-permute-start(bf16[128,2048]{1,0:T(8,128)(2,1)S(1)} %get-tuple-element.174), channel_id=1, source_target_pairs={{0,1},{1,2},{2,3},{3,0},{4,5},{5,6},{6,7},{7,4},{8,9},{9,10},{10,1... | collective-permute-start | bytes 1572872 | tf_op jit(solution)/shard_map/ppermute | solution.py:41
  171.8 24.9 %collective-permute-start.18 = (bf16[128,2048]{1,0:T(8,128)(2,1)S(1)}, bf16[128,2048]{1,0:T(8,128)(2,1)S(1)}, u32[]{:S(2)}, u32[]{:S(2)}) collective-permute-start(bf16[128,2048]{1,0:T(8,128)(2,1)S(1)} %get-tuple-element.171), channel_id=1, source_target_pairs={{0,3},{1,0},{2,1},{3,2},{4,7},{5,4},{6,5},{7,6},{8,11},{9,8},{10,9... | collective-permute-start | bytes 1572872 | tf_op jit(solution)/shard_map/ppermute | solution.py:41
  200.0 16.5 %collective-permute-start.27 = (bf16[2,256,2048]{2,1,0:T(8,128)(2,1)}, bf16[2,256,2048]{2,1,0:T(8,128)(2,1)}, u32[]{:S(2)}, u32[]{:S(2)}) collective-permute-start(bf16[2,256,2048]{2,1,0:T(8,128)(2,1)} %get-tuple-element.193.refs_1_), channel_id=1, source_target_pairs={{0,4},{4,0},{8,12},{12,8},{16,20},{20,16},{24,28},{28,24},{1,5},{5... | collective-permute-start | bytes 6291464 | tf_op jit(solution)/shard_map/ppermute | solution.py:45
  200.2 16.0 %collective-permute-start.20 = (bf16[128,2048]{1,0:T(8,128)(2,1)S(1)}, bf16[128,2048]{1,0:T(8,128)(2,1)S(1)}, u32[]{:S(2)}, u32[]{:S(2)}) collective-permute-start(bf16[128,2048]{1,0:T(8,128)(2,1)S(1)} %ring_sum.6), channel_id=1, source_target_pairs={{0,1},{1,2},{2,3},{3,0},{4,5},{5,6},{6,7},{7,4},{8,9},{9,10},{10,1... | collective-permute-start | bytes 1572872 | tf_op jit(solution)/shard_map/ppermute | solution.py:41
  212.4 25.8 %collective-permute-start.28 = (bf16[2,1024,256]{2,1,0:T(8,128)(2,1)}, bf16[2,1024,256]{2,1,0:T(8,128)(2,1)}, u32[]{:S(2)}, u32[]{:S(2)}) collective-permute-start(bf16[2,1024,256]{2,1,0:T(8,128)(2,1)} %get-tuple-element.184), channel_id=1, source_target_pairs={{0,8},{4,12},{8,0},{12,4},{16,24},{20,28},{24,16},{28,20},{1,9},{5... | collective-permute-start | bytes 3145736 | tf_op jit(solution)/shard_map/ppermute | solution.py:45
  212.7 25.5 %collective-permute-start.29 = (bf16[2,1024,256]{2,1,0:T(8,128)(2,1)}, bf16[2,1024,256]{2,1,0:T(8,128)(2,1)}, u32[]{:S(2)}, u32[]{:S(2)}) collective-permute-start(bf16[2,1024,256]{2,1,0:T(8,128)(2,1)} %get-tuple-element.194), channel_id=1, source_target_pairs={{0,16},{4,20},{8,24},{12,28},{16,0},{20,4},{24,8},{28,12},{1,17},{... | collective-permute-start | bytes 3145736 | tf_op jit(solution)/shard_map/ppermute | solution.py:45
  216.4 16.0 %collective-permute-start.25 = (bf16[128,2048]{1,0:T(8,128)(2,1)S(1)}, bf16[128,2048]{1,0:T(8,128)(2,1)S(1)}, u32[]{:S(2)}, u32[]{:S(2)}) collective-permute-start(bf16[128,2048]{1,0:T(8,128)(2,1)S(1)} %ring_sum.7), channel_id=1, source_target_pairs={{0,1},{1,2},{2,3},{3,0},{4,5},{5,6},{6,7},{7,4},{8,9},{9,10},{10,1... | collective-permute-start | bytes 1572872 | tf_op jit(solution)/shard_map/ppermute | solution.py:41
  239.3 13.5 %collective-permute-start.30 = (bf16[128,2048]{1,0:T(8,128)(2,1)S(1)}, bf16[128,2048]{1,0:T(8,128)(2,1)S(1)}, u32[]{:S(2)}, u32[]{:S(2)}) collective-permute-start(bf16[128,2048]{1,0:T(8,128)(2,1)S(1)} %copy-done.37), channel_id=1, source_target_pairs={{0,3},{1,0},{2,1},{3,2},{4,7},{5,4},{6,5},{7,6},{8,11},{9,8},{10,9... | collective-permute-start | bytes 1572872 | tf_op jit(solution)/shard_map/ppermute | solution.py:41
  257.1 9.7 %collective-permute-start.32 = (bf16[128,512]{1,0:T(8,128)(2,1)}, bf16[128,512]{1,0:T(8,128)(2,1)S(1)}, u32[]{:S(2)}, u32[]{:S(2)}) collective-permute-start(bf16[128,512]{1,0:T(8,128)(2,1)} %get-tuple-element.204), channel_id=1, source_target_pairs={{0,2},{1,3},{2,0},{3,1},{4,6},{5,7},{6,4},{7,5},{8,10},{9,11},{10,... | collective-permute-start | bytes 393224 | tf_op jit(solution)/shard_map/ppermute | solution.py:41
  257.1 9.7 %collective-permute-start.31 = (bf16[128,512]{1,0:T(8,128)(2,1)}, bf16[128,512]{1,0:T(8,128)(2,1)S(1)}, u32[]{:S(2)}, u32[]{:S(2)}) collective-permute-start(bf16[128,512]{1,0:T(8,128)(2,1)} %get-tuple-element.202), channel_id=1, source_target_pairs={{0,1},{1,2},{2,3},{3,0},{4,5},{5,6},{6,7},{7,4},{8,9},{9,10},{10,1... | collective-permute-start | bytes 393224 | tf_op jit(solution)/shard_map/ppermute | solution.py:41
  259.9 9.9 %collective-permute-start.37 = (bf16[128,256]{1,0:T(8,128)(2,1)S(1)}, bf16[128,256]{1,0:T(8,128)(2,1)S(1)}, u32[]{:S(2)}, u32[]{:S(2)}) collective-permute-start(bf16[128,256]{1,0:T(8,128)(2,1)S(1)} %get-tuple-element.220), channel_id=1, source_target_pairs={{0,4},{4,0},{8,12},{12,8},{16,20},{20,16},{24,28},{28,24},{1,5},{5... | collective-permute-start | bytes 196616 | tf_op jit(solution)/shard_map/ppermute | solution.py:45
  259.9 10.2 %collective-permute-start.38 = (bf16[128,256]{1,0:T(8,128)(2,1)S(1)}, bf16[128,256]{1,0:T(8,128)(2,1)S(1)}, u32[]{:S(2)}, u32[]{:S(2)}) collective-permute-start(bf16[128,256]{1,0:T(8,128)(2,1)S(1)} %get-tuple-element.221), channel_id=1, source_target_pairs={{0,8},{4,12},{8,0},{12,4},{16,24},{20,28},{24,16},{28,20},{1,9},{5... | collective-permute-start | bytes 196616 | tf_op jit(solution)/shard_map/ppermute | solution.py:45
  261.4 10.3 %collective-permute-start.39 = (bf16[128,256]{1,0:T(8,128)(2,1)S(1)}, bf16[128,256]{1,0:T(8,128)(2,1)S(1)}, u32[]{:S(2)}, u32[]{:S(2)}) collective-permute-start(bf16[128,256]{1,0:T(8,128)(2,1)S(1)} %get-tuple-element.222), channel_id=1, source_target_pairs={{0,12},{4,8},{8,4},{12,0},{16,28},{20,24},{24,20},{28,16},{1,13},{... | collective-permute-start | bytes 196616 | tf_op jit(solution)/shard_map/ppermute | solution.py:45
  266.8 30.0 %collective-permute-start.34 = (bf16[128,2048]{1,0:T(8,128)(2,1)S(1)}, bf16[128,2048]{1,0:T(8,128)(2,1)S(1)}, u32[]{:S(2)}, u32[]{:S(2)}) collective-permute-start(bf16[128,2048]{1,0:T(8,128)(2,1)S(1)} %collective-permute-done.30), channel_id=1, source_target_pairs={{0,3},{1,0},{2,1},{3,2},{4,7},{5,4},{6,5},{7,6},{8,11},{9,8},{10,9... | collective-permute-start | bytes 1572872 | tf_op jit(solution)/shard_map/ppermute | solution.py:41
  269.0 27.8 %collective-permute-start.35 = (bf16[128,2048]{1,0:T(8,128)(2,1)S(1)}, bf16[128,2048]{1,0:T(8,128)(2,1)S(1)}, u32[]{:S(2)}, u32[]{:S(2)}) collective-permute-start(bf16[128,2048]{1,0:T(8,128)(2,1)S(1)} %copy-done.35), channel_id=1, source_target_pairs={{0,1},{1,2},{2,3},{3,0},{4,5},{5,6},{6,7},{7,4},{8,9},{9,10},{10,1... | collective-permute-start | bytes 1572872 | tf_op jit(solution)/shard_map/ppermute | solution.py:41
  299.4 16.6 %collective-permute-start.44 = (bf16[128,2048]{1,0:T(8,128)(2,1)}, bf16[128,2048]{1,0:T(8,128)(2,1)S(1)}, u32[]{:S(2)}, u32[]{:S(2)}) collective-permute-start(bf16[128,2048]{1,0:T(8,128)(2,1)} %get-tuple-element.230), channel_id=1, source_target_pairs={{0,1},{1,2},{2,3},{3,0},{4,5},{5,6},{6,7},{7,4},{8,9},{9,10},{10,1... | collective-permute-start | bytes 1572872 | tf_op jit(solution)/shard_map/ppermute | solution.py:41
  303.1 10.9 %collective-permute-start.46 = (f32[5632]{0:T(1024)S(1)}, f32[5632]{0:T(1024)S(1)}, u32[]{:S(2)}, u32[]{:S(2)}) collective-permute-start(f32[5632]{0:T(1024)S(1)} %add.226), channel_id=1, source_target_pairs={{0,8},{4,12},{8,0},{12,4},{16,24},{20,28},{24,16},{28,20},{1,9},{5... | collective-permute-start | bytes 67592 | tf_op jit(solution)/shard_map/ppermute | solution.py:45
  314.1 31.4 %collective-permute-start.53 = (bf16[2,256,768]{2,1,0:T(8,128)(2,1)}, bf16[2,256,768]{2,1,0:T(8,128)(2,1)S(1)}, u32[]{:S(2)}, u32[]{:S(2)}) collective-permute-start(bf16[2,256,768]{2,1,0:T(8,128)(2,1)} %get-tuple-element.260), channel_id=1, source_target_pairs={{0,16},{4,20},{8,24},{12,28},{16,0},{20,4},{24,8},{28,12},{1,17},{... | collective-permute-start | bytes 2359304 | tf_op jit(solution)/shard_map/ppermute | solution.py:45
  314.6 32.3 %collective-permute-start.52 = (bf16[2,256,768]{2,1,0:T(8,128)(2,1)}, bf16[2,256,768]{2,1,0:T(8,128)(2,1)S(1)}, u32[]{:S(2)}, u32[]{:S(2)}) collective-permute-start(bf16[2,256,768]{2,1,0:T(8,128)(2,1)} %get-tuple-element.257), channel_id=1, source_target_pairs={{0,8},{4,12},{8,0},{12,4},{16,24},{20,28},{24,16},{28,20},{1,9},{5... | collective-permute-start | bytes 2359304 | tf_op jit(solution)/shard_map/ppermute | solution.py:45
  316.1 20.8 %collective-permute-start.49 = (bf16[128,2048]{1,0:T(8,128)(2,1)S(1)}, bf16[128,2048]{1,0:T(8,128)(2,1)S(1)}, u32[]{:S(2)}, u32[]{:S(2)}) collective-permute-start(bf16[128,2048]{1,0:T(8,128)(2,1)S(1)} %ring_sum.8), channel_id=1, source_target_pairs={{0,1},{1,2},{2,3},{3,0},{4,5},{5,6},{6,7},{7,4},{8,9},{9,10},{10,1... | collective-permute-start | bytes 1572872 | tf_op jit(solution)/shard_map/ppermute | solution.py:41
  324.7 12.3 %collective-permute-start.50 = (bf16[512,256]{1,0:T(8,128)(2,1)S(1)}, bf16[512,256]{1,0:T(8,128)(2,1)S(1)}, u32[]{:S(2)}, u32[]{:S(2)}) collective-permute-start(bf16[512,256]{1,0:T(8,128)(2,1)S(1)} %get-tuple-element.282), channel_id=1, source_target_pairs={{0,1},{1,2},{2,3},{3,0},{4,5},{5,6},{6,7},{7,4},{8,9},{9,10},{10,1... | collective-permute-start | bytes 786440 | tf_op jit(solution)/shard_map/ppermute | solution.py:41
  327.3 31.8 %collective-permute-start.54 = (f32[5632]{0:T(1024)S(1)}, f32[5632]{0:T(1024)S(1)}, u32[]{:S(2)}, u32[]{:S(2)}) collective-permute-start(f32[5632]{0:T(1024)S(1)} %add.227), channel_id=1, source_target_pairs={{0,16},{4,20},{8,24},{12,28},{16,0},{20,4},{24,8},{28,12},{1,17},{... | collective-permute-start | bytes 67592 | tf_op jit(solution)/shard_map/ppermute | solution.py:45
  337.1 22.6 %collective-permute-start.51 = (bf16[128,2048]{1,0:T(8,128)(2,1)S(1)}, bf16[128,2048]{1,0:T(8,128)(2,1)S(1)}, u32[]{:S(2)}, u32[]{:S(2)}) collective-permute-start(bf16[128,2048]{1,0:T(8,128)(2,1)S(1)} %ring_sum.9), channel_id=1, source_target_pairs={{0,1},{1,2},{2,3},{3,0},{4,5},{5,6},{6,7},{7,4},{8,9},{9,10},{10,1... | collective-permute-start | bytes 1572872 | tf_op jit(solution)/shard_map/ppermute | solution.py:41
  337.3 20.2 %collective-permute-start.55 = (bf16[512,256]{1,0:T(8,128)(2,1)S(1)}, bf16[512,256]{1,0:T(8,128)(2,1)S(1)}, u32[]{:S(2)}, u32[]{:S(2)}) collective-permute-start(bf16[512,256]{1,0:T(8,128)(2,1)S(1)} %ring_sum.10), channel_id=1, source_target_pairs={{0,1},{1,2},{2,3},{3,0},{4,5},{5,6},{6,7},{7,4},{8,9},{9,10},{10,1... | collective-permute-start | bytes 786440 | tf_op jit(solution)/shard_map/ppermute | solution.py:41
  345.5 16.2 %collective-permute-start.58 = (bf16[1,1024,256]{2,1,0:T(8,128)(2,1)}, bf16[1,1024,256]{2,1,0:T(8,128)(2,1)}, u32[]{:S(2)}, u32[]{:S(2)}) collective-permute-start(bf16[1,1024,256]{2,1,0:T(8,128)(2,1)} %get-tuple-element.272), channel_id=1, source_target_pairs={{0,8},{4,12},{8,0},{12,4},{16,24},{20,28},{24,16},{28,20},{1,9},{5... | collective-permute-start | bytes 1572872 | tf_op jit(solution)/shard_map/ppermute | solution.py:45
  346.9 15.4 %collective-permute-start.57 = (bf16[1,1024,256]{2,1,0:T(8,128)(2,1)}, bf16[1,1024,256]{2,1,0:T(8,128)(2,1)}, u32[]{:S(2)}, u32[]{:S(2)}) collective-permute-start(bf16[1,1024,256]{2,1,0:T(8,128)(2,1)} %get-tuple-element.270), channel_id=1, source_target_pairs={{0,16},{4,20},{8,24},{12,28},{16,0},{20,4},{24,8},{28,12},{1,17},{... | collective-permute-start | bytes 1572872 | tf_op jit(solution)/shard_map/ppermute | solution.py:45
  357.5 13.1 %collective-permute-start.60 = (bf16[1,256,768]{2,1,0:T(8,128)(2,1)}, bf16[1,256,768]{2,1,0:T(8,128)(2,1)S(1)}, u32[]{:S(2)}, u32[]{:S(2)}) collective-permute-start(bf16[1,256,768]{2,1,0:T(8,128)(2,1)} %get-tuple-element.261), channel_id=1, source_target_pairs={{0,16},{4,20},{8,24},{12,28},{16,0},{20,4},{24,8},{28,12},{1,17},{... | collective-permute-start | bytes 1179656 | tf_op jit(solution)/shard_map/ppermute | solution.py:45
  359.1 11.5 %collective-permute-start.61 = (bf16[1,256,768]{2,1,0:T(8,128)(2,1)}, bf16[1,256,768]{2,1,0:T(8,128)(2,1)S(1)}, u32[]{:S(2)}, u32[]{:S(2)}) collective-permute-start(bf16[1,256,768]{2,1,0:T(8,128)(2,1)} %get-tuple-element.275), channel_id=1, source_target_pairs={{0,8},{4,12},{8,0},{12,4},{16,24},{20,28},{24,16},{28,20},{1,9},{5... | collective-permute-start | bytes 1179656 | tf_op jit(solution)/shard_map/ppermute | solution.py:45
  361.7 11.6 %collective-permute-start.62 = (bf16[512,256]{1,0:T(8,128)(2,1)S(1)}, bf16[512,256]{1,0:T(8,128)(2,1)S(1)}, u32[]{:S(2)}, u32[]{:S(2)}) collective-permute-start(bf16[512,256]{1,0:T(8,128)(2,1)S(1)} %ring_sum.11), channel_id=1, source_target_pairs={{0,1},{1,2},{2,3},{3,0},{4,5},{5,6},{6,7},{7,4},{8,9},{9,10},{10,1... | collective-permute-start | bytes 786440 | tf_op jit(solution)/shard_map/ppermute | solution.py:41
  (87 other events, 734.0 us)
Sparse Core Ops, SparseCore 0:
  60.5 47.0 all-gather.2
  145.2 34.2 all-gather.4
  238.4 103.1 reduce-scatter.1

commit v7 on v6

--- a/solution.py
+++ b/solution.py
@@ -1092,7 +1092,7 @@
             held = jnp.concatenate([held, swapped(held, "seq", 2 * bit)], axis=0)
         halves[place] = held
         second_arrived.append(swapped(held, "seq", 2 * order[-1]))
-    grad_out = lax.all_gather(after(cotangent, tok_three), "chan", axis=0, tiled=True)
+    grad_out = lax.all_gather(after(cotangent, w_three, tok_one), "chan", axis=0, tiled=True)
     tok_blocks = [tokens, tok_one, tok_two, tok_three]
     for place, order in enumerate(orders):
         held = jnp.concatenate([halves[place], after(second_arrived[place], tok_two)], axis=0)

time: 383 us -> 383 us (level)
  no operation moved by 1% of the time
where the time goes in v7:
time: 383 us; the launch traced here: 382 us
  Pallas kernels  143 us (37%)
  waiting for transfers between devices  111 us (29%)
  starting transfers between devices  72.1 us (19%)
  local copies, waits for them, and re-layouts  23.3 us (6%)
  other arithmetic  17.1 us (4%)
  between operations  14.6 us (4%)
    ppermute x28, waiting for transfers between devices, turned(): lax.ppermute(block, axis, [(i, (i + distance) % count) for i in range(cou...  78.1 us
    pallas_call x2, Pallas kernels, feed_forward(): pl.pallas_call(functools.partial(ffn_body, count), grid_spec=pltpu.Prefet...  41.9 us
    ppermute x28, starting transfers between devices, turned(): lax.ppermute(block, axis, [(i, (i + distance) % count) for i in range(cou...  39.2 us
    ppermute x33, starting transfers between devices, swapped(): lax.ppermute(block, axis, [(i, i ^ bit) for i in range(lax.axis_size(axis...  28.8 us
    ppermute x33, waiting for transfers between devices, swapped(): lax.ppermute(block, axis, [(i, i ^ bit) for i in range(lax.axis_size(axis...  24.5 us
    pallas_call x2, Pallas kernels, __init__(): pl.pallas_call(functools.partial(product_body, slots, part, tiles, tall,...  17.7 us
    unnamed x138, local copies, waits for them, and re-layouts  16.4 us
    pallas_call x1, Pallas kernels, whole_product(): pl.pallas_call(functools.partial(whole_body, part, len(units[0])), grid=(...  14.9 us
  transfers between devices with their start and end apart: 66, of which 24 were waited for; matrix products, arithmetic and copies ran while one was open for 6% of the time, Pallas kernels for 36%

profile of v7, /device:TPU:0, one launch (start us, length us, event | category | flops | bytes accessed | tf_op | source)
XLA Modules:
  0.0 381.7 jit_solution(10323585796159237946)
XLA Ops:
  7.2 3.1 collective-permute-start.2
  11.3 2.1 collective-permute-start.1
  13.4 17.5 %collective-permute-done.1 = bf16[512,256]{1,0:T(8,128)(2,1)S(1)} collective-permute-done((bf16[512,256]{1,0:T(8,128)(2,1)S(1)}, bf16[512,256]{1,0:T(8,128)(2,1)S(1)}, u32[]{:S(2)}, u32[]{:S(2)}) %collective-permute-start.1) | collective-permute-done | bytes 262176 | tf_op jit(solution)/shard_map/ppermute | solution.py:41
  30.9 4.9 %collective-permute-done = bf16[512,256]{1,0:T(8,128)(2,1)S(1)} collective-permute-done((bf16[512,256]{1,0:T(8,128)(2,1)S(1)}, bf16[512,256]{1,0:T(8,128)(2,1)S(1)}, u32[]{:S(2)}, u32[]{:S(2)}) %collective-permute-start) | collective-permute-done | bytes 262176 | tf_op jit(solution)/shard_map/ppermute | solution.py:41
  35.7 3.8 %collective-permute-start.5 = (bf16[128,2048]{1,0:T(8,128)(2,1)}, bf16[128,2048]{1,0:T(8,128)(2,1)S(1)}, u32[]{:S(2)}, u32[]{:S(2)}) collective-permute-start(bf16[128,2048]{1,0:T(8,128)(2,1)} %refs_2_.1), channel_id=1, source_target_pairs={{0,3},{1,0},{2,1},{3,2},{4,7},{5,4},{6,5},{7,6},{8,11},{9,8},{10,9... | collective-permute-start | bytes 1572872 | tf_op jit(solution)/shard_map/ppermute | solution.py:41
  39.6 7.2 %collective-permute-done.3 = bf16[512,256]{1,0:T(8,128)(2,1)S(1)} collective-permute-done((bf16[512,256]{1,0:T(8,128)(2,1)S(1)}, bf16[512,256]{1,0:T(8,128)(2,1)S(1)}, u32[]{:S(2)}, u32[]{:S(2)}) %collective-permute-start.3) | collective-permute-done | bytes 262176 | tf_op jit(solution)/shard_map/ppermute | solution.py:41
  50.0 4.7 %collective-permute-done.5.refs_3_.refs_5_ = bf16[128,2048]{1,0:T(8,128)(2,1)S(1)} collective-permute-done((bf16[128,2048]{1,0:T(8,128)(2,1)}, bf16[128,2048]{1,0:T(8,128)(2,1)S(1)}, u32[]{:S(2)}, u32[]{:S(2)}) %collective-permute-start.5) | collective-permute-done | bytes 524320 | tf_op jit(solution)/shard_map/ppermute | solution.py:41
  60.4 15.1 %collective-permute-done.7.refs_2_.refs_4_ = bf16[128,2048]{1,0:T(8,128)(2,1)S(1)} collective-permute-done((bf16[128,2048]{1,0:T(8,128)(2,1)S(1)}, bf16[128,2048]{1,0:T(8,128)(2,1)S(1)}, u32[]{:S(2)}, u32[]{:S(2)}) %collective-permute-start.7) | collective-permute-done | bytes 524320 | tf_op jit(solution)/shard_map/ppermute | solution.py:41
  77.2 2.9 pad_maximum_fusion.refs_5_.refs_1_
  82.7 8.7 %in_projection.1 = (f32[512,512]{1,0:T(8,128)}, f32[512,512]{1,0:T(8,128)}, f32[512,512]{1,0:T(8,128)}, bf16[512,512]{1,0:T(8,128)(2,1)}, bf16[512,2048]{1,0:T(8,128)(2,1)}, /*index=5*/f32[512,1]{1,0:T(8,128)}) custom-call(bf16[128,2048]{1,0:T(8,128)(2,1)} %refs_2_.1, bf16[128,2048]{1,0:T(8,128)(2,1)} %copy-done.39, bf16[128,2048]{1,0:T(8,128)(2,1)} %copy-done.41, ...), custom_call_target="tpu_custom_call" | custom-call | flops 1024 | bytes 1024 | tf_op jit(solution)/shard_map/in_projection/pallas_call | solution.py:677
  92.3 2.4 collective-permute-start.10
  96.2 2.9 conv_forward.1
  99.1 8.4 %all-gather.3.cloned.1.call-done.refs_0_.refs_2_.refs_3_ = bf16[512,2048]{1,0:T(8,128)(2,1)} async-done(((bf16[128,2048]{1,0:T(8,128)(2,1)}), bf16[512,2048]{1,0:T(8,128)(2,1)}) %all-gather.3.cloned.1.call-update) | async-done | bytes 2097168 | tf_op jit(solution)/shard_map/all_gather | solution.py:1095
  109.0 2.4 collective-permute-start.11
  111.5 4.6 %collective-permute-done.13.refs_3_ = bf16[128,512]{1,0:T(8,128)(2,1)S(1)} collective-permute-done((bf16[128,512]{1,0:T(8,128)(2,1)}, bf16[128,512]{1,0:T(8,128)(2,1)S(1)}, u32[]{:S(2)}, u32[]{:S(2)}) %collective-permute-start.13) | collective-permute-done | bytes 131104 | tf_op jit(solution)/shard_map/ppermute | solution.py:41
  116.1 4.6 %collective-permute-done.12.refs_2_ = bf16[128,512]{1,0:T(8,128)(2,1)S(1)} collective-permute-done((bf16[128,512]{1,0:T(8,128)(2,1)}, bf16[128,512]{1,0:T(8,128)(2,1)S(1)}, u32[]{:S(2)}, u32[]{:S(2)}) %collective-permute-start.12) | collective-permute-done | bytes 131104 | tf_op jit(solution)/shard_map/ppermute | solution.py:41
  123.2 6.1 %mixer_rows.1 = (f32[128,2048]{1,0:T(8,128)S(1)}, bf16[128,2048]{1,0:T(8,128)(2,1)S(1)}, f32[128,1]{1,0:T(8,128)S(1)}, bf16[128,2048]{1,0:T(8,128)(2,1)}) custom-call(s32[5]{0:T(128)S(1)} %pad_add_fusion.ids, bf16[128,512]{1,0:T(8,128)(2,1)S(1)} %copy-done.24, bf16[128,512]{1,0:T(8,128)(2,1)S(1)} %collective-permute-done.11.refs_1_, ...), custom_call_target="tpu_custom_call" | custom-call | flops 1024 | bytes 1024 | tf_op jit(solution)/shard_map/mixer_rows/pallas_call | solution.py:917
  130.9 2.5 collective-permute-start.15
  139.2 5.8 %collective-permute-done.15.refs_1_ = bf16[128,2048]{1,0:T(8,128)(2,1)S(1)} collective-permute-done((bf16[128,2048]{1,0:T(8,128)(2,1)S(1)}, bf16[128,2048]{1,0:T(8,128)(2,1)S(1)}, u32[]{:S(2)}, u32[]{:S(2)}) %collective-permute-start.15) | collective-permute-done | bytes 524320 | tf_op jit(solution)/shard_map/ppermute | solution.py:41
  145.1 1.8 collective-permute-start.17
  147.2 21.1 %feed_forward.2 = (bf16[1,256,2048]{2,1,0:T(8,128)(2,1)S(1)}, bf16[2,256,2048]{2,1,0:T(8,128)(2,1)}, bf16[128,2048]{1,0:T(8,128)(2,1)S(1)}, bf16[128,2048]{1,0:T...) custom-call(s32[4]{0:T(128)S(1)} %and_select_fusion.ids, ...), custom_call_target="tpu_custom_call" | custom-call | flops 1024 | bytes 1024 | tf_op jit(solution)/shard_map/feed_forward/pallas_call | solution.py:141
  171.8 2.5 collective-permute-start.18
  174.3 20.8 %feed_forward.3 = (bf16[1,256,2048]{2,1,0:T(8,128)(2,1)S(1)}, bf16[2,256,2048]{2,1,0:T(8,128)(2,1)}, bf16[128,2048]{1,0:T(8,128)(2,1)S(1)}, bf16[128,2048]{1,0:T...) custom-call(s32[4]{0:T(128)S(1)} %and_select_fusion.ids, ...), custom_call_target="tpu_custom_call" | custom-call | flops 1024 | bytes 1024 | tf_op jit(solution)/shard_map/feed_forward/pallas_call | solution.py:141
  197.3 2.8 collective-permute-done.24.refs_5_
  201.6 8.9 %product.2 = (bf16[2,1024,256]{2,1,0:T(8,128)(2,1)}, bf16[2,1024,256]{2,1,0:T(8,128)(2,1)}, bf16[2,1024,256]{2,1,0:T(8,128)(2,1)}, bf16[2,1024,256]{2,1,0:T(8,128)(2,1)}) custom-call(bf16[512,1024]{1,0:T(8,128)(2,1)} %copy-done.15, bf16[512,1024]{1,0:T(8,128)(2,1)} %collective-permute-done.21.refs_1_, bf16[1,256,2048]{2,1,0:T(8,128)(2,1)} %copy-done.16, ...), custom_call_target="tpu_custom_call" | custom-call | flops 1024 | bytes 1024 | tf_op jit(solution)/shard_map/product/pallas_call | solution.py:337
  213.1 3.1 collective-permute-done.20.a
  217.5 14.9 %whole_product.1 = bf16[4,2,256,2048]{3,2,1,0:T(8,128)(2,1)} custom-call(bf16[512,1024]{1,0:T(8,128)(2,1)} %copy-done.14, bf16[512,1024]{1,0:T(8,128)(2,1)} %copy-done.44, bf16[2,256,2048]{2,1,0:T(8,128)(2,1)} %get-tuple-element.182.refs_0_, bf16[2,256,2048]{2,1,0:T(8,128)(2,1)} %get-tuple-element.193.refs_1_, bf16[2,256,2048]{2,1,0:T(8,128)(2,1)} %copy-done.38, ...), custom_call_target="tpu_custom_call" | custom-call | flops 1024 | bytes 1024 | tf_op jit(solution)/shard_map/whole_product/pallas_call | solution.py:416
  232.4 5.8 %collective-permute-done.28.refs_1_ = bf16[2,1024,256]{2,1,0:T(8,128)(2,1)} collective-permute-done((bf16[2,1024,256]{2,1,0:T(8,128)(2,1)}, bf16[2,1024,256]{2,1,0:T(8,128)(2,1)}, u32[]{:S(2)}, u32[]{:S(2)}) %collective-permute-start.28) | collective-permute-done | bytes 1048608 | tf_op jit(solution)/shard_map/ppermute | solution.py:45
  239.3 2.5 collective-permute-start.30
  241.9 10.3 %gated_rows.1 = (bf16[128,512]{1,0:T(8,128)(2,1)}, bf16[128,512]{1,0:T(8,128)(2,1)}, bf16[128,512]{1,0:T(8,128)(2,1)}, bf16[128,512]{1,0:T(8,128)(2,1)}, f32[128...) custom-call(s32[5]{0:T(128)} %copy-done.28, bf16[512,2048]{1,0:T(8,128)(2,1)} %refs_0_.2, ...), custom_call_target="tpu_custom_call" | custom-call | flops 1024 | bytes 1024 | tf_op jit(solution)/shard_map/gated_rows/pallas_call | solution.py:1006
  252.8 4.3 %collective-permute-start.33 = (bf16[128,512]{1,0:T(8,128)(2,1)}, bf16[128,512]{1,0:T(8,128)(2,1)S(1)}, u32[]{:S(2)}, u32[]{:S(2)}) collective-permute-start(bf16[128,512]{1,0:T(8,128)(2,1)} %get-tuple-element.206), channel_id=1, source_target_pairs={{0,3},{1,0},{2,1},{3,2},{4,7},{5,4},{6,5},{7,6},{8,11},{9,8},{10,9... | collective-permute-start | bytes 393224 | tf_op jit(solution)/shard_map/ppermute | solution.py:41
  261.8 5.0 %collective-permute-done.32.refs_2_ = bf16[128,512]{1,0:T(8,128)(2,1)S(1)} collective-permute-done((bf16[128,512]{1,0:T(8,128)(2,1)}, bf16[128,512]{1,0:T(8,128)(2,1)S(1)}, u32[]{:S(2)}, u32[]{:S(2)}) %collective-permute-start.32) | collective-permute-done | bytes 131104 | tf_op jit(solution)/shard_map/ppermute | solution.py:41
  266.8 2.3 collective-permute-start.34
  271.7 2.6 collective-permute-start.41
  277.3 1.8 collective-permute-done.41.refs_5_
  279.1 3.7 collective-permute-done.42.refs_6_
  283.2 5.6 %conv_backward.1 = (bf16[3,512,512]{2,1,0:T(8,128)(2,1)}, f32[3,512]{1,0:T(4,128)}) custom-call(bf16[128,512]{1,0:T(8,128)(2,1)} %get-tuple-element.200.refs_0_, bf16[128,512]{1,0:T(8,128)(2,1)} %copy-done.55, bf16[128,512]{1,0:T(8,128)(2,1)} %copy-done.54, bf16[128,512]{1,0:T(8,128)(2,1)} %copy-done.53, f32[512,512]{1,0:T(8,128)} %get-tuple-element.214.refs_4_, ...), custom_call_target="tpu_custom_call" | custom-call | flops 1024 | bytes 1024 | tf_op jit(solution)/shard_map/conv_backward/pallas_call | solution.py:790
  288.9 7.9 %mixer_back.1 = (bf16[128,2048]{1,0:T(8,128)(2,1)}, bf16[128,2048]{1,0:T(8,128)(2,1)}, bf16[128,2048]{1,0:T(8,128)(2,1)}, bf16[128,2048]{1,0:T(8,128)(2,1)}, f32[1,2048]{1,0:T(1,128)}) custom-call(bf16[3,512,512]{2,1,0:T(8,128)(2,1)} %get-tuple-element.237.refs_0_.refs_2_, bf16[3,2048,512]{2,1,0:T(8,128)(2,1)} %refs_1_.1, bf16[128,2048]{1,0:T(8,128)(2,1)} %refs_2_.1, ...), custom_call_target="tpu_custom_call" | custom-call | flops 1024 | bytes 1024 | tf_op jit(solution)/shard_map/mixer_back/pallas_call | solution.py:834
  305.2 8.8 %product.3 = (bf16[2,256,768]{2,1,0:T(8,128)(2,1)}, bf16[2,256,768]{2,1,0:T(8,128)(2,1)}, bf16[2,256,768]{2,1,0:T(8,128)(2,1)}, bf16[2,256,768]{2,1,0:T(8,128)(2,1)}) custom-call(bf16[512,1024]{1,0:T(8,128)(2,1)} %copy-done.13, bf16[512,1024]{1,0:T(8,128)(2,1)} %copy-done.43, bf16[3,512,512]{2,1,0:T(8,128)(2,1)} %get-tuple-element.237.refs_0_.refs_2_, ...), custom_call_target="tpu_custom_call" | custom-call | flops 1024 | bytes 1024 | tf_op jit(solution)/shard_map/product/pallas_call | solution.py:337
  317.7 5.9 %rows_product.1 = bf16[4,512,256]{2,1,0:T(8,128)(2,1)} custom-call(s32[8]{0:T(128)} %copy-done.29, bf16[1024,2048]{1,0:T(8,128)(2,1)} %all-gather.5.cloned.1.call-done.gated, bf16[128,256]{1,0:T(8,128)(2,1)} %copy-done.27, bf16[128,256]{1,0:T(8,128)(2,1)} %copy-done.57, bf16[128,256]{1,0:T(8,128)(2,1)} %copy-done.58, bf16[128,256]{1,0:T(8,128)(2,1)} %copy-done.59, ...), custom_call_target="tpu_custom_call" | custom-call | flops 1024 | bytes 1024 | tf_op jit(solution)/shard_map/rows_product/pallas_call | solution.py:603
  328.6 4.0 %upper_sums.2 = (bf16[1,1024,256]{2,1,0:T(8,128)(2,1)}, bf16[1,1024,256]{2,1,0:T(8,128)(2,1)}) custom-call(bf16[2,1024,256]{2,1,0:T(8,128)(2,1)} %get-tuple-element.269.refs_0_, bf16[2,1024,256]{2,1,0:T(8,128)(2,1)} %collective-permute-done.28.refs_1_, bf16[2,1024,256]{2,1,0:T(8,128)(2,1)} %get-tuple-element.248.refs_2_.refs_3_, ...), custom_call_target="tpu_custom_call" | custom-call | flops 1024 | bytes 1024 | tf_op jit(solution)/shard_map/upper_sums/pallas_call | solution.py:473
  332.6 4.4 %collective-permute-done.50.a = bf16[512,256]{1,0:T(8,128)(2,1)S(1)} collective-permute-done((bf16[512,256]{1,0:T(8,128)(2,1)S(1)}, bf16[512,256]{1,0:T(8,128)(2,1)S(1)}, u32[]{:S(2)}, u32[]{:S(2)}) %collective-permute-start.50) | collective-permute-done | bytes 262176 | tf_op jit(solution)/shard_map/ppermute | solution.py:41
  338.6 6.9 %collective-permute-done.53.refs_3_.refs_4_ = bf16[2,256,768]{2,1,0:T(8,128)(2,1)S(1)} collective-permute-done((bf16[2,256,768]{2,1,0:T(8,128)(2,1)}, bf16[2,256,768]{2,1,0:T(8,128)(2,1)S(1)}, u32[]{:S(2)}, u32[]{:S(2)}) %collective-permute-start.53) | collective-permute-done | bytes 786464 | tf_op jit(solution)/shard_map/ppermute | solution.py:45
  347.5 2.4 add_convert_fusion
  349.9 3.8 %upper_sums.3 = (bf16[1,256,768]{2,1,0:T(8,128)(2,1)}, bf16[1,256,768]{2,1,0:T(8,128)(2,1)}) custom-call(bf16[2,256,768]{2,1,0:T(8,128)(2,1)} %get-tuple-element.274.refs_0_, bf16[2,256,768]{2,1,0:T(8,128)(2,1)} %copy-done.10, bf16[2,256,768]{2,1,0:T(8,128)(2,1)} %get-tuple-element.258.refs_2_.refs_3_, bf16[2,256,768]{2,1,0:T(8,128)(2,1)} %copy-done.8), custom_call_target="tpu_custom_call" | custom-call | flops 1024 | bytes 1024 | tf_op jit(solution)/shard_map/upper_sums/pallas_call | solution.py:473
  353.7 3.8 final_sums.2
  362.3 4.4 %final_sums.3 = f32[2048,256]{1,0:T(8,128)} custom-call(bf16[2,1024,256]{2,1,0:T(8,128)(2,1)} %get-tuple-element.269.refs_0_, bf16[2,1024,256]{2,1,0:T(8,128)(2,1)} %collective-permute-done.28.refs_1_, bf16[1,1024,256]{2,1,0:T(8,128)(2,1)} %collective-permute-done.57.refs_2_, bf16[2,1024,256]{2,1,0:T(8,128)(2,1)} %get-tuple-element.248.refs_2_.refs_3_, ...), custom_call_target="tpu_custom_call" | custom-call | flops 1024 | bytes 1024 | tf_op jit(solution)/shard_map/final_sums/pallas_call | solution.py:516
  366.8 2.5 collective-permute-start.59
  (308 shorter events, 82.8 us)
Async XLA Ops:
  7.2 100.4 %all-gather.3.cloned.1.call-start = ((), (), s32[]{:S(2)}) async-start(), calls=%async_computation.1 | async-start | bytes 2621440 | tf_op jit(solution)/shard_map/all_gather | solution.py:1095
  7.2 28.5 %collective-permute-start.2 = (bf16[128,2048]{1,0:T(8,128)(2,1)}, bf16[128,2048]{1,0:T(8,128)(2,1)S(1)}, u32[]{:S(2)}, u32[]{:S(2)}) collective-permute-start(bf16[128,2048]{1,0:T(8,128)(2,1)} %refs_2_.1), channel_id=1, source_target_pairs={{0,1},{1,2},{2,3},{3,0},{4,5},{5,6},{6,7},{7,4},{8,9},{9,10},{10,1... | collective-permute-start | bytes 1572872 | tf_op jit(solution)/shard_map/ppermute | solution.py:41
  11.3 19.6 %collective-permute-start.1 = (bf16[512,256]{1,0:T(8,128)(2,1)S(1)}, bf16[512,256]{1,0:T(8,128)(2,1)S(1)}, u32[]{:S(2)}, u32[]{:S(2)}) collective-permute-start(bf16[512,256]{1,0:T(8,128)(2,1)S(1)} %constant_dynamic-slice_fusion), channel_id=1, source_target_pairs={{0,3},{1,0},{2,1},{3,2},{4,7},{5,4},{6,5},{7,6},{8,11},{9,8},{10,9... | collective-permute-start | bytes 786440 | tf_op jit(solution)/shard_map/ppermute | solution.py:41
  13.4 22.4 %collective-permute-start = (bf16[512,256]{1,0:T(8,128)(2,1)S(1)}, bf16[512,256]{1,0:T(8,128)(2,1)S(1)}, u32[]{:S(2)}, u32[]{:S(2)}) collective-permute-start(bf16[512,256]{1,0:T(8,128)(2,1)S(1)} %constant_dynamic-slice_fusion), channel_id=1, source_target_pairs={{0,1},{1,2},{2,3},{3,0},{4,5},{5,6},{6,7},{7,4},{8,9},{9,10},{10,1... | collective-permute-start | bytes 786440 | tf_op jit(solution)/shard_map/ppermute | solution.py:41
  35.7 11.0 %collective-permute-start.3 = (bf16[512,256]{1,0:T(8,128)(2,1)S(1)}, bf16[512,256]{1,0:T(8,128)(2,1)S(1)}, u32[]{:S(2)}, u32[]{:S(2)}) collective-permute-start(bf16[512,256]{1,0:T(8,128)(2,1)S(1)} %collective-permute-done), channel_id=1, source_target_pairs={{0,1},{1,2},{2,3},{3,0},{4,5},{5,6},{6,7},{7,4},{8,9},{9,10},{10,1... | collective-permute-start | bytes 786440 | tf_op jit(solution)/shard_map/ppermute | solution.py:41
  35.7 19.0 %collective-permute-start.5 = (bf16[128,2048]{1,0:T(8,128)(2,1)}, bf16[128,2048]{1,0:T(8,128)(2,1)S(1)}, u32[]{:S(2)}, u32[]{:S(2)}) collective-permute-start(bf16[128,2048]{1,0:T(8,128)(2,1)} %refs_2_.1), channel_id=1, source_target_pairs={{0,3},{1,0},{2,1},{3,2},{4,7},{5,4},{6,5},{7,6},{8,11},{9,8},{10,9... | collective-permute-start | bytes 1572872 | tf_op jit(solution)/shard_map/ppermute | solution.py:41
  55.8 19.8 %collective-permute-start.9 = (bf16[2,3,256,256]{3,2,1,0:T(8,128)(2,1)}, bf16[2,3,256,256]{3,2,1,0:T(8,128)(2,1)}, u32[]{:S(2)}, u32[]{:S(2)}) collective-permute-start(bf16[2,3,256,256]{3,2,1,0:T(8,128)(2,1)} %pad_maximum_fusion.3), channel_id=1, source_target_pairs={{0,8},{4,12},{8,0},{12,4},{16,24},{20,28},{24,16},{28,20},{1,9},{5... | collective-permute-start | bytes 2359304 | tf_op jit(solution)/shard_map/ppermute | solution.py:45
  58.2 19.0 %collective-permute-start.6 = (bf16[2,3,256,256]{3,2,1,0:T(8,128)(2,1)}, bf16[2,3,256,256]{3,2,1,0:T(8,128)(2,1)}, u32[]{:S(2)}, u32[]{:S(2)}) collective-permute-start(bf16[2,3,256,256]{3,2,1,0:T(8,128)(2,1)} %pad_maximum_fusion.2), channel_id=1, source_target_pairs={{0,16},{4,20},{8,24},{12,28},{16,0},{20,4},{24,8},{28,12},{1,17},{... | collective-permute-start | bytes 2359304 | tf_op jit(solution)/shard_map/ppermute | solution.py:45
  59.7 15.8 %collective-permute-start.7 = (bf16[128,2048]{1,0:T(8,128)(2,1)S(1)}, bf16[128,2048]{1,0:T(8,128)(2,1)S(1)}, u32[]{:S(2)}, u32[]{:S(2)}) collective-permute-start(bf16[128,2048]{1,0:T(8,128)(2,1)S(1)} %collective-permute-done.2.refs_1_.refs_3_), channel_id=1, source_target_pairs={{0,1},{1,2},{2,3},{3,0},{4,5},{5,6},{6,7},{7,4},{8,9},{9,10},{10,1... | collective-permute-start | bytes 1572872 | tf_op jit(solution)/shard_map/ppermute | solution.py:41
  60.4 177.9 %all-gather.5.cloned.1.call-start = ((), (), s32[]{:S(2)}) async-start(), calls=%async_computation.2 | async-start | bytes 4718592 | tf_op jit(solution)/shard_map/all_gather | solution.py:1144
  80.1 40.6 %collective-permute-start.14 = (bf16[4,3,512,256]{3,2,1,0:T(8,128)(2,1)}, bf16[4,3,512,256]{3,2,1,0:T(8,128)(2,1)}, u32[]{:S(2)}, u32[]{:S(2)}) collective-permute-start(bf16[4,3,512,256]{3,2,1,0:T(8,128)(2,1)} %pad_maximum_fusion.refs_5_.refs_1_), channel_id=1, source_target_pairs={{0,4},{4,0},{8,12},{12,8},{16,20},{20,16},{24,28},{28,24},{1,5},{5... | collective-permute-start | bytes 9437192 | tf_op jit(solution)/shard_map/ppermute | solution.py:45
  107.6 13.1 %collective-permute-start.12 = (bf16[128,512]{1,0:T(8,128)(2,1)}, bf16[128,512]{1,0:T(8,128)(2,1)S(1)}, u32[]{:S(2)}, u32[]{:S(2)}) collective-permute-start(bf16[128,512]{1,0:T(8,128)(2,1)} %get-tuple-element.158), channel_id=1, source_target_pairs={{0,2},{1,3},{2,0},{3,1},{4,6},{5,7},{6,4},{7,5},{8,10},{9,11},{10,... | collective-permute-start | bytes 393224 | tf_op jit(solution)/shard_map/ppermute | solution.py:41
  109.0 11.7 %collective-permute-start.11 = (bf16[128,512]{1,0:T(8,128)(2,1)}, bf16[128,512]{1,0:T(8,128)(2,1)S(1)}, u32[]{:S(2)}, u32[]{:S(2)}) collective-permute-start(bf16[128,512]{1,0:T(8,128)(2,1)} %get-tuple-element.156), channel_id=1, source_target_pairs={{0,3},{1,0},{2,1},{3,2},{4,7},{5,4},{6,5},{7,6},{8,11},{9,8},{10,9... | collective-permute-start | bytes 393224 | tf_op jit(solution)/shard_map/ppermute | solution.py:41
  130.9 14.1 %collective-permute-start.15 = (bf16[128,2048]{1,0:T(8,128)(2,1)S(1)}, bf16[128,2048]{1,0:T(8,128)(2,1)S(1)}, u32[]{:S(2)}, u32[]{:S(2)}) collective-permute-start(bf16[128,2048]{1,0:T(8,128)(2,1)S(1)} %get-tuple-element.170.refs_0_), channel_id=1, source_target_pairs={{0,1},{1,2},{2,3},{3,0},{4,5},{5,6},{6,7},{7,4},{8,9},{9,10},{10,1... | collective-permute-start | bytes 1572872 | tf_op jit(solution)/shard_map/ppermute | solution.py:41
  145.0 208.7 %reduce-scatter.2.cloned.1.call-start = ((), (), s32[]{:S(2)}) async-start(), calls=%async_computation.3 | async-start | bytes 10485760 | tf_op jit(solution)/shard_map/reduce_scatter | solution.py:435
  145.1 24.8 %collective-permute-start.17 = (bf16[128,2048]{1,0:T(8,128)(2,1)S(1)}, bf16[128,2048]{1,0:T(8,128)(2,1)S(1)}, u32[]{:S(2)}, u32[]{:S(2)}) collective-permute-start(bf16[128,2048]{1,0:T(8,128)(2,1)S(1)} %get-tuple-element.170.refs_0_), channel_id=1, source_target_pairs={{0,3},{1,0},{2,1},{3,2},{4,7},{5,4},{6,5},{7,6},{8,11},{9,8},{10,9... | collective-permute-start | bytes 1572872 | tf_op jit(solution)/shard_map/ppermute | solution.py:41
  146.9 23.0 %collective-permute-start.16 = (bf16[128,2048]{1,0:T(8,128)(2,1)S(1)}, bf16[128,2048]{1,0:T(8,128)(2,1)S(1)}, u32[]{:S(2)}, u32[]{:S(2)}) collective-permute-start(bf16[128,2048]{1,0:T(8,128)(2,1)S(1)} %collective-permute-done.15.refs_1_), channel_id=1, source_target_pairs={{0,1},{1,2},{2,3},{3,0},{4,5},{5,6},{6,7},{7,4},{8,9},{9,10},{10,1... | collective-permute-start | bytes 1572872 | tf_op jit(solution)/shard_map/ppermute | solution.py:41
  169.9 26.8 %collective-permute-start.23 = (bf16[2,256,2048]{2,1,0:T(8,128)(2,1)}, bf16[2,256,2048]{2,1,0:T(8,128)(2,1)S(1)}, u32[]{:S(2)}, u32[]{:S(2)}) collective-permute-start(bf16[2,256,2048]{2,1,0:T(8,128)(2,1)} %get-tuple-element.182.refs_0_), channel_id=1, source_target_pairs={{0,4},{4,0},{8,12},{12,8},{16,20},{20,16},{24,28},{28,24},{1,5},{5... | collective-permute-start | bytes 6291464 | tf_op jit(solution)/shard_map/ppermute | solution.py:45
  169.9 26.7 %collective-permute-start.22 = (bf16[1,256,2048]{2,1,0:T(8,128)(2,1)S(1)}, bf16[1,256,2048]{2,1,0:T(8,128)(2,1)S(1)}, u32[]{:S(2)}, u32[]{:S(2)}) collective-permute-start(bf16[1,256,2048]{2,1,0:T(8,128)(2,1)S(1)} %get-tuple-element.179.refs_2_), channel_id=1, source_target_pairs={{0,4},{4,0},{8,12},{12,8},{16,20},{20,16},{24,28},{28,24},{1,5},{5... | collective-permute-start | bytes 3145736 | tf_op jit(solution)/shard_map/ppermute | solution.py:45
  170.4 25.5 %collective-permute-start.19 = (bf16[128,2048]{1,0:T(8,128)(2,1)S(1)}, bf16[128,2048]{1,0:T(8,128)(2,1)S(1)}, u32[]{:S(2)}, u32[]{:S(2)}) collective-permute-start(bf16[128,2048]{1,0:T(8,128)(2,1)S(1)} %get-tuple-element.174), channel_id=1, source_target_pairs={{0,1},{1,2},{2,3},{3,0},{4,5},{5,6},{6,7},{7,4},{8,9},{9,10},{10,1... | collective-permute-start | bytes 1572872 | tf_op jit(solution)/shard_map/ppermute | solution.py:41
  171.8 24.9 %collective-permute-start.18 = (bf16[128,2048]{1,0:T(8,128)(2,1)S(1)}, bf16[128,2048]{1,0:T(8,128)(2,1)S(1)}, u32[]{:S(2)}, u32[]{:S(2)}) collective-permute-start(bf16[128,2048]{1,0:T(8,128)(2,1)S(1)} %get-tuple-element.171), channel_id=1, source_target_pairs={{0,3},{1,0},{2,1},{3,2},{4,7},{5,4},{6,5},{7,6},{8,11},{9,8},{10,9... | collective-permute-start | bytes 1572872 | tf_op jit(solution)/shard_map/ppermute | solution.py:41
  200.0 16.5 %collective-permute-start.27 = (bf16[2,256,2048]{2,1,0:T(8,128)(2,1)}, bf16[2,256,2048]{2,1,0:T(8,128)(2,1)}, u32[]{:S(2)}, u32[]{:S(2)}) collective-permute-start(bf16[2,256,2048]{2,1,0:T(8,128)(2,1)} %get-tuple-element.193.refs_1_), channel_id=1, source_target_pairs={{0,4},{4,0},{8,12},{12,8},{16,20},{20,16},{24,28},{28,24},{1,5},{5... | collective-permute-start | bytes 6291464 | tf_op jit(solution)/shard_map/ppermute | solution.py:45
  200.2 16.0 %collective-permute-start.20 = (bf16[128,2048]{1,0:T(8,128)(2,1)S(1)}, bf16[128,2048]{1,0:T(8,128)(2,1)S(1)}, u32[]{:S(2)}, u32[]{:S(2)}) collective-permute-start(bf16[128,2048]{1,0:T(8,128)(2,1)S(1)} %ring_sum.6), channel_id=1, source_target_pairs={{0,1},{1,2},{2,3},{3,0},{4,5},{5,6},{6,7},{7,4},{8,9},{9,10},{10,1... | collective-permute-start | bytes 1572872 | tf_op jit(solution)/shard_map/ppermute | solution.py:41
  212.4 25.8 %collective-permute-start.28 = (bf16[2,1024,256]{2,1,0:T(8,128)(2,1)}, bf16[2,1024,256]{2,1,0:T(8,128)(2,1)}, u32[]{:S(2)}, u32[]{:S(2)}) collective-permute-start(bf16[2,1024,256]{2,1,0:T(8,128)(2,1)} %get-tuple-element.184), channel_id=1, source_target_pairs={{0,8},{4,12},{8,0},{12,4},{16,24},{20,28},{24,16},{28,20},{1,9},{5... | collective-permute-start | bytes 3145736 | tf_op jit(solution)/shard_map/ppermute | solution.py:45
  212.7 25.5 %collective-permute-start.29 = (bf16[2,1024,256]{2,1,0:T(8,128)(2,1)}, bf16[2,1024,256]{2,1,0:T(8,128)(2,1)}, u32[]{:S(2)}, u32[]{:S(2)}) collective-permute-start(bf16[2,1024,256]{2,1,0:T(8,128)(2,1)} %get-tuple-element.194), channel_id=1, source_target_pairs={{0,16},{4,20},{8,24},{12,28},{16,0},{20,4},{24,8},{28,12},{1,17},{... | collective-permute-start | bytes 3145736 | tf_op jit(solution)/shard_map/ppermute | solution.py:45
  216.4 16.0 %collective-permute-start.25 = (bf16[128,2048]{1,0:T(8,128)(2,1)S(1)}, bf16[128,2048]{1,0:T(8,128)(2,1)S(1)}, u32[]{:S(2)}, u32[]{:S(2)}) collective-permute-start(bf16[128,2048]{1,0:T(8,128)(2,1)S(1)} %ring_sum.7), channel_id=1, source_target_pairs={{0,1},{1,2},{2,3},{3,0},{4,5},{5,6},{6,7},{7,4},{8,9},{9,10},{10,1... | collective-permute-start | bytes 1572872 | tf_op jit(solution)/shard_map/ppermute | solution.py:41
  239.3 13.5 %collective-permute-start.30 = (bf16[128,2048]{1,0:T(8,128)(2,1)S(1)}, bf16[128,2048]{1,0:T(8,128)(2,1)S(1)}, u32[]{:S(2)}, u32[]{:S(2)}) collective-permute-start(bf16[128,2048]{1,0:T(8,128)(2,1)S(1)} %copy-done.37), channel_id=1, source_target_pairs={{0,3},{1,0},{2,1},{3,2},{4,7},{5,4},{6,5},{7,6},{8,11},{9,8},{10,9... | collective-permute-start | bytes 1572872 | tf_op jit(solution)/shard_map/ppermute | solution.py:41
  257.1 9.7 %collective-permute-start.32 = (bf16[128,512]{1,0:T(8,128)(2,1)}, bf16[128,512]{1,0:T(8,128)(2,1)S(1)}, u32[]{:S(2)}, u32[]{:S(2)}) collective-permute-start(bf16[128,512]{1,0:T(8,128)(2,1)} %get-tuple-element.204), channel_id=1, source_target_pairs={{0,2},{1,3},{2,0},{3,1},{4,6},{5,7},{6,4},{7,5},{8,10},{9,11},{10,... | collective-permute-start | bytes 393224 | tf_op jit(solution)/shard_map/ppermute | solution.py:41
  257.1 9.7 %collective-permute-start.31 = (bf16[128,512]{1,0:T(8,128)(2,1)}, bf16[128,512]{1,0:T(8,128)(2,1)S(1)}, u32[]{:S(2)}, u32[]{:S(2)}) collective-permute-start(bf16[128,512]{1,0:T(8,128)(2,1)} %get-tuple-element.202), channel_id=1, source_target_pairs={{0,1},{1,2},{2,3},{3,0},{4,5},{5,6},{6,7},{7,4},{8,9},{9,10},{10,1... | collective-permute-start | bytes 393224 | tf_op jit(solution)/shard_map/ppermute | solution.py:41
  259.9 9.9 %collective-permute-start.37 = (bf16[128,256]{1,0:T(8,128)(2,1)S(1)}, bf16[128,256]{1,0:T(8,128)(2,1)S(1)}, u32[]{:S(2)}, u32[]{:S(2)}) collective-permute-start(bf16[128,256]{1,0:T(8,128)(2,1)S(1)} %get-tuple-element.220), channel_id=1, source_target_pairs={{0,4},{4,0},{8,12},{12,8},{16,20},{20,16},{24,28},{28,24},{1,5},{5... | collective-permute-start | bytes 196616 | tf_op jit(solution)/shard_map/ppermute | solution.py:45
  259.9 10.2 %collective-permute-start.38 = (bf16[128,256]{1,0:T(8,128)(2,1)S(1)}, bf16[128,256]{1,0:T(8,128)(2,1)S(1)}, u32[]{:S(2)}, u32[]{:S(2)}) collective-permute-start(bf16[128,256]{1,0:T(8,128)(2,1)S(1)} %get-tuple-element.221), channel_id=1, source_target_pairs={{0,8},{4,12},{8,0},{12,4},{16,24},{20,28},{24,16},{28,20},{1,9},{5... | collective-permute-start | bytes 196616 | tf_op jit(solution)/shard_map/ppermute | solution.py:45
  261.4 10.3 %collective-permute-start.39 = (bf16[128,256]{1,0:T(8,128)(2,1)S(1)}, bf16[128,256]{1,0:T(8,128)(2,1)S(1)}, u32[]{:S(2)}, u32[]{:S(2)}) collective-permute-start(bf16[128,256]{1,0:T(8,128)(2,1)S(1)} %get-tuple-element.222), channel_id=1, source_target_pairs={{0,12},{4,8},{8,4},{12,0},{16,28},{20,24},{24,20},{28,16},{1,13},{... | collective-permute-start | bytes 196616 | tf_op jit(solution)/shard_map/ppermute | solution.py:45
  266.8 30.0 %collective-permute-start.34 = (bf16[128,2048]{1,0:T(8,128)(2,1)S(1)}, bf16[128,2048]{1,0:T(8,128)(2,1)S(1)}, u32[]{:S(2)}, u32[]{:S(2)}) collective-permute-start(bf16[128,2048]{1,0:T(8,128)(2,1)S(1)} %collective-permute-done.30), channel_id=1, source_target_pairs={{0,3},{1,0},{2,1},{3,2},{4,7},{5,4},{6,5},{7,6},{8,11},{9,8},{10,9... | collective-permute-start | bytes 1572872 | tf_op jit(solution)/shard_map/ppermute | solution.py:41
  269.0 27.8 %collective-permute-start.35 = (bf16[128,2048]{1,0:T(8,128)(2,1)S(1)}, bf16[128,2048]{1,0:T(8,128)(2,1)S(1)}, u32[]{:S(2)}, u32[]{:S(2)}) collective-permute-start(bf16[128,2048]{1,0:T(8,128)(2,1)S(1)} %copy-done.35), channel_id=1, source_target_pairs={{0,1},{1,2},{2,3},{3,0},{4,5},{5,6},{6,7},{7,4},{8,9},{9,10},{10,1... | collective-permute-start | bytes 1572872 | tf_op jit(solution)/shard_map/ppermute | solution.py:41
  299.4 16.6 %collective-permute-start.44 = (bf16[128,2048]{1,0:T(8,128)(2,1)}, bf16[128,2048]{1,0:T(8,128)(2,1)S(1)}, u32[]{:S(2)}, u32[]{:S(2)}) collective-permute-start(bf16[128,2048]{1,0:T(8,128)(2,1)} %get-tuple-element.230), channel_id=1, source_target_pairs={{0,1},{1,2},{2,3},{3,0},{4,5},{5,6},{6,7},{7,4},{8,9},{9,10},{10,1... | collective-permute-start | bytes 1572872 | tf_op jit(solution)/shard_map/ppermute | solution.py:41
  303.1 10.9 %collective-permute-start.46 = (f32[5632]{0:T(1024)S(1)}, f32[5632]{0:T(1024)S(1)}, u32[]{:S(2)}, u32[]{:S(2)}) collective-permute-start(f32[5632]{0:T(1024)S(1)} %add.226), channel_id=1, source_target_pairs={{0,8},{4,12},{8,0},{12,4},{16,24},{20,28},{24,16},{28,20},{1,9},{5... | collective-permute-start | bytes 67592 | tf_op jit(solution)/shard_map/ppermute | solution.py:45
  314.1 31.4 %collective-permute-start.53 = (bf16[2,256,768]{2,1,0:T(8,128)(2,1)}, bf16[2,256,768]{2,1,0:T(8,128)(2,1)S(1)}, u32[]{:S(2)}, u32[]{:S(2)}) collective-permute-start(bf16[2,256,768]{2,1,0:T(8,128)(2,1)} %get-tuple-element.260), channel_id=1, source_target_pairs={{0,16},{4,20},{8,24},{12,28},{16,0},{20,4},{24,8},{28,12},{1,17},{... | collective-permute-start | bytes 2359304 | tf_op jit(solution)/shard_map/ppermute | solution.py:45
  314.6 32.3 %collective-permute-start.52 = (bf16[2,256,768]{2,1,0:T(8,128)(2,1)}, bf16[2,256,768]{2,1,0:T(8,128)(2,1)S(1)}, u32[]{:S(2)}, u32[]{:S(2)}) collective-permute-start(bf16[2,256,768]{2,1,0:T(8,128)(2,1)} %get-tuple-element.257), channel_id=1, source_target_pairs={{0,8},{4,12},{8,0},{12,4},{16,24},{20,28},{24,16},{28,20},{1,9},{5... | collective-permute-start | bytes 2359304 | tf_op jit(solution)/shard_map/ppermute | solution.py:45
  316.1 20.8 %collective-permute-start.49 = (bf16[128,2048]{1,0:T(8,128)(2,1)S(1)}, bf16[128,2048]{1,0:T(8,128)(2,1)S(1)}, u32[]{:S(2)}, u32[]{:S(2)}) collective-permute-start(bf16[128,2048]{1,0:T(8,128)(2,1)S(1)} %ring_sum.8), channel_id=1, source_target_pairs={{0,1},{1,2},{2,3},{3,0},{4,5},{5,6},{6,7},{7,4},{8,9},{9,10},{10,1... | collective-permute-start | bytes 1572872 | tf_op jit(solution)/shard_map/ppermute | solution.py:41
  324.7 12.3 %collective-permute-start.50 = (bf16[512,256]{1,0:T(8,128)(2,1)S(1)}, bf16[512,256]{1,0:T(8,128)(2,1)S(1)}, u32[]{:S(2)}, u32[]{:S(2)}) collective-permute-start(bf16[512,256]{1,0:T(8,128)(2,1)S(1)} %get-tuple-element.282), channel_id=1, source_target_pairs={{0,1},{1,2},{2,3},{3,0},{4,5},{5,6},{6,7},{7,4},{8,9},{9,10},{10,1... | collective-permute-start | bytes 786440 | tf_op jit(solution)/shard_map/ppermute | solution.py:41
  327.3 31.8 %collective-permute-start.54 = (f32[5632]{0:T(1024)S(1)}, f32[5632]{0:T(1024)S(1)}, u32[]{:S(2)}, u32[]{:S(2)}) collective-permute-start(f32[5632]{0:T(1024)S(1)} %add.227), channel_id=1, source_target_pairs={{0,16},{4,20},{8,24},{12,28},{16,0},{20,4},{24,8},{28,12},{1,17},{... | collective-permute-start | bytes 67592 | tf_op jit(solution)/shard_map/ppermute | solution.py:45
  337.1 22.6 %collective-permute-start.51 = (bf16[128,2048]{1,0:T(8,128)(2,1)S(1)}, bf16[128,2048]{1,0:T(8,128)(2,1)S(1)}, u32[]{:S(2)}, u32[]{:S(2)}) collective-permute-start(bf16[128,2048]{1,0:T(8,128)(2,1)S(1)} %ring_sum.9), channel_id=1, source_target_pairs={{0,1},{1,2},{2,3},{3,0},{4,5},{5,6},{6,7},{7,4},{8,9},{9,10},{10,1... | collective-permute-start | bytes 1572872 | tf_op jit(solution)/shard_map/ppermute | solution.py:41
  337.3 20.2 %collective-permute-start.55 = (bf16[512,256]{1,0:T(8,128)(2,1)S(1)}, bf16[512,256]{1,0:T(8,128)(2,1)S(1)}, u32[]{:S(2)}, u32[]{:S(2)}) collective-permute-start(bf16[512,256]{1,0:T(8,128)(2,1)S(1)} %ring_sum.10), channel_id=1, source_target_pairs={{0,1},{1,2},{2,3},{3,0},{4,5},{5,6},{6,7},{7,4},{8,9},{9,10},{10,1... | collective-permute-start | bytes 786440 | tf_op jit(solution)/shard_map/ppermute | solution.py:41
  345.5 16.2 %collective-permute-start.58 = (bf16[1,1024,256]{2,1,0:T(8,128)(2,1)}, bf16[1,1024,256]{2,1,0:T(8,128)(2,1)}, u32[]{:S(2)}, u32[]{:S(2)}) collective-permute-start(bf16[1,1024,256]{2,1,0:T(8,128)(2,1)} %get-tuple-element.272), channel_id=1, source_target_pairs={{0,8},{4,12},{8,0},{12,4},{16,24},{20,28},{24,16},{28,20},{1,9},{5... | collective-permute-start | bytes 1572872 | tf_op jit(solution)/shard_map/ppermute | solution.py:45
  346.9 15.4 %collective-permute-start.57 = (bf16[1,1024,256]{2,1,0:T(8,128)(2,1)}, bf16[1,1024,256]{2,1,0:T(8,128)(2,1)}, u32[]{:S(2)}, u32[]{:S(2)}) collective-permute-start(bf16[1,1024,256]{2,1,0:T(8,128)(2,1)} %get-tuple-element.270), channel_id=1, source_target_pairs={{0,16},{4,20},{8,24},{12,28},{16,0},{20,4},{24,8},{28,12},{1,17},{... | collective-permute-start | bytes 1572872 | tf_op jit(solution)/shard_map/ppermute | solution.py:45
  357.5 13.1 %collective-permute-start.60 = (bf16[1,256,768]{2,1,0:T(8,128)(2,1)}, bf16[1,256,768]{2,1,0:T(8,128)(2,1)S(1)}, u32[]{:S(2)}, u32[]{:S(2)}) collective-permute-start(bf16[1,256,768]{2,1,0:T(8,128)(2,1)} %get-tuple-element.261), channel_id=1, source_target_pairs={{0,16},{4,20},{8,24},{12,28},{16,0},{20,4},{24,8},{28,12},{1,17},{... | collective-permute-start | bytes 1179656 | tf_op jit(solution)/shard_map/ppermute | solution.py:45
  359.1 11.5 %collective-permute-start.61 = (bf16[1,256,768]{2,1,0:T(8,128)(2,1)}, bf16[1,256,768]{2,1,0:T(8,128)(2,1)S(1)}, u32[]{:S(2)}, u32[]{:S(2)}) collective-permute-start(bf16[1,256,768]{2,1,0:T(8,128)(2,1)} %get-tuple-element.275), channel_id=1, source_target_pairs={{0,8},{4,12},{8,0},{12,4},{16,24},{20,28},{24,16},{28,20},{1,9},{5... | collective-permute-start | bytes 1179656 | tf_op jit(solution)/shard_map/ppermute | solution.py:45
  361.7 11.6 %collective-permute-start.62 = (bf16[512,256]{1,0:T(8,128)(2,1)S(1)}, bf16[512,256]{1,0:T(8,128)(2,1)S(1)}, u32[]{:S(2)}, u32[]{:S(2)}) collective-permute-start(bf16[512,256]{1,0:T(8,128)(2,1)S(1)} %ring_sum.11), channel_id=1, source_target_pairs={{0,1},{1,2},{2,3},{3,0},{4,5},{5,6},{6,7},{7,4},{8,9},{9,10},{10,1... | collective-permute-start | bytes 786440 | tf_op jit(solution)/shard_map/ppermute | solution.py:41
  (87 other events, 734.0 us)
Sparse Core Ops, SparseCore 0:
  60.5 47.0 all-gather.2
  145.2 34.2 all-gather.4
  238.4 103.1 reduce-scatter.1
